TPU v7x, 32 devices: a whole 2x2x4 slice. The times are simulated.
32 devices in a mesh: section: 2 (over core), row: 4 (over y, x), col: 4 (over z).
Axes of the slice: x: 2, y: 2, z: 4, core: 2. Of those that a mesh axis runs over, the one named last changes fastest.
Arguments:
- tokens: float32 [2, 2048, 1536], P(None, ('row', 'col')), may hold values from -6 to 6
- cotangent: float32 [2, 2048, 1536], P(None, ('row', 'col')), may hold values from -6 to 6
- doc_lengths: int32 [2, 4, 4], replicated, may hold values from 1 to 256, 512 in all within a row
- routes: int32 [2, 2, 2048, 6], P('section', None, ('row', 'col')), may hold values from 0 to 15, all different within a row; in each aligned block of 128 rows (0 to 127, 128 to 255, ..., all dimensions but the last counted through in order) at most 64 rows name the same one
- gates: float32 [2, 2, 2048, 6], P('section', None, ('row', 'col')), may hold values from 0.05 to 0.35
- norm_in: float32 [2, 1536], P('section'), may hold values from 0.5 to 1.5
- proj_gate: bfloat16 [2, 1536, 3072], P('section', 'row', 'col'), may hold values from -0.15625 to 0.15625
- proj_input: bfloat16 [2, 1536, 3072], P('section', 'row', 'col'), may hold values from -0.15625 to 0.15625
- proj_state: bfloat16 [2, 1536, 256], P('section', 'row'), may hold values from -0.15625 to 0.15625
- proj_step: bfloat16 [2, 1536, 48], P('section', 'row', 'col'), may hold values from -0.15625 to 0.15625
- step_bias: float32 [2, 48], P('section', 'col'), may hold values from -4 to -1
- decay_log: float32 [2, 48], P('section', 'col'), may hold values from 0 to 2.5
- skip_gain: float32 [2, 48], P('section', 'col'), may hold values from 0.5 to 1.5
- conv_input: float32 [2, 4, 3072], P('section', None, 'col'), may hold values from -3 to 3
- conv_state: float32 [2, 4, 256], P('section'), may hold values from -3 to 3
- gate_norm: float32 [2, 3072], P('section', 'col'), may hold values from 0.5 to 1.5
- proj_output: bfloat16 [2, 1536, 3072], P('section', 'row', 'col'), may hold values from -0.109375 to 0.109375
- norm_mid: float32 [2, 1536], P('section'), may hold values from 0.5 to 1.5
- expert_gate: bfloat16 [2, 16, 1536, 512], P('section', ('row', 'col')), may hold values from -0.15625 to 0.15625
- expert_up: bfloat16 [2, 16, 1536, 512], P('section', ('row', 'col')), may hold values from -0.15625 to 0.15625
- expert_down: bfloat16 [2, 16, 512, 1536], P('section', ('row', 'col')), may hold values from -0.25 to 0.25
- shared_gate: bfloat16 [2, 1536, 1024], P('section', 'row', 'col'), may hold values from -0.15625 to 0.15625
- shared_up: bfloat16 [2, 1536, 1024], P('section', 'row', 'col'), may hold values from -0.15625 to 0.15625
- shared_down: bfloat16 [2, 1536, 1024], P('section', 'row', 'col'), may hold values from -0.1875 to 0.1875
Outputs:
- layer_out: float32 [2, 2, 2048, 1536], P('section', None, ('row', 'col'))
- input_grad: float32 [2, 2, 2048, 1536], P('section', None, ('row', 'col'))
- grad_norm_in: float32 [2, 1536], P('section')
- grad_proj_gate: float32 [2, 1536, 3072], P('section', 'row', 'col')
- grad_proj_input: float32 [2, 1536, 3072], P('section', 'row', 'col')
- grad_proj_state: float32 [2, 1536, 256], P('section', 'row')
- grad_proj_step: float32 [2, 1536, 48], P('section', 'row', 'col')
- grad_step_bias: float32 [2, 48], P('section', 'col')
- grad_decay_log: float32 [2, 48], P('section', 'col')
- grad_skip_gain: float32 [2, 48], P('section', 'col')
- grad_conv_input: float32 [2, 4, 3072], P('section', None, 'col')
- grad_conv_state: float32 [2, 4, 256], P('section')
- grad_gate_norm: float32 [2, 3072], P('section', 'col')
- grad_proj_output: float32 [2, 1536, 3072], P('section', 'row', 'col')
- grad_norm_mid: float32 [2, 1536], P('section')
- grad_expert_gate: float32 [2, 16, 1536, 512], P('section', ('row', 'col'))
- grad_expert_up: float32 [2, 16, 1536, 512], P('section', ('row', 'col'))
- grad_expert_down: float32 [2, 16, 512, 1536], P('section', ('row', 'col'))
- grad_shared_gate: float32 [2, 1536, 1024], P('section', 'row', 'col')
- grad_shared_up: float32 [2, 1536, 1024], P('section', 'row', 'col')
- grad_shared_down: float32 [2, 1536, 1024], P('section', 'row', 'col')
Inputs may be any that keep to these rules, and one draw needn't show every extreme that they name: `doc_lengths`: each sequence's 4 lengths sum to 512; its longest document has exactly 256 tokens. `routes`: a token's 6 experts are distinct; in each layer and micro-batch the 128 tokens of one device name any one expert at most 64 times, a bound that some block reaches.
All inputs are finite; a program needn't handle non-finite values.
Results may differ from a plain program's by a relative error of at most 0.039.
Values may be sent and summed in bfloat16 or wider, within the bound.
No kernel may reach another device: no remote copies, remote signals or barrier semaphores. Data moves between devices by JAX's collectives and lax.ppermute only.
A program may use at most 448 MiB of HBM per device.

v0:
```python
import jax
import jax.numpy as jnp
from jax import lax
from jax.sharding import PartitionSpec as P

BLOCK = 512
DI = 3072


EPS = 1e-05
HIGH = lax.Precision.HIGHEST
FLOAT = jnp.float32
HALF = jnp.bfloat16


def passed_along(block, axis, distance):
    devices = range(lax.axis_size(axis))
    route = [(i - distance, i) for i in devices if i - distance in devices]
    return lax.ppermute(block, axis, route)


def shortened(value):
    return jax.tree.map(lambda a: a.astype(jnp.bfloat16) if a.dtype == jnp.float32 else a, value)


def rms_norm(value, gain):
    return value * lax.rsqrt(jnp.mean(value * value, axis=-1, keepdims=True) + EPS) * gain


def causal_conv(values, weight, docs):
    width = weight.shape[0]
    result = values * weight[width - 1]
    for back in range(1, width):
        moved = jnp.pad(values, ((back, 0), (0, 0)))[:-back]
        prior = jnp.pad(docs, (back, 0), constant_values=-1)[:-back]
        same = (prior == docs).astype(values.dtype)[:, None]
        result = result + moved * same * weight[width - 1 - back]
    return result


def ssd_scan(inputs, step_size, rate, state_in, state_out, docs, skip_gain):
    length, heads, width = inputs.shape
    count = length // BLOCK
    order = jnp.arange(BLOCK, dtype=jnp.int32)
    causal = order[:, None] >= order[None, :]

    def advance(carry, block):
        state, previous = carry
        values, sizes, keys, queries, labels = block
        logs = sizes * rate[None, :]
        running = jnp.cumsum(logs, axis=0)
        same = causal & (labels[:, None] == labels[None, :])
        spread_log = running[:, None, :] - running[None, :, :]
        decay = jnp.exp(jnp.where(same[:, :, None], spread_log, -1e30))
        scores = jnp.dot(queries, keys.T, precision=HIGH)
        mixing = decay * scores[:, :, None] * sizes[None, :, :]
        inner = jnp.einsum("tsh,shp->thp", mixing, values, precision=HIGH)
        carried = (labels == previous).astype(values.dtype)
        reach = jnp.exp(running) * carried[:, None]
        outer = jnp.einsum("tn,hpn->thp", queries, state, precision=HIGH) * reach[:, :, None]
        final = labels[BLOCK - 1]
        tail = (
            jnp.exp(running[BLOCK - 1][None, :] - running)
            * sizes
            * (labels == final).astype(values.dtype)[:, None]
        )
        kept = jnp.exp(running[BLOCK - 1]) * (final == previous).astype(values.dtype)
        fresh = jnp.einsum("sh,shp,sn->hpn", tail, values, keys, precision=HIGH)
        new_state = state * kept[:, None, None] + fresh
        output = inner + outer + skip_gain[None, :, None] * values
        return ((new_state, final), output)

    blocks = (
        inputs.reshape(count, BLOCK, heads, width),
        step_size.reshape(count, BLOCK, heads),
        state_in.reshape(count, BLOCK, -1),
        state_out.reshape(count, BLOCK, -1),
        docs.reshape(count, BLOCK),
    )
    start = (jnp.zeros((heads, width, state_in.shape[1]), inputs.dtype), jnp.array(-1, jnp.int32))
    _, result = lax.scan(jax.checkpoint(advance), start, blocks)
    return result.reshape(length, heads, width)


def mamba_core(
    gate_pre,
    input_pre,
    state_pre,
    step_pre,
    conv_input,
    conv_state,
    step_bias,
    decay_log,
    skip_gain,
    docs,
):
    heads = step_pre.shape[1]
    length = input_pre.shape[0]
    mixed_input = jax.nn.silu(causal_conv(input_pre, conv_input, docs))
    mixed_state = jax.nn.silu(causal_conv(state_pre, conv_state, docs))
    half = state_pre.shape[1] // 2
    step_size = jax.nn.softplus(step_pre + step_bias)
    rate = -jnp.exp(decay_log)
    result = ssd_scan(
        mixed_input.reshape(length, heads, -1),
        step_size,
        rate,
        mixed_state[:, :half],
        mixed_state[:, half:],
        docs,
        skip_gain,
    )
    return result.reshape(length, -1) * jax.nn.silu(gate_pre)


def gated_scale(values, total, gain):
    return values * lax.rsqrt(total[:, None] / DI + EPS) * gain


def route_slots(routes, experts, capacity):
    flat = routes.reshape(-1)
    hits = (flat[:, None] == jnp.arange(experts, dtype=jnp.int32)[None, :]).astype(jnp.int32)
    before = jnp.sum((jnp.cumsum(hits, axis=0) - 1) * hits, axis=1)
    return flat * capacity + before


def slot_sources(places, slots):
    count = places.shape[0]
    return jnp.full((slots,), count, jnp.int32).at[places].set(jnp.arange(count, dtype=jnp.int32))


def local_docs(lengths, row_now, length):
    bounds = jnp.cumsum(lengths)[:-1]
    place = jnp.arange(length, dtype=jnp.int32)
    inner = jnp.sum((place[:, None] >= bounds[None, :]).astype(jnp.int32), axis=1)
    return inner + row_now * lengths.shape[0]


def spread(value):
    return lax.all_gather(value, "col", axis=0, tiled=True)


def col_total(value):
    return lax.psum(value, "col")


def collect(pairs, rows):
    result = jnp.zeros((lax.axis_size("col") * rows, pairs[0][1].shape[0]), FLOAT)
    for left, right in pairs:
        result = result + lax.dot_general(
            left, right, (((1,), (1,)), ((), ())), preferred_element_type=FLOAT
        )
    return lax.psum_scatter(
        result.astype(jnp.bfloat16), "col", scatter_dimension=0, tiled=True
    ).astype(jnp.float32)


def project(left, right):
    return jnp.dot(left, right, preferred_element_type=FLOAT)


def outer(left, right):
    return lax.dot_general(left, right, (((0,), (0,)), ((), ())), preferred_element_type=FLOAT)


def silu_slope(value):
    sigma = jax.nn.sigmoid(value)
    return sigma * (1.0 + value * (1.0 - sigma))


def expert_hidden(rows_in, expert_gate, expert_up):
    gate_pre = jnp.einsum("erd,edf->erf", rows_in, expert_gate, preferred_element_type=FLOAT)
    lift_pre = jnp.einsum("erd,edf->erf", rows_in, expert_up, preferred_element_type=FLOAT)
    return (gate_pre, lift_pre)


def route_layout(routes, experts):
    count, top = routes.shape
    capacity = count * top * 4 // (3 * experts)
    places = route_slots(routes, experts, capacity)
    sources = slot_sources(places, experts * capacity)
    return (capacity, places, sources)


def routed_forward(normed, routes, gates, expert_gate, expert_up, expert_down):
    count, top = routes.shape
    width = normed.shape[1]
    local = expert_gate.shape[0]
    peers = lax.axis_size("row") * lax.axis_size("col")
    experts = peers * local
    capacity, places, sources = route_layout(routes, experts)
    padded = jnp.concatenate([normed, jnp.zeros((1, width), HALF)], axis=0)
    outgoing = jnp.take(padded, sources // top, axis=0).reshape(peers, local, capacity, width)
    arrived = lax.all_to_all(outgoing, ("row", "col"), split_axis=0, concat_axis=0, tiled=True)
    slots = arrived.shape[2]
    rows_in = arrived.transpose(1, 0, 2, 3).reshape(local, peers * slots, width)
    gate_pre, lift_pre = expert_hidden(rows_in, expert_gate, expert_up)
    active = (jax.nn.silu(gate_pre) * lift_pre).astype(HALF)
    result = jnp.einsum("erf,efd->erd", active, expert_down, preferred_element_type=FLOAT).astype(
        HALF
    )
    result = result.reshape(local, peers, slots, width).transpose(1, 0, 2, 3)
    returned = lax.all_to_all(result, ("row", "col"), split_axis=0, concat_axis=0, tiled=True)
    returned, arrived = (returned, arrived)
    picked = jnp.take(returned.reshape(experts * capacity, width), places, axis=0).reshape(
        count, top, width
    )
    routed = jnp.sum(picked.astype(FLOAT) * gates[:, :, None], axis=1)
    return (routed, arrived)


def routed_backward(grad_out, normed, routes, gates, expert_gate, expert_up, expert_down):
    count, top = routes.shape
    width = normed.shape[1]
    local = expert_gate.shape[0]
    peers = lax.axis_size("row") * lax.axis_size("col")
    experts = peers * local
    capacity, places, sources = route_layout(routes, experts)
    weighted = (gates[:, :, None] * grad_out[:, None, :]).reshape(count * top, width).astype(HALF)
    padded_grad = jnp.concatenate([weighted, jnp.zeros((1, width), HALF)], axis=0)
    outgoing = jnp.take(padded_grad, sources, axis=0).reshape(peers, local, capacity, width)
    padded = jnp.concatenate([normed, jnp.zeros((1, width), HALF)], axis=0)
    resent = jnp.take(padded, sources // top, axis=0).reshape(peers, local, capacity, width)
    grads_in, rows_back = (
        lax.all_to_all(outgoing, ("row", "col"), split_axis=0, concat_axis=0, tiled=True),
        lax.all_to_all(resent, ("row", "col"), split_axis=0, concat_axis=0, tiled=True),
    )
    rows_in = rows_back.transpose(1, 0, 2, 3).reshape(local, peers * capacity, width)
    grad_rows = grads_in.transpose(1, 0, 2, 3).reshape(local, peers * capacity, width)
    gate_pre, lift_pre = expert_hidden(rows_in, expert_gate, expert_up)
    active = (jax.nn.silu(gate_pre) * lift_pre).astype(HALF)
    grad_active = jnp.einsum("erd,efd->erf", grad_rows, expert_down, preferred_element_type=FLOAT)
    grad_down = jnp.einsum("erf,erd->efd", active, grad_rows, preferred_element_type=FLOAT)
    grad_gate_pre = (grad_active * lift_pre * silu_slope(gate_pre)).astype(HALF)
    grad_lift_pre = (grad_active * jax.nn.silu(gate_pre)).astype(HALF)
    grad_gate = jnp.einsum("erd,erf->edf", rows_in, grad_gate_pre, preferred_element_type=FLOAT)
    grad_up = jnp.einsum("erd,erf->edf", rows_in, grad_lift_pre, preferred_element_type=FLOAT)
    grad_rows_in = (
        jnp.einsum("erf,edf->erd", grad_gate_pre, expert_gate, preferred_element_type=FLOAT)
        + jnp.einsum("erf,edf->erd", grad_lift_pre, expert_up, preferred_element_type=FLOAT)
    ).astype(HALF)
    grad_rows_in = grad_rows_in.reshape(local, peers, capacity, width).transpose(1, 0, 2, 3)
    grads_back = lax.all_to_all(
        grad_rows_in, ("row", "col"), split_axis=0, concat_axis=0, tiled=True
    )
    picked = jnp.take(grads_back.reshape(experts * capacity, width), places, axis=0).reshape(
        count, top, width
    )
    grad_normed = jnp.sum(picked.astype(FLOAT), axis=1)
    return (grad_normed, (grad_gate, grad_up, grad_down))


def layer_forward(resid, params, dense, labels, routes, gates):
    (
        norm_in,
        step_bias,
        decay_log,
        skip_gain,
        conv_input,
        conv_state,
        gate_norm,
        norm_mid,
        expert_gate,
        expert_up,
        expert_down,
    ) = params
    (
        proj_gate,
        proj_input,
        proj_state,
        proj_step,
        proj_output,
        shared_gate,
        shared_up,
        shared_down,
    ) = dense
    count = resid.shape[0]
    wide_in = spread(rms_norm(resid, norm_in).astype(HALF))
    gate_pre = project(wide_in, proj_gate)
    input_pre = project(wide_in, proj_input)
    state_pre = project(wide_in, proj_state)
    step_pre = project(wide_in, proj_step)
    gated = mamba_core(
        gate_pre,
        input_pre,
        state_pre,
        step_pre,
        conv_input,
        conv_state,
        step_bias,
        decay_log,
        skip_gain,
        labels,
    )
    total = col_total(jnp.sum(gated * gated, axis=1))
    scaled = gated_scale(gated, total, gate_norm).astype(HALF)
    middle = resid + collect(((scaled, proj_output),), count)
    normed = rms_norm(middle, norm_mid).astype(HALF)
    wide_mid = spread(normed)
    shared_pre = project(wide_mid, shared_gate)
    lift_pre = project(wide_mid, shared_up)
    shared_act = (jax.nn.silu(shared_pre) * lift_pre).astype(HALF)
    shared_out = collect(((shared_act, shared_down),), count)
    routed, arrived = routed_forward(normed, routes, gates, expert_gate, expert_up, expert_down)
    saved = (
        resid,
        middle,
        wide_in,
        gate_pre,
        input_pre,
        state_pre,
        step_pre,
        total,
        wide_mid,
        shared_pre,
        lift_pre,
        arrived,
    )
    return (middle + shared_out + routed, saved)


def layer_backward(grad_out, saved, params, dense, labels, routes, gates):
    (
        norm_in,
        step_bias,
        decay_log,
        skip_gain,
        conv_input,
        conv_state,
        gate_norm,
        norm_mid,
        expert_gate,
        expert_up,
        expert_down,
    ) = params
    (
        proj_gate,
        proj_input,
        proj_state,
        proj_step,
        proj_output,
        shared_gate,
        shared_up,
        shared_down,
    ) = dense
    (
        resid,
        middle,
        wide_in,
        gate_pre,
        input_pre,
        state_pre,
        step_pre,
        total,
        wide_mid,
        shared_pre,
        lift_pre,
        arrived,
    ) = saved
    count = resid.shape[0]
    normed = rms_norm(middle, norm_mid).astype(HALF)
    grad_routed, expert_grads = routed_backward(
        grad_out, normed, routes, gates, expert_gate, expert_up, expert_down
    )
    wide_out = spread(grad_out.astype(HALF))
    shared_act = (jax.nn.silu(shared_pre) * lift_pre).astype(HALF)
    grad_act = project(wide_out, shared_down)
    grad_shared_down = outer(wide_out, shared_act)
    grad_shared_pre = (grad_act * lift_pre * silu_slope(shared_pre)).astype(HALF)
    grad_lift_pre = (grad_act * jax.nn.silu(shared_pre)).astype(HALF)
    grad_shared_gate = outer(wide_mid, grad_shared_pre)
    grad_shared_up = outer(wide_mid, grad_lift_pre)
    grad_normed = grad_routed + collect(
        ((grad_shared_pre, shared_gate), (grad_lift_pre, shared_up)), count
    )
    _, pull_mid = jax.vjp(rms_norm, middle, norm_mid)
    grad_middle, grad_norm_mid = pull_mid(grad_normed)
    grad_middle = grad_middle + grad_out
    wide_mix = spread(grad_middle.astype(HALF))

    def core(*inputs):
        return mamba_core(*inputs, labels)

    gated, pull_core = jax.vjp(
        core,
        gate_pre,
        input_pre,
        state_pre,
        step_pre,
        conv_input,
        conv_state,
        step_bias,
        decay_log,
        skip_gain,
    )
    scaled_full, pull_scale = jax.vjp(gated_scale, gated, total, gate_norm)
    scaled = scaled_full.astype(HALF)
    grad_scaled = project(wide_mix, proj_output)
    grad_proj_output = outer(wide_mix, scaled)
    grad_gated, grad_total, grad_gate_norm = pull_scale(grad_scaled)
    grad_total = col_total(grad_total)
    grad_gated = grad_gated + 2.0 * gated * grad_total[:, None]
    (
        grad_gate_pre,
        grad_input_pre,
        grad_state_pre,
        grad_step_pre,
        grad_conv_input,
        grad_conv_state,
        grad_step_bias,
        grad_decay_log,
        grad_skip_gain,
    ) = pull_core(grad_gated)
    grad_gate_pre = grad_gate_pre.astype(HALF)
    grad_input_pre = grad_input_pre.astype(HALF)
    grad_state_pre = grad_state_pre.astype(HALF)
    grad_step_pre = grad_step_pre.astype(HALF)
    grad_proj_gate = outer(wide_in, grad_gate_pre)
    grad_proj_input = outer(wide_in, grad_input_pre)
    grad_proj_state = outer(wide_in, grad_state_pre)
    grad_proj_step = outer(wide_in, grad_step_pre)
    grad_normed_in = collect(
        (
            (grad_gate_pre, proj_gate),
            (grad_input_pre, proj_input),
            (grad_state_pre, proj_state),
            (grad_step_pre, proj_step),
        ),
        count,
    )
    _, pull_in = jax.vjp(rms_norm, resid, norm_in)
    grad_resid, grad_norm_in = pull_in(grad_normed_in)
    small = (
        grad_norm_in,
        grad_step_bias,
        grad_decay_log,
        grad_skip_gain,
        grad_conv_input,
        grad_conv_state,
        grad_gate_norm,
        grad_norm_mid,
    )
    dense_grads = (
        grad_proj_gate,
        grad_proj_input,
        grad_proj_state,
        grad_proj_step,
        grad_proj_output,
        grad_shared_gate,
        grad_shared_up,
        grad_shared_down,
    )
    return (grad_resid + grad_middle, (small, dense_grads, expert_grads))


def shards(
    tokens,
    cotangent,
    doc_lengths,
    routes,
    gates,
    norm_in,
    proj_gate,
    proj_input,
    proj_state,
    proj_step,
    step_bias,
    decay_log,
    skip_gain,
    conv_input,
    conv_state,
    gate_norm,
    proj_output,
    norm_mid,
    expert_gate,
    expert_up,
    expert_down,
    shared_gate,
    shared_up,
    shared_down,
):
    first = lax.axis_index("section") == 0
    row_now = lax.axis_index("row")
    micro = tokens.shape[0]
    span = lax.axis_size("col") * tokens.shape[1]
    dense = (
        lax.all_gather(proj_gate[0], "row", axis=0, tiled=True),
        lax.all_gather(proj_input[0], "row", axis=0, tiled=True),
        lax.all_gather(proj_state[0], "row", axis=0, tiled=True),
        lax.all_gather(proj_step[0], "row", axis=0, tiled=True),
        lax.all_gather(proj_output[0], "row", axis=0, tiled=True),
        lax.all_gather(shared_gate[0], "row", axis=0, tiled=True),
        lax.all_gather(shared_up[0], "row", axis=0, tiled=True),
        lax.all_gather(shared_down[0], "row", axis=0, tiled=True),
    )
    params = (
        norm_in[0],
        step_bias[0],
        decay_log[0],
        skip_gain[0],
        conv_input[0],
        conv_state[0],
        gate_norm[0],
        norm_mid[0],
        expert_gate[0],
        expert_up[0],
        expert_down[0],
    )
    labels = jnp.stack(
        [
            local_docs(
                lax.dynamic_index_in_dim(doc_lengths[index], row_now, 0, keepdims=False),
                row_now,
                span,
            )
            for index in range(micro)
        ]
    )

    def pick(table, index):
        return lax.dynamic_index_in_dim(table, index, 0, keepdims=False)

    received = jnp.zeros(tokens.shape[1:], FLOAT)
    outputs = []
    stored = []
    for step in range(micro + 1):
        feed = tokens[step] if step < micro else jnp.zeros_like(received)
        layer_in = jnp.where(first, feed, received)
        index = jnp.where(first, min(step, micro - 1), max(step - 1, 0)).astype(jnp.int32)
        layer_result, saved = layer_forward(
            layer_in,
            params,
            dense,
            pick(labels, index),
            pick(routes[0], index),
            pick(gates[0], index),
        )
        if step < micro:
            received = passed_along(layer_result.astype(jnp.bfloat16), "section", 1).astype(
                layer_result.dtype
            )
        outputs.append(layer_result)
        stored.append(saved)
    returned_grad = jnp.zeros(tokens.shape[1:], FLOAT)
    totals = None
    back_list = []
    for step in range(micro + 1):
        feed = cotangent[step] if step < micro else jnp.zeros_like(returned_grad)
        grad_in = jnp.where(first, returned_grad, feed)
        index = jnp.where(first, max(step - 1, 0), min(step, micro - 1)).astype(jnp.int32)
        saved = jax.tree.map(
            lambda early, late: jnp.where(first, early, late),
            stored[max(step - 1, 0)],
            stored[min(step + 1, micro)],
        )
        grad_layer, grads = layer_backward(
            grad_in,
            saved,
            params,
            dense,
            pick(labels, index),
            pick(routes[0], index),
            pick(gates[0], index),
        )
        totals = grads if totals is None else jax.tree.map(jnp.add, totals, grads)
        if step < micro:
            returned_grad = passed_along(grad_layer.astype(jnp.bfloat16), "section", -1).astype(
                grad_layer.dtype
            )
        back_list.append(grad_layer)
    small, dense_grads, expert_grads = totals
    dense_grads = jax.tree.map(
        lambda part: part.astype(jnp.float32),
        lax.psum_scatter(shortened(dense_grads), "row", scatter_dimension=0, tiled=True),
    )
    small = lax.psum(small, "row")
    grad_norm_in, grad_conv_state, grad_norm_mid, grad_proj_state = (
        lax.psum(small[0].astype(jnp.bfloat16), "col").astype(jnp.float32),
        lax.psum(small[5].astype(jnp.bfloat16), "col").astype(jnp.float32),
        lax.psum(small[7].astype(jnp.bfloat16), "col").astype(jnp.float32),
        lax.psum(dense_grads[2].astype(jnp.bfloat16), "col").astype(jnp.float32),
    )
    layer_outs = jnp.stack(
        [jnp.where(first, outputs[index], outputs[index + 1]) for index in range(micro)]
    )
    input_grads = jnp.stack(
        [jnp.where(first, back_list[index + 1], back_list[index]) for index in range(micro)]
    )
    return (
        layer_outs[None],
        input_grads[None],
        grad_norm_in[None],
        dense_grads[0][None],
        dense_grads[1][None],
        grad_proj_state[None],
        dense_grads[3][None],
        small[1][None],
        small[2][None],
        small[3][None],
        small[4][None],
        grad_conv_state[None],
        small[6][None],
        dense_grads[4][None],
        grad_norm_mid[None],
        expert_grads[0][None],
        expert_grads[1][None],
        expert_grads[2][None],
        dense_grads[5][None],
        dense_grads[6][None],
        dense_grads[7][None],
    )


def solution(mesh):
    in_specs = (
        P(None, ("row", "col"), None),
        P(None, ("row", "col"), None),
        P(),
        P("section", None, ("row", "col"), None),
        P("section", None, ("row", "col"), None),
        P("section", None),
        P("section", "row", "col"),
        P("section", "row", "col"),
        P("section", "row", None),
        P("section", "row", "col"),
        P("section", "col"),
        P("section", "col"),
        P("section", "col"),
        P("section", None, "col"),
        P("section", None, None),
        P("section", "col"),
        P("section", "row", "col"),
        P("section", None),
        P("section", ("row", "col"), None, None),
        P("section", ("row", "col"), None, None),
        P("section", ("row", "col"), None, None),
        P("section", "row", "col"),
        P("section", "row", "col"),
        P("section", "row", "col"),
    )
    out_specs = (
        P("section", None, ("row", "col"), None),
        P("section", None, ("row", "col"), None),
        P("section", None),
        P("section", "row", "col"),
        P("section", "row", "col"),
        P("section", "row", None),
        P("section", "row", "col"),
        P("section", "col"),
        P("section", "col"),
        P("section", "col"),
        P("section", None, "col"),
        P("section", None, None),
        P("section", "col"),
        P("section", "row", "col"),
        P("section", None),
        P("section", ("row", "col"), None, None),
        P("section", ("row", "col"), None, None),
        P("section", ("row", "col"), None, None),
        P("section", "row", "col"),
        P("section", "row", "col"),
        P("section", "row", "col"),
    )
    return jax.shard_map(shards, mesh=mesh, in_specs=in_specs, out_specs=out_specs, check_vma=False)
```

profile of v0, /device:TPU:0, one launch (start us, length us, event | category | flops | bytes accessed | tf_op | source)
XLA Modules:
  0.0 2801.6 jit_solution(12218490860557732909)
XLA Ops:
  62.7 27.0 all-gather.48.cloned.1.call-done
  146.1 22.1 all-gather.52.cloned.1.call-done
  219.6 77.0 %all_to_all.75 = bf16[16,1,64,1536]{3,2,1,0:T(8,128)(2,1)S(1)} all-to-all(bf16[16,1,64,1536]{3,2,1,0:T(8,128)(2,1)S(1)} %bitcast.1033), channel_id=1, replica_groups=mesh['section'=2,'row'=4,'col'=4] {'row','col'}, dimensions={0} | all-to-all | bytes 6291456 | tf_op jit(solution)/shard_map/all_to_all | solution.py:194
  314.7 35.0 %all-gather.6 = bf16[1,1536,256]{2,1,0:T(8,128)(2,1)} all-gather(bf16[1,384,256]{2,1,0:T(8,128)(2,1)S(1)} %copy-done.281), channel_id=8, replica_groups=mesh['section'=2,'row'=4,'col'=4] {'row'}, dimensions={1}, use_global_device_ids=true | all-gather | bytes 983040 | tf_op jit(solution)/shard_map/all_gather | solution.py:493
  396.5 26.1 all-to-all-done.1
  457.3 32.1 %all-gather.28.cloned.1.call-done = bf16[512,1536]{1,0:T(8,128)(2,1)} async-done(((bf16[128,1536]{1,0:T(8,128)(2,1)}), bf16[512,1536]{1,0:T(8,128)(2,1)}) %all-gather.28.cloned.1.call-update) | async-done | bytes 1572880 | tf_op jit(solution)/shard_map/all_gather | solution.py:140
  551.0 33.1 %reduce-scatter.27.cloned.1.call-done = bf16[128,1536]{1,0:T(8,128)(2,1)} async-done(((bf16[512,1536]{1,0:T(8,128)(2,1)}), bf16[128,1536]{1,0:T(8,128)(2,1)}) %reduce-scatter.27.cloned.1.call-update) | async-done | bytes 393232 | tf_op jit(solution)/shard_map/reduce_scatter | solution.py:153
  594.3 77.0 %all_to_all.76 = bf16[16,1,64,1536]{3,2,1,0:T(8,128)(2,1)S(1)} all-to-all(bf16[16,1,64,1536]{3,2,1,0:T(8,128)(2,1)S(1)} %bitcast.1032), channel_id=1, replica_groups=mesh['section'=2,'row'=4,'col'=4] {'row','col'}, dimensions={0} | all-to-all | bytes 6291456 | tf_op jit(solution)/shard_map/all_to_all | solution.py:194
  689.2 74.6 %all-gather.30.cloned.1.call-done = bf16[512,1536]{1,0:T(8,128)(2,1)} async-done(((bf16[128,1536]{1,0:T(8,128)(2,1)}), bf16[512,1536]{1,0:T(8,128)(2,1)}) %all-gather.30.cloned.1.call-update) | async-done | bytes 1572880 | tf_op jit(solution)/shard_map/all_gather | solution.py:140
  771.1 25.4 all-to-all-done.3
  870.2 41.3 %all-to-all-done.7 = bf16[16,1,64,1536]{3,2,1,0:T(8,128)(2,1)} async-done(((bf16[16,1,64,1536]{3,2,1,0:T(8,128)(2,1)}), bf16[16,1,64,1536]{3,2,1,0:T(8,128)(2,1)}, u32[]{:S(2)}, u32[]{:S(2)}) %all-to-all-start.7) | async-done | bytes 3145760 | tf_op jit(solution)/shard_map/all_to_all | solution.py:226
  928.8 63.3 %all-gather.36.cloned.1.call-done = bf16[512,1536]{1,0:T(8,128)(2,1)} async-done(((bf16[128,1536]{1,0:T(8,128)(2,1)}), bf16[512,1536]{1,0:T(8,128)(2,1)}) %all-gather.36.cloned.1.call-update) | async-done | bytes 1572880 | tf_op jit(solution)/shard_map/all_gather | solution.py:140
  1103.3 33.4 %all-to-all-done.8 = bf16[16,1,64,1536]{3,2,1,0:T(8,128)(2,1)} async-done(((bf16[16,1,64,1536]{3,2,1,0:T(8,128)(2,1)}), bf16[16,1,64,1536]{3,2,1,0:T(8,128)(2,1)}, u32[]{:S(2)}, u32[]{:S(2)}) %all-to-all-start.8) | async-done | bytes 3145760 | tf_op jit(solution)/shard_map/all_to_all | solution.py:243
  1247.9 20.2 fusion.52
  1338.1 23.9 reduce-scatter.37.cloned.1.call-done
  1398.9 21.5 all-to-all-done.10
  1435.7 87.0 %all-to-all-done.9 = bf16[16,1,64,1536]{3,2,1,0:T(8,128)(2,1)} async-done(((bf16[16,1,64,1536]{3,2,1,0:T(8,128)(2,1)}), bf16[16,1,64,1536]{3,2,1,0:T(8,128)(2,1)}, u32[]{:S(2)}, u32[]{:S(2)}) %all-to-all-start.9) | async-done | bytes 3145760 | tf_op jit(solution)/shard_map/all_to_all | solution.py:225
  1550.5 64.1 %all-gather.40.cloned.1.call-done = bf16[512,1536]{1,0:T(8,128)(2,1)} async-done(((bf16[128,1536]{1,0:T(8,128)(2,1)}), bf16[512,1536]{1,0:T(8,128)(2,1)}) %all-gather.40.cloned.1.call-update) | async-done | bytes 1572880 | tf_op jit(solution)/shard_map/all_gather | solution.py:140
  1624.3 22.5 all-to-all-done.11
  1723.6 30.8 %all-to-all-done.4 = bf16[16,1,64,1536]{3,2,1,0:T(8,128)(2,1)} async-done(((bf16[16,1,64,1536]{3,2,1,0:T(8,128)(2,1)}), bf16[16,1,64,1536]{3,2,1,0:T(8,128)(2,1)}, u32[]{:S(2)}, u32[]{:S(2)}) %all-to-all-start.4) | async-done | bytes 3145760 | tf_op jit(solution)/shard_map/all_to_all | solution.py:194
  1779.9 59.2 %psum.130 = f32[512]{0:T(512)S(1)} all-reduce(f32[512]{0:T(512)S(1)} %get-tuple-element.897), channel_id=1, replica_groups=mesh['section'=2,'row'=4,'col'=4] {'col'}, use_global_device_ids=true, to_apply=%region_76.81 | all-reduce | flops 512 | bytes 4096 | tf_op jit(solution)/shard_map/psum | solution.py:144
  1876.0 20.1 fusion.54
  1976.7 22.2 reduce-scatter.41.cloned.1.call-done
  2055.3 35.8 %all-to-all-done.13 = bf16[16,1,64,1536]{3,2,1,0:T(8,128)(2,1)} async-done(((bf16[16,1,64,1536]{3,2,1,0:T(8,128)(2,1)}), bf16[16,1,64,1536]{3,2,1,0:T(8,128)(2,1)}, u32[]{:S(2)}, u32[]{:S(2)}) %all-to-all-start.13) | async-done | bytes 3145760 | tf_op jit(solution)/shard_map/all_to_all | solution.py:226
  2106.3 86.5 %all-to-all-done.12 = bf16[16,1,64,1536]{3,2,1,0:T(8,128)(2,1)} async-done(((bf16[16,1,64,1536]{3,2,1,0:T(8,128)(2,1)}), bf16[16,1,64,1536]{3,2,1,0:T(8,128)(2,1)}, u32[]{:S(2)}, u32[]{:S(2)}) %all-to-all-start.12) | async-done | bytes 3145760 | tf_op jit(solution)/shard_map/all_to_all | solution.py:225
  2223.3 82.9 %all-to-all-done.14 = bf16[16,1,64,1536]{3,2,1,0:T(8,128)(2,1)} async-done(((bf16[16,1,64,1536]{3,2,1,0:T(8,128)(2,1)}), bf16[16,1,64,1536]{3,2,1,0:T(8,128)(2,1)}, u32[]{:S(2)}, u32[]{:S(2)}) %all-to-all-start.14) | async-done | bytes 3145760 | tf_op jit(solution)/shard_map/all_to_all | solution.py:243
  2422.8 20.2 fusion.56
  2634.8 36.2 %reduce-scatter.45.cloned.1.call-done = bf16[128,1536]{1,0:T(8,128)(2,1)} async-done(((bf16[512,1536]{1,0:T(8,128)(2,1)}), bf16[128,1536]{1,0:T(8,128)(2,1)}) %reduce-scatter.45.cloned.1.call-update) | async-done | bytes 393232 | tf_op jit(solution)/shard_map/reduce_scatter | solution.py:153
  2673.4 18.5 all-reduce.112
  2693.9 18.0 all-reduce.113
  2721.5 30.4 %reduce-scatter.49.cloned.1.call-done = bf16[384,768]{1,0:T(8,128)(2,1)} async-done(((bf16[1536,768]{1,0:T(8,128)(2,1)}), bf16[384,768]{1,0:T(8,128)(2,1)}) %reduce-scatter.49.cloned.1.call-update) | async-done | bytes 589840 | tf_op jit(solution)/shard_map/reduce_scatter | solution.py:574
  2754.1 38.4 %reduce-scatter.47.cloned.1.call-done = bf16[384,768]{1,0:T(8,128)(2,1)} async-done(((bf16[1536,768]{1,0:T(8,128)(2,1)}), bf16[384,768]{1,0:T(8,128)(2,1)}) %reduce-scatter.47.cloned.1.call-update) | async-done | bytes 589840 | tf_op jit(solution)/shard_map/reduce_scatter | solution.py:574
  (1937 shorter events, 1471.9 us)
Async XLA Ops:
  12.3 116.7 %all-gather.50.cloned.1.call-start = ((), (), s32[]{:S(2)}) async-start(), calls=%async_computation.68 | async-start | bytes 2949120 | tf_op jit(solution)/shard_map/all_gather | solution.py:487
  13.1 155.2 %all-gather.52.cloned.1.call-start = ((), (), s32[]{:S(2)}) async-start(), calls=%async_computation.69 | async-start | bytes 2949120 | tf_op jit(solution)/shard_map/all_gather | solution.py:491
  13.6 195.6 %reduce-scatter.23.cloned.1.call-start = ((), (), s32[]{:S(2)}) async-start(), calls=%async_computation.36 | async-start | bytes 1966080 | tf_op jit(solution)/shard_map/reduce_scatter | solution.py:153
  309.5 113.1 %all-to-all-start.1 = ((bf16[16,1,64,1536]{3,2,1,0:T(8,128)(2,1)}), bf16[16,1,64,1536]{3,2,1,0:T(8,128)(2,1)}, u32[]{:S(2)}, u32[]{:S(2)}) async-start(bf16[16,1,64,1536]{3,2,1,0:T(8,128)(2,1)} %bitcast.1035), calls=%async_computation.3 | async-start | bytes 6291456 | tf_op jit(solution)/shard_map/all_to_all | solution.py:203
  314.7 132.6 %reduce-scatter.25.cloned.1.call-start = ((), (), s32[]{:S(2)}) async-start(), calls=%async_computation.38 | async-start | bytes 1966080 | tf_op jit(solution)/shard_map/reduce_scatter | solution.py:153
  454.0 130.0 %reduce-scatter.27.cloned.1.call-start = ((), (), s32[]{:S(2)}) async-start(), calls=%async_computation.40 | async-start | bytes 1966080 | tf_op jit(solution)/shard_map/reduce_scatter | solution.py:153
  689.2 132.0 %reduce-scatter.29.cloned.1.call-start = ((), (), s32[]{:S(2)}) async-start(), calls=%async_computation.42 | async-start | bytes 1966080 | tf_op jit(solution)/shard_map/reduce_scatter | solution.py:153
  916.7 126.2 %all-gather.32.cloned.1.call-start = ((), (), s32[]{:S(2)}) async-start(), calls=%async_computation.43 | async-start | bytes 1966080 | tf_op jit(solution)/shard_map/all_gather | solution.py:140
  1039.7 121.1 %reduce-scatter.35.cloned.1.call-start = ((), (), s32[]{:S(2)}) async-start(), calls=%async_computation.48 | async-start | bytes 1966080 | tf_op jit(solution)/shard_map/reduce_scatter | solution.py:153
  1042.7 157.5 %all-gather.38.cloned.1.call-start = ((), (), s32[]{:S(2)}) async-start(), calls=%async_computation.49 | async-start | bytes 1966080 | tf_op jit(solution)/shard_map/all_gather | solution.py:140
  1165.8 152.8 %reduce-scatter.31.cloned.1.call-start = ((), (), s32[]{:S(2)}) async-start(), calls=%async_computation.44 | async-start | bytes 1966080 | tf_op jit(solution)/shard_map/reduce_scatter | solution.py:153
  1233.3 128.7 %reduce-scatter.37.cloned.1.call-start = ((), (), s32[]{:S(2)}) async-start(), calls=%async_computation.50 | async-start | bytes 1966080 | tf_op jit(solution)/shard_map/reduce_scatter | solution.py:153
  1424.9 121.2 %all-gather.34.cloned.1.call-start = ((), (), s32[]{:S(2)}) async-start(), calls=%async_computation.45 | async-start | bytes 1966080 | tf_op jit(solution)/shard_map/all_gather | solution.py:140
  1533.9 112.8 %all-to-all-start.11 = ((bf16[16,1,64,1536]{3,2,1,0:T(8,128)(2,1)}), bf16[16,1,64,1536]{3,2,1,0:T(8,128)(2,1)}, u32[]{:S(2)}, u32[]{:S(2)}) async-start(bf16[16,1,64,1536]{3,2,1,0:T(8,128)(2,1)} %bitcast.1026), calls=%async_computation.19 | async-start | bytes 6291456 | tf_op jit(solution)/shard_map/all_to_all | solution.py:243
  1539.3 149.4 %reduce-scatter.39.cloned.1.call-start = ((), (), s32[]{:S(2)}) async-start(), calls=%async_computation.52 | async-start | bytes 1966080 | tf_op jit(solution)/shard_map/reduce_scatter | solution.py:153
  1651.5 121.3 %all-gather.42.cloned.1.call-start = ((), (), s32[]{:S(2)}) async-start(), calls=%async_computation.53 | async-start | bytes 1966080 | tf_op jit(solution)/shard_map/all_gather | solution.py:140
  1693.8 282.9 %reduce-scatter.33.cloned.1.call-start = ((), (), s32[]{:S(2)}) async-start(), calls=%async_computation.46 | async-start | bytes 1966080 | tf_op jit(solution)/shard_map/reduce_scatter | solution.py:153
  1768.0 183.9 %all-to-all-start.5 = ((bf16[16,1,64,1536]{3,2,1,0:T(8,128)(2,1)}), bf16[16,1,64,1536]{3,2,1,0:T(8,128)(2,1)}, u32[]{:S(2)}, u32[]{:S(2)}) async-start(bf16[16,1,64,1536]{3,2,1,0:T(8,128)(2,1)} %bitcast.1034), calls=%async_computation.11 | async-start | bytes 6291456 | tf_op jit(solution)/shard_map/all_to_all | solution.py:203
  1772.7 226.2 %reduce-scatter.41.cloned.1.call-start = ((), (), s32[]{:S(2)}) async-start(), calls=%async_computation.54 | async-start | bytes 1966080 | tf_op jit(solution)/shard_map/reduce_scatter | solution.py:153
  2095.6 113.6 %all-gather.44.cloned.1.call-start = ((), (), s32[]{:S(2)}) async-start(), calls=%async_computation.55 | async-start | bytes 1966080 | tf_op jit(solution)/shard_map/all_gather | solution.py:140
  2209.1 121.3 %reduce-scatter.43.cloned.1.call-start = ((), (), s32[]{:S(2)}) async-start(), calls=%async_computation.56 | async-start | bytes 1966080 | tf_op jit(solution)/shard_map/reduce_scatter | solution.py:153
  2214.9 154.8 %all-gather.46.cloned.1.call-start = ((), (), s32[]{:S(2)}) async-start(), calls=%async_computation.57 | async-start | bytes 1966080 | tf_op jit(solution)/shard_map/all_gather | solution.py:140
  2335.3 187.0 %reduce-scatter.51.cloned.1.call-start = ((), (), s32[]{:S(2)}) async-start(), calls=%async_computation.61 | async-start | bytes 983040 | tf_op jit(solution)/shard_map/reduce_scatter | solution.py:574
  2456.5 134.6 %reduce-scatter.59.cloned.1.call-start = ((), (), s32[]{:S(2)}) async-start(), calls=%async_computation.66 | async-start | bytes 983040 | tf_op jit(solution)/shard_map/reduce_scatter | solution.py:574
  2462.9 130.0 %reduce-scatter.57.cloned.1.call-start = ((), (), s32[]{:S(2)}) async-start(), calls=%async_computation.65 | async-start | bytes 983040 | tf_op jit(solution)/shard_map/reduce_scatter | solution.py:574
  2468.2 126.5 %reduce-scatter.55.cloned.1.call-start = ((), (), s32[]{:S(2)}) async-start(), calls=%async_computation.64 | async-start | bytes 983040 | tf_op jit(solution)/shard_map/reduce_scatter | solution.py:574
  2476.5 150.7 %reduce-scatter.61.cloned.1.call-start = ((), (), s32[]{:S(2)}) async-start(), calls=%async_computation.70 | async-start | bytes 491520
  2512.6 120.5 %all-reduce.116.cloned.1.call-start = ((), (), s32[]{:S(2)}) async-start(), calls=%async_computation.62 | async-start | bytes 393216 | tf_op jit(solution)/shard_map/psum | solution.py:581
  2522.3 148.7 %reduce-scatter.45.cloned.1.call-start = ((), (), s32[]{:S(2)}) async-start(), calls=%async_computation.58 | async-start | bytes 1966080 | tf_op jit(solution)/shard_map/reduce_scatter | solution.py:153
  2526.1 193.3 %reduce-scatter.53.cloned.1.call-start = ((), (), s32[]{:S(2)}) async-start(), calls=%async_computation.63 | async-start | bytes 2949120 | tf_op jit(solution)/shard_map/reduce_scatter | solution.py:574
  2535.3 216.6 %reduce-scatter.49.cloned.1.call-start = ((), (), s32[]{:S(2)}) async-start(), calls=%async_computation.60 | async-start | bytes 2949120 | tf_op jit(solution)/shard_map/reduce_scatter | solution.py:574
  2564.7 227.8 %reduce-scatter.47.cloned.1.call-start = ((), (), s32[]{:S(2)}) async-start(), calls=%async_computation.59 | async-start | bytes 2949120 | tf_op jit(solution)/shard_map/reduce_scatter | solution.py:574
  (610 other events, 10320.7 us)
Sparse Core Ops, SparseCore 0:
  11.7 39.7 all-gather.23
  53.3 36.3 all-gather.47
  91.5 37.4 all-gather.49
  130.7 37.4 all-gather.51
  173.8 35.3 reduce-scatter.22
  316.8 72.5 all-gather.25
  395.2 39.2 reduce-scatter.24
  454.1 35.1 all-gather.27
  550.4 33.5 reduce-scatter.26
  691.3 72.5 all-gather.29
  769.8 39.2 reduce-scatter.28
  918.8 73.1 all-gather.35
  995.9 41.1 all-gather.31
  1042.8 72.9 reduce-scatter.34
  1165.9 34.3 all-gather.37
  1233.4 33.6 reduce-scatter.30
  1318.6 43.3 reduce-scatter.36
  1427.6 73.9 all-gather.33
  1541.5 72.9 all-gather.39
  1619.8 42.9 reduce-scatter.38
  1693.9 54.6 all-gather.41
  1750.9 40.2 reduce-scatter.32
  1950.1 48.7 reduce-scatter.40
  2098.3 73.1 all-gather.43
  2215.1 70.5 reduce-scatter.42
  2335.4 34.2 all-gather.45
  2483.9 26.1 reduce-scatter.58
  2598.2 34.8 all-reduce.115
  2635.9 34.9 reduce-scatter.44
  2674.3 36.8 reduce-scatter.52
  2714.5 37.3 reduce-scatter.48
  2755.1 37.3 reduce-scatter.46
  (4 shorter events, 100.8 us)
where the time goes:
time: 2820 us; the launch traced here: 2800 us
  waiting for transfers between devices  1050 us (37%)
  matrix products  599 us (21%)
  blocking collectives  375 us (13%)
  local copies, waits for them, and re-layouts  344 us (12%)
  other arithmetic  340 us (12%)
  starting transfers between devices  69.5 us (2%)
    all_gather x12, waiting for transfers between devices, spread(): return lax.all_gather(value, 'col', axis=0, tiled=True)  272 us
    dot_general x12, matrix products, advance(): inner = jnp.einsum('tsh,shp->thp', mixing, values, precision=HIGH)  198 us
    all_to_all x3, waiting for transfers between devices, routed_backward(): lax.all_to_all(outgoing, ('row', 'col'), split_axis=0, concat_axis=0, til...  191 us
    all_to_all x2, blocking collectives, routed_forward(): lax.all_to_all(outgoing, ('row', 'col'), split_axis=0, concat_axis=0, til...  154 us
    all_to_all x3, waiting for transfers between devices, routed_backward(): lax.all_to_all(grad_rows_in, ('row', 'col'), split_axis=0, concat_axis=0,...  139 us
    reduce_scatter x12, waiting for transfers between devices, collect(): lax.psum_scatter(result.astype(jnp.bfloat16), 'col', scatter_dimension=0,...  129 us
    psum x5, blocking collectives, col_total(): return lax.psum(value, 'col')  101 us
    all_to_all x3, waiting for transfers between devices, routed_backward(): lax.all_to_all(resent, ('row', 'col'), split_axis=0, concat_axis=0, tiled...  98.6 us
  transfers between devices with their start and end apart: 53, of which 34 were waited for; matrix products, arithmetic and copies ran while one was open for 36% of the time, Pallas kernels for 0%

commit v1 on v0

v1 whole, which is shorter than its diff:
```python
import jax
import jax.numpy as jnp
from jax import lax
from jax.sharding import PartitionSpec as P

BLOCK = 512
DI = 3072


EPS = 1e-05
HIGH = lax.Precision.HIGHEST
FLOAT = jnp.float32
HALF = jnp.bfloat16


def shifted(block, axis, distance):
    count = lax.axis_size(axis)
    if distance % count == 0:
        return block
    return lax.ppermute(block, axis, [(i, (i + distance) % count) for i in range(count)])


def swapped(block):
    return lax.ppermute(block, "section", [(0, 1), (1, 0)])


def rms_norm(value, gain):
    return value * lax.rsqrt(jnp.mean(value * value, axis=-1, keepdims=True) + EPS) * gain


def causal_conv(values, weight, docs):
    width = weight.shape[0]
    result = values * weight[width - 1]
    for back in range(1, width):
        moved = jnp.pad(values, ((back, 0), (0, 0)))[:-back]
        prior = jnp.pad(docs, (back, 0), constant_values=-1)[:-back]
        same = (prior == docs).astype(values.dtype)[:, None]
        result = result + moved * same * weight[width - 1 - back]
    return result


def ssd_scan(inputs, step_size, rate, state_in, state_out, docs, skip_gain):
    length, heads, width = inputs.shape
    count = length // BLOCK
    order = jnp.arange(BLOCK, dtype=jnp.int32)
    causal = order[:, None] >= order[None, :]

    def advance(carry, block):
        state, previous = carry
        values, sizes, keys, queries, labels = block
        logs = sizes * rate[None, :]
        running = jnp.cumsum(logs, axis=0)
        same = causal & (labels[:, None] == labels[None, :])
        spread_log = running[:, None, :] - running[None, :, :]
        decay = jnp.exp(jnp.where(same[:, :, None], spread_log, -1e30))
        scores = jnp.dot(queries, keys.T, precision=HIGH)
        mixing = decay * scores[:, :, None] * sizes[None, :, :]
        inner = jnp.einsum("tsh,shp->thp", mixing, values, precision=HIGH)
        carried = (labels == previous).astype(values.dtype)
        reach = jnp.exp(running) * carried[:, None]
        outer = jnp.einsum("tn,hpn->thp", queries, state, precision=HIGH) * reach[:, :, None]
        final = labels[BLOCK - 1]
        tail = (
            jnp.exp(running[BLOCK - 1][None, :] - running)
            * sizes
            * (labels == final).astype(values.dtype)[:, None]
        )
        kept = jnp.exp(running[BLOCK - 1]) * (final == previous).astype(values.dtype)
        fresh = jnp.einsum("sh,shp,sn->hpn", tail, values, keys, precision=HIGH)
        new_state = state * kept[:, None, None] + fresh
        output = inner + outer + skip_gain[None, :, None] * values
        return ((new_state, final), output)

    blocks = (
        inputs.reshape(count, BLOCK, heads, width),
        step_size.reshape(count, BLOCK, heads),
        state_in.reshape(count, BLOCK, -1),
        state_out.reshape(count, BLOCK, -1),
        docs.reshape(count, BLOCK),
    )
    start = (jnp.zeros((heads, width, state_in.shape[1]), inputs.dtype), jnp.array(-1, jnp.int32))
    _, result = lax.scan(jax.checkpoint(advance), start, blocks)
    return result.reshape(length, heads, width)


def mamba_core(
    gate_pre,
    input_pre,
    state_pre,
    step_pre,
    conv_input,
    conv_state,
    step_bias,
    decay_log,
    skip_gain,
    docs,
):
    heads = step_pre.shape[1]
    length = input_pre.shape[0]
    mixed_input = jax.nn.silu(causal_conv(input_pre, conv_input, docs))
    mixed_state = jax.nn.silu(causal_conv(state_pre, conv_state, docs))
    half = state_pre.shape[1] // 2
    step_size = jax.nn.softplus(step_pre + step_bias)
    rate = -jnp.exp(decay_log)
    result = ssd_scan(
        mixed_input.reshape(length, heads, -1),
        step_size,
        rate,
        mixed_state[:, :half],
        mixed_state[:, half:],
        docs,
        skip_gain,
    )
    return result.reshape(length, -1) * jax.nn.silu(gate_pre)


def local_docs(lengths, row_now, length):
    bounds = jnp.cumsum(lengths)[:-1]
    place = jnp.arange(length, dtype=jnp.int32)
    inner = jnp.sum((place[:, None] >= bounds[None, :]).astype(jnp.int32), axis=1)
    return inner + row_now * lengths.shape[0]


def project(left, right):
    return jnp.dot(left, right, preferred_element_type=FLOAT)


def project_back(left, right):
    return lax.dot_general(left, right, (((1,), (1,)), ((), ())), preferred_element_type=FLOAT)


def outer(left, right):
    return lax.dot_general(left, right, (((0,), (0,)), ((), ())), preferred_element_type=FLOAT)


def silu_slope(value):
    sigma = jax.nn.sigmoid(value)
    return sigma * (1.0 + value * (1.0 - sigma))


def groups():
    count = lax.axis_size("col")
    return count if count <= 4 else 1


def spread(block):
    if groups() == 1:
        return [lax.all_gather(block, "col", axis=0, tiled=True)]
    return [shifted(block, "col", back) for back in range(lax.axis_size("col"))]


def in_order(blocks):
    count = len(blocks)
    if count == 1:
        return blocks[0]
    rows = blocks[0].shape[0]
    line = jnp.concatenate(blocks[::-1] + blocks[:0:-1], axis=0)
    start = (count - 1 - lax.axis_index("col")) * rows
    return lax.dynamic_slice_in_dim(line, start, count * rows, axis=0)


def gathered_sum(parts):
    if len(parts) == 1:
        return lax.psum_scatter(parts[0], "col", scatter_dimension=0, tiled=True).astype(FLOAT)
    total = parts[0].astype(FLOAT)
    for back in range(1, len(parts)):
        total = total + shifted(parts[back], "col", -back).astype(FLOAT)
    return total


def block_of(values, back, rows):
    if groups() == 1:
        return values
    count = lax.axis_size("col")
    index = lax.rem(lax.axis_index("col") - back + count, count)
    return lax.dynamic_slice_in_dim(values, index * rows, rows, axis=0)


def route_tables(meta, top, capacity):
    n_row, n_col = lax.axis_size("row"), lax.axis_size("col")
    row_now, col_now = lax.axis_index("row"), lax.axis_index("col")
    tables = []
    blocks = meta.shape[0] // groups()
    slots = blocks * capacity
    for back in range(groups()):
        block = lax.rem(col_now - back + n_col, n_col) if blocks == 1 else 0
        now = lax.dynamic_slice_in_dim(meta, block, blocks, axis=0).reshape(-1, 2 * top)
        routes, gates = now[:, :top], now[:, top:]
        count = routes.shape[0]
        experts = (lax.rem(row_now + jnp.arange(n_row), n_row) * n_col + col_now).astype(FLOAT)
        match = routes[None, :, :] == experts[:, None, None]
        hit = jnp.any(match, axis=2)
        weight = jnp.sum(jnp.where(match, gates[None], 0.0), axis=2)
        place = jnp.cumsum(hit.astype(jnp.int32), axis=1) - 1
        slot = jnp.arange(slots, dtype=jnp.int32)
        chosen = (place[:, None, :] == slot[None, :, None]) & hit[:, None, :]
        plain = chosen.astype(HALF).reshape(n_row * slots, count)
        scaled = jnp.where(chosen, weight[:, None, :], 0.0).astype(HALF)
        tables.append((plain, scaled.reshape(n_row * slots, count)))
    return tables


def dispatch(table, block):
    n_row = lax.axis_size("row")
    rows = project(table, block).astype(HALF)
    rows = rows.reshape(n_row, rows.shape[0] // n_row, rows.shape[1])
    return jnp.concatenate([shifted(rows[ahead], "row", ahead) for ahead in range(n_row)], axis=0)


def give_back(rows):
    n_row = lax.axis_size("row")
    rows = rows.astype(HALF).reshape(n_row, rows.shape[0] // n_row, rows.shape[1])
    return jnp.concatenate([shifted(rows[ahead], "row", -ahead) for ahead in range(n_row)], axis=0)


def layer_forward(resid, params, dense, labels, tables):
    (
        norm_in,
        step_bias,
        decay_log,
        skip_gain,
        conv_input,
        conv_state,
        gate_norm,
        norm_mid,
    ) = params
    proj, proj_output, shared, expert_gate, expert_up, expert_down = dense
    count = resid.shape[0]
    inner = gate_norm.shape[0]
    state = conv_state.shape[1]
    hidden = shared.shape[1] // 3
    wide_in = in_order(spread(rms_norm(resid, norm_in).astype(HALF)))
    pre = project(wide_in, proj)
    gate_pre = pre[:, :inner]
    input_pre = pre[:, inner : 2 * inner]
    state_pre = pre[:, 2 * inner : 2 * inner + state]
    step_pre = pre[:, 2 * inner + state :]

    def core(*inputs):
        return mamba_core(*inputs, labels)

    gated, pull_core = jax.vjp(
        core,
        gate_pre,
        input_pre,
        state_pre,
        step_pre,
        conv_input,
        conv_state,
        step_bias,
        decay_log,
        skip_gain,
    )
    total_part = jnp.sum(gated * gated, axis=1, keepdims=True)
    scaled = (gated * gate_norm).astype(HALF)
    backs = range(groups())
    total = gathered_sum([block_of(total_part, back, count) for back in backs])
    mixed = gathered_sum(
        [project_back(block_of(scaled, back, count), proj_output).astype(HALF) for back in backs]
    )
    rr = lax.rsqrt(total / DI + EPS)
    middle = resid + mixed * rr
    normed = rms_norm(middle, norm_mid).astype(HALF)
    wide_mid = spread(normed)
    shared_pre, lift_pre, shared_act, arrived, expert_pre, active, parts = [], [], [], [], [], [], []
    for back in backs:
        rows = dispatch(tables[back][0], wide_mid[back])
        gate_e = project(rows, expert_gate)
        lift_e = project(rows, expert_up)
        act_e = (jax.nn.silu(gate_e) * lift_e).astype(HALF)
        result = give_back(project(act_e, expert_down))
        arrived.append(rows)
        expert_pre.append((gate_e, lift_e))
        active.append(act_e)
        both = project(wide_mid[back], shared[:, : 2 * hidden])
        gate_s, lift_s = both[:, :hidden], both[:, hidden:]
        act_s = (jax.nn.silu(gate_s) * lift_s).astype(HALF)
        shared_pre.append(gate_s)
        lift_pre.append(lift_s)
        shared_act.append(act_s)
        part = outer(tables[back][1], result) + project_back(act_s, shared[:, 2 * hidden :])
        parts.append(part.astype(HALF))
    saved = (
        resid,
        middle,
        mixed,
        rr,
        wide_in,
        gated,
        pull_core,
        wide_mid,
        shared_pre,
        lift_pre,
        shared_act,
        arrived,
        expert_pre,
        active,
    )
    return (middle + gathered_sum(parts), saved)


def layer_backward(grad_out, saved, params, dense, tables):
    (
        norm_in,
        step_bias,
        decay_log,
        skip_gain,
        conv_input,
        conv_state,
        gate_norm,
        norm_mid,
    ) = params
    proj, proj_output, shared, expert_gate, expert_up, expert_down = dense
    (
        resid,
        middle,
        mixed,
        rr,
        wide_in,
        gated,
        pull_core,
        wide_mid,
        shared_pre,
        lift_pre,
        shared_act,
        arrived,
        expert_pre,
        active,
    ) = saved
    count = resid.shape[0]
    hidden = shared.shape[1] // 3
    backs = range(groups())
    wide_out = spread(grad_out.astype(HALF))
    parts, rows_grad, gate_grads, lift_grads, shared_grads = [], [], [], [], []
    for back in backs:
        rows = dispatch(tables[back][1], wide_out[back])
        gate_e, lift_e = expert_pre[back]
        grad_act = project_back(rows, expert_down)
        grad_gate_e = (grad_act * lift_e * silu_slope(gate_e)).astype(HALF)
        grad_lift_e = (grad_act * jax.nn.silu(gate_e)).astype(HALF)
        result = give_back(
            project_back(grad_gate_e, expert_gate) + project_back(grad_lift_e, expert_up)
        )
        rows_grad.append(rows)
        gate_grads.append(grad_gate_e)
        lift_grads.append(grad_lift_e)
        gate_s, lift_s = shared_pre[back], lift_pre[back]
        grad_act_s = project(wide_out[back], shared[:, 2 * hidden :])
        grad_gate_s = grad_act_s * lift_s * silu_slope(gate_s)
        grad_lift_s = grad_act_s * jax.nn.silu(gate_s)
        grad_s = jnp.concatenate([grad_gate_s, grad_lift_s], axis=1).astype(HALF)
        shared_grads.append(grad_s)
        part = outer(tables[back][0], result) + project_back(grad_s, shared[:, : 2 * hidden])
        parts.append(part.astype(HALF))
    grad_normed = gathered_sum(parts)
    rows_in = jnp.concatenate(arrived, axis=0)
    rows_out = jnp.concatenate(rows_grad, axis=0)
    expert_grads = (
        outer(rows_in, jnp.concatenate(gate_grads, axis=0)),
        outer(rows_in, jnp.concatenate(lift_grads, axis=0)),
        outer(jnp.concatenate(active, axis=0), rows_out),
    )
    mids, outs = jnp.concatenate(wide_mid, axis=0), jnp.concatenate(wide_out, axis=0)
    grad_shared = jnp.concatenate(
        [
            outer(mids, jnp.concatenate(shared_grads, axis=0)).astype(HALF),
            outer(outs, jnp.concatenate(shared_act, axis=0)).astype(HALF),
        ],
        axis=1,
    )
    _, pull_mid = jax.vjp(rms_norm, middle, norm_mid)
    grad_middle, grad_norm_mid = pull_mid(grad_normed)
    grad_middle = grad_middle + grad_out
    along = jnp.sum(grad_middle * mixed, axis=1, keepdims=True)
    wide_mix = in_order(spread(grad_middle.astype(HALF)))
    sides = in_order(spread(jnp.concatenate([rr, along], axis=1)))
    rr_all, along_all = sides[:, :1], sides[:, 1:]
    grad_scaled = project(wide_mix, proj_output)
    normed_gate = gated * rr_all
    grad_proj_output = outer(wide_mix, (normed_gate * gate_norm).astype(HALF)).astype(HALF)
    grad_gate_norm = jnp.sum(grad_scaled * normed_gate, axis=0)
    grad_gated = rr_all * gate_norm * grad_scaled - gated * rr_all**3 * along_all / DI
    (
        grad_gate_pre,
        grad_input_pre,
        grad_state_pre,
        grad_step_pre,
        grad_conv_input,
        grad_conv_state,
        grad_step_bias,
        grad_decay_log,
        grad_skip_gain,
    ) = pull_core(grad_gated)
    grad_pre = jnp.concatenate(
        [
            grad_gate_pre.astype(HALF),
            grad_input_pre.astype(HALF),
            grad_state_pre.astype(HALF),
            grad_step_pre.astype(HALF),
        ],
        axis=1,
    )
    grad_proj = outer(wide_in, grad_pre).astype(HALF)
    grad_normed_in = gathered_sum(
        [project_back(block_of(grad_pre, back, count), proj).astype(HALF) for back in backs]
    )
    _, pull_in = jax.vjp(rms_norm, resid, norm_in)
    grad_resid, grad_norm_in = pull_in(grad_normed_in)
    small = (
        grad_norm_in,
        grad_norm_mid,
        grad_conv_state,
        grad_conv_input,
        grad_gate_norm,
        grad_step_bias,
        grad_decay_log,
        grad_skip_gain,
    )
    return (grad_resid + grad_middle, small, (grad_proj, grad_proj_output, grad_shared), expert_grads)


def flat(parts):
    return jnp.concatenate([part.reshape(-1) for part in parts])


def unflat(vector, shapes):
    result, start = [], 0
    for shape in shapes:
        size = 1
        for entry in shape:
            size *= entry
        result.append(vector[start : start + size].reshape(shape))
        start += size
    return result


def shards(
    tokens,
    cotangent,
    doc_lengths,
    routes,
    gates,
    norm_in,
    proj_gate,
    proj_input,
    proj_state,
    proj_step,
    step_bias,
    decay_log,
    skip_gain,
    conv_input,
    conv_state,
    gate_norm,
    proj_output,
    norm_mid,
    expert_gate,
    expert_up,
    expert_down,
    shared_gate,
    shared_up,
    shared_down,
):
    section_now = lax.axis_index("section")
    first = section_now == 0
    row_now = lax.axis_index("row")
    n_row, n_col = lax.axis_size("row"), lax.axis_size("col")
    count = tokens.shape[1]
    top = routes.shape[3]
    capacity = count * top * 4 // (3 * n_row * n_col)
    width = tokens.shape[2]

    def pair(own, other):
        return (jnp.where(first, own, other), jnp.where(first, other, own))

    small_in = (
        norm_in[0],
        step_bias[0],
        decay_log[0],
        skip_gain[0],
        conv_input[0],
        conv_state[0],
        gate_norm[0],
        norm_mid[0],
    )
    vector = flat(small_in)
    params = [unflat(part, [v.shape for v in small_in]) for part in pair(vector, swapped(vector))]

    def both_layers(weight):
        whole = lax.all_gather(weight, ("section", "row"), axis=0, tiled=True)
        return whole.reshape(2, n_row * weight.shape[0], weight.shape[1])

    proj = both_layers(
        jnp.concatenate([proj_gate[0], proj_input[0], proj_state[0], proj_step[0]], axis=1)
    )
    proj_out = both_layers(proj_output[0])
    shared = both_layers(jnp.concatenate([shared_gate[0], shared_up[0], shared_down[0]], axis=1))
    gate_all = lax.all_gather(expert_gate[0, 0], "section")
    up_all = lax.all_gather(expert_up[0, 0], "section")
    down_all = lax.all_gather(expert_down[0, 0], "section")
    dense = [
        (proj[s], proj_out[s], shared[s], gate_all[s], up_all[s], down_all[s]) for s in range(2)
    ]

    meta = jnp.concatenate([routes.astype(FLOAT), gates], axis=3)[0]
    keep = lax.dynamic_index_in_dim(meta, section_now, 0, keepdims=False)
    give = lax.dynamic_index_in_dim(meta, 1 - section_now, 0, keepdims=False)
    meta = jnp.concatenate(pair(keep, swapped(give)), axis=1)
    meta = lax.all_gather(meta, "col", axis=0)
    tables = [
        route_tables(meta[:, :, : 2 * top], top, capacity),
        route_tables(meta[:, :, 2 * top :], top, capacity),
    ]
    lengths = lax.dynamic_slice(
        doc_lengths, (section_now, row_now, 0), (1, 1, doc_lengths.shape[2])
    )
    labels = local_docs(lengths[0, 0], row_now, n_col * count)

    resid = lax.dynamic_index_in_dim(tokens, section_now, 0, keepdims=False)
    grad = lax.dynamic_index_in_dim(cotangent, section_now, 0, keepdims=False)
    outputs, stored = [], []
    for s in range(2):
        resid, saved = layer_forward(resid, params[s], dense[s], labels, tables[s])
        outputs.append(resid)
        stored.append(saved)
    grads = [None, None]
    backs = [None, None]
    for s in (1, 0):
        grad, small, dense_grads, expert_grads = layer_backward(
            grad, stored[s], params[s], dense[s], tables[s]
        )
        backs[s] = grad
        grads[s] = (small, dense_grads, expert_grads)

    def own_layer(first_value, second_value):
        keep = jnp.where(first, first_value, second_value)
        give = jnp.where(first, second_value, first_value).astype(HALF)
        return keep.astype(FLOAT) + swapped(give).astype(FLOAT)

    def own_rows(index):
        both = jnp.concatenate([grads[0][1][index], grads[1][1][index]], axis=0)
        return lax.psum_scatter(both, ("section", "row"), scatter_dimension=0, tiled=True)

    grad_proj, grad_out, grad_shared = [own_rows(index) for index in range(3)]
    expert_out = [own_layer(a, b) for a, b in zip(grads[0][2], grads[1][2])]
    shapes = [part.shape for part in grads[0][0]]
    vector = jnp.stack([flat(grads[0][0]), flat(grads[1][0])])
    vector = lax.psum(vector, ("section", "row"))
    vector = lax.dynamic_index_in_dim(vector, section_now, 0, keepdims=False)
    wide = 2 * width + conv_state.shape[1] * conv_state.shape[2]
    inner = gate_norm.shape[1]
    state = conv_state.shape[2]
    state_grad = grad_proj[:, 2 * inner : 2 * inner + state]
    shared_sum, state_grad = lax.psum((vector[:wide], state_grad), "col")
    (
        out_norm_in,
        out_norm_mid,
        out_conv_state,
        out_conv_input,
        out_gate_norm,
        out_step_bias,
        out_decay_log,
        out_skip_gain,
    ) = unflat(jnp.concatenate([shared_sum, vector[wide:]]), shapes)

    def per_micro(first_value, second_value):
        keep = jnp.where(first, first_value, second_value)
        other = swapped(jnp.where(first, second_value, first_value).astype(HALF)).astype(FLOAT)
        return jnp.stack(pair(keep, other))[None]

    hidden = shared_gate.shape[2]
    grad_proj, grad_out, grad_shared, state_grad = [
        part.astype(FLOAT)[None] for part in (grad_proj, grad_out, grad_shared, state_grad)
    ]
    return (
        per_micro(outputs[0], outputs[1]),
        per_micro(backs[0], backs[1]),
        out_norm_in[None],
        grad_proj[:, :, :inner],
        grad_proj[:, :, inner : 2 * inner],
        state_grad,
        grad_proj[:, :, 2 * inner + state :],
        out_step_bias[None],
        out_decay_log[None],
        out_skip_gain[None],
        out_conv_input[None],
        out_conv_state[None],
        out_gate_norm[None],
        grad_out,
        out_norm_mid[None],
        expert_out[0][None, None],
        expert_out[1][None, None],
        expert_out[2][None, None],
        grad_shared[:, :, :hidden],
        grad_shared[:, :, hidden : 2 * hidden],
        grad_shared[:, :, 2 * hidden :],
    )


def solution(mesh):
    in_specs = (
        P(None, ("row", "col"), None),
        P(None, ("row", "col"), None),
        P(),
        P("section", None, ("row", "col"), None),
        P("section", None, ("row", "col"), None),
        P("section", None),
        P("section", "row", "col"),
        P("section", "row", "col"),
        P("section", "row", None),
        P("section", "row", "col"),
        P("section", "col"),
        P("section", "col"),
        P("section", "col"),
        P("section", None, "col"),
        P("section", None, None),
        P("section", "col"),
        P("section", "row", "col"),
        P("section", None),
        P("section", ("row", "col"), None, None),
        P("section", ("row", "col"), None, None),
        P("section", ("row", "col"), None, None),
        P("section", "row", "col"),
        P("section", "row", "col"),
        P("section", "row", "col"),
    )
    out_specs = (
        P("section", None, ("row", "col"), None),
        P("section", None, ("row", "col"), None),
        P("section", None),
        P("section", "row", "col"),
        P("section", "row", "col"),
        P("section", "row", None),
        P("section", "row", "col"),
        P("section", "col"),
        P("section", "col"),
        P("section", "col"),
        P("section", None, "col"),
        P("section", None, None),
        P("section", "col"),
        P("section", "row", "col"),
        P("section", None),
        P("section", ("row", "col"), None, None),
        P("section", ("row", "col"), None, None),
        P("section", ("row", "col"), None, None),
        P("section", "row", "col"),
        P("section", "row", "col"),
        P("section", "row", "col"),
    )
    return jax.shard_map(shards, mesh=mesh, in_specs=in_specs, out_specs=out_specs, check_vma=False)
```

time: 2820 us -> 1400 us (0.50)
  waiting for transfers between devices: 1050 us -> 288 us
  blocking collectives: 375 us -> 67.6 us
  matrix products: 599 us -> 320 us
  starting transfers between devices: 69.5 us -> 333 us
  local copies, waits for them, and re-layouts: 344 us -> 157 us
  other arithmetic: 340 us -> 194 us
    all_to_all x13 -> x0, waiting for transfers between devices: 511 us -> none  [the longest x3 191 us: routed_backward(): lax.all_to_all(outgoing, ('row', 'col'), split_axis=0, concat_axis=0, til...]
    all_gather x15 -> x6, waiting for transfers between devices: 330 us -> 0.01 us  [the longest x3 0.01 us: both_layers(): whole = lax.all_gather(weight, ('section', 'row'), axis=0, tiled=True)]
    ppermute x4 -> x163, starting transfers between devices: 5.41 us -> 332 us  [the longest x156 332 us: shifted(): lax.ppermute(block, axis, [(i, (i + distance) % count) for i in range(cou...]
    ppermute x4 -> x163, waiting for transfers between devices: 3.9 us -> 261 us  [the longest x156 261 us: shifted(): lax.ppermute(block, axis, [(i, (i + distance) % count) for i in range(cou...]
    reduce_scatter x19 -> x1, waiting for transfers between devices: 198 us -> 0.01 us  [own_rows(): lax.psum_scatter(both, ('section', 'row'), scatter_dimension=0, tiled=True)]
    all_to_all x2 -> x0, blocking collectives: 154 us -> none  [routed_forward(): lax.all_to_all(outgoing, ('row', 'col'), split_axis=0, concat_axis=0, til...]
    dot_general x54 -> x56, matrix products: 205 us -> 68.1 us  [project_back(): lax.dot_general(left, right, (((1,), (1,)), ((), ())), preferred_element_...]
    gather x15 -> x0, local copies, waits for them, and re-layouts: 111 us -> none  [the longest x3 27.7 us: routed_backward(): jnp.take(padded_grad, sources, axis=0)]
  transfers between devices with their start and end apart: 53 -> 173, of which waited for: 34 -> 57; matrix products, arithmetic and copies ran while one was open for 36% -> 43% of each run, Pallas kernels for 0% -> 0%
where the time goes in v1:
time: 1400 us; the launch traced here: 1380 us
  starting transfers between devices  333 us (24%)
  matrix products  320 us (23%)
  waiting for transfers between devices  288 us (21%)
  other arithmetic  194 us (14%)
  local copies, waits for them, and re-layouts  157 us (11%)
  blocking collectives  67.6 us (5%)
  between operations  23.5 us (2%)
    ppermute x156, starting transfers between devices, shifted(): lax.ppermute(block, axis, [(i, (i + distance) % count) for i in range(cou...  332 us
    ppermute x156, waiting for transfers between devices, shifted(): lax.ppermute(block, axis, [(i, (i + distance) % count) for i in range(cou...  261 us
    unnamed x995, local copies, waits for them, and re-layouts  100 us
    dot_general x6, matrix products, advance(): inner = jnp.einsum('tsh,shp->thp', mixing, values, precision=HIGH)  90.1 us
    dot_general x56, matrix products, project_back(): lax.dot_general(left, right, (((1,), (1,)), ((), ())), preferred_element_...  68.1 us
    dot_general x60, matrix products, project(): return jnp.dot(left, right, preferred_element_type=FLOAT)  61.3 us
    dot_general x30, matrix products, outer(): lax.dot_general(left, right, (((0,), (0,)), ((), ())), preferred_element_...  60.3 us
    another operation x23, other arithmetic  33.6 us
  transfers between devices with their start and end apart: 173, of which 57 were waited for; matrix products, arithmetic and copies ran while one was open for 43% of the time, Pallas kernels for 0%

profile of v1, /device:TPU:0, one launch (start us, length us, event | category | flops | bytes accessed | tf_op | source)
XLA Modules:
  0.0 1383.5 jit_solution(12470374227590013040)
XLA Ops:
  38.7 22.4 %all-gather.1 = f32[512,24]{0,1:T(8,128)} all-gather(f32[128,24]{0,1:T(8,128)S(1)} %pad_maximum_fusion.31), channel_id=3, replica_groups=mesh['section'=2,'row'=4,'col'=4] {'col'}, dimensions={0}, use_global_device_ids=true | all-gather | bytes 61440 | tf_op jit(solution)/shard_map/all_gather | solution.py:508
  135.4 17.0 %collective-permute-done.2 = bf16[128,1536]{1,0:T(8,128)(2,1)S(1)} collective-permute-done((bf16[128,1536]{1,0:T(8,128)(2,1)S(1)}, bf16[128,1536]{1,0:T(8,128)(2,1)S(1)}, u32[]{:S(2)}, u32[]{:S(2)}) %collective-permute-start.2) | collective-permute-done | bytes 393248 | tf_op jit(solution)/shard_map/ppermute | solution.py:20
  161.6 6.9 collective-permute-done.96
  190.1 14.3 %fusion.16 = f32[12,64,512]{2,1,0:T(8,128)S(1)} fusion(f32[512,12,64]{0,2,1:T(8,128)S(1)} %bitcast.721, f32[512,12]{0,1:T(8,128)S(1)} %get-tuple-element.272, f32[512,512]{1,0:T(8,128)S(1)} %fusion.877, f32[512,12]{0,1:T(8,128)S(1)} %bitcast.771, pred[512,512]{1,0:T(8,128)(4,1)S(1)} %copy-done.177), kind=kOutput, calls=%fused_computation.24 | convolution fusion | flops 2428502016 | bytes 4505600 | tf_op jit(solution)/shard_map/jvp()/while/body/eval_jaxpr/tsh,shp->thp/dot_general | solution.py:58
  230.5 22.2 %collective-permute-start.9 = (f32[128,1]{0,1:T(1,128)S(1)}, f32[128,1]{0,1:T(1,128)S(1)}, u32[]{:S(2)}, u32[]{:S(2)}) collective-permute-start(f32[128,1]{0,1:T(1,128)S(1)} %get-tuple-element.771), channel_id=1, source_target_pairs={{0,1},{1,2},{2,3},{3,0},{4,5},{5,6},{6,7},{7,4},{8,9},{9,10},{10,1... | collective-permute-start | bytes 1544 | tf_op jit(solution)/shard_map/ppermute | solution.py:20
  384.1 22.8 %collective-permute-done.42 = bf16[128,1536]{1,0:T(8,128)(2,1)S(1)} collective-permute-done((bf16[128,1536]{1,0:T(8,128)(2,1)S(1)}, bf16[128,1536]{1,0:T(8,128)(2,1)S(1)}, u32[]{:S(2)}, u32[]{:S(2)}) %collective-permute-start.42) | collective-permute-done | bytes 393248 | tf_op jit(solution)/shard_map/ppermute | solution.py:20
  419.9 14.3 %fusion.10 = f32[12,64,512]{2,1,0:T(8,128)S(1)} fusion(f32[512,12,64]{0,2,1:T(8,128)S(1)} %bitcast.726, f32[512,12]{0,1:T(8,128)S(1)} %get-tuple-element.240, f32[512,512]{1,0:T(8,128)S(1)} %fusion.875, f32[512,12]{0,1:T(8,128)S(1)} %bitcast.773, pred[512,512]{1,0:T(8,128)(4,1)S(1)} %copy-done.178), kind=kOutput, calls=%fused_computation.18 | convolution fusion | flops 2428502016 | bytes 4505600 | tf_op jit(solution)/shard_map/jvp()/while/body/eval_jaxpr/tsh,shp->thp/dot_general | solution.py:58
  445.5 8.6 collective-permute-done.47
  454.1 20.7 %collective-permute-start.49 = (f32[128,1]{0,1:T(1,128)S(1)}, f32[128,1]{0,1:T(1,128)S(1)}, u32[]{:S(2)}, u32[]{:S(2)}) collective-permute-start(f32[128,1]{0,1:T(1,128)S(1)} %get-tuple-element.768), channel_id=1, source_target_pairs={{0,1},{1,2},{2,3},{3,0},{4,5},{5,6},{6,7},{7,4},{8,9},{9,10},{10,1... | collective-permute-start | bytes 1544 | tf_op jit(solution)/shard_map/ppermute | solution.py:20
  506.4 8.8 collective-permute-done.64
  574.5 14.4 %collective-permute-start.84 = (bf16[64,1536]{1,0:T(8,128)(2,1)S(1)}, bf16[64,1536]{1,0:T(8,128)(2,1)S(1)}, u32[]{:S(2)}, u32[]{:S(2)}) collective-permute-start(bf16[64,1536]{1,0:T(8,128)(2,1)S(1)} %get-tuple-element.622), channel_id=1, source_target_pairs={{0,12},{4,0},{8,4},{12,8},{1,13},{5,1},{9,5},{13,9},{2,14},{6,2},{... | collective-permute-start | bytes 589832 | tf_op jit(solution)/shard_map/ppermute | solution.py:20
  616.0 8.2 collective-permute-start.94
  645.2 12.8 collective-permute-done.102
  658.1 19.5 %collective-permute-start.79 = (bf16[128,1536]{1,0:T(8,128)(2,1)S(1)}, bf16[128,1536]{1,0:T(8,128)(2,1)S(1)}, u32[]{:S(2)}, u32[]{:S(2)}) collective-permute-start(bf16[128,1536]{1,0:T(8,128)(2,1)S(1)} %fusion.95), channel_id=1, source_target_pairs={{0,1},{1,2},{2,3},{3,0},{4,5},{5,6},{6,7},{7,4},{8,9},{9,10},{10,1... | collective-permute-start | bytes 1179656 | tf_op jit(solution)/shard_map/ppermute | solution.py:20
  693.1 11.7 collective-permute-start.112
  706.3 6.7 collective-permute-start.113
  754.6 20.4 %fusion.23 = (f32[512,12]{0,1:T(8,128)}, f32[512,12]{0,1:T(8,128)}, f32[512,12]{0,1:T(8,128)}, f32[512,512]{1,0:T(8,128)}) fusion(f32[512,12]{0,1:T(8,128)S(1)} %copy-done.101, f32[512,512]{1,0:T(8,128)} %fusion.937, f32[512,12]{0,1:T(8,128)S(1)} %bitcast.753, pred[512,512]{1,0:T(8,128)(4,1)S(1)} %compare_and_fusion.1, f32[512,12,64]{0,2,1:T(8,128)S(1)} %bitcast.730, ...), kind=kOutput, calls=%fused_computation.34 | convolution fusion | flops 2456532992 | bytes 5627904 | tf_op jit(solution)/shard_map/transpose(jvp())/while/body/eval_jaxpr/checkpoint/tsh,shp->thp/dot_general | solution.py:58
  775.1 10.7 bitcast_add_fusion.1
  837.5 8.5 convolution_convert_fusion
  846.1 15.7 %collective-permute-done.118 = bf16[128,1536]{1,0:T(8,128)(2,1)S(1)} collective-permute-done((bf16[128,1536]{1,0:T(8,128)(2,1)S(1)}, bf16[128,1536]{1,0:T(8,128)(2,1)S(1)}, u32[]{:S(2)}, u32[]{:S(2)}) %collective-permute-start.118) | collective-permute-done | bytes 393248 | tf_op jit(solution)/shard_map/ppermute | solution.py:20
  958.1 11.1 collective-permute-start.133
  974.3 20.7 %maximum_maximum_fusion = bf16[3072,768]{0,1:T(8,128)(2,1)} fusion(bf16[1536,256]{0,1:T(8,128)(2,1)S(1)} %copy-done.102, bf16[1536,512]{0,1:T(8,128)(2,1)S(1)} %copy-done.78, bf16[1536,256]{0,1:T(8,128)(2,1)S(1)} %convolution_convert_fusion.7, bf16[1536,512]{0,1:T(8,128)(2,1)S(1)} %convolution_convert_fusion.5), kind=kLoop, calls=%fused_computation.62 | loop fusion | flops 18874368 | bytes 9437184 | tf_op jit(solution)/shard_map/concatenate | solution.py:540
  1021.1 21.5 %collective-permute-done.151 = f32[128,2]{0,1:T(2,128)S(1)} collective-permute-done((f32[128,2]{0,1:T(2,128)S(1)}, f32[128,2]{0,1:T(2,128)S(1)}, u32[]{:S(2)}, u32[]{:S(2)}) %collective-permute-start.151) | collective-permute-done | bytes 1056 | tf_op jit(solution)/shard_map/ppermute | solution.py:20
  1084.3 19.1 %fusion.25 = (f32[512,12]{0,1:T(8,128)}, f32[512,12]{0,1:T(8,128)}, f32[512,12]{0,1:T(8,128)}, f32[512,512]{1,0:T(8,128)}) fusion(f32[512,12]{0,1:T(8,128)S(1)} %copy-done.97, f32[512,512]{1,0:T(8,128)S(1)} %fusion.938, f32[512,12]{0,1:T(8,128)S(1)} %bitcast.746, pred[512,512]{1,0:T(8,128)(4,1)S(1)} %copy-done.179, f32[512,12,64]{0,2,1:T(8,128)S(1)} %bitcast.724, ...), kind=kOutput, calls=%fused_computation.36 | convolution fusion | flops 2456532992 | bytes 5627904 | tf_op jit(solution)/shard_map/transpose(jvp())/while/body/eval_jaxpr/checkpoint/tsh,shp->thp/dot_general | solution.py:58
  1136.9 11.2 bitcast_add_fusion
  1154.3 6.8 convolution_convert_fusion.1
  1167.1 14.9 %copy.289 = bf16[3072,1804]{1,0:T(8,128)(2,1)} copy(bf16[3072,1804]{0,1:T(8,128)(2,1)} %pad_maximum_fusion) | data formatting | bytes 22167552
  1194.9 6.9 select_convert_fusion
  1233.5 24.3 %collective-permute-done.157 = bf16[128,1536]{1,0:T(8,128)(2,1)} collective-permute-done((bf16[128,1536]{1,0:T(8,128)(2,1)}, bf16[128,1536]{1,0:T(8,128)(2,1)}, u32[]{:S(2)}, u32[]{:S(2)}) %collective-permute-start.157) | collective-permute-done | bytes 393248 | tf_op jit(solution)/shard_map/ppermute | solution.py:20
  1264.5 28.2 %psum.21 = f32[2,7972]{1,0:T(2,128)S(1)} all-reduce(f32[2,7972]{1,0:T(2,128)S(1)} %pad_maximum_fusion.30), channel_id=1, replica_groups=mesh['section'=2,'row'=4,'col'=4] {'section','row'}, use_global_device_ids=true, to_apply=%region_92.94 | all-reduce | flops 15944 | bytes 127552 | tf_op jit(solution)/shard_map/psum | solution.py:547
  1292.7 17.1 %psum.22 = f32[4096]{0:T(1024)S(1)} all-reduce(f32[4096]{0:T(1024)S(1)} %bitcast.776), channel_id=1, replica_groups=mesh['section'=2,'row'=4,'col'=4] {'col'}, use_global_device_ids=true, to_apply=%region_93.95 | all-reduce | flops 4096 | bytes 32768 | tf_op jit(solution)/shard_map/psum | solution.py:553
  1348.5 26.0 %all-reduce.53.cloned.1.call-done = bf16[1,384,256]{1,2,0:T(8,128)(2,1)} async-done(((bf16[1,384,256]{1,2,0:T(8,128)(2,1)}), bf16[1,384,256]{1,2,0:T(8,128)(2,1)}) %all-reduce.53.cloned.1.call-update) | async-done | bytes 196624 | tf_op jit(solution)/shard_map/psum | solution.py:553
  (1786 shorter events, 865.6 us)
Async XLA Ops:
  7.2 165.4 %all-gather.12.cloned.1.call-start = ((), (), s32[]{:S(2)}) async-start(), calls=%async_computation.3 | async-start | bytes 13271040 | tf_op jit(solution)/shard_map/all_gather | solution.py:489
  10.7 199.4 %all-gather.16.cloned.1.call-start = ((), (), s32[]{:S(2)}) async-start(), calls=%async_computation.7 | async-start | bytes 5308416 | tf_op jit(solution)/shard_map/all_gather | solution.py:489
  11.5 252.8 %all-gather.14.cloned.1.call-start = ((), (), s32[]{:S(2)}) async-start(), calls=%async_computation.4 | async-start | bytes 5308416 | tf_op jit(solution)/shard_map/all_gather | solution.py:489
  12.7 257.5 %all-gather.18.cloned.1.call-start = ((), (), s32[]{:S(2)}) async-start(), calls=%async_computation.8 | async-start | bytes 4718592 | tf_op jit(solution)/shard_map/all_gather | solution.py:497
  13.3 260.0 %all-gather.20.cloned.1.call-start = ((), (), s32[]{:S(2)}) async-start(), calls=%async_computation.9 | async-start | bytes 4718592 | tf_op jit(solution)/shard_map/all_gather | solution.py:498
  13.8 262.7 %all-gather.22.cloned.1.call-start = ((), (), s32[]{:S(2)}) async-start(), calls=%async_computation.10 | async-start | bytes 4718592 | tf_op jit(solution)/shard_map/all_gather | solution.py:499
  14.9 109.7 %collective-permute-start.87 = (bf16[128,1536]{1,0:T(8,128)(2,1)}, bf16[128,1536]{1,0:T(8,128)(2,1)S(1)}, u32[]{:S(2)}, u32[]{:S(2)}) collective-permute-start(bf16[128,1536]{1,0:T(8,128)(2,1)} %bitcast_convert_fusion.1), channel_id=1, source_target_pairs={{0,1},{1,2},{2,3},{3,0},{4,5},{5,6},{6,7},{7,4},{8,9},{9,10},{10,1... | collective-permute-start | bytes 1179656 | tf_op jit(solution)/shard_map/ppermute | solution.py:20
  17.9 110.4 %collective-permute-start.95 = (bf16[128,1536]{1,0:T(8,128)(2,1)}, bf16[128,1536]{1,0:T(8,128)(2,1)}, u32[]{:S(2)}, u32[]{:S(2)}) collective-permute-start(bf16[128,1536]{1,0:T(8,128)(2,1)} %bitcast_convert_fusion.1), channel_id=1, source_target_pairs={{0,2},{1,3},{2,0},{3,1},{4,6},{5,7},{6,4},{7,5},{8,10},{9,11},{10,... | collective-permute-start | bytes 1179656 | tf_op jit(solution)/shard_map/ppermute | solution.py:20
  20.5 110.5 %collective-permute-start.103 = (bf16[128,1536]{1,0:T(8,128)(2,1)}, bf16[128,1536]{1,0:T(8,128)(2,1)}, u32[]{:S(2)}, u32[]{:S(2)}) collective-permute-start(bf16[128,1536]{1,0:T(8,128)(2,1)} %bitcast_convert_fusion.1), channel_id=1, source_target_pairs={{0,3},{1,0},{2,1},{3,2},{4,7},{5,4},{6,5},{7,6},{8,11},{9,8},{10,9... | collective-permute-start | bytes 1179656 | tf_op jit(solution)/shard_map/ppermute | solution.py:20
  31.8 74.2 %collective-permute-start = (f32[7972]{0:T(1024)}, f32[7972]{0:T(1024)}, u32[]{:S(2)}, u32[]{:S(2)}) collective-permute-start(f32[7972]{0:T(1024)} %concatenate.252), channel_id=1, source_target_pairs={{0,16},{16,0},{1,17},{17,1},{2,18},{18,2},{3,19},{19,3},{4,20},{20... | collective-permute-start | bytes 95672 | tf_op jit(solution)/shard_map/ppermute | solution.py:24
  32.4 1297.4 %reduce-scatter.12.cloned.1.call-start = ((), (), s32[]{:S(2)}) async-start(), calls=%async_computation.12 | async-start | bytes 5308416
  158.5 65.7 %collective-permute-start.98 = (bf16[64,1536]{1,0:T(8,128)(2,1)S(1)}, bf16[64,1536]{1,0:T(8,128)(2,1)}, u32[]{:S(2)}, u32[]{:S(2)}) collective-permute-start(bf16[64,1536]{1,0:T(8,128)(2,1)S(1)} %get-tuple-element.535), channel_id=1, source_target_pairs={{0,12},{4,0},{8,4},{12,8},{1,13},{5,1},{9,5},{13,9},{2,14},{6,2},{... | collective-permute-start | bytes 589832 | tf_op jit(solution)/shard_map/ppermute | solution.py:20
  213.4 41.0 %collective-permute-start.4 = (bf16[128,1536]{1,0:T(8,128)(2,1)S(1)}, bf16[128,1536]{1,0:T(8,128)(2,1)S(1)}, u32[]{:S(2)}, u32[]{:S(2)}) collective-permute-start(bf16[128,1536]{1,0:T(8,128)(2,1)S(1)} %convolution_convert_fusion.38), channel_id=1, source_target_pairs={{0,3},{1,0},{2,1},{3,2},{4,7},{5,4},{6,5},{7,6},{8,11},{9,8},{10,9... | collective-permute-start | bytes 1179656 | tf_op jit(solution)/shard_map/ppermute | solution.py:20
  278.8 83.9 %collective-permute-start.14 = (bf16[64,1536]{1,0:T(8,128)(2,1)S(1)}, bf16[64,1536]{1,0:T(8,128)(2,1)S(1)}, u32[]{:S(2)}, u32[]{:S(2)}) collective-permute-start(bf16[64,1536]{1,0:T(8,128)(2,1)S(1)} %get-tuple-element.654), channel_id=1, source_target_pairs={{0,12},{4,0},{8,4},{12,8},{1,13},{5,1},{9,5},{13,9},{2,14},{6,2},{... | collective-permute-start | bytes 589832 | tf_op jit(solution)/shard_map/ppermute | solution.py:20
  315.9 53.4 %collective-permute-start.24 = (bf16[128,1536]{1,0:T(8,128)(2,1)S(1)}, bf16[128,1536]{1,0:T(8,128)(2,1)S(1)}, u32[]{:S(2)}, u32[]{:S(2)}) collective-permute-start(bf16[128,1536]{1,0:T(8,128)(2,1)S(1)} %fusion.84), channel_id=1, source_target_pairs={{0,3},{1,0},{2,1},{3,2},{4,7},{5,4},{6,5},{7,6},{8,11},{9,8},{10,9... | collective-permute-start | bytes 1179656 | tf_op jit(solution)/shard_map/ppermute | solution.py:20
  475.6 114.4 %collective-permute-start.104 = (bf16[64,1536]{1,0:T(8,128)(2,1)}, bf16[64,1536]{1,0:T(8,128)(2,1)S(1)}, u32[]{:S(2)}, u32[]{:S(2)}) collective-permute-start(bf16[64,1536]{1,0:T(8,128)(2,1)} %get-tuple-element.532), channel_id=1, source_target_pairs={{0,4},{4,8},{8,12},{12,0},{1,5},{5,9},{9,13},{13,1},{2,6},{6,10},{... | collective-permute-start | bytes 589832 | tf_op jit(solution)/shard_map/ppermute | solution.py:20
  476.1 114.1 %collective-permute-start.105 = (bf16[64,1536]{1,0:T(8,128)(2,1)}, bf16[64,1536]{1,0:T(8,128)(2,1)S(1)}, u32[]{:S(2)}, u32[]{:S(2)}) collective-permute-start(bf16[64,1536]{1,0:T(8,128)(2,1)} %get-tuple-element.531), channel_id=1, source_target_pairs={{0,8},{4,12},{8,0},{12,4},{1,9},{5,13},{9,1},{13,5},{2,10},{6,14},... | collective-permute-start | bytes 589832 | tf_op jit(solution)/shard_map/ppermute | solution.py:20
  574.5 41.5 %collective-permute-start.84 = (bf16[64,1536]{1,0:T(8,128)(2,1)S(1)}, bf16[64,1536]{1,0:T(8,128)(2,1)S(1)}, u32[]{:S(2)}, u32[]{:S(2)}) collective-permute-start(bf16[64,1536]{1,0:T(8,128)(2,1)S(1)} %get-tuple-element.622), channel_id=1, source_target_pairs={{0,12},{4,0},{8,4},{12,8},{1,13},{5,1},{9,5},{13,9},{2,14},{6,2},{... | collective-permute-start | bytes 589832 | tf_op jit(solution)/shard_map/ppermute | solution.py:20
  638.8 40.5 %collective-permute-start.53 = (bf16[64,1536]{1,0:T(8,128)(2,1)S(1)}, bf16[64,1536]{1,0:T(8,128)(2,1)S(1)}, u32[]{:S(2)}, u32[]{:S(2)}) collective-permute-start(bf16[64,1536]{1,0:T(8,128)(2,1)S(1)} %get-tuple-element.638), channel_id=1, source_target_pairs={{0,12},{4,0},{8,4},{12,8},{1,13},{5,1},{9,5},{13,9},{2,14},{6,2},{... | collective-permute-start | bytes 589832 | tf_op jit(solution)/shard_map/ppermute | solution.py:20
  640.0 41.2 %collective-permute-start.54 = (bf16[64,1536]{1,0:T(8,128)(2,1)S(1)}, bf16[64,1536]{1,0:T(8,128)(2,1)S(1)}, u32[]{:S(2)}, u32[]{:S(2)}) collective-permute-start(bf16[64,1536]{1,0:T(8,128)(2,1)S(1)} %get-tuple-element.637), channel_id=1, source_target_pairs={{0,8},{4,12},{8,0},{12,4},{1,9},{5,13},{9,1},{13,5},{2,10},{6,14},... | collective-permute-start | bytes 589832 | tf_op jit(solution)/shard_map/ppermute | solution.py:20
  641.3 46.5 %collective-permute-start.63 = (bf16[128,1536]{1,0:T(8,128)(2,1)S(1)}, bf16[128,1536]{1,0:T(8,128)(2,1)S(1)}, u32[]{:S(2)}, u32[]{:S(2)}) collective-permute-start(bf16[128,1536]{1,0:T(8,128)(2,1)S(1)} %fusion.93), channel_id=1, source_target_pairs={{0,3},{1,0},{2,1},{3,2},{4,7},{5,4},{6,5},{7,6},{8,11},{9,8},{10,9... | collective-permute-start | bytes 1179656 | tf_op jit(solution)/shard_map/ppermute | solution.py:20
  713.0 151.5 %collective-permute-start.80 = (bf16[128,1536]{1,0:T(8,128)(2,1)}, bf16[128,1536]{1,0:T(8,128)(2,1)}, u32[]{:S(2)}, u32[]{:S(2)}) collective-permute-start(bf16[128,1536]{1,0:T(8,128)(2,1)} %get-tuple-element.807), channel_id=1, source_target_pairs={{0,16},{16,0},{1,17},{17,1},{2,18},{18,2},{3,19},{19,3},{4,20},{20... | collective-permute-start | bytes 1179656 | tf_op jit(solution)/shard_map/ppermute | solution.py:24
  887.0 86.1 %collective-permute-start.123 = (bf16[64,1536]{1,0:T(8,128)(2,1)S(1)}, bf16[64,1536]{1,0:T(8,128)(2,1)S(1)}, u32[]{:S(2)}, u32[]{:S(2)}) collective-permute-start(bf16[64,1536]{1,0:T(8,128)(2,1)S(1)} %get-tuple-element.604), channel_id=1, source_target_pairs={{0,12},{4,0},{8,4},{12,8},{1,13},{5,1},{9,5},{13,9},{2,14},{6,2},{... | collective-permute-start | bytes 589832 | tf_op jit(solution)/shard_map/ppermute | solution.py:20
  888.7 113.0 %collective-permute-start.124 = (bf16[64,1536]{1,0:T(8,128)(2,1)}, bf16[64,1536]{1,0:T(8,128)(2,1)}, u32[]{:S(2)}, u32[]{:S(2)}) collective-permute-start(bf16[64,1536]{1,0:T(8,128)(2,1)} %get-tuple-element.603), channel_id=1, source_target_pairs={{0,8},{4,12},{8,0},{12,4},{1,9},{5,13},{9,1},{13,5},{2,10},{6,14},... | collective-permute-start | bytes 589832 | tf_op jit(solution)/shard_map/ppermute | solution.py:20
  951.1 50.7 %collective-permute-start.125 = (bf16[64,1536]{1,0:T(8,128)(2,1)}, bf16[64,1536]{1,0:T(8,128)(2,1)}, u32[]{:S(2)}, u32[]{:S(2)}) collective-permute-start(bf16[64,1536]{1,0:T(8,128)(2,1)} %get-tuple-element.602), channel_id=1, source_target_pairs={{0,4},{4,8},{8,12},{12,0},{1,5},{5,9},{9,13},{13,1},{2,6},{6,10},{... | collective-permute-start | bytes 589832 | tf_op jit(solution)/shard_map/ppermute | solution.py:20
  958.1 43.6 %collective-permute-start.133 = (bf16[128,1536]{1,0:T(8,128)(2,1)}, bf16[128,1536]{1,0:T(8,128)(2,1)S(1)}, u32[]{:S(2)}, u32[]{:S(2)}) collective-permute-start(bf16[128,1536]{1,0:T(8,128)(2,1)} %fusion.109), channel_id=1, source_target_pairs={{0,3},{1,0},{2,1},{3,2},{4,7},{5,4},{6,5},{7,6},{8,11},{9,8},{10,9... | collective-permute-start | bytes 1179656 | tf_op jit(solution)/shard_map/ppermute | solution.py:20
  1001.7 332.4 %reduce-scatter.8.cloned.1.call-start = ((), (), s32[]{:S(2)}) async-start(), calls=%async_computation.6 | async-start | bytes 5308416 | tf_op jit(solution)/shard_map/reduce_scatter | solution.py:541
  1076.5 259.7 %reduce-scatter.10.cloned.1.call-start = ((), (), s32[]{:S(2)}) async-start(), calls=%async_computation.11 | async-start | bytes 13271040
  1182.0 192.4 %all-reduce.53.cloned.1.call-start = ((), (), s32[]{:S(2)}) async-start(), calls=%async_computation.5 | async-start | bytes 393216 | tf_op jit(solution)/shard_map/psum | solution.py:553
  1201.8 114.2 %collective-permute-start.162 = (bf16[512,1536]{1,0:T(8,128)(2,1)}, bf16[512,1536]{1,0:T(8,128)(2,1)}, u32[]{:S(2)}, u32[]{:S(2)}) collective-permute-start(bf16[512,1536]{1,0:T(8,128)(2,1)} %get-tuple-element.816), channel_id=1, source_target_pairs={{0,16},{16,0},{1,17},{17,1},{2,18},{18,2},{3,19},{19,3},{4,20},{20... | collective-permute-start | bytes 4718600 | tf_op jit(solution)/shard_map/ppermute | solution.py:24
  1208.4 111.7 %collective-permute-start.161 = (bf16[1536,512]{1,0:T(8,128)(2,1)}, bf16[1536,512]{1,0:T(8,128)(2,1)}, u32[]{:S(2)}, u32[]{:S(2)}) collective-permute-start(bf16[1536,512]{1,0:T(8,128)(2,1)} %get-tuple-element.814), channel_id=1, source_target_pairs={{0,16},{16,0},{1,17},{17,1},{2,18},{18,2},{3,19},{19,3},{4,20},{20... | collective-permute-start | bytes 4718600 | tf_op jit(solution)/shard_map/ppermute | solution.py:24
  1233.4 90.8 %collective-permute-start.160 = (bf16[1536,512]{1,0:T(8,128)(2,1)}, bf16[1536,512]{1,0:T(8,128)(2,1)}, u32[]{:S(2)}, u32[]{:S(2)}) collective-permute-start(bf16[1536,512]{1,0:T(8,128)(2,1)} %get-tuple-element.812), channel_id=1, source_target_pairs={{0,16},{16,0},{1,17},{17,1},{2,18},{18,2},{3,19},{19,3},{4,20},{20... | collective-permute-start | bytes 4718600 | tf_op jit(solution)/shard_map/ppermute | solution.py:24
  (576 other events, 5832.8 us)
Sparse Core Ops, SparseCore 0:
  10.8 71.4 all-gather.11
  84.2 43.1 all-gather.15
  129.9 50.2 all-gather.13
  181.7 11.3 all-gather.17
  194.5 13.2 all-gather.19
  209.2 13.2 all-gather.21
  1001.8 54.7 reduce-scatter.11
  1076.6 55.4 reduce-scatter.7
  1182.1 89.8 reduce-scatter.9
  1342.3 32.1 all-reduce.52

commit v2 on v1

v2 whole, which is shorter than its diff:
```python
import functools

import jax
import jax.numpy as jnp
from jax import lax
from jax.experimental import pallas as pl
from jax.experimental.pallas import tpu as pltpu
from jax.sharding import PartitionSpec as P

DI = 3072
HEAD = 64
LANES = 128
CHUNK = 256
VMEM_BYTES = 48 * 2**20

EPS = 1e-05
HIGH = lax.Precision.HIGHEST
FLOAT = jnp.float32
HALF = jnp.bfloat16


def shifted(block, axis, distance):
    count = lax.axis_size(axis)
    if distance % count == 0:
        return block
    return lax.ppermute(block, axis, [(i, (i + distance) % count) for i in range(count)])


def swapped(block):
    return lax.ppermute(block, "section", [(0, 1), (1, 0)])


def after(value, *others):
    return lax.optimization_barrier((value, *others))[0]


def rms_norm(value, gain):
    return value * lax.rsqrt(jnp.mean(value * value, axis=-1, keepdims=True) + EPS) * gain


def local_docs(lengths, row_now, length):
    bounds = jnp.cumsum(lengths)[:-1]
    place = jnp.arange(length, dtype=jnp.int32)
    inner = jnp.sum((place[:, None] >= bounds[None, :]).astype(jnp.int32), axis=1)
    return inner + row_now * lengths.shape[0]


def project(left, right):
    return jnp.dot(left, right, preferred_element_type=FLOAT)


def project_back(left, right):
    return lax.dot_general(left, right, (((1,), (1,)), ((), ())), preferred_element_type=FLOAT)


def outer(left, right):
    return lax.dot_general(left, right, (((0,), (0,)), ((), ())), preferred_element_type=FLOAT)


def silu_slope(value):
    sigma = jax.nn.sigmoid(value)
    return sigma * (1.0 + value * (1.0 - sigma))


def groups():
    count = lax.axis_size("col")
    return count if count <= 4 else 1


def chunks():
    count = groups()
    order = [0] + [step * side for step in range(1, count // 2 + 1) for side in (1, -1)]
    order = [back % count for back in order]
    order = list(dict.fromkeys(order))
    return [tuple(order[at : at + 2]) for at in range(0, count, 2)]


def spread(block, staged=False):
    count = groups()
    if count == 1:
        return [lax.all_gather(block, "col", axis=0, tiled=True)]
    result = [block] * count
    result[1] = shifted(block, "col", 1)
    source = after(block, result[1]) if staged else block
    for back in range(count - 1, 1, -1):
        result[back] = shifted(source, "col", back)
    return result


def joined(blocks):
    return blocks[0] if len(blocks) == 1 else jnp.concatenate(blocks, axis=0)


def in_order(blocks, axis):
    count = len(blocks)
    if count == 1:
        return blocks[0]
    rows = blocks[0].shape[0]
    line = jnp.concatenate(blocks[::-1] + blocks[:0:-1], axis=0)
    start = (count - 1 - lax.axis_index(axis)) * rows
    return lax.dynamic_slice_in_dim(line, start, count * rows, axis=0)


def gathered_sum(parts):
    if len(parts) == 1:
        return lax.psum_scatter(parts[0], "col", scatter_dimension=0, tiled=True).astype(FLOAT)
    total = parts[0].astype(FLOAT)
    for back in range(1, len(parts)):
        total = total + shifted(parts[back], "col", -back).astype(FLOAT)
    return total


def block_of(values, back):
    rows = values.shape[0] // groups()
    return values[back * rows : (back + 1) * rows]


def turn():
    place = lax.axis_index("col") if groups() > 1 else jnp.int32(0)
    return place.astype(jnp.int32).reshape(1)


def route_tables(blocks, top, capacity, layers):
    n_row, n_col = lax.axis_size("row"), lax.axis_size("col")
    slots = len(chunks()[0]) * (n_col // groups()) * capacity
    experts = (jnp.arange(n_row) * n_col + lax.axis_index("col")).astype(FLOAT)
    now = jnp.stack([joined([blocks[back] for back in chunk]) for chunk in chunks()])
    parts, count = now.shape[:2]
    now = now.reshape(parts, count, layers, 2, top).transpose(2, 0, 3, 4, 1)
    match = now[:, :, 0, None] == experts[None, None, :, None, None]
    hit = jnp.any(match, axis=3)
    weight = jnp.sum(jnp.where(match, now[:, :, 1, None], 0.0), axis=3)
    order = jnp.arange(count, dtype=jnp.int32)
    triangle = (order[:, None] <= order[None, :]).astype(HALF)
    place = project(hit.astype(HALF).reshape(-1, count), triangle).reshape(hit.shape)
    slot = jnp.arange(1, slots + 1, dtype=jnp.int32).astype(FLOAT)
    chosen = (place[:, :, :, None, :] == slot[:, None]) & hit[:, :, :, None, :]
    shape = (layers, parts, n_row * slots, count)
    plain = chosen.astype(HALF).reshape(shape)
    scaled = jnp.where(chosen, weight[:, :, :, None, :], 0.0).astype(HALF).reshape(shape)
    return [[(plain[s, i], scaled[s, i]) for i in range(parts)] for s in range(layers)]


def to_experts(rows):
    return lax.all_to_all(rows.astype(HALF), "row", split_axis=0, concat_axis=0, tiled=True)


def summed_rows(values, reverse):
    step = min(values.shape[0], CHUNK)
    count = values.shape[0] // step
    place = lax.broadcasted_iota(jnp.int32, (step, step), 0)
    other = lax.broadcasted_iota(jnp.int32, (step, step), 1)
    before = (place <= other) if reverse else (place >= other)
    triangle = before.astype(FLOAT)
    carry = jnp.zeros((1, values.shape[1]), FLOAT)
    parts = [None] * count
    for index in reversed(range(count)) if reverse else range(count):
        part = values[index * step : (index + 1) * step]
        run = jnp.dot(triangle, part, precision=HIGH, preferred_element_type=FLOAT) + carry
        carry = run[:1] if reverse else run[step - 1 :]
        parts[index] = run
    return parts[0] if count == 1 else jnp.concatenate(parts, axis=0)


def head_columns(rows, columns, head_width):
    head = lax.broadcasted_iota(jnp.int32, (rows, columns), 0) * head_width
    column = lax.broadcasted_iota(jnp.int32, (rows, columns), 1)
    return ((column >= head) & (column < head + head_width)).astype(FLOAT)


def sigmoid(value):
    return 1.0 / (1.0 + jnp.exp(-value))


def step_sizes(step_pre, step_row_ref):
    shifted_pre = step_pre + step_row_ref[0:1, :]
    sizes = jnp.maximum(shifted_pre, 0.0) + jnp.log1p(jnp.exp(-jnp.abs(shifted_pre)))
    return shifted_pre, sizes, -jnp.exp(step_row_ref[1:2, :])


def conv_rows(values, weight_ref, columns, marks_ref):
    width = weight_ref.shape[0]
    result = values * weight_ref[width - 1 : width, columns]
    for back in range(1, width):
        moved = pltpu.roll(values, back, 0) * marks_ref[:, back : back + 1]
        result = result + moved * weight_ref[width - 1 - back : width - back, columns]
    return result


def conv_rows_back(grad, values, weight_ref, columns, marks_ref, weight_grad_ref):
    width = weight_ref.shape[0]
    rows = values.shape[0]
    result = grad * weight_ref[width - 1 : width, columns]
    weight_grad_ref[width - 1 : width, columns] = jnp.sum(grad * values, axis=0, keepdims=True)
    for back in range(1, width):
        kept = grad * marks_ref[:, back : back + 1]
        taps = jnp.sum(kept * pltpu.roll(values, back, 0), axis=0, keepdims=True)
        weight_grad_ref[width - 1 - back : width - back, columns] = taps
        moved = pltpu.roll(kept, rows - back, 0)
        result = result + moved * weight_ref[width - 1 - back : width - back, columns]
    return result


def copy_in_order(source_ref, target_ref, place_ref, parts):
    if parts == 1:
        return source_ref
    rows = source_ref.shape[0] // parts
    for index in range(parts):
        target_ref[index * rows : (index + 1) * rows, :] = source_ref[
            block_rows(index, rows, place_ref, parts), :
        ]
    return target_ref


def block_rows(index, rows, place_ref, parts):
    if parts == 1:
        return slice(0, rows)
    back = lax.rem(place_ref[0] - index + parts, parts)
    return pl.ds(pl.multiple_of(back * rows, rows), rows)


def mixer_forward_kernel(
    heads,
    parts,
    pre_in_ref,
    conv_input_ref,
    conv_state_ref,
    step_row_ref,
    wide_row_ref,
    marks_ref,
    labels_ref,
    place_ref,
    y_ref,
    scaled_ref,
    total_ref,
    pre_ref,
    x_ref,
    dosed_ref,
    keys_ref,
    queries_ref,
):
    length, wide = y_ref.shape
    states = conv_state_ref.shape[1] // 2
    state_at, step_at = 2 * wide, 2 * wide + 2 * states
    head_width = HEAD
    pre_ref = copy_in_order(pre_in_ref, pre_ref, place_ref, parts)
    _, sizes, rate = step_sizes(pre_ref[:, step_at : step_at + LANES], step_row_ref)
    running = summed_rows(sizes * rate, False)
    running_t = running.T
    expand = head_columns(LANES, wide, head_width)
    for start in range(0, wide, LANES):
        columns = slice(start, start + LANES)
        conv = conv_rows(
            pre_ref[:, wide + start : wide + start + LANES], conv_input_ref, columns, marks_ref
        )
        x = conv * sigmoid(conv)
        x_ref[:, columns] = x
        dose = jnp.dot(sizes, expand[:, columns], precision=HIGH, preferred_element_type=FLOAT)
        dosed_ref[:, columns] = (x * dose).astype(HALF)
    for part, target in ((0, keys_ref), (1, queries_ref)):
        columns = slice(part * states, (part + 1) * states)
        conv = conv_rows(
            pre_ref[:, state_at + part * states : state_at + (part + 1) * states],
            conv_state_ref,
            columns,
            marks_ref,
        )
        target[...] = (conv * sigmoid(conv)).astype(HALF)
    block = min(length, CHUNK)
    place = lax.broadcasted_iota(jnp.int32, (block, block), 0)
    other = lax.broadcasted_iota(jnp.int32, (block, block), 1)
    for late in range(length // block):
        rows = slice(late * block, (late + 1) * block)
        for early in range(late + 1):
            past = slice(early * block, (early + 1) * block)
            same = marks_ref[rows, 0:1] == labels_ref[:, past]
            if late == early:
                same = same & (place >= other)
            mask = jnp.where(same, 0.0, -1e30)
            scores = lax.dot_general(
                queries_ref[rows, :],
                keys_ref[past, :],
                (((1,), (1,)), ((), ())),
                preferred_element_type=FLOAT,
            )
            for head in range(heads):
                columns = slice(head * head_width, (head + 1) * head_width)
                spread_log = running[rows, head : head + 1] - running_t[head : head + 1, past]
                mixing = (jnp.exp(spread_log + mask) * scores).astype(HALF)
                inner = jnp.dot(mixing, dosed_ref[past, columns], preferred_element_type=FLOAT)
                if early == 0:
                    y_ref[rows, columns] = inner
                else:
                    y_ref[rows, columns] += inner
    total = jnp.zeros((length, 1), FLOAT)
    for start in range(0, wide, LANES):
        columns = slice(start, start + LANES)
        y = y_ref[:, columns]
        if heads * head_width < start + LANES:
            lane = lax.broadcasted_iota(jnp.int32, y.shape, 1) + start
            y = jnp.where(lane < heads * head_width, y, 0.0)
        y = y + wide_row_ref[1:2, columns] * x_ref[:, columns]
        gate = pre_ref[:, columns]
        gated = y * gate * sigmoid(gate)
        y_ref[:, columns] = y
        scaled = (gated * wide_row_ref[0:1, columns]).astype(HALF)
        each = length // parts
        for index in range(parts):
            block_at = block_rows(index, each, place_ref, parts)
            scaled_ref[block_at, columns] = scaled[index * each : (index + 1) * each]
        total = total + jnp.sum(gated * gated, axis=1, keepdims=True)
    each = length // parts
    for index in range(parts):
        block_at = block_rows(index, each, place_ref, parts)
        total_ref[block_at, :] = total[index * each : (index + 1) * each]


def mixer_backward_kernel(
    heads,
    parts,
    inner_all,
    pre_in_ref,
    y_ref,
    grad_in_ref,
    sides_in_ref,
    conv_input_ref,
    conv_state_ref,
    step_row_ref,
    wide_row_ref,
    marks_ref,
    labels_ref,
    place_ref,
    grad_pre_ref,
    wide_grad_ref,
    conv_input_grad_ref,
    conv_state_grad_ref,
    step_grad_ref,
    pre_ref,
    grad_ref,
    sides_ref,
    x_ref,
    dosed_ref,
    dose_ref,
    slope_ref,
    dy_ref,
    z_ref,
    bc_ref,
    bc_slope_ref,
    bc_grad_ref,
):
    length, wide = y_ref.shape
    states = conv_state_ref.shape[1] // 2
    state_at, step_at = 2 * wide, 2 * wide + 2 * states
    head_width = HEAD
    each = length // parts
    pre_ref = copy_in_order(pre_in_ref, pre_ref, place_ref, parts)
    grad_ref = copy_in_order(grad_in_ref, grad_ref, place_ref, parts)
    sides_ref = copy_in_order(sides_in_ref, sides_ref, place_ref, parts)

    def put(value, start):
        for index in range(parts):
            grad_pre_ref[block_rows(index, each, place_ref, parts), start : start + LANES] = value[
                index * each : (index + 1) * each
            ]

    shifted_pre, sizes, rate = step_sizes(pre_ref[:, step_at : step_at + LANES], step_row_ref)
    running = summed_rows(sizes * rate, False)
    running_t = running.T
    expand = head_columns(LANES, wide, head_width)
    rr = sides_ref[:, 0:1]
    pull = rr * rr * rr * sides_ref[:, 1:2] * (1.0 / inner_all)
    for start in range(0, wide, LANES):
        columns = slice(start, start + LANES)
        gate = pre_ref[:, columns]
        y = y_ref[:, columns]
        grad = grad_ref[:, columns]
        gain = wide_row_ref[0:1, columns]
        sigma = sigmoid(gate)
        silu = gate * sigma
        gated = y * silu
        normed = gated * rr
        wide_grad_ref[0:1, columns] = jnp.sum(grad * normed, axis=0, keepdims=True)
        grad_gated = rr * gain * grad - gated * pull
        slope = sigma * (1.0 + gate * (1.0 - sigma))
        put((grad_gated * y * slope).astype(HALF), start)
        dy = grad_gated * silu
        dy_ref[:, columns] = dy
        conv = conv_rows(
            pre_ref[:, wide + start : wide + start + LANES], conv_input_ref, columns, marks_ref
        )
        sigma = sigmoid(conv)
        x = conv * sigma
        x_ref[:, columns] = x
        slope_ref[:, columns] = sigma * (1.0 + conv * (1.0 - sigma))
        dose = jnp.dot(sizes, expand[:, columns], precision=HIGH, preferred_element_type=FLOAT)
        dose_ref[:, columns] = dose
        dosed_ref[:, columns] = (x * dose).astype(HALF)
        wide_grad_ref[1:2, columns] = jnp.sum(dy * x, axis=0, keepdims=True)
    for start in range(0, 2 * states, LANES):
        columns = slice(start, start + LANES)
        conv = conv_rows(
            pre_ref[:, state_at + start : state_at + start + LANES],
            conv_state_ref,
            columns,
            marks_ref,
        )
        sigma = sigmoid(conv)
        bc_ref[:, columns] = (conv * sigma).astype(HALF)
        bc_slope_ref[:, columns] = sigma * (1.0 + conv * (1.0 - sigma))
    block = min(length, CHUNK)
    place = lax.broadcasted_iota(jnp.int32, (block, block), 0)
    other = lax.broadcasted_iota(jnp.int32, (block, block), 1)
    z_ref[...] = jnp.zeros(z_ref.shape, FLOAT)
    bc_grad_ref[...] = jnp.zeros(bc_grad_ref.shape, FLOAT)
    for late in range(length // block):
        rows = slice(late * block, (late + 1) * block)
        for early in range(late + 1):
            past = slice(early * block, (early + 1) * block)
            same = marks_ref[past, 0:1] == labels_ref[:, rows]
            if late == early:
                same = same & (place <= other)
            mask = jnp.where(same, 0.0, -1e30)
            keys = bc_ref[past, :states]
            queries = bc_ref[rows, states:]
            scores = lax.dot_general(
                keys, queries, (((1,), (1,)), ((), ())), preferred_element_type=FLOAT
            )
            mixed = jnp.zeros((block, block), FLOAT)
            for head in range(heads):
                columns = slice(head * head_width, (head + 1) * head_width)
                spread_log = running_t[head : head + 1, rows] - running[past, head : head + 1]
                decay = jnp.exp(spread_log + mask)
                mixing = (decay * scores).astype(HALF)
                dy = dy_ref[rows, columns].astype(HALF)
                z_ref[past, columns] += jnp.dot(mixing, dy, preferred_element_type=FLOAT)
                along = lax.dot_general(
                    dosed_ref[past, columns],
                    dy,
                    (((1,), (1,)), ((), ())),
                    preferred_element_type=FLOAT,
                )
                mixed = mixed + decay * along
            mixed = mixed.astype(HALF)
            bc_grad_ref[past, :states] += jnp.dot(mixed, queries, preferred_element_type=FLOAT)
            bc_grad_ref[rows, states:] += lax.dot_general(
                mixed, keys, (((0,), (0,)), ((), ())), preferred_element_type=FLOAT
            )
    direct = jnp.zeros((length, LANES), FLOAT)
    balance = jnp.zeros((length, LANES), FLOAT)
    for start in range(0, wide, LANES):
        columns = slice(start, start + LANES)
        x, z, dy = x_ref[:, columns], z_ref[:, columns], dy_ref[:, columns]
        skip = wide_row_ref[1:2, columns]
        collapse = (((1,), (1,)), ((), ()))
        both = dy.astype(HALF).astype(FLOAT) * (y_ref[:, columns] - skip * x)
        both = both - dosed_ref[:, columns].astype(FLOAT) * z
        heads_of = expand[:, columns]
        direct = direct + lax.dot_general(
            x * z, heads_of, collapse, precision=HIGH, preferred_element_type=FLOAT
        )
        balance = balance + lax.dot_general(
            both, heads_of, collapse, precision=HIGH, preferred_element_type=FLOAT
        )
        grad_conv = (dose_ref[:, columns] * z + skip * dy) * slope_ref[:, columns]
        grad_in = conv_rows_back(
            grad_conv,
            pre_ref[:, wide + start : wide + start + LANES],
            conv_input_ref,
            columns,
            marks_ref,
            conv_input_grad_ref,
        )
        put(grad_in.astype(HALF), wide + start)
    for start in range(0, 2 * states, LANES):
        columns = slice(start, start + LANES)
        grad_in = conv_rows_back(
            bc_grad_ref[:, columns] * bc_slope_ref[:, columns],
            pre_ref[:, state_at + start : state_at + start + LANES],
            conv_state_ref,
            columns,
            marks_ref,
            conv_state_grad_ref,
        )
        put(grad_in.astype(HALF), state_at + start)
    crossing = summed_rows(balance, True)
    grad_step = (direct + rate * crossing) * sigmoid(shifted_pre)
    put(grad_step.astype(HALF), step_at)
    step_grad_ref[0:1, :] = jnp.sum(grad_step, axis=0, keepdims=True)
    step_grad_ref[1:2, :] = rate * jnp.sum(sizes * crossing, axis=0, keepdims=True)


def ordered_copy(shape):
    return pltpu.VMEM(shape if groups() > 1 else (8, LANES), FLOAT)


def whole_call(kernel, inputs, results, scratch, name):
    whole = pl.BlockSpec(memory_space=pltpu.VMEM)
    place = pl.BlockSpec(memory_space=pltpu.SMEM)
    return pl.pallas_call(
        kernel,
        in_specs=[whole] * (inputs - 1) + [place],
        out_shape=results,
        scratch_shapes=scratch,
        compiler_params=pltpu.CompilerParams(vmem_limit_bytes=VMEM_BYTES),
        name=name,
    )


def mixer_forward(pre, heads, wide, mixer):
    length = pre.shape[0]
    kernel = functools.partial(mixer_forward_kernel, heads, groups())
    states = mixer[1].shape[1] // 2
    return whole_call(
        kernel,
        1 + len(mixer),
        (
            jax.ShapeDtypeStruct((length, wide), FLOAT),
            jax.ShapeDtypeStruct((length, wide), HALF),
            jax.ShapeDtypeStruct((length, 1), FLOAT),
        ),
        [
            ordered_copy(pre.shape),
            pltpu.VMEM((length, wide), FLOAT),
            pltpu.VMEM((length, wide), HALF),
            pltpu.VMEM((length, states), HALF),
            pltpu.VMEM((length, states), HALF),
        ],
        "mixer_forward",
    )(pre, *mixer)


def mixer_backward(pre, y, grad, sides, heads, mixer):
    length, wide = y.shape
    kernel = functools.partial(mixer_backward_kernel, heads, groups(), DI)
    double = mixer[1].shape[1]
    square = pltpu.VMEM((length, wide), FLOAT)
    return whole_call(
        kernel,
        4 + len(mixer),
        (
            jax.ShapeDtypeStruct(pre.shape, HALF),
            jax.ShapeDtypeStruct((2, wide), FLOAT),
            jax.ShapeDtypeStruct((4, wide), FLOAT),
            jax.ShapeDtypeStruct((4, double), FLOAT),
            jax.ShapeDtypeStruct((2, LANES), FLOAT),
        ),
        [
            ordered_copy(pre.shape),
            ordered_copy(y.shape),
            ordered_copy(sides.shape),
            square,
            pltpu.VMEM((length, wide), HALF),
            square,
            square,
            square,
            square,
            pltpu.VMEM((length, double), HALF),
            pltpu.VMEM((length, double), FLOAT),
            pltpu.VMEM((length, double), FLOAT),
        ],
        "mixer_backward",
    )(pre, y, grad, sides, *mixer)


def layer_forward(resid, params, dense, mixer, tables):
    norm_in, norm_mid = params
    proj, proj_output, shared, expert_gate, expert_up, expert_down = dense
    wide = mixer[0].shape[1]
    heads = mixer[-1]
    hidden = shared.shape[1] // 3
    backs = range(groups())
    wide_in = joined(spread(rms_norm(resid, norm_in).astype(HALF)))
    pre = project(wide_in, proj)
    y, scaled, total_part = mixer_forward(pre, heads, wide, mixer[:-1])
    total = gathered_sum([block_of(total_part, back) for back in backs])
    mixed = gathered_sum(
        [project_back(block_of(scaled, back), proj_output).astype(HALF) for back in backs]
    )
    if callable(tables):
        tables = tables(scaled)
    rr = lax.rsqrt(total / DI + EPS)
    middle = resid + mixed * rr
    wide_mid = spread(rms_norm(middle, norm_mid).astype(HALF), staged=True)
    shared_pre, shared_act, arrived, expert_pre, active = [], [], [], [], []
    parts = [None] * groups()
    for index, chunk in enumerate(chunks()):
        tokens = joined([wide_mid[back] for back in chunk])
        plain, scaling = tables[0][index]
        rows = to_experts(project(plain, tokens))
        gate_e = project(rows, expert_gate)
        lift_e = project(rows, expert_up)
        act_e = (jax.nn.silu(gate_e) * lift_e).astype(HALF)
        result = to_experts(project(act_e, expert_down))
        arrived.append(rows)
        expert_pre.append((gate_e, lift_e))
        active.append(act_e)
        gate_s = project(tokens, shared[:, :hidden])
        lift_s = project(tokens, shared[:, hidden : 2 * hidden])
        act_s = (jax.nn.silu(gate_s) * lift_s).astype(HALF)
        shared_pre.append((gate_s, lift_s))
        shared_act.append(act_s)
        part = outer(scaling, result) + project_back(act_s, shared[:, 2 * hidden :])
        part = part.astype(HALF)
        rows_each = part.shape[0] // len(chunk)
        for at, back in enumerate(chunk):
            parts[back] = part[at * rows_each : (at + 1) * rows_each]
    saved = (
        resid,
        middle,
        mixed,
        rr,
        wide_in,
        pre,
        y,
        scaled,
        wide_mid,
        shared_pre,
        shared_act,
        arrived,
        expert_pre,
        active,
    )
    return (middle + gathered_sum(parts), saved, tables)


def layer_backward(grad_out, saved, params, dense, mixer, tables, pending):
    norm_in, norm_mid = params
    proj, proj_output, shared, expert_gate, expert_up, expert_down = dense
    (
        resid,
        middle,
        mixed,
        rr,
        wide_in,
        pre,
        y,
        scaled,
        wide_mid,
        shared_pre,
        shared_act,
        arrived,
        expert_pre,
        active,
    ) = saved
    heads = mixer[-1]
    hidden = shared.shape[1] // 3
    backs = range(groups())
    wide_out = spread(grad_out.astype(HALF), staged=True)
    parts = [None] * groups()
    rows_grad, gate_grads, lift_grads, shared_grads = [], [], [], []
    for index, chunk in enumerate(chunks()):
        tokens = joined([wide_out[back] for back in chunk])
        plain, scaling = tables[index]
        rows = to_experts(project(scaling, tokens))
        gate_e, lift_e = expert_pre[index]
        grad_act = project_back(rows, expert_down)
        grad_gate_e = (grad_act * lift_e * silu_slope(gate_e)).astype(HALF)
        grad_lift_e = (grad_act * jax.nn.silu(gate_e)).astype(HALF)
        result = to_experts(
            project_back(grad_gate_e, expert_gate) + project_back(grad_lift_e, expert_up)
        )
        rows_grad.append(rows)
        gate_grads.append(grad_gate_e)
        lift_grads.append(grad_lift_e)
        gate_s, lift_s = shared_pre[index]
        grad_act_s = project(tokens, shared[:, 2 * hidden :])
        grad_gate_s = (grad_act_s * lift_s * silu_slope(gate_s)).astype(HALF)
        grad_lift_s = (grad_act_s * jax.nn.silu(gate_s)).astype(HALF)
        shared_grads.append((grad_gate_s, grad_lift_s))
        part = (
            outer(plain, result)
            + project_back(grad_gate_s, shared[:, :hidden])
            + project_back(grad_lift_s, shared[:, hidden : 2 * hidden])
        )
        part = part.astype(HALF)
        rows_each = part.shape[0] // len(chunk)
        for at, back in enumerate(chunk):
            parts[back] = part[at * rows_each : (at + 1) * rows_each]
    grad_normed = gathered_sum(parts)
    _, pull_mid = jax.vjp(rms_norm, middle, norm_mid)
    grad_middle, grad_norm_mid = pull_mid(grad_normed)
    grad_middle = grad_middle + grad_out
    along = jnp.sum(grad_middle * mixed, axis=1, keepdims=True)
    wide_mix = joined(spread(grad_middle.astype(HALF)))
    sides = joined(spread(jnp.concatenate([rr, along], axis=1)))
    rows_in, rows_out = joined(arrived), joined(rows_grad)
    expert_grads = (
        outer(rows_in, joined(gate_grads)),
        outer(rows_in, joined(lift_grads)),
        outer(joined(active), rows_out),
    )
    order = [back for chunk in chunks() for back in chunk]
    mids, outs = joined([wide_mid[back] for back in order]), joined([wide_out[back] for back in order])
    grad_shared = (
        outer(mids, joined([pair[0] for pair in shared_grads])).astype(HALF),
        outer(mids, joined([pair[1] for pair in shared_grads])).astype(HALF),
        outer(outs, joined(shared_act)).astype(HALF),
    )
    expert_grads, grad_shared = pending(expert_grads, grad_shared)
    wide_mix = after(wide_mix, expert_grads, grad_shared)
    grad_proj_output = outer((wide_mix * sides[:, :1]).astype(HALF), scaled).astype(HALF)
    grad_scaled = project(wide_mix, proj_output)
    grad_pre, wide_grads, grad_conv_input, grad_conv_state, step_grads = mixer_backward(
        pre, y, grad_scaled, sides, heads, mixer[:-1]
    )
    grad_normed_in = gathered_sum(
        [project_back(block_of(grad_pre, back), proj).astype(HALF) for back in backs]
    )
    grad_proj = outer(wide_in, grad_pre).astype(HALF)
    _, pull_in = jax.vjp(rms_norm, resid, norm_in)
    grad_resid, grad_norm_in = pull_in(grad_normed_in)
    small = (
        grad_norm_in,
        grad_norm_mid,
        grad_conv_state,
        grad_conv_input,
        wide_grads,
        step_grads,
    )
    return (grad_resid + grad_middle, small, (grad_proj, grad_proj_output, grad_shared), expert_grads)


def flat(parts):
    return jnp.concatenate([part.reshape(-1) for part in parts])


def unflat(vector, shapes):
    result, start = [], 0
    for shape in shapes:
        size = 1
        for entry in shape:
            size *= entry
        result.append(vector[start : start + size].reshape(shape))
        start += size
    return result


def widened(value, columns):
    return jnp.pad(value, ((0, 0), (0, columns - value.shape[1])))


def shards(
    tokens,
    cotangent,
    doc_lengths,
    routes,
    gates,
    norm_in,
    proj_gate,
    proj_input,
    proj_state,
    proj_step,
    step_bias,
    decay_log,
    skip_gain,
    conv_input,
    conv_state,
    gate_norm,
    proj_output,
    norm_mid,
    expert_gate,
    expert_up,
    expert_down,
    shared_gate,
    shared_up,
    shared_down,
):
    section_now = lax.axis_index("section")
    first = section_now == 0
    row_now = lax.axis_index("row")
    n_row, n_col = lax.axis_size("row"), lax.axis_size("col")
    count = tokens.shape[1]
    top = routes.shape[3]
    capacity = count * top * 4 // (3 * n_row * n_col)
    width = tokens.shape[2]
    heads = step_bias.shape[1]
    inner = gate_norm.shape[1]
    state = conv_state.shape[2]
    wide = -(-inner // LANES) * LANES

    def pair(own, other):
        return (jnp.where(first, own, other), jnp.where(first, other, own))

    small_in = (
        norm_in[0],
        norm_mid[0],
        widened(conv_input[0], wide),
        conv_state[0],
        widened(jnp.concatenate([step_bias, decay_log], axis=0), LANES),
        widened(jnp.concatenate([gate_norm, jnp.repeat(skip_gain, HEAD, axis=1)], axis=0), wide),
    )
    vector = flat(small_in)
    small_all = [unflat(part, [v.shape for v in small_in]) for part in pair(vector, swapped(vector))]

    def both_layers(weight):
        whole = lax.all_gather(weight, ("section", "row"), axis=0, tiled=True)
        return whole.reshape(2, n_row * weight.shape[0], weight.shape[1])

    proj = both_layers(
        jnp.concatenate(
            [
                widened(proj_gate[0], wide),
                widened(proj_input[0], wide),
                proj_state[0],
                widened(proj_step[0], LANES),
            ],
            axis=1,
        )
    )
    proj_out = both_layers(widened(proj_output[0], wide))
    gate_all = lax.all_gather(expert_gate[0, 0], "section")
    up_all = lax.all_gather(expert_up[0, 0], "section")
    down_all = lax.all_gather(expert_down[0, 0], "section")
    shared = both_layers(jnp.concatenate([shared_gate[0], shared_up[0], shared_down[0]], axis=1))
    dense = [
        (proj[s], proj_out[s], shared[s], gate_all[s], up_all[s], down_all[s]) for s in range(2)
    ]

    meta = jnp.concatenate([routes.astype(FLOAT), gates], axis=3)[0]
    keep = lax.dynamic_index_in_dim(meta, section_now, 0, keepdims=False)
    give = lax.dynamic_index_in_dim(meta, 1 - section_now, 0, keepdims=False)
    meta = jnp.concatenate(pair(keep, swapped(give)), axis=1)

    def tables_once(scaled):
        return route_tables(spread(after(meta, scaled)), top, capacity, 2)

    lengths = lax.dynamic_slice(
        doc_lengths, (section_now, row_now, 0), (1, 1, doc_lengths.shape[2])
    )
    labels = local_docs(lengths[0, 0], row_now, n_col * count)
    marks = [labels.astype(FLOAT)]
    for back in range(1, conv_input.shape[1]):
        prior = jnp.pad(labels, (back, 0), constant_values=-1)[:-back]
        marks.append((prior == labels).astype(FLOAT))
    marks = jnp.stack(marks, axis=1)
    label_row = labels.astype(FLOAT)[None]
    place = turn()
    mixers = [
        (conv_in, conv_st, step_row, wide_row, marks, label_row, place, heads)
        for _, _, conv_in, conv_st, step_row, wide_row in small_all
    ]
    params = [part[:2] for part in small_all]

    resid = lax.dynamic_index_in_dim(tokens, section_now, 0, keepdims=False)
    grad = lax.dynamic_index_in_dim(cotangent, section_now, 0, keepdims=False)
    outputs, stored = [], []
    tables = tables_once
    for s in range(2):
        resid, saved, tables = layer_forward(
            resid, params[s], dense[s], mixers[s], tables if s == 0 else both_tables[1:]
        )
        outputs.append(resid)
        stored.append(saved)
        if s == 0:
            both_tables = tables

    def own_layer(first_value, second_value):
        keep = jnp.where(first, first_value, second_value)
        give = jnp.where(first, second_value, first_value).astype(HALF)
        return keep + swapped(give).astype(FLOAT)

    def row_sums(halves):
        both = jnp.concatenate(halves, axis=0)
        return lax.psum_scatter(both, ("section", "row"), scatter_dimension=0, tiled=True)

    def own_halves(first_value, second_value):
        keep = jnp.where(first, first_value, second_value)
        give = jnp.where(first, second_value, first_value)
        return pair(keep, swapped(give))

    held = {}

    def keep_first(expert_grads, grad_shared):
        held["experts"] = expert_grads
        return expert_grads, grad_shared

    def settle(expert_grads, grad_shared):
        return [own_layer(a, b) for a, b in zip(expert_grads, held["experts"])], grad_shared

    grads = [None, None]
    backs = [None, None]
    sums = [None, None]
    for s in (1, 0):
        grad, small, (grad_proj, grad_out, grad_shared), expert_grads = layer_backward(
            grad,
            stored[s],
            params[s],
            dense[s],
            mixers[s],
            both_tables[s],
            keep_first if s else settle,
        )
        backs[s] = grad
        grads[s] = small
        mixed = jnp.concatenate([*grad_shared, grad_out], axis=1)
        middle = mixed.shape[1] // 2
        tail = grad_proj[:, 2 * wide :]
        half = tail.shape[1] // 2
        sums[s] = (
            row_sums([mixed[:, :middle], mixed[:, middle:]]),
            row_sums(
                [
                    jnp.concatenate([grad_proj[:, :wide], tail[:, :half]], axis=1),
                    jnp.concatenate([grad_proj[:, wide : 2 * wide], tail[:, half:]], axis=1),
                ]
            ),
        )
    expert_out = expert_grads
    grad_mixed = jnp.concatenate(own_halves(sums[0][0], sums[1][0]), axis=1)
    first_half, second_half = own_halves(sums[0][1], sums[1][1])
    tail = jnp.concatenate([first_half[:, wide:], second_half[:, wide:]], axis=1)
    state_grad = lax.psum(tail[:, :state], "col")

    shapes = [part.shape for part in grads[0]]
    vector = own_layer(flat(grads[0]), flat(grads[1]))
    lines = [shifted(vector[None], "row", back) for back in range(n_row)]
    vector = jnp.sum(in_order(lines, "row"), axis=0)
    common = 2 * width + conv_state.shape[1] * state
    if groups() > 1:
        lines = [shifted(vector[None, :common], "col", back) for back in range(n_col)]
        shared_sum = jnp.sum(in_order(lines, "col"), axis=0)
    else:
        shared_sum = lax.psum(vector[:common], "col")
    (
        out_norm_in,
        out_norm_mid,
        out_conv_state,
        out_conv_input,
        out_wide,
        out_step,
    ) = unflat(jnp.concatenate([shared_sum, vector[common:]]), shapes)

    def per_micro(first_value, second_value):
        keep = jnp.where(first, first_value, second_value)
        other = swapped(jnp.where(first, second_value, first_value).astype(HALF)).astype(FLOAT)
        return jnp.stack(pair(keep, other))[None]

    hidden = shared_gate.shape[2]

    def out(value):
        return value.astype(FLOAT)[None]

    return (
        per_micro(outputs[0], outputs[1]),
        per_micro(backs[0], backs[1]),
        out_norm_in[None],
        out(first_half[:, :inner]),
        out(second_half[:, :inner]),
        out(state_grad),
        out(tail[:, state : state + heads]),
        out_step[:1, :heads],
        out_step[1:, :heads],
        jnp.sum(out_wide[1, :inner].reshape(heads, HEAD), axis=1)[None],
        out_conv_input[None, :, :inner],
        out_conv_state[None],
        out_wide[:1, :inner],
        out(grad_mixed[:, 3 * hidden : 3 * hidden + inner]),
        out_norm_mid[None],
        expert_out[0][None, None],
        expert_out[1][None, None],
        expert_out[2][None, None],
        out(grad_mixed[:, :hidden]),
        out(grad_mixed[:, hidden : 2 * hidden]),
        out(grad_mixed[:, 2 * hidden : 3 * hidden]),
    )


def solution(mesh):
    in_specs = (
        P(None, ("row", "col"), None),
        P(None, ("row", "col"), None),
        P(),
        P("section", None, ("row", "col"), None),
        P("section", None, ("row", "col"), None),
        P("section", None),
        P("section", "row", "col"),
        P("section", "row", "col"),
        P("section", "row", None),
        P("section", "row", "col"),
        P("section", "col"),
        P("section", "col"),
        P("section", "col"),
        P("section", None, "col"),
        P("section", None, None),
        P("section", "col"),
        P("section", "row", "col"),
        P("section", None),
        P("section", ("row", "col"), None, None),
        P("section", ("row", "col"), None, None),
        P("section", ("row", "col"), None, None),
        P("section", "row", "col"),
        P("section", "row", "col"),
        P("section", "row", "col"),
    )
    out_specs = (
        P("section", None, ("row", "col"), None),
        P("section", None, ("row", "col"), None),
        P("section", None),
        P("section", "row", "col"),
        P("section", "row", "col"),
        P("section", "row", None),
        P("section", "row", "col"),
        P("section", "col"),
        P("section", "col"),
        P("section", "col"),
        P("section", None, "col"),
        P("section", None, None),
        P("section", "col"),
        P("section", "row", "col"),
        P("section", None),
        P("section", ("row", "col"), None, None),
        P("section", ("row", "col"), None, None),
        P("section", ("row", "col"), None, None),
        P("section", "row", "col"),
        P("section", "row", "col"),
        P("section", "row", "col"),
    )
    return jax.shard_map(shards, mesh=mesh, in_specs=in_specs, out_specs=out_specs, check_vma=False)
```

time: 1400 us -> 1290 us (0.921)
  waiting for transfers between devices: 288 us -> 482 us
  starting transfers between devices: 333 us -> 219 us
  local copies, waits for them, and re-layouts: 157 us -> 64 us
  blocking collectives: 67.6 us -> 0 us
  Pallas kernels: 0 us -> 61.4 us
  other arithmetic: 194 us -> 133 us
  matrix products: 320 us -> 300 us
    ppermute x156 -> x69, starting transfers between devices: 332 us -> 146 us  [shifted(): lax.ppermute(block, axis, [(i, (i + distance) % count) for i in range(cou...]
    dot_general x24 -> x0, matrix products: 130 us -> none  [the longest x6 90.1 us: advance(): inner = jnp.einsum('tsh,shp->thp', mixing, values, precision=HIGH)]
    all_to_all x0 -> x16, waiting for transfers between devices: none -> 71.3 us  [to_experts(): lax.all_to_all(rows.astype(HALF), 'row', split_axis=0, concat_axis=0, til...]
    all_to_all x0 -> x16, starting transfers between devices: none -> 70.4 us  [to_experts(): lax.all_to_all(rows.astype(HALF), 'row', split_axis=0, concat_axis=0, til...]
    pallas_call x0 -> x4, Pallas kernels: none -> 61.4 us  [the longest x2 36.2 us: mixer_backward(): whole_call(kernel, 4 + len(mixer), (jax.ShapeDtypeStruct(pre.shape, HALF)...]
    unnamed x995 -> x414, local copies, waits for them, and re-layouts: 100 us -> 41 us
    concatenate x8 -> x14, other arithmetic: 31.9 us -> 86.5 us  [the longest x4 81.6 us: row_sums(): both = jnp.concatenate(halves, axis=0)]
    ppermute x156 -> x69, waiting for transfers between devices: 261 us -> 314 us  [shifted(): lax.ppermute(block, axis, [(i, (i + distance) % count) for i in range(cou...]
  transfers between devices with their start and end apart: 173 -> 106, of which waited for: 57 -> 44; matrix products, arithmetic and copies ran while one was open for 43% -> 36% of each run, Pallas kernels for 0% -> 5%
where the time goes in v2:
time: 1290 us; the launch traced here: 1280 us
  waiting for transfers between devices  482 us (37%)
  matrix products  300 us (23%)
  starting transfers between devices  219 us (17%)
  other arithmetic  133 us (10%)
  local copies, waits for them, and re-layouts  64 us (5%)
  Pallas kernels  61.4 us (5%)
  between operations  17.2 us (1%)
    ppermute x69, waiting for transfers between devices, shifted(): lax.ppermute(block, axis, [(i, (i + distance) % count) for i in range(cou...  314 us
    ppermute x69, starting transfers between devices, shifted(): lax.ppermute(block, axis, [(i, (i + distance) % count) for i in range(cou...  146 us
    dot_general x40, matrix products, project_back(): lax.dot_general(left, right, (((1,), (1,)), ((), ())), preferred_element_...  113 us
    dot_general x37, matrix products, project(): return jnp.dot(left, right, preferred_element_type=FLOAT)  108 us
    concatenate x4, other arithmetic, row_sums(): both = jnp.concatenate(halves, axis=0)  81.6 us
    dot_general x24, matrix products, outer(): lax.dot_general(left, right, (((0,), (0,)), ((), ())), preferred_element_...  78.6 us
    all_to_all x16, waiting for transfers between devices, to_experts(): lax.all_to_all(rows.astype(HALF), 'row', split_axis=0, concat_axis=0, til...  71.3 us
    all_to_all x16, starting transfers between devices, to_experts(): lax.all_to_all(rows.astype(HALF), 'row', split_axis=0, concat_axis=0, til...  70.4 us
  transfers between devices with their start and end apart: 106, of which 44 were waited for; matrix products, arithmetic and copies ran while one was open for 36% of the time, Pallas kernels for 5%

profile of v2, /device:TPU:0, one launch (start us, length us, event | category | flops | bytes accessed | tf_op | source)
XLA Modules:
  0.0 1275.6 jit_solution(4511980610304330878)
XLA Ops:
  23.0 8.4 collective-permute-done.3
  31.4 24.2 %collective-permute-done.2 = bf16[128,1536]{1,0:T(8,128)(2,1)S(1)} collective-permute-done((bf16[128,1536]{1,0:T(8,128)(2,1)S(1)}, bf16[128,1536]{1,0:T(8,128)(2,1)S(1)}, u32[]{:S(2)}, u32[]{:S(2)}) %collective-permute-start.2) | collective-permute-done | bytes 393248 | tf_op jit(solution)/shard_map/ppermute | solution.py:26
  55.6 26.8 %all-gather.11.cloned.1.call-done = bf16[3072,1920]{1,0:T(8,128)(2,1)} async-done(((bf16[384,1920]{1,0:T(8,128)(2,1)}), bf16[3072,1920]{1,0:T(8,128)(2,1)}) %all-gather.11.cloned.1.call-update) | async-done | bytes 11796496 | tf_op jit(solution)/shard_map/all_gather | solution.py:796
  90.5 12.7 mixer_forward.2
  112.7 10.5 all-gather.15.cloned.1.call-done
  140.4 21.8 %collective-permute-done.11 = f32[128,24]{0,1:T(8,128)S(1)} collective-permute-done((f32[128,24]{0,1:T(8,128)S(1)}, f32[128,24]{0,1:T(8,128)S(1)}, u32[]{:S(2)}, u32[]{:S(2)}) %collective-permute-start.11) | collective-permute-done | bytes 12320 | tf_op jit(solution)/shard_map/ppermute | solution.py:26
  176.2 8.7 collective-permute-done.14
  203.4 24.5 %collective-permute-done.17 = bf16[128,1536]{1,0:T(8,128)(2,1)S(1)} collective-permute-done((bf16[128,1536]{1,0:T(8,128)(2,1)}, bf16[128,1536]{1,0:T(8,128)(2,1)S(1)}, u32[]{:S(2)}, u32[]{:S(2)}) %collective-permute-start.17) | collective-permute-done | bytes 393248 | tf_op jit(solution)/shard_map/ppermute | solution.py:26
  308.8 10.3 collective-permute-done.19
  319.1 14.9 %collective-permute-done.18 = bf16[128,1536]{1,0:T(8,128)(2,1)} collective-permute-done((bf16[128,1536]{1,0:T(8,128)(2,1)}, bf16[128,1536]{1,0:T(8,128)(2,1)}, u32[]{:S(2)}, u32[]{:S(2)}) %collective-permute-start.18) | collective-permute-done | bytes 393248 | tf_op jit(solution)/shard_map/ppermute | solution.py:26
  352.6 32.8 %collective-permute-done.21 = bf16[128,1536]{1,0:T(8,128)(2,1)S(1)} collective-permute-done((bf16[128,1536]{1,0:T(8,128)(2,1)S(1)}, bf16[128,1536]{1,0:T(8,128)(2,1)S(1)}, u32[]{:S(2)}, u32[]{:S(2)}) %collective-permute-start.21) | collective-permute-done | bytes 393248 | tf_op jit(solution)/shard_map/ppermute | solution.py:26
  386.1 8.3 fusion.16.pre_in_ref
  394.4 12.5 mixer_forward.3
  427.7 14.3 %collective-permute-done.24 = bf16[128,1536]{1,0:T(8,128)(2,1)} collective-permute-done((bf16[128,1536]{1,0:T(8,128)(2,1)}, bf16[128,1536]{1,0:T(8,128)(2,1)}, u32[]{:S(2)}, u32[]{:S(2)}) %collective-permute-start.24) | collective-permute-done | bytes 393248 | tf_op jit(solution)/shard_map/ppermute | solution.py:26
  447.2 8.4 collective-permute-start.29
  482.8 9.8 collective-permute-done.32
  660.8 14.8 %collective-permute-done.40 = bf16[128,1536]{1,0:T(8,128)(2,1)} collective-permute-done((bf16[128,1536]{1,0:T(8,128)(2,1)}, bf16[128,1536]{1,0:T(8,128)(2,1)}, u32[]{:S(2)}, u32[]{:S(2)}) %collective-permute-start.40) | collective-permute-done | bytes 393248 | tf_op jit(solution)/shard_map/ppermute | solution.py:26
  690.3 29.1 %collective-permute-done.46 = f32[128,2]{0,1:T(2,128)S(1)} collective-permute-done((f32[128,2]{0,1:T(2,128)S(1)}, f32[128,2]{0,1:T(2,128)S(1)}, u32[]{:S(2)}, u32[]{:S(2)}) %collective-permute-start.46) | collective-permute-done | bytes 1056 | tf_op jit(solution)/shard_map/ppermute | solution.py:26
  727.2 17.9 %mixer_backward.2 = (bf16[512,1920]{1,0:T(8,128)(2,1)S(1)}, f32[2,768]{1,0:T(2,128)S(1)}, f32[4,768]{1,0:T(4,128)S(1)}, f32[4,256]{1,0:T(4,128)S(1)}, f32[2,128]{1,0:T(2,128)S(1)}) custom-call(f32[512,1920]{1,0:T(8,128)} %fusion.16.pre_in_ref, f32[512,768]{1,0:T(8,128)S(1)} %get-tuple-element.52.y_ref, f32[512,768]{1,0:T(8,128)S(1)} %fusion.97.grad_in_ref, ...), custom_call_target="tpu_custom_call" | custom-call | tf_op jit(solution)/shard_map/mixer_backward/pallas_call | solution.py:537
  769.5 9.9 collective-permute-done.49
  794.2 14.6 %pad_maximum_fusion = bf16[3072,768]{0,1:T(8,128)(2,1)} fusion(bf16[1536,768]{0,1:T(8,128)(2,1)S(1)} %convolution_convert_fusion.3, bf16[1536,256]{0,1:T(8,128)(2,1)S(1)} %copy-done.81, bf16[1536,256]{0,1:T(8,128)(2,1)S(1)} %copy-done.80, bf16[1536,256]{0,1:T(8,128)(2,1)S(1)} %copy-done.79), kind=kLoop, calls=%fused_computation.4 | loop fusion | flops 18874368 | bytes 9437184 | tf_op jit(solution)/shard_map/concatenate | solution.py:863
  829.5 14.4 %collective-permute-done.54 = bf16[128,1536]{1,0:T(8,128)(2,1)} collective-permute-done((bf16[128,1536]{1,0:T(8,128)(2,1)S(1)}, bf16[128,1536]{1,0:T(8,128)(2,1)}, u32[]{:S(2)}, u32[]{:S(2)}) %collective-permute-start.54) | collective-permute-done | bytes 393248 | tf_op jit(solution)/shard_map/ppermute | solution.py:26
  868.2 15.9 %all-to-all-done.14 = bf16[4,128,1536]{2,1,0:T(8,128)(2,1)} async-done(((bf16[4,128,1536]{2,1,0:T(8,128)(2,1)}), bf16[4,128,1536]{2,1,0:T(8,128)(2,1)}, u32[]{:S(2)}, u32[]{:S(2)}) %all-to-all-start.14) | async-done | bytes 1572896 | tf_op jit(solution)/shard_map/all_to_all | solution.py:145
  951.6 15.2 %collective-permute-done.55 = bf16[128,1536]{1,0:T(8,128)(2,1)S(1)} collective-permute-done((bf16[128,1536]{1,0:T(8,128)(2,1)S(1)}, bf16[128,1536]{1,0:T(8,128)(2,1)S(1)}, u32[]{:S(2)}, u32[]{:S(2)}) %collective-permute-start.55) | collective-permute-done | bytes 393248 | tf_op jit(solution)/shard_map/ppermute | solution.py:26
  987.4 12.4 collective-permute-done.65
  1013.2 14.5 %pad_maximum_fusion.1 = bf16[3072,768]{0,1:T(8,128)(2,1)} fusion(bf16[1536,768]{0,1:T(8,128)(2,1)S(1)} %convolution_convert_fusion.2, bf16[1536,256]{0,1:T(8,128)(2,1)S(1)} %copy-done.82, bf16[1536,256]{0,1:T(8,128)(2,1)S(1)} %copy-done.84, bf16[1536,256]{0,1:T(8,128)(2,1)S(1)} %copy-done.83), kind=kLoop, calls=%fused_computation.5 | loop fusion | flops 18874368 | bytes 9437184 | tf_op jit(solution)/shard_map/concatenate | solution.py:863
  1041.4 26.2 %maximum_maximum_fusion.1 = bf16[3072,960]{1,0:T(8,128)(2,1)} fusion(bf16[1536,192]{1,0:T(8,128)(2,1)S(1)} %get-tuple-element.209, bf16[1536,768]{1,0:T(8,128)(2,1)S(1)} %get-tuple-element.207, bf16[1536,192]{1,0:T(8,128)(2,1)S(1)} %get-tuple-element.208, bf16[1536,768]{1,0:T(8,128)(2,1)S(1)} %get-tuple-element.206), kind=kLoop, calls=%fused_computation.3 | loop fusion | flops 23592960 | bytes 11796480 | tf_op jit(solution)/shard_map/concatenate | solution.py:863
  1071.8 18.3 %mixer_backward.3 = (bf16[512,1920]{1,0:T(8,128)(2,1)S(1)}, f32[2,768]{1,0:T(2,128)S(1)}, f32[4,768]{1,0:T(4,128)S(1)}, f32[4,256]{1,0:T(4,128)S(1)}, f32[2,128]{1,0:T(2,128)S(1)}) custom-call(f32[512,1920]{1,0:T(8,128)} %fusion.26.pre_in_ref, f32[512,768]{1,0:T(8,128)S(1)} %get-tuple-element.51.y_ref, f32[512,768]{1,0:T(8,128)S(1)} %fusion.96.grad_in_ref, ...), custom_call_target="tpu_custom_call" | custom-call | tf_op jit(solution)/shard_map/mixer_backward/pallas_call | solution.py:537
  1094.5 26.3 %maximum_maximum_fusion = bf16[3072,960]{1,0:T(8,128)(2,1)} fusion(bf16[1536,192]{1,0:T(8,128)(2,1)S(1)} %get-tuple-element.205, bf16[1536,768]{1,0:T(8,128)(2,1)S(1)} %get-tuple-element.203, bf16[1536,192]{1,0:T(8,128)(2,1)S(1)} %get-tuple-element.204, bf16[1536,768]{1,0:T(8,128)(2,1)S(1)} %get-tuple-element.202), kind=kLoop, calls=%fused_computation.2 | loop fusion | flops 23592960 | bytes 11796480 | tf_op jit(solution)/shard_map/concatenate | solution.py:863
  1144.3 12.3 collective-permute-done.67
  1196.2 22.2 %reduce-scatter.9.cloned.1.call-done = bf16[384,960]{1,0:T(8,128)(2,1)} async-done(((bf16[3072,960]{1,0:T(8,128)(2,1)}), bf16[384,960]{1,0:T(8,128)(2,1)}) %reduce-scatter.9.cloned.1.call-update) | async-done | bytes 737296 | tf_op jit(solution)/shard_map/reduce_scatter | solution.py:864
  1234.4 32.8 %all-reduce.7.cloned.1.call-done = bf16[1,384,256]{2,1,0:T(8,128)(2,1)} async-done(((bf16[1,384,256]{2,1,0:T(8,128)(2,1)}), bf16[1,384,256]{2,1,0:T(8,128)(2,1)}) %all-reduce.7.cloned.1.call-update) | async-done | bytes 196624 | tf_op jit(solution)/shard_map/psum | solution.py:912
  (872 shorter events, 713.0 us)
Async XLA Ops:
  7.2 75.1 %all-gather.11.cloned.1.call-start = ((), (), s32[]{:S(2)}) async-start(), calls=%async_computation.20 | async-start | bytes 13271040 | tf_op jit(solution)/shard_map/all_gather | solution.py:796
  10.7 112.5 %all-gather.15.cloned.1.call-start = ((), (), s32[]{:S(2)}) async-start(), calls=%async_computation.25 | async-start | bytes 5308416 | tf_op jit(solution)/shard_map/all_gather | solution.py:796
  11.6 225.6 %all-gather.17.cloned.1.call-start = ((), (), s32[]{:S(2)}) async-start(), calls=%async_computation.26 | async-start | bytes 4718592 | tf_op jit(solution)/shard_map/all_gather | solution.py:811
  12.4 228.7 %all-gather.19.cloned.1.call-start = ((), (), s32[]{:S(2)}) async-start(), calls=%async_computation.27 | async-start | bytes 4718592 | tf_op jit(solution)/shard_map/all_gather | solution.py:812
  12.9 232.2 %all-gather.21.cloned.1.call-start = ((), (), s32[]{:S(2)}) async-start(), calls=%async_computation.28 | async-start | bytes 4718592 | tf_op jit(solution)/shard_map/all_gather | solution.py:813
  13.5 244.6 %all-gather.13.cloned.1.call-start = ((), (), s32[]{:S(2)}) async-start(), calls=%async_computation.21 | async-start | bytes 5308416 | tf_op jit(solution)/shard_map/all_gather | solution.py:796
  103.2 35.8 %collective-permute-start.13 = (f32[128,24]{0,1:T(8,128)S(1)}, f32[128,24]{0,1:T(8,128)}, u32[]{:S(2)}, u32[]{:S(2)}) collective-permute-start(f32[128,24]{0,1:T(8,128)S(1)} %pad_maximum_fusion.40), channel_id=1, source_target_pairs={{0,2},{1,3},{2,0},{3,1},{4,6},{5,7},{6,4},{7,5},{8,10},{9,11},{10,... | collective-permute-start | bytes 36872 | tf_op jit(solution)/shard_map/ppermute | solution.py:26
  186.6 44.7 %all-to-all-start = ((bf16[4,128,1536]{2,1,0:T(8,128)(2,1)}), bf16[4,128,1536]{2,1,0:T(8,128)(2,1)}, u32[]{:S(2)}, u32[]{:S(2)}) async-start(bf16[4,128,1536]{2,1,0:T(8,128)(2,1)} %bitcast.376), calls=%async_computation | async-start | bytes 3145728 | tf_op jit(solution)/shard_map/all_to_all | solution.py:145
  192.7 35.1 %collective-permute-start.17 = (bf16[128,1536]{1,0:T(8,128)(2,1)}, bf16[128,1536]{1,0:T(8,128)(2,1)S(1)}, u32[]{:S(2)}, u32[]{:S(2)}) collective-permute-start(bf16[128,1536]{1,0:T(8,128)(2,1)} %copy-done.106), channel_id=1, source_target_pairs={{0,2},{1,3},{2,0},{3,1},{4,6},{5,7},{6,4},{7,5},{8,10},{9,11},{10,... | collective-permute-start | bytes 1179656 | tf_op jit(solution)/shard_map/ppermute | solution.py:26
  196.1 108.9 %collective-permute-start.36 = (bf16[128,1536]{1,0:T(8,128)(2,1)}, bf16[128,1536]{1,0:T(8,128)(2,1)}, u32[]{:S(2)}, u32[]{:S(2)}) collective-permute-start(bf16[128,1536]{1,0:T(8,128)(2,1)} %bitcast_convert_fusion), channel_id=1, source_target_pairs={{0,1},{1,2},{2,3},{3,0},{4,5},{5,6},{6,7},{7,4},{8,9},{9,10},{10,1... | collective-permute-start | bytes 1179656 | tf_op jit(solution)/shard_map/ppermute | solution.py:26
  305.0 41.0 %collective-permute-start.38 = (bf16[128,1536]{1,0:T(8,128)(2,1)}, bf16[128,1536]{1,0:T(8,128)(2,1)S(1)}, u32[]{:S(2)}, u32[]{:S(2)}) collective-permute-start(bf16[128,1536]{1,0:T(8,128)(2,1)} %bitcast_convert_fusion), channel_id=1, source_target_pairs={{0,3},{1,0},{2,1},{3,2},{4,7},{5,4},{6,5},{7,6},{8,11},{9,8},{10,9... | collective-permute-start | bytes 1179656 | tf_op jit(solution)/shard_map/ppermute | solution.py:26
  343.0 42.4 %collective-permute-start.21 = (bf16[128,1536]{1,0:T(8,128)(2,1)S(1)}, bf16[128,1536]{1,0:T(8,128)(2,1)S(1)}, u32[]{:S(2)}, u32[]{:S(2)}) collective-permute-start(bf16[128,1536]{1,0:T(8,128)(2,1)S(1)} %multiply_convert_fusion.17), channel_id=1, source_target_pairs={{0,2},{1,3},{2,0},{3,1},{4,6},{5,7},{6,4},{7,5},{8,10},{9,11},{10,... | collective-permute-start | bytes 1179656 | tf_op jit(solution)/shard_map/ppermute | solution.py:26
  343.0 42.4 %collective-permute-start.20 = (bf16[128,1536]{1,0:T(8,128)(2,1)S(1)}, bf16[128,1536]{1,0:T(8,128)(2,1)S(1)}, u32[]{:S(2)}, u32[]{:S(2)}) collective-permute-start(bf16[128,1536]{1,0:T(8,128)(2,1)S(1)} %multiply_convert_fusion.17), channel_id=1, source_target_pairs={{0,1},{1,2},{2,3},{3,0},{4,5},{5,6},{6,7},{7,4},{8,9},{9,10},{10,1... | collective-permute-start | bytes 1179656 | tf_op jit(solution)/shard_map/ppermute | solution.py:26
  343.6 73.7 %collective-permute-start.39 = (bf16[128,1536]{1,0:T(8,128)(2,1)}, bf16[128,1536]{1,0:T(8,128)(2,1)S(1)}, u32[]{:S(2)}, u32[]{:S(2)}) collective-permute-start(bf16[128,1536]{1,0:T(8,128)(2,1)} %bitcast_convert_fusion), channel_id=1, source_target_pairs={{0,2},{1,3},{2,0},{3,1},{4,6},{5,7},{6,4},{7,5},{8,10},{9,11},{10,... | collective-permute-start | bytes 1179656 | tf_op jit(solution)/shard_map/ppermute | solution.py:26
  623.6 37.1 %collective-permute-start.37 = (bf16[128,1536]{1,0:T(8,128)(2,1)}, bf16[128,1536]{1,0:T(8,128)(2,1)}, u32[]{:S(2)}, u32[]{:S(2)}) collective-permute-start(bf16[128,1536]{1,0:T(8,128)(2,1)} %slice.632), channel_id=1, source_target_pairs={{0,3},{1,0},{2,1},{3,2},{4,7},{5,4},{6,5},{7,6},{8,11},{9,8},{10,9... | collective-permute-start | bytes 1179656 | tf_op jit(solution)/shard_map/ppermute | solution.py:26
  639.7 551.4 %reduce-scatter.13.cloned.1.call-start = ((), (), s32[]{:S(2)}) async-start(), calls=%async_computation.29 | async-start | bytes 5308416
  681.7 40.9 %collective-permute-start.44 = (bf16[128,1536]{1,0:T(8,128)(2,1)}, bf16[128,1536]{1,0:T(8,128)(2,1)}, u32[]{:S(2)}, u32[]{:S(2)}) collective-permute-start(bf16[128,1536]{1,0:T(8,128)(2,1)} %convert_element_type.533), channel_id=1, source_target_pairs={{0,3},{1,0},{2,1},{3,2},{4,7},{5,4},{6,5},{7,6},{8,11},{9,8},{10,9... | collective-permute-start | bytes 1179656 | tf_op jit(solution)/shard_map/ppermute | solution.py:26
  682.5 40.2 %collective-permute-start.43 = (bf16[128,1536]{1,0:T(8,128)(2,1)}, bf16[128,1536]{1,0:T(8,128)(2,1)}, u32[]{:S(2)}, u32[]{:S(2)}) collective-permute-start(bf16[128,1536]{1,0:T(8,128)(2,1)} %convert_element_type.533), channel_id=1, source_target_pairs={{0,2},{1,3},{2,0},{3,1},{4,6},{5,7},{6,4},{7,5},{8,10},{9,11},{10,... | collective-permute-start | bytes 1179656 | tf_op jit(solution)/shard_map/ppermute | solution.py:26
  685.0 37.7 %collective-permute-start.42 = (bf16[128,1536]{1,0:T(8,128)(2,1)}, bf16[128,1536]{1,0:T(8,128)(2,1)}, u32[]{:S(2)}, u32[]{:S(2)}) collective-permute-start(bf16[128,1536]{1,0:T(8,128)(2,1)} %convert_element_type.533), channel_id=1, source_target_pairs={{0,1},{1,2},{2,3},{3,0},{4,5},{5,6},{6,7},{7,4},{8,9},{9,10},{10,1... | collective-permute-start | bytes 1179656 | tf_op jit(solution)/shard_map/ppermute | solution.py:26
  719.3 44.7 %collective-permute-start.30 = (bf16[128,1536]{1,0:T(8,128)(2,1)}, bf16[128,1536]{1,0:T(8,128)(2,1)}, u32[]{:S(2)}, u32[]{:S(2)}) collective-permute-start(bf16[128,1536]{1,0:T(8,128)(2,1)} %slice.626), channel_id=1, source_target_pairs={{0,3},{1,0},{2,1},{3,2},{4,7},{5,4},{6,5},{7,6},{8,11},{9,8},{10,9... | collective-permute-start | bytes 1179656 | tf_op jit(solution)/shard_map/ppermute | solution.py:26
  720.6 45.7 %collective-permute-start.34 = (bf16[128,1536]{1,0:T(8,128)(2,1)}, bf16[128,1536]{1,0:T(8,128)(2,1)}, u32[]{:S(2)}, u32[]{:S(2)}) collective-permute-start(bf16[128,1536]{1,0:T(8,128)(2,1)} %get-tuple-element.233), channel_id=1, source_target_pairs={{0,1},{1,2},{2,3},{3,0},{4,5},{5,6},{6,7},{7,4},{8,9},{9,10},{10,1... | collective-permute-start | bytes 1179656 | tf_op jit(solution)/shard_map/ppermute | solution.py:26
  722.6 43.7 %collective-permute-start.33 = (bf16[128,1536]{1,0:T(8,128)(2,1)}, bf16[128,1536]{1,0:T(8,128)(2,1)S(1)}, u32[]{:S(2)}, u32[]{:S(2)}) collective-permute-start(bf16[128,1536]{1,0:T(8,128)(2,1)} %get-tuple-element.232), channel_id=1, source_target_pairs={{0,2},{1,3},{2,0},{3,1},{4,6},{5,7},{6,4},{7,5},{8,10},{9,11},{10,... | collective-permute-start | bytes 1179656 | tf_op jit(solution)/shard_map/ppermute | solution.py:26
  911.6 280.9 %reduce-scatter.15.cloned.1.call-start = ((), (), s32[]{:S(2)}) async-start(), calls=%async_computation.30 | async-start | bytes 5308416
  918.9 55.4 %collective-permute-start.60 = (bf16[1536,512]{1,0:T(8,128)(2,1)}, bf16[1536,512]{1,0:T(8,128)(2,1)}, u32[]{:S(2)}, u32[]{:S(2)}) collective-permute-start(bf16[1536,512]{1,0:T(8,128)(2,1)} %get-tuple-element.287), channel_id=1, source_target_pairs={{0,16},{16,0},{1,17},{17,1},{2,18},{18,2},{3,19},{19,3},{4,20},{20... | collective-permute-start | bytes 4718600 | tf_op jit(solution)/shard_map/ppermute | solution.py:30
  918.9 60.2 %collective-permute-start.61 = (bf16[1536,512]{1,0:T(8,128)(2,1)}, bf16[1536,512]{1,0:T(8,128)(2,1)}, u32[]{:S(2)}, u32[]{:S(2)}) collective-permute-start(bf16[1536,512]{1,0:T(8,128)(2,1)} %get-tuple-element.289), channel_id=1, source_target_pairs={{0,16},{16,0},{1,17},{17,1},{2,18},{18,2},{3,19},{19,3},{4,20},{20... | collective-permute-start | bytes 4718600 | tf_op jit(solution)/shard_map/ppermute | solution.py:30
  945.9 40.4 %collective-permute-start.62 = (bf16[512,1536]{1,0:T(8,128)(2,1)S(1)}, bf16[512,1536]{1,0:T(8,128)(2,1)S(1)}, u32[]{:S(2)}, u32[]{:S(2)}) collective-permute-start(bf16[512,1536]{1,0:T(8,128)(2,1)S(1)} %get-tuple-element.291), channel_id=1, source_target_pairs={{0,16},{16,0},{1,17},{17,1},{2,18},{18,2},{3,19},{19,3},{4,20},{20... | collective-permute-start | bytes 4718600 | tf_op jit(solution)/shard_map/ppermute | solution.py:30
  971.0 39.3 %collective-permute-start.59 = (bf16[128,1536]{1,0:T(8,128)(2,1)S(1)}, bf16[128,1536]{1,0:T(8,128)(2,1)S(1)}, u32[]{:S(2)}, u32[]{:S(2)}) collective-permute-start(bf16[128,1536]{1,0:T(8,128)(2,1)S(1)} %convert_element_type.564), channel_id=1, source_target_pairs={{0,3},{1,0},{2,1},{3,2},{4,7},{5,4},{6,5},{7,6},{8,11},{9,8},{10,9... | collective-permute-start | bytes 1179656 | tf_op jit(solution)/shard_map/ppermute | solution.py:26
  974.3 36.1 %collective-permute-start.58 = (bf16[128,1536]{1,0:T(8,128)(2,1)S(1)}, bf16[128,1536]{1,0:T(8,128)(2,1)S(1)}, u32[]{:S(2)}, u32[]{:S(2)}) collective-permute-start(bf16[128,1536]{1,0:T(8,128)(2,1)S(1)} %convert_element_type.564), channel_id=1, source_target_pairs={{0,2},{1,3},{2,0},{3,1},{4,6},{5,7},{6,4},{7,5},{8,10},{9,11},{10,... | collective-permute-start | bytes 1179656 | tf_op jit(solution)/shard_map/ppermute | solution.py:26
  974.3 36.0 %collective-permute-start.57 = (bf16[128,1536]{1,0:T(8,128)(2,1)S(1)}, bf16[128,1536]{1,0:T(8,128)(2,1)S(1)}, u32[]{:S(2)}, u32[]{:S(2)}) collective-permute-start(bf16[128,1536]{1,0:T(8,128)(2,1)S(1)} %convert_element_type.564), channel_id=1, source_target_pairs={{0,1},{1,2},{2,3},{3,0},{4,5},{5,6},{6,7},{7,4},{8,9},{9,10},{10,1... | collective-permute-start | bytes 1179656 | tf_op jit(solution)/shard_map/ppermute | solution.py:26
  1034.3 161.9 %reduce-scatter.11.cloned.1.call-start = ((), (), s32[]{:S(2)}) async-start(), calls=%async_computation.23 | async-start | bytes 7077888 | tf_op jit(solution)/shard_map/reduce_scatter | solution.py:864
  1067.7 150.7 %reduce-scatter.9.cloned.1.call-start = ((), (), s32[]{:S(2)}) async-start(), calls=%async_computation.22 | async-start | bytes 7077888 | tf_op jit(solution)/shard_map/reduce_scatter | solution.py:864
  1120.8 146.4 %all-reduce.7.cloned.1.call-start = ((), (), s32[]{:S(2)}) async-start(), calls=%async_computation.24 | async-start | bytes 393216 | tf_op jit(solution)/shard_map/psum | solution.py:912
  (265 other events, 4122.7 us)
Sparse Core Ops, SparseCore 0:
  10.8 71.4 all-gather.10
  84.2 38.9 all-gather.14
  124.7 12.1 all-gather.16
  138.3 13.2 all-gather.18
  153.0 13.2 all-gather.20
  168.6 54.9 all-gather.12
  815.6 68.4 reduce-scatter.12
  1034.5 53.2 reduce-scatter.14
  1091.2 61.7 reduce-scatter.10
  1156.6 61.7 reduce-scatter.8
  1232.2 34.9 all-reduce.6

commit v3 on v2

--- a/solution.py
+++ b/solution.py
@@ -69,10 +69,7 @@
 
 def chunks():
     count = groups()
-    order = [0] + [step * side for step in range(1, count // 2 + 1) for side in (1, -1)]
-    order = [back % count for back in order]
-    order = list(dict.fromkeys(order))
-    return [tuple(order[at : at + 2]) for at in range(0, count, 2)]
+    return {1: [(0,)], 2: [(0,), (1,)], 3: [(0,), (1, 2)], 4: [(0,), (1, 3), (2,)]}[count]
 
 
 def spread(block, staged=False):
@@ -80,9 +77,10 @@
     if count == 1:
         return [lax.all_gather(block, "col", axis=0, tiled=True)]
     result = [block] * count
-    result[1] = shifted(block, "col", 1)
-    source = after(block, result[1]) if staged else block
-    for back in range(count - 1, 1, -1):
+    for back in (1, count - 1):
+        result[back] = shifted(block, "col", back)
+    source = after(block, result[1], result[-1]) if staged else block
+    for back in range(2, count - 1):
         result[back] = shifted(source, "col", back)
     return result
 
@@ -122,23 +120,27 @@
 
 def route_tables(blocks, top, capacity, layers):
     n_row, n_col = lax.axis_size("row"), lax.axis_size("col")
-    slots = len(chunks()[0]) * (n_col // groups()) * capacity
     experts = (jnp.arange(n_row) * n_col + lax.axis_index("col")).astype(FLOAT)
-    now = jnp.stack([joined([blocks[back] for back in chunk]) for chunk in chunks()])
-    parts, count = now.shape[:2]
-    now = now.reshape(parts, count, layers, 2, top).transpose(2, 0, 3, 4, 1)
-    match = now[:, :, 0, None] == experts[None, None, :, None, None]
-    hit = jnp.any(match, axis=3)
-    weight = jnp.sum(jnp.where(match, now[:, :, 1, None], 0.0), axis=3)
-    order = jnp.arange(count, dtype=jnp.int32)
-    triangle = (order[:, None] <= order[None, :]).astype(HALF)
-    place = project(hit.astype(HALF).reshape(-1, count), triangle).reshape(hit.shape)
-    slot = jnp.arange(1, slots + 1, dtype=jnp.int32).astype(FLOAT)
-    chosen = (place[:, :, :, None, :] == slot[:, None]) & hit[:, :, :, None, :]
-    shape = (layers, parts, n_row * slots, count)
-    plain = chosen.astype(HALF).reshape(shape)
-    scaled = jnp.where(chosen, weight[:, :, :, None, :], 0.0).astype(HALF).reshape(shape)
-    return [[(plain[s, i], scaled[s, i]) for i in range(parts)] for s in range(layers)]
+    tables = [[] for _ in range(layers)]
+    for chunk in chunks():
+        now = joined([blocks[back] for back in chunk])
+        count = now.shape[0]
+        slots = len(chunk) * (n_col // groups()) * capacity
+        now = now.reshape(count, layers, 2, top).transpose(1, 2, 3, 0)
+        match = now[:, None, 0] == experts[None, :, None, None]
+        hit = jnp.any(match, axis=2)
+        weight = jnp.sum(jnp.where(match, now[:, None, 1], 0.0), axis=2)
+        order = jnp.arange(count, dtype=jnp.int32)
+        triangle = (order[:, None] <= order[None, :]).astype(HALF)
+        place = project(hit.astype(HALF).reshape(-1, count), triangle).reshape(hit.shape)
+        slot = jnp.arange(1, slots + 1, dtype=jnp.int32).astype(FLOAT)
+        chosen = (place[:, :, None, :] == slot[:, None]) & hit[:, :, None, :]
+        shape = (layers, n_row * slots, count)
+        plain = chosen.astype(HALF).reshape(shape)
+        scaled = jnp.where(chosen, weight[:, :, None, :], 0.0).astype(HALF).reshape(shape)
+        for s in range(layers):
+            tables[s].append((plain[s], scaled[s]))
+    return tables
 
 
 def to_experts(rows):
@@ -562,6 +564,28 @@
     )(pre, y, grad, sides, *mixer)
 
 
+def through_experts(blocks, tables, expert, beside):
+    tokens = [joined([blocks[back] for back in chunk]) for chunk in chunks()]
+    count = len(tokens)
+    sent = [project(table, values).astype(HALF) for table, values in zip(tables, tokens)]
+    parts = [None] * groups()
+    arrived = []
+    rows = to_experts(sent[0])
+    for index, chunk in enumerate(chunks()):
+        if index and index + 1 < count:
+            rows = after(rows, sent[index + 1])
+        arrived.append(rows)
+        answer = expert(index, rows)
+        if index + 1 < count:
+            following = sent[index + 1] if index else after(sent[1], answer)
+            rows = to_experts(following)
+        part = beside(index, tokens[index], to_experts(answer))
+        rows_each = part.shape[0] // len(chunk)
+        for at, back in enumerate(chunk):
+            parts[back] = part[at * rows_each : (at + 1) * rows_each]
+    return parts, arrived
+
+
 def layer_forward(resid, params, dense, mixer, tables):
     norm_in, norm_mid = params
     proj, proj_output, shared, expert_gate, expert_up, expert_down = dense
@@ -581,29 +605,26 @@
     rr = lax.rsqrt(total / DI + EPS)
     middle = resid + mixed * rr
     wide_mid = spread(rms_norm(middle, norm_mid).astype(HALF), staged=True)
-    shared_pre, shared_act, arrived, expert_pre, active = [], [], [], [], []
-    parts = [None] * groups()
-    for index, chunk in enumerate(chunks()):
-        tokens = joined([wide_mid[back] for back in chunk])
-        plain, scaling = tables[0][index]
-        rows = to_experts(project(plain, tokens))
+    shared_pre, shared_act, expert_pre, active, returned = [], [], [], [], []
+
+    def expert(index, rows):
         gate_e = project(rows, expert_gate)
         lift_e = project(rows, expert_up)
         act_e = (jax.nn.silu(gate_e) * lift_e).astype(HALF)
-        result = to_experts(project(act_e, expert_down))
-        arrived.append(rows)
         expert_pre.append((gate_e, lift_e))
         active.append(act_e)
+        return project(act_e, expert_down).astype(HALF)
+
+    def beside(index, tokens, result):
         gate_s = project(tokens, shared[:, :hidden])
         lift_s = project(tokens, shared[:, hidden : 2 * hidden])
         act_s = (jax.nn.silu(gate_s) * lift_s).astype(HALF)
         shared_pre.append((gate_s, lift_s))
         shared_act.append(act_s)
-        part = outer(scaling, result) + project_back(act_s, shared[:, 2 * hidden :])
-        part = part.astype(HALF)
-        rows_each = part.shape[0] // len(chunk)
-        for at, back in enumerate(chunk):
-            parts[back] = part[at * rows_each : (at + 1) * rows_each]
+        part = outer(tables[0][index][1], result) + project_back(act_s, shared[:, 2 * hidden :])
+        return part.astype(HALF)
+
+    parts, arrived = through_experts(wide_mid, [table[0] for table in tables[0]], expert, beside)
     saved = (
         resid,
         middle,
@@ -642,40 +663,36 @@
         expert_pre,
         active,
     ) = saved
-    heads = mixer[-1]
+    wide, heads = mixer[0].shape[1], mixer[-1]
     hidden = shared.shape[1] // 3
     backs = range(groups())
     wide_out = spread(grad_out.astype(HALF), staged=True)
-    parts = [None] * groups()
-    rows_grad, gate_grads, lift_grads, shared_grads = [], [], [], []
-    for index, chunk in enumerate(chunks()):
-        tokens = joined([wide_out[back] for back in chunk])
-        plain, scaling = tables[index]
-        rows = to_experts(project(scaling, tokens))
+    gate_grads, lift_grads, shared_grads = [], [], []
+
+    def expert(index, rows):
         gate_e, lift_e = expert_pre[index]
         grad_act = project_back(rows, expert_down)
         grad_gate_e = (grad_act * lift_e * silu_slope(gate_e)).astype(HALF)
         grad_lift_e = (grad_act * jax.nn.silu(gate_e)).astype(HALF)
-        result = to_experts(
-            project_back(grad_gate_e, expert_gate) + project_back(grad_lift_e, expert_up)
-        )
-        rows_grad.append(rows)
         gate_grads.append(grad_gate_e)
         lift_grads.append(grad_lift_e)
+        back = project_back(grad_gate_e, expert_gate) + project_back(grad_lift_e, expert_up)
+        return back.astype(HALF)
+
+    def beside(index, tokens, result):
         gate_s, lift_s = shared_pre[index]
         grad_act_s = project(tokens, shared[:, 2 * hidden :])
         grad_gate_s = (grad_act_s * lift_s * silu_slope(gate_s)).astype(HALF)
         grad_lift_s = (grad_act_s * jax.nn.silu(gate_s)).astype(HALF)
         shared_grads.append((grad_gate_s, grad_lift_s))
         part = (
-            outer(plain, result)
+            outer(tables[index][0], result)
             + project_back(grad_gate_s, shared[:, :hidden])
             + project_back(grad_lift_s, shared[:, hidden : 2 * hidden])
         )
-        part = part.astype(HALF)
-        rows_each = part.shape[0] // len(chunk)
-        for at, back in enumerate(chunk):
-            parts[back] = part[at * rows_each : (at + 1) * rows_each]
+        return part.astype(HALF)
+
+    parts, rows_grad = through_experts(wide_out, [table[1] for table in tables], expert, beside)
     grad_normed = gathered_sum(parts)
     _, pull_mid = jax.vjp(rms_norm, middle, norm_mid)
     grad_middle, grad_norm_mid = pull_mid(grad_normed)
@@ -692,13 +709,12 @@
     order = [back for chunk in chunks() for back in chunk]
     mids, outs = joined([wide_mid[back] for back in order]), joined([wide_out[back] for back in order])
     grad_shared = (
-        outer(mids, joined([pair[0] for pair in shared_grads])).astype(HALF),
-        outer(mids, joined([pair[1] for pair in shared_grads])).astype(HALF),
-        outer(outs, joined(shared_act)).astype(HALF),
-    )
-    expert_grads, grad_shared = pending(expert_grads, grad_shared)
+        section_half(mids, *[joined(list(part)) for part in zip(*shared_grads)]),
+        section_half(outs, *two_halves(joined(shared_act))),
+    )
+    expert_grads = pending(expert_grads)
     wide_mix = after(wide_mix, expert_grads, grad_shared)
-    grad_proj_output = outer((wide_mix * sides[:, :1]).astype(HALF), scaled).astype(HALF)
+    grad_proj_output = section_half((wide_mix * sides[:, :1]).astype(HALF), *two_halves(scaled))
     grad_scaled = project(wide_mix, proj_output)
     grad_pre, wide_grads, grad_conv_input, grad_conv_state, step_grads = mixer_backward(
         pre, y, grad_scaled, sides, heads, mixer[:-1]
@@ -706,7 +722,8 @@
     grad_normed_in = gathered_sum(
         [project_back(block_of(grad_pre, back), proj).astype(HALF) for back in backs]
     )
-    grad_proj = outer(wide_in, grad_pre).astype(HALF)
+    grad_proj = section_half(wide_in, grad_pre[:, :wide], grad_pre[:, wide : 2 * wide])
+    grad_tail = outer(wide_in, grad_pre[:, 2 * wide :]).astype(HALF)
     _, pull_in = jax.vjp(rms_norm, resid, norm_in)
     grad_resid, grad_norm_in = pull_in(grad_normed_in)
     small = (
@@ -717,7 +734,47 @@
         wide_grads,
         step_grads,
     )
-    return (grad_resid + grad_middle, small, (grad_proj, grad_proj_output, grad_shared), expert_grads)
+    dense_grads = (grad_proj, grad_proj_output, *grad_shared)
+    return (grad_resid + grad_middle, small, dense_grads, grad_tail, expert_grads)
+
+
+def two_halves(values):
+    middle = values.shape[1] // 2
+    return values[:, :middle], values[:, middle:]
+
+
+def section_half(left, first_right, second_right):
+    first = lax.axis_index("section") == 0
+    give = outer(left, jnp.where(first, second_right, first_right)).astype(HALF)
+    keep = outer(left, jnp.where(first, first_right, second_right))
+    return (keep + swapped(give).astype(FLOAT)).astype(HALF)
+
+
+def row_share(values):
+    n_row = lax.axis_size("row")
+    rows = values.shape[0] // n_row
+    total = None
+    for ahead in range(n_row):
+        index = lax.rem(lax.axis_index("row") + ahead, n_row)
+        part = lax.dynamic_slice_in_dim(values, index * rows, rows, axis=0)
+        part = shifted(part, "row", ahead).astype(FLOAT)
+        total = part if total is None else total + part
+    return total.astype(HALF)
+
+
+def col_sum(values):
+    n_col = lax.axis_size("col")
+    if groups() == 1:
+        return lax.psum(values, "col")
+    rows = values.shape[0] // n_col
+    total = None
+    for ahead in range(n_col):
+        index = lax.rem(lax.axis_index("col") + ahead, n_col)
+        part = lax.dynamic_slice_in_dim(values, index * rows, rows, axis=0)
+        part = shifted(part, "col", ahead).astype(FLOAT)
+        total = part if total is None else total + part
+    total = total.astype(values.dtype)
+    return in_order([shifted(total, "col", back) for back in range(n_col)], "col")
 
 
 def flat(parts):
@@ -857,11 +914,10 @@
     def own_layer(first_value, second_value):
         keep = jnp.where(first, first_value, second_value)
         give = jnp.where(first, second_value, first_value).astype(HALF)
-        return keep + swapped(give).astype(FLOAT)
-
-    def row_sums(halves):
-        both = jnp.concatenate(halves, axis=0)
-        return lax.psum_scatter(both, ("section", "row"), scatter_dimension=0, tiled=True)
+        return keep.astype(FLOAT) + swapped(give).astype(FLOAT)
+
+    def row_sums(value):
+        return lax.psum_scatter(value, "row", scatter_dimension=0, tiled=True)
 
     def own_halves(first_value, second_value):
         keep = jnp.where(first, first_value, second_value)
@@ -870,18 +926,22 @@
 
     held = {}
 
-    def keep_first(expert_grads, grad_shared):
-        held["experts"] = expert_grads
-        return expert_grads, grad_shared
-
-    def settle(expert_grads, grad_shared):
-        return [own_layer(a, b) for a, b in zip(expert_grads, held["experts"])], grad_shared
+    def keep_first(expert_grads):
+        held["experts"] = [grad.astype(HALF) for grad in expert_grads]
+        return held["experts"]
+
+    def settle(expert_grads):
+        return [
+            own_layer(a.astype(HALF), b).astype(FLOAT)
+            for a, b in zip(expert_grads, held["experts"])
+        ]
 
     grads = [None, None]
     backs = [None, None]
     sums = [None, None]
+    tails = [None, None]
     for s in (1, 0):
-        grad, small, (grad_proj, grad_out, grad_shared), expert_grads = layer_backward(
+        grad, small, (grad_proj, *others), tails[s], expert_out = layer_backward(
             grad,
             stored[s],
             params[s],
@@ -892,24 +952,14 @@
         )
         backs[s] = grad
         grads[s] = small
-        mixed = jnp.concatenate([*grad_shared, grad_out], axis=1)
-        middle = mixed.shape[1] // 2
-        tail = grad_proj[:, 2 * wide :]
-        half = tail.shape[1] // 2
-        sums[s] = (
-            row_sums([mixed[:, :middle], mixed[:, middle:]]),
-            row_sums(
-                [
-                    jnp.concatenate([grad_proj[:, :wide], tail[:, :half]], axis=1),
-                    jnp.concatenate([grad_proj[:, wide : 2 * wide], tail[:, half:]], axis=1),
-                ]
-            ),
-        )
-    expert_out = expert_grads
-    grad_mixed = jnp.concatenate(own_halves(sums[0][0], sums[1][0]), axis=1)
-    first_half, second_half = own_halves(sums[0][1], sums[1][1])
-    tail = jnp.concatenate([first_half[:, wide:], second_half[:, wide:]], axis=1)
-    state_grad = lax.psum(tail[:, :state], "col")
+        sums[s] = [
+            row_sums(grad_proj) if s else row_share(grad_proj),
+            *[row_sums(value) for value in others],
+        ]
+    tail = row_share(own_layer(tails[0], tails[1]).astype(HALF))
+    state_grad = col_sum(tail[:, :state])
+    grad_gates, grad_out, grad_shared, grad_down = [own_halves(a, b) for a, b in zip(*sums)]
+    grad_out, grad_down = [jnp.concatenate(both, axis=1) for both in (grad_out, grad_down)]
 
     shapes = [part.shape for part in grads[0]]
     vector = own_layer(flat(grads[0]), flat(grads[1]))
@@ -935,8 +985,6 @@
         other = swapped(jnp.where(first, second_value, first_value).astype(HALF)).astype(FLOAT)
         return jnp.stack(pair(keep, other))[None]
 
-    hidden = shared_gate.shape[2]
-
     def out(value):
         return value.astype(FLOAT)[None]
 
@@ -944,8 +992,8 @@
         per_micro(outputs[0], outputs[1]),
         per_micro(backs[0], backs[1]),
         out_norm_in[None],
-        out(first_half[:, :inner]),
-        out(second_half[:, :inner]),
+        out(grad_gates[0][:, :inner]),
+        out(grad_gates[1][:, :inner]),
         out(state_grad),
         out(tail[:, state : state + heads]),
         out_step[:1, :heads],
@@ -954,14 +1002,14 @@
         out_conv_input[None, :, :inner],
         out_conv_state[None],
         out_wide[:1, :inner],
-        out(grad_mixed[:, 3 * hidden : 3 * hidden + inner]),
+        out(grad_out[:, :inner]),
         out_norm_mid[None],
         expert_out[0][None, None],
         expert_out[1][None, None],
         expert_out[2][None, None],
-        out(grad_mixed[:, :hidden]),
-        out(grad_mixed[:, hidden : 2 * hidden]),
-        out(grad_mixed[:, 2 * hidden : 3 * hidden]),
+        out(grad_shared[0]),
+        out(grad_shared[1]),
+        out(grad_down),
     )
 
 

time: 1290 us -> 1270 us (0.984)
  other arithmetic: 133 us -> 55.4 us
  matrix products: 300 us -> 375 us
  waiting for transfers between devices: 482 us -> 440 us
  starting transfers between devices: 219 us -> 251 us
  local copies, waits for them, and re-layouts: 64 us -> 48.7 us
    concatenate x4 -> x2, other arithmetic: 81.6 us -> 0.99 us  [shards(): jnp.concatenate(both, axis=1)]
    all_to_all x16 -> x24, waiting for transfers between devices: 71.3 us -> 115 us  [to_experts(): lax.all_to_all(rows.astype(HALF), 'row', split_axis=0, concat_axis=0, til...]
    psum x1 -> x0, waiting for transfers between devices: 32.8 us -> none  [shards(): state_grad = lax.psum(tail[:, :state], 'col')]
    all_to_all x16 -> x24, starting transfers between devices: 70.4 us -> 99.5 us  [to_experts(): lax.all_to_all(rows.astype(HALF), 'row', split_axis=0, concat_axis=0, til...]
    dot_general x24 -> x36, matrix products: 78.6 us -> 106 us  [outer(): lax.dot_general(left, right, (((0,), (0,)), ((), ())), preferred_element_...]
    dot_general x37 -> x55, matrix products: 108 us -> 132 us  [project(): return jnp.dot(left, right, preferred_element_type=FLOAT)]
    dot_general x40 -> x52, matrix products: 113 us -> 137 us  [project_back(): lax.dot_general(left, right, (((1,), (1,)), ((), ())), preferred_element_...]
    reduce_scatter x2 -> x7, waiting for transfers between devices: 22.2 us -> 0.01 us  [row_sums(): return lax.psum_scatter(value, 'row', scatter_dimension=0, tiled=True)]
  transfers between devices with their start and end apart: 106 -> 139, of which waited for: 44 -> 58; matrix products, arithmetic and copies ran while one was open for 36% -> 35% of each run, Pallas kernels for 5% -> 4%
where the time goes in v3:
time: 1270 us; the launch traced here: 1250 us
  waiting for transfers between devices  440 us (35%)
  matrix products  375 us (30%)
  starting transfers between devices  251 us (20%)
  Pallas kernels  61.2 us (5%)
  other arithmetic  55.4 us (4%)
  local copies, waits for them, and re-layouts  48.7 us (4%)
  between operations  18.2 us (1%)
    ppermute x81, waiting for transfers between devices, shifted(): lax.ppermute(block, axis, [(i, (i + distance) % count) for i in range(cou...  302 us
    ppermute x81, starting transfers between devices, shifted(): lax.ppermute(block, axis, [(i, (i + distance) % count) for i in range(cou...  147 us
    dot_general x52, matrix products, project_back(): lax.dot_general(left, right, (((1,), (1,)), ((), ())), preferred_element_...  137 us
    dot_general x55, matrix products, project(): return jnp.dot(left, right, preferred_element_type=FLOAT)  132 us
    all_to_all x24, waiting for transfers between devices, to_experts(): lax.all_to_all(rows.astype(HALF), 'row', split_axis=0, concat_axis=0, til...  115 us
    dot_general x36, matrix products, outer(): lax.dot_general(left, right, (((0,), (0,)), ((), ())), preferred_element_...  106 us
    all_to_all x24, starting transfers between devices, to_experts(): lax.all_to_all(rows.astype(HALF), 'row', split_axis=0, concat_axis=0, til...  99.5 us
    pallas_call x2, Pallas kernels, mixer_backward(): whole_call(kernel, 4 + len(mixer), (jax.ShapeDtypeStruct(pre.shape, HALF)...  36.1 us
  transfers between devices with their start and end apart: 139, of which 58 were waited for; matrix products, arithmetic and copies ran while one was open for 35% of the time, Pallas kernels for 4%

profile of v3, /device:TPU:0, one launch (start us, length us, event | category | flops | bytes accessed | tf_op | source)
XLA Modules:
  0.0 1249.9 jit_solution(3325586645800551571)
XLA Ops:
  30.7 9.3 collective-permute-done.36
  40.7 10.4 collective-permute-start.38
  52.2 28.9 %collective-permute-done.2 = bf16[128,1536]{1,0:T(8,128)(2,1)S(1)} collective-permute-done((bf16[128,1536]{1,0:T(8,128)(2,1)}, bf16[128,1536]{1,0:T(8,128)(2,1)S(1)}, u32[]{:S(2)}, u32[]{:S(2)}) %collective-permute-start.2) | collective-permute-done | bytes 393248 | tf_op jit(solution)/shard_map/ppermute | solution.py:26
  90.7 12.7 %mixer_forward.2 = (f32[512,768]{1,0:T(8,128)S(1)}, bf16[512,768]{1,0:T(8,128)(2,1)S(1)}, f32[512,1]{1,0:T(8,128)S(1)}) custom-call(f32[512,1920]{1,0:T(8,128)} %fusion.30.pre_in_ref, f32[4,768]{1,0:T(4,128)S(1)} %reshape.490.conv_input_ref, f32[4,256]{1,0:T(4,128)S(1)} %slice.476.conv_state_ref, f32[2,128]{1,0:T(2,128)S(1)} %slice_bitcast_fusion.67.step_row_ref, ...), custom_call_target="tpu_custom_call" | custom-call | tf_op jit(solution)/shard_map/mixer_forward/pallas_call | solution.py:515
  109.2 14.1 %all-gather.15.cloned.1.call-done = bf16[1,3072,768]{2,1,0:T(8,128)(2,1)} async-done(((bf16[1,384,768]{2,1,0:T(8,128)(2,1)}), bf16[1,3072,768]{2,1,0:T(8,128)(2,1)}) %all-gather.15.cloned.1.call-update) | async-done | bytes 4718608 | tf_op jit(solution)/shard_map/all_gather | solution.py:853
  151.4 20.4 %collective-permute-done.5 = bf16[128,1536]{1,0:T(8,128)(2,1)} collective-permute-done((bf16[128,1536]{1,0:T(8,128)(2,1)}, bf16[128,1536]{1,0:T(8,128)(2,1)}, u32[]{:S(2)}, u32[]{:S(2)}) %collective-permute-start.5) | collective-permute-done | bytes 393248 | tf_op jit(solution)/shard_map/ppermute | solution.py:26
  190.1 11.4 collective-permute-done.13
  210.2 8.8 collective-permute-done.16
  250.2 9.9 all-to-all-done.2
  287.1 9.8 all-to-all-done.3
  311.3 12.9 %collective-permute-done.17 = bf16[128,1536]{1,0:T(8,128)(2,1)} collective-permute-done((bf16[128,1536]{1,0:T(8,128)(2,1)}, bf16[128,1536]{1,0:T(8,128)(2,1)}, u32[]{:S(2)}, u32[]{:S(2)}) %collective-permute-start.17) | collective-permute-done | bytes 393248 | tf_op jit(solution)/shard_map/ppermute | solution.py:26
  337.2 25.1 %collective-permute-done.21 = bf16[128,1536]{1,0:T(8,128)(2,1)S(1)} collective-permute-done((bf16[128,1536]{1,0:T(8,128)(2,1)S(1)}, bf16[128,1536]{1,0:T(8,128)(2,1)S(1)}, u32[]{:S(2)}, u32[]{:S(2)}) %collective-permute-start.21) | collective-permute-done | bytes 393248 | tf_op jit(solution)/shard_map/ppermute | solution.py:26
  370.7 12.5 mixer_forward.3
  399.5 25.3 %collective-permute-done.24 = bf16[128,1536]{1,0:T(8,128)(2,1)} collective-permute-done((bf16[128,1536]{1,0:T(8,128)(2,1)}, bf16[128,1536]{1,0:T(8,128)(2,1)}, u32[]{:S(2)}, u32[]{:S(2)}) %collective-permute-start.24) | collective-permute-done | bytes 393248 | tf_op jit(solution)/shard_map/ppermute | solution.py:26
  536.1 8.6 all-to-all-done.8
  559.1 8.7 all-to-all-done.14
  684.2 25.3 %collective-permute-start.34 = (bf16[128,1536]{1,0:T(8,128)(2,1)}, bf16[128,1536]{1,0:T(8,128)(2,1)}, u32[]{:S(2)}, u32[]{:S(2)}) collective-permute-start(bf16[128,1536]{1,0:T(8,128)(2,1)} %get-tuple-element.256), channel_id=1, source_target_pairs={{0,1},{1,2},{2,3},{3,0},{4,5},{5,6},{6,7},{7,4},{8,9},{9,10},{10,1... | collective-permute-start | bytes 1179656 | tf_op jit(solution)/shard_map/ppermute | solution.py:26
  709.6 16.9 %collective-permute-done.43 = bf16[128,1536]{1,0:T(8,128)(2,1)} collective-permute-done((bf16[128,1536]{1,0:T(8,128)(2,1)}, bf16[128,1536]{1,0:T(8,128)(2,1)}, u32[]{:S(2)}, u32[]{:S(2)}) %collective-permute-start.43) | collective-permute-done | bytes 393248 | tf_op jit(solution)/shard_map/ppermute | solution.py:26
  731.6 17.9 %mixer_backward.2 = (bf16[512,1920]{1,0:T(8,128)(2,1)S(1)}, f32[2,768]{1,0:T(2,128)S(1)}, f32[4,768]{1,0:T(4,128)S(1)}, f32[4,256]{1,0:T(4,128)S(1)}, f32[2,128]{1,0:T(2,128)S(1)}) custom-call(f32[512,1920]{1,0:T(8,128)} %fusion.20.pre_in_ref, f32[512,768]{1,0:T(8,128)S(1)} %get-tuple-element.64.y_ref, f32[512,768]{1,0:T(8,128)S(1)} %fusion.99.grad_in_ref, ...), custom_call_target="tpu_custom_call" | custom-call | tf_op jit(solution)/shard_map/mixer_backward/pallas_call | solution.py:539
  772.9 16.6 %collective-permute-done.51 = bf16[128,1536]{1,0:T(8,128)(2,1)} collective-permute-done((bf16[128,1536]{1,0:T(8,128)(2,1)}, bf16[128,1536]{1,0:T(8,128)(2,1)}, u32[]{:S(2)}, u32[]{:S(2)}) %collective-permute-start.51) | collective-permute-done | bytes 393248 | tf_op jit(solution)/shard_map/ppermute | solution.py:26
  808.2 9.6 collective-permute-done.53
  818.0 17.8 %collective-permute-done.55 = bf16[128,1536]{1,0:T(8,128)(2,1)S(1)} collective-permute-done((bf16[128,1536]{1,0:T(8,128)(2,1)}, bf16[128,1536]{1,0:T(8,128)(2,1)S(1)}, u32[]{:S(2)}, u32[]{:S(2)}) %collective-permute-start.55) | collective-permute-done | bytes 393248 | tf_op jit(solution)/shard_map/ppermute | solution.py:26
  922.0 8.9 all-to-all-done.22
  943.9 12.8 %all-to-all-done.20 = bf16[4,128,1536]{2,1,0:T(8,128)(2,1)} async-done(((bf16[4,128,1536]{2,1,0:T(8,128)(2,1)}), bf16[4,128,1536]{2,1,0:T(8,128)(2,1)}, u32[]{:S(2)}, u32[]{:S(2)}) %all-to-all-start.20) | async-done | bytes 1572896 | tf_op jit(solution)/shard_map/all_to_all | solution.py:147
  999.4 10.2 all-to-all-done.21
  1020.9 15.6 %collective-permute-done.56 = bf16[128,1536]{1,0:T(8,128)(2,1)} collective-permute-done((bf16[128,1536]{1,0:T(8,128)(2,1)}, bf16[128,1536]{1,0:T(8,128)(2,1)}, u32[]{:S(2)}, u32[]{:S(2)}) %collective-permute-start.56) | collective-permute-done | bytes 393248 | tf_op jit(solution)/shard_map/ppermute | solution.py:26
  1057.2 10.0 collective-permute-done.69
  1067.3 10.8 collective-permute-start.67
  1084.6 18.1 %mixer_backward.3 = (bf16[512,1920]{1,0:T(8,128)(2,1)S(1)}, f32[2,768]{1,0:T(2,128)S(1)}, f32[4,768]{1,0:T(4,128)S(1)}, f32[4,256]{1,0:T(4,128)S(1)}, f32[2,128]{1,0:T(2,128)S(1)}) custom-call(f32[512,1920]{1,0:T(8,128)} %fusion.30.pre_in_ref, f32[512,768]{1,0:T(8,128)S(1)} %get-tuple-element.63.y_ref, f32[512,768]{1,0:T(8,128)S(1)} %fusion.98.grad_in_ref, ...), custom_call_target="tpu_custom_call" | custom-call | tf_op jit(solution)/shard_map/mixer_backward/pallas_call | solution.py:539
  1135.5 9.8 collective-permute-done.71
  1212.3 10.7 collective-permute-done.82
  1222.9 11.5 collective-permute-done.84
  (1095 shorter events, 780.5 us)
Async XLA Ops:
  7.2 75.2 %all-gather.11.cloned.1.call-start = ((), (), s32[]{:S(2)}) async-start(), calls=%async_computation.31 | async-start | bytes 13271040 | tf_op jit(solution)/shard_map/all_gather | solution.py:853
  10.8 112.5 %all-gather.15.cloned.1.call-start = ((), (), s32[]{:S(2)}) async-start(), calls=%async_computation.40 | async-start | bytes 5308416 | tf_op jit(solution)/shard_map/all_gather | solution.py:853
  11.5 175.5 %all-gather.13.cloned.1.call-start = ((), (), s32[]{:S(2)}) async-start(), calls=%async_computation.32 | async-start | bytes 5308416 | tf_op jit(solution)/shard_map/all_gather | solution.py:853
  12.6 194.5 %all-gather.17.cloned.1.call-start = ((), (), s32[]{:S(2)}) async-start(), calls=%async_computation.41 | async-start | bytes 4718592 | tf_op jit(solution)/shard_map/all_gather | solution.py:868
  13.2 212.2 %all-gather.19.cloned.1.call-start = ((), (), s32[]{:S(2)}) async-start(), calls=%async_computation.42 | async-start | bytes 4718592 | tf_op jit(solution)/shard_map/all_gather | solution.py:869
  13.8 214.9 %all-gather.21.cloned.1.call-start = ((), (), s32[]{:S(2)}) async-start(), calls=%async_computation.43 | async-start | bytes 4718592 | tf_op jit(solution)/shard_map/all_gather | solution.py:870
  29.6 51.4 %collective-permute-start.2 = (bf16[128,1536]{1,0:T(8,128)(2,1)}, bf16[128,1536]{1,0:T(8,128)(2,1)S(1)}, u32[]{:S(2)}, u32[]{:S(2)}) collective-permute-start(bf16[128,1536]{1,0:T(8,128)(2,1)} %multiply_convert_fusion.11), channel_id=1, source_target_pairs={{0,2},{1,3},{2,0},{3,1},{4,6},{5,7},{6,4},{7,5},{8,10},{9,11},{10,... | collective-permute-start | bytes 1179656 | tf_op jit(solution)/shard_map/ppermute | solution.py:26
  29.6 51.4 %collective-permute-start.1 = (bf16[128,1536]{1,0:T(8,128)(2,1)}, bf16[128,1536]{1,0:T(8,128)(2,1)S(1)}, u32[]{:S(2)}, u32[]{:S(2)}) collective-permute-start(bf16[128,1536]{1,0:T(8,128)(2,1)} %multiply_convert_fusion.11), channel_id=1, source_target_pairs={{0,1},{1,2},{2,3},{3,0},{4,5},{5,6},{6,7},{7,4},{8,9},{9,10},{10,1... | collective-permute-start | bytes 1179656 | tf_op jit(solution)/shard_map/ppermute | solution.py:26
  40.7 289.5 %collective-permute-start.38 = (bf16[128,1536]{1,0:T(8,128)(2,1)}, bf16[128,1536]{1,0:T(8,128)(2,1)}, u32[]{:S(2)}, u32[]{:S(2)}) collective-permute-start(bf16[128,1536]{1,0:T(8,128)(2,1)} %bitcast_convert_fusion), channel_id=1, source_target_pairs={{0,2},{1,3},{2,0},{3,1},{4,6},{5,7},{6,4},{7,5},{8,10},{9,11},{10,... | collective-permute-start | bytes 1179656 | tf_op jit(solution)/shard_map/ppermute | solution.py:26
  103.4 38.0 %collective-permute-start.15 = (f32[128,24]{0,1:T(8,128)S(1)}, f32[128,24]{0,1:T(8,128)S(1)}, u32[]{:S(2)}, u32[]{:S(2)}) collective-permute-start(f32[128,24]{0,1:T(8,128)S(1)} %pad_maximum_fusion.38), channel_id=1, source_target_pairs={{0,2},{1,3},{2,0},{3,1},{4,6},{5,7},{6,4},{7,5},{8,10},{9,11},{10,... | collective-permute-start | bytes 36872 | tf_op jit(solution)/shard_map/ppermute | solution.py:26
  450.9 36.7 %collective-permute-start.31 = (bf16[128,1536]{1,0:T(8,128)(2,1)}, bf16[128,1536]{1,0:T(8,128)(2,1)}, u32[]{:S(2)}, u32[]{:S(2)}) collective-permute-start(bf16[128,1536]{1,0:T(8,128)(2,1)} %multiply_convert_fusion.8), channel_id=1, source_target_pairs={{0,2},{1,3},{2,0},{3,1},{4,6},{5,7},{6,4},{7,5},{8,10},{9,11},{10,... | collective-permute-start | bytes 1179656 | tf_op jit(solution)/shard_map/ppermute | solution.py:26
  513.9 42.0 %collective-permute-start.45 = (bf16[1536,256]{1,0:T(8,128)(2,1)}, bf16[1536,256]{1,0:T(8,128)(2,1)}, u32[]{:S(2)}, u32[]{:S(2)}) collective-permute-start(bf16[1536,256]{1,0:T(8,128)(2,1)} %convolution_convert_fusion.19), channel_id=1, source_target_pairs={{0,16},{16,0},{1,17},{17,1},{2,18},{18,2},{3,19},{19,3},{4,20},{20... | collective-permute-start | bytes 2359304 | tf_op jit(solution)/shard_map/ppermute | solution.py:30
  621.5 39.3 %collective-permute-start.40 = (bf16[128,1536]{1,0:T(8,128)(2,1)}, bf16[128,1536]{1,0:T(8,128)(2,1)}, u32[]{:S(2)}, u32[]{:S(2)}) collective-permute-start(bf16[128,1536]{1,0:T(8,128)(2,1)} %fusion.59), channel_id=1, source_target_pairs={{0,2},{1,3},{2,0},{3,1},{4,6},{5,7},{6,4},{7,5},{8,10},{9,11},{10,... | collective-permute-start | bytes 1179656 | tf_op jit(solution)/shard_map/ppermute | solution.py:26
  654.3 115.0 %all-to-all-start.7 = ((bf16[4,64,1536]{2,1,0:T(8,128)(2,1)}), bf16[4,64,1536]{2,1,0:T(8,128)(2,1)}, u32[]{:S(2)}, u32[]{:S(2)}) async-start(bf16[4,64,1536]{2,1,0:T(8,128)(2,1)} %bitcast.461), calls=%async_computation.7 | async-start | bytes 1572864 | tf_op jit(solution)/shard_map/all_to_all | solution.py:147
  658.5 332.9 %reduce-scatter.20.cloned.1.call-start = ((), (), s32[]{:S(2)}) async-start(), calls=%async_computation.39 | async-start | bytes 491520 | tf_op jit(solution)/shard_map/reduce_scatter | solution.py:920
  673.5 53.0 %collective-permute-start.43 = (bf16[128,1536]{1,0:T(8,128)(2,1)}, bf16[128,1536]{1,0:T(8,128)(2,1)}, u32[]{:S(2)}, u32[]{:S(2)}) collective-permute-start(bf16[128,1536]{1,0:T(8,128)(2,1)} %convert_element_type.791), channel_id=1, source_target_pairs={{0,2},{1,3},{2,0},{3,1},{4,6},{5,7},{6,4},{7,5},{8,10},{9,11},{10,... | collective-permute-start | bytes 1179656 | tf_op jit(solution)/shard_map/ppermute | solution.py:26
  674.0 52.5 %collective-permute-start.42 = (bf16[128,1536]{1,0:T(8,128)(2,1)}, bf16[128,1536]{1,0:T(8,128)(2,1)}, u32[]{:S(2)}, u32[]{:S(2)}) collective-permute-start(bf16[128,1536]{1,0:T(8,128)(2,1)} %convert_element_type.791), channel_id=1, source_target_pairs={{0,1},{1,2},{2,3},{3,0},{4,5},{5,6},{6,7},{7,4},{8,9},{9,10},{10,1... | collective-permute-start | bytes 1179656 | tf_op jit(solution)/shard_map/ppermute | solution.py:26
  676.2 91.0 %collective-permute-start.33 = (bf16[128,1536]{1,0:T(8,128)(2,1)}, bf16[128,1536]{1,0:T(8,128)(2,1)}, u32[]{:S(2)}, u32[]{:S(2)}) collective-permute-start(bf16[128,1536]{1,0:T(8,128)(2,1)} %fusion.56), channel_id=1, source_target_pairs={{0,2},{1,3},{2,0},{3,1},{4,6},{5,7},{6,4},{7,5},{8,10},{9,11},{10,... | collective-permute-start | bytes 1179656 | tf_op jit(solution)/shard_map/ppermute | solution.py:26
  677.4 93.4 %collective-permute-start.32 = (bf16[128,1536]{1,0:T(8,128)(2,1)}, bf16[128,1536]{1,0:T(8,128)(2,1)}, u32[]{:S(2)}, u32[]{:S(2)}) collective-permute-start(bf16[128,1536]{1,0:T(8,128)(2,1)} %get-tuple-element.255), channel_id=1, source_target_pairs={{0,3},{1,0},{2,1},{3,2},{4,7},{5,4},{6,5},{7,6},{8,11},{9,8},{10,9... | collective-permute-start | bytes 1179656 | tf_op jit(solution)/shard_map/ppermute | solution.py:26
  684.2 86.5 %collective-permute-start.34 = (bf16[128,1536]{1,0:T(8,128)(2,1)}, bf16[128,1536]{1,0:T(8,128)(2,1)}, u32[]{:S(2)}, u32[]{:S(2)}) collective-permute-start(bf16[128,1536]{1,0:T(8,128)(2,1)} %get-tuple-element.256), channel_id=1, source_target_pairs={{0,1},{1,2},{2,3},{3,0},{4,5},{5,6},{6,7},{7,4},{8,9},{9,10},{10,1... | collective-permute-start | bytes 1179656 | tf_op jit(solution)/shard_map/ppermute | solution.py:26
  817.9 173.5 %reduce-scatter.18.cloned.1.call-start = ((), (), s32[]{:S(2)}) async-start(), calls=%async_computation.38 | async-start | bytes 491520 | tf_op jit(solution)/shard_map/reduce_scatter | solution.py:920
  841.9 177.9 %reduce-scatter.16.cloned.1.call-start = ((), (), s32[]{:S(2)}) async-start(), calls=%async_computation.37 | async-start | bytes 983040 | tf_op jit(solution)/shard_map/reduce_scatter | solution.py:920
  842.6 177.1 %reduce-scatter.14.cloned.1.call-start = ((), (), s32[]{:S(2)}) async-start(), calls=%async_computation.36 | async-start | bytes 983040 | tf_op jit(solution)/shard_map/reduce_scatter | solution.py:920
  860.1 375.2 %reduce-scatter.8.cloned.1.call-start = ((), (), s32[]{:S(2)}) async-start(), calls=%async_computation.33 | async-start | bytes 2949120 | tf_op jit(solution)/shard_map/reduce_scatter | solution.py:920
  870.3 47.5 %collective-permute-start.98 = (bf16[1536,384]{1,0:T(8,128)(2,1)}, bf16[1536,384]{1,0:T(8,128)(2,1)}, u32[]{:S(2)}, u32[]{:S(2)}) collective-permute-start(bf16[1536,384]{1,0:T(8,128)(2,1)} %convolution_convert_fusion.12), channel_id=1, source_target_pairs={{0,16},{16,0},{1,17},{17,1},{2,18},{18,2},{3,19},{19,3},{4,20},{20... | collective-permute-start | bytes 3538952 | tf_op jit(solution)/shard_map/ppermute | solution.py:30
  917.7 321.1 %reduce-scatter.12.cloned.1.call-start = ((), (), s32[]{:S(2)}) async-start(), calls=%async_computation.35 | async-start | bytes 1474560 | tf_op jit(solution)/shard_map/reduce_scatter | solution.py:920
  984.7 254.1 %reduce-scatter.10.cloned.1.call-start = ((), (), s32[]{:S(2)}) async-start(), calls=%async_computation.34 | async-start | bytes 1474560 | tf_op jit(solution)/shard_map/reduce_scatter | solution.py:920
  990.9 51.4 %collective-permute-start.64 = (bf16[512,1536]{1,0:T(8,128)(2,1)}, bf16[512,1536]{1,0:T(8,128)(2,1)}, u32[]{:S(2)}, u32[]{:S(2)}) collective-permute-start(bf16[512,1536]{1,0:T(8,128)(2,1)} %get-tuple-element.353), channel_id=1, source_target_pairs={{0,16},{16,0},{1,17},{17,1},{2,18},{18,2},{3,19},{19,3},{4,20},{20... | collective-permute-start | bytes 4718600 | tf_op jit(solution)/shard_map/ppermute | solution.py:30
  990.9 55.4 %collective-permute-start.63 = (bf16[1536,512]{1,0:T(8,128)(2,1)}, bf16[1536,512]{1,0:T(8,128)(2,1)}, u32[]{:S(2)}, u32[]{:S(2)}) collective-permute-start(bf16[1536,512]{1,0:T(8,128)(2,1)} %get-tuple-element.351), channel_id=1, source_target_pairs={{0,16},{16,0},{1,17},{17,1},{2,18},{18,2},{3,19},{19,3},{4,20},{20... | collective-permute-start | bytes 4718600 | tf_op jit(solution)/shard_map/ppermute | solution.py:30
  1040.3 39.2 %collective-permute-start.61 = (bf16[128,1536]{1,0:T(8,128)(2,1)S(1)}, bf16[128,1536]{1,0:T(8,128)(2,1)}, u32[]{:S(2)}, u32[]{:S(2)}) collective-permute-start(bf16[128,1536]{1,0:T(8,128)(2,1)S(1)} %convert_element_type.835), channel_id=1, source_target_pairs={{0,3},{1,0},{2,1},{3,2},{4,7},{5,4},{6,5},{7,6},{8,11},{9,8},{10,9... | collective-permute-start | bytes 1179656 | tf_op jit(solution)/shard_map/ppermute | solution.py:26
  1042.4 37.1 %collective-permute-start.60 = (bf16[128,1536]{1,0:T(8,128)(2,1)S(1)}, bf16[128,1536]{1,0:T(8,128)(2,1)}, u32[]{:S(2)}, u32[]{:S(2)}) collective-permute-start(bf16[128,1536]{1,0:T(8,128)(2,1)S(1)} %convert_element_type.835), channel_id=1, source_target_pairs={{0,2},{1,3},{2,0},{3,1},{4,6},{5,7},{6,4},{7,5},{8,10},{9,11},{10,... | collective-permute-start | bytes 1179656 | tf_op jit(solution)/shard_map/ppermute | solution.py:26
  1124.8 63.9 %collective-permute-start.97 = (bf16[1536,384]{1,0:T(8,128)(2,1)}, bf16[1536,384]{1,0:T(8,128)(2,1)}, u32[]{:S(2)}, u32[]{:S(2)}) collective-permute-start(bf16[1536,384]{1,0:T(8,128)(2,1)} %convolution_convert_fusion.13), channel_id=1, source_target_pairs={{0,16},{16,0},{1,17},{17,1},{2,18},{18,2},{3,19},{19,3},{4,20},{20... | collective-permute-start | bytes 3538952 | tf_op jit(solution)/shard_map/ppermute | solution.py:30
  (353 other events, 4719.1 us)
Sparse Core Ops, SparseCore 0:
  10.9 71.4 all-gather.10
  84.3 38.9 all-gather.14
  125.7 38.9 all-gather.12
  166.1 12.1 all-gather.16
  179.6 13.2 all-gather.18
  194.4 13.2 all-gather.20
  818.1 25.1 reduce-scatter.19
  846.0 24.4 reduce-scatter.17
  873.4 30.1 reduce-scatter.15
  906.3 44.6 reduce-scatter.13
  954.0 55.6 reduce-scatter.7
  1012.5 29.5 reduce-scatter.11
  1192.3 45.2 reduce-scatter.9

commit v4 on v3

--- a/solution.py
+++ b/solution.py
@@ -72,17 +72,10 @@
     return {1: [(0,)], 2: [(0,), (1,)], 3: [(0,), (1, 2)], 4: [(0,), (1, 3), (2,)]}[count]
 
 
-def spread(block, staged=False):
-    count = groups()
-    if count == 1:
+def spread(block):
+    if groups() == 1:
         return [lax.all_gather(block, "col", axis=0, tiled=True)]
-    result = [block] * count
-    for back in (1, count - 1):
-        result[back] = shifted(block, "col", back)
-    source = after(block, result[1], result[-1]) if staged else block
-    for back in range(2, count - 1):
-        result[back] = shifted(source, "col", back)
-    return result
+    return [shifted(block, "col", back) for back in range(groups())]
 
 
 def joined(blocks):
@@ -225,6 +218,7 @@
     heads,
     parts,
     pre_in_ref,
+    pre_other_in_ref,
     conv_input_ref,
     conv_state_ref,
     step_row_ref,
@@ -236,6 +230,7 @@
     scaled_ref,
     total_ref,
     pre_ref,
+    pre_other_ref,
     x_ref,
     dosed_ref,
     keys_ref,
@@ -243,17 +238,18 @@
 ):
     length, wide = y_ref.shape
     states = conv_state_ref.shape[1] // 2
-    state_at, step_at = 2 * wide, 2 * wide + 2 * states
+    state_at, step_at = wide, wide
     head_width = HEAD
     pre_ref = copy_in_order(pre_in_ref, pre_ref, place_ref, parts)
-    _, sizes, rate = step_sizes(pre_ref[:, step_at : step_at + LANES], step_row_ref)
+    pre_other_ref = copy_in_order(pre_other_in_ref, pre_other_ref, place_ref, parts)
+    _, sizes, rate = step_sizes(pre_other_ref[:, step_at : step_at + LANES], step_row_ref)
     running = summed_rows(sizes * rate, False)
     running_t = running.T
     expand = head_columns(LANES, wide, head_width)
     for start in range(0, wide, LANES):
         columns = slice(start, start + LANES)
         conv = conv_rows(
-            pre_ref[:, wide + start : wide + start + LANES], conv_input_ref, columns, marks_ref
+            pre_other_ref[:, columns], conv_input_ref, columns, marks_ref
         )
         x = conv * sigmoid(conv)
         x_ref[:, columns] = x
@@ -322,6 +318,7 @@
     parts,
     inner_all,
     pre_in_ref,
+    pre_other_in_ref,
     y_ref,
     grad_in_ref,
     sides_in_ref,
@@ -333,11 +330,13 @@
     labels_ref,
     place_ref,
     grad_pre_ref,
+    grad_pre_other_ref,
     wide_grad_ref,
     conv_input_grad_ref,
     conv_state_grad_ref,
     step_grad_ref,
     pre_ref,
+    pre_other_ref,
     grad_ref,
     sides_ref,
     x_ref,
@@ -352,20 +351,21 @@
 ):
     length, wide = y_ref.shape
     states = conv_state_ref.shape[1] // 2
-    state_at, step_at = 2 * wide, 2 * wide + 2 * states
+    state_at, step_at = wide, wide
     head_width = HEAD
     each = length // parts
     pre_ref = copy_in_order(pre_in_ref, pre_ref, place_ref, parts)
+    pre_other_ref = copy_in_order(pre_other_in_ref, pre_other_ref, place_ref, parts)
     grad_ref = copy_in_order(grad_in_ref, grad_ref, place_ref, parts)
     sides_ref = copy_in_order(sides_in_ref, sides_ref, place_ref, parts)
 
-    def put(value, start):
+    def put(target_ref, value, start):
         for index in range(parts):
-            grad_pre_ref[block_rows(index, each, place_ref, parts), start : start + LANES] = value[
+            target_ref[block_rows(index, each, place_ref, parts), start : start + LANES] = value[
                 index * each : (index + 1) * each
             ]
 
-    shifted_pre, sizes, rate = step_sizes(pre_ref[:, step_at : step_at + LANES], step_row_ref)
+    shifted_pre, sizes, rate = step_sizes(pre_other_ref[:, step_at : step_at + LANES], step_row_ref)
     running = summed_rows(sizes * rate, False)
     running_t = running.T
     expand = head_columns(LANES, wide, head_width)
@@ -384,11 +384,11 @@
         wide_grad_ref[0:1, columns] = jnp.sum(grad * normed, axis=0, keepdims=True)
         grad_gated = rr * gain * grad - gated * pull
         slope = sigma * (1.0 + gate * (1.0 - sigma))
-        put((grad_gated * y * slope).astype(HALF), start)
+        put(grad_pre_ref, (grad_gated * y * slope).astype(HALF), start)
         dy = grad_gated * silu
         dy_ref[:, columns] = dy
         conv = conv_rows(
-            pre_ref[:, wide + start : wide + start + LANES], conv_input_ref, columns, marks_ref
+            pre_other_ref[:, columns], conv_input_ref, columns, marks_ref
         )
         sigma = sigmoid(conv)
         x = conv * sigma
@@ -466,13 +466,13 @@
         grad_conv = (dose_ref[:, columns] * z + skip * dy) * slope_ref[:, columns]
         grad_in = conv_rows_back(
             grad_conv,
-            pre_ref[:, wide + start : wide + start + LANES],
+            pre_other_ref[:, columns],
             conv_input_ref,
             columns,
             marks_ref,
             conv_input_grad_ref,
         )
-        put(grad_in.astype(HALF), wide + start)
+        put(grad_pre_other_ref, grad_in.astype(HALF), start)
     for start in range(0, 2 * states, LANES):
         columns = slice(start, start + LANES)
         grad_in = conv_rows_back(
@@ -483,10 +483,12 @@
             marks_ref,
             conv_state_grad_ref,
         )
-        put(grad_in.astype(HALF), state_at + start)
+        put(grad_pre_ref, grad_in.astype(HALF), state_at + start)
     crossing = summed_rows(balance, True)
     grad_step = (direct + rate * crossing) * sigmoid(shifted_pre)
-    put(grad_step.astype(HALF), step_at)
+    put(grad_pre_other_ref, grad_step.astype(HALF), step_at)
+    for start in range(step_at + LANES, grad_pre_other_ref.shape[1], LANES):
+        put(grad_pre_other_ref, jnp.zeros((length, LANES), HALF), start)
     step_grad_ref[0:1, :] = jnp.sum(grad_step, axis=0, keepdims=True)
     step_grad_ref[1:2, :] = rate * jnp.sum(sizes * crossing, axis=0, keepdims=True)
 
@@ -509,26 +511,27 @@
 
 
 def mixer_forward(pre, heads, wide, mixer):
-    length = pre.shape[0]
+    length = pre[0].shape[0]
     kernel = functools.partial(mixer_forward_kernel, heads, groups())
     states = mixer[1].shape[1] // 2
     return whole_call(
         kernel,
-        1 + len(mixer),
+        2 + len(mixer),
         (
             jax.ShapeDtypeStruct((length, wide), FLOAT),
             jax.ShapeDtypeStruct((length, wide), HALF),
             jax.ShapeDtypeStruct((length, 1), FLOAT),
         ),
         [
-            ordered_copy(pre.shape),
+            ordered_copy(pre[0].shape),
+            ordered_copy(pre[1].shape),
             pltpu.VMEM((length, wide), FLOAT),
             pltpu.VMEM((length, wide), HALF),
             pltpu.VMEM((length, states), HALF),
             pltpu.VMEM((length, states), HALF),
         ],
         "mixer_forward",
-    )(pre, *mixer)
+    )(*pre, *mixer)
 
 
 def mixer_backward(pre, y, grad, sides, heads, mixer):
@@ -538,16 +541,18 @@
     square = pltpu.VMEM((length, wide), FLOAT)
     return whole_call(
         kernel,
-        4 + len(mixer),
+        5 + len(mixer),
         (
-            jax.ShapeDtypeStruct(pre.shape, HALF),
+            jax.ShapeDtypeStruct(pre[0].shape, HALF),
+            jax.ShapeDtypeStruct(pre[1].shape, HALF),
             jax.ShapeDtypeStruct((2, wide), FLOAT),
             jax.ShapeDtypeStruct((4, wide), FLOAT),
             jax.ShapeDtypeStruct((4, double), FLOAT),
             jax.ShapeDtypeStruct((2, LANES), FLOAT),
         ),
         [
-            ordered_copy(pre.shape),
+            ordered_copy(pre[0].shape),
+            ordered_copy(pre[1].shape),
             ordered_copy(y.shape),
             ordered_copy(sides.shape),
             square,
@@ -561,181 +566,113 @@
             pltpu.VMEM((length, double), FLOAT),
         ],
         "mixer_backward",
-    )(pre, y, grad, sides, *mixer)
-
-
-def through_experts(blocks, tables, expert, beside):
-    tokens = [joined([blocks[back] for back in chunk]) for chunk in chunks()]
-    count = len(tokens)
-    sent = [project(table, values).astype(HALF) for table, values in zip(tables, tokens)]
+    )(*pre, y, grad, sides, *mixer)
+
+
+def to_blocks(per_chunk):
     parts = [None] * groups()
-    arrived = []
-    rows = to_experts(sent[0])
-    for index, chunk in enumerate(chunks()):
-        if index and index + 1 < count:
-            rows = after(rows, sent[index + 1])
-        arrived.append(rows)
-        answer = expert(index, rows)
-        if index + 1 < count:
-            following = sent[index + 1] if index else after(sent[1], answer)
-            rows = to_experts(following)
-        part = beside(index, tokens[index], to_experts(answer))
+    for chunk, part in zip(chunks(), per_chunk):
         rows_each = part.shape[0] // len(chunk)
         for at, back in enumerate(chunk):
             parts[back] = part[at * rows_each : (at + 1) * rows_each]
-    return parts, arrived
-
-
-def layer_forward(resid, params, dense, mixer, tables):
-    norm_in, norm_mid = params
-    proj, proj_output, shared, expert_gate, expert_up, expert_down = dense
-    wide = mixer[0].shape[1]
-    heads = mixer[-1]
+    return parts
+
+
+def through_experts(block, tables, expert, beside):
+    if groups() < 4:
+        blocks = spread(block)
+        tokens = [joined([blocks[back] for back in chunk]) for chunk in chunks()]
+        arrived = [to_experts(project(table, each)) for table, each in zip(tables, tokens)]
+        answers = [to_experts(expert(index, rows)) for index, rows in enumerate(arrived)]
+        made = [beside(*each) for each in zip(range(len(tokens)), tokens, answers)]
+        return to_blocks(made), arrived, tokens
+    near, far = shifted(block, "col", 1), shifted(block, "col", 3)
+    rows = to_experts(project(tables[0], block))
+    answer = expert(0, rows)
+    answered = to_experts(answer)
+    near, far = after(near, answer), after(far, answer)
+    last = shifted(after(block, near, far), "col", 2)
+    near = jnp.concatenate([near, far], axis=0)
+    sent = project(tables[1], near).astype(HALF)
+    rows_near = to_experts(sent)
+    part = beside(0, block, answered)
+    last = after(last, sent, part)
+    sent = project(tables[2], last).astype(HALF)
+    rows_last = to_experts(sent)
+    answer = expert(1, after(rows_near, sent))
+    answered = to_experts(answer)
+    answer = expert(2, after(rows_last, answer))
+    answered_last = to_experts(answer)
+    part_near = beside(1, near, after(answered, answer))
+    part_last = beside(2, last, answered_last)
+    parts = to_blocks([part, part_near, part_last])
+    return parts, [rows, rows_near, rows_last], [block, near, last]
+
+
+def line_shares(values, weights):
+    whole = sum(project_back(value, weight) for value, weight in zip(values, weights)).astype(HALF)
+    return gathered_sum([block_of(whole, back) for back in range(groups())]), whole
+
+
+def expert_forward(rows, experts):
+    gate_e = project(rows, experts[0])
+    lift_e = project(rows, experts[1])
+    act_e = (jax.nn.silu(gate_e) * lift_e).astype(HALF)
+    return (gate_e, lift_e, act_e), project(act_e, experts[2]).astype(HALF)
+
+
+def expert_backward(rows, kept, experts):
+    gate_e, lift_e, _ = kept
+    grad_act = project_back(rows, experts[2])
+    grad_gate = (grad_act * lift_e * silu_slope(gate_e)).astype(HALF)
+    grad_lift = (grad_act * jax.nn.silu(gate_e)).astype(HALF)
+    back = project_back(grad_gate, experts[0]) + project_back(grad_lift, experts[1])
+    return (grad_gate, grad_lift), back.astype(HALF)
+
+
+def shared_forward(tokens, shared):
     hidden = shared.shape[1] // 3
-    backs = range(groups())
-    wide_in = joined(spread(rms_norm(resid, norm_in).astype(HALF)))
-    pre = project(wide_in, proj)
-    y, scaled, total_part = mixer_forward(pre, heads, wide, mixer[:-1])
-    total = gathered_sum([block_of(total_part, back) for back in backs])
-    mixed = gathered_sum(
-        [project_back(block_of(scaled, back), proj_output).astype(HALF) for back in backs]
-    )
-    if callable(tables):
-        tables = tables(scaled)
-    rr = lax.rsqrt(total / DI + EPS)
-    middle = resid + mixed * rr
-    wide_mid = spread(rms_norm(middle, norm_mid).astype(HALF), staged=True)
-    shared_pre, shared_act, expert_pre, active, returned = [], [], [], [], []
-
-    def expert(index, rows):
-        gate_e = project(rows, expert_gate)
-        lift_e = project(rows, expert_up)
-        act_e = (jax.nn.silu(gate_e) * lift_e).astype(HALF)
-        expert_pre.append((gate_e, lift_e))
-        active.append(act_e)
-        return project(act_e, expert_down).astype(HALF)
-
-    def beside(index, tokens, result):
-        gate_s = project(tokens, shared[:, :hidden])
-        lift_s = project(tokens, shared[:, hidden : 2 * hidden])
-        act_s = (jax.nn.silu(gate_s) * lift_s).astype(HALF)
-        shared_pre.append((gate_s, lift_s))
-        shared_act.append(act_s)
-        part = outer(tables[0][index][1], result) + project_back(act_s, shared[:, 2 * hidden :])
-        return part.astype(HALF)
-
-    parts, arrived = through_experts(wide_mid, [table[0] for table in tables[0]], expert, beside)
-    saved = (
-        resid,
-        middle,
-        mixed,
-        rr,
-        wide_in,
-        pre,
-        y,
-        scaled,
-        wide_mid,
-        shared_pre,
-        shared_act,
-        arrived,
-        expert_pre,
-        active,
-    )
-    return (middle + gathered_sum(parts), saved, tables)
-
-
-def layer_backward(grad_out, saved, params, dense, mixer, tables, pending):
-    norm_in, norm_mid = params
-    proj, proj_output, shared, expert_gate, expert_up, expert_down = dense
-    (
-        resid,
-        middle,
-        mixed,
-        rr,
-        wide_in,
-        pre,
-        y,
-        scaled,
-        wide_mid,
-        shared_pre,
-        shared_act,
-        arrived,
-        expert_pre,
-        active,
-    ) = saved
-    wide, heads = mixer[0].shape[1], mixer[-1]
+    gate_s = project(tokens, shared[:, :hidden])
+    lift_s = project(tokens, shared[:, hidden : 2 * hidden])
+    return gate_s, lift_s, (jax.nn.silu(gate_s) * lift_s).astype(HALF)
+
+
+def shared_backward(tokens, kept, shared):
     hidden = shared.shape[1] // 3
-    backs = range(groups())
-    wide_out = spread(grad_out.astype(HALF), staged=True)
-    gate_grads, lift_grads, shared_grads = [], [], []
-
-    def expert(index, rows):
-        gate_e, lift_e = expert_pre[index]
-        grad_act = project_back(rows, expert_down)
-        grad_gate_e = (grad_act * lift_e * silu_slope(gate_e)).astype(HALF)
-        grad_lift_e = (grad_act * jax.nn.silu(gate_e)).astype(HALF)
-        gate_grads.append(grad_gate_e)
-        lift_grads.append(grad_lift_e)
-        back = project_back(grad_gate_e, expert_gate) + project_back(grad_lift_e, expert_up)
-        return back.astype(HALF)
-
-    def beside(index, tokens, result):
-        gate_s, lift_s = shared_pre[index]
-        grad_act_s = project(tokens, shared[:, 2 * hidden :])
-        grad_gate_s = (grad_act_s * lift_s * silu_slope(gate_s)).astype(HALF)
-        grad_lift_s = (grad_act_s * jax.nn.silu(gate_s)).astype(HALF)
-        shared_grads.append((grad_gate_s, grad_lift_s))
-        part = (
-            outer(tables[index][0], result)
-            + project_back(grad_gate_s, shared[:, :hidden])
-            + project_back(grad_lift_s, shared[:, hidden : 2 * hidden])
-        )
-        return part.astype(HALF)
-
-    parts, rows_grad = through_experts(wide_out, [table[1] for table in tables], expert, beside)
-    grad_normed = gathered_sum(parts)
+    gate_s, lift_s, _ = kept
+    grad_act = project(tokens, shared[:, 2 * hidden :])
+    grad_gate = (grad_act * lift_s * silu_slope(gate_s)).astype(HALF)
+    grad_lift = (grad_act * jax.nn.silu(gate_s)).astype(HALF)
+    part = project_back(grad_gate, shared[:, :hidden])
+    part = part + project_back(grad_lift, shared[:, hidden : 2 * hidden])
+    return (grad_gate, grad_lift), part
+
+
+def home_part(table, result, act_s, shared):
+    hidden = shared.shape[1] // 3
+    return (outer(table, result) + project_back(act_s, shared[:, 2 * hidden :])).astype(HALF)
+
+
+def weight_sums(rows_in, rows_out, kept, grads, tokens_in, tokens_out, kept_s, grads_s):
+    rows_in, rows_out = joined(rows_in), joined(rows_out)
+    experts = (
+        outer(rows_in, joined([each[0] for each in grads])),
+        outer(rows_in, joined([each[1] for each in grads])),
+        outer(joined([each[2] for each in kept]), rows_out),
+    )
+    tokens_in, tokens_out = joined(tokens_in), joined(tokens_out)
+    pairs = [joined([each[at] for each in grads_s]) for at in range(2)]
+    act_s = joined([each[2] for each in kept_s])
+    shared = (section_half(tokens_in, *pairs), section_half(tokens_out, *two_halves(act_s)))
+    return experts, shared
+
+
+def middle_backward(grad_normed, grad_out, middle, mixed, norm_mid):
     _, pull_mid = jax.vjp(rms_norm, middle, norm_mid)
     grad_middle, grad_norm_mid = pull_mid(grad_normed)
     grad_middle = grad_middle + grad_out
     along = jnp.sum(grad_middle * mixed, axis=1, keepdims=True)
-    wide_mix = joined(spread(grad_middle.astype(HALF)))
-    sides = joined(spread(jnp.concatenate([rr, along], axis=1)))
-    rows_in, rows_out = joined(arrived), joined(rows_grad)
-    expert_grads = (
-        outer(rows_in, joined(gate_grads)),
-        outer(rows_in, joined(lift_grads)),
-        outer(joined(active), rows_out),
-    )
-    order = [back for chunk in chunks() for back in chunk]
-    mids, outs = joined([wide_mid[back] for back in order]), joined([wide_out[back] for back in order])
-    grad_shared = (
-        section_half(mids, *[joined(list(part)) for part in zip(*shared_grads)]),
-        section_half(outs, *two_halves(joined(shared_act))),
-    )
-    expert_grads = pending(expert_grads)
-    wide_mix = after(wide_mix, expert_grads, grad_shared)
-    grad_proj_output = section_half((wide_mix * sides[:, :1]).astype(HALF), *two_halves(scaled))
-    grad_scaled = project(wide_mix, proj_output)
-    grad_pre, wide_grads, grad_conv_input, grad_conv_state, step_grads = mixer_backward(
-        pre, y, grad_scaled, sides, heads, mixer[:-1]
-    )
-    grad_normed_in = gathered_sum(
-        [project_back(block_of(grad_pre, back), proj).astype(HALF) for back in backs]
-    )
-    grad_proj = section_half(wide_in, grad_pre[:, :wide], grad_pre[:, wide : 2 * wide])
-    grad_tail = outer(wide_in, grad_pre[:, 2 * wide :]).astype(HALF)
-    _, pull_in = jax.vjp(rms_norm, resid, norm_in)
-    grad_resid, grad_norm_in = pull_in(grad_normed_in)
-    small = (
-        grad_norm_in,
-        grad_norm_mid,
-        grad_conv_state,
-        grad_conv_input,
-        wide_grads,
-        step_grads,
-    )
-    dense_grads = (grad_proj, grad_proj_output, *grad_shared)
-    return (grad_resid + grad_middle, small, dense_grads, grad_tail, expert_grads)
+    return grad_middle, along, grad_norm_mid
 
 
 def two_halves(values):
@@ -743,11 +680,20 @@
     return values[:, :middle], values[:, middle:]
 
 
+def half_to_give(left, first_right, second_right):
+    first = lax.axis_index("section") == 0
+    return outer(left, jnp.where(first, second_right, first_right)).astype(HALF)
+
+
+def half_to_keep(left, first_right, second_right, given):
+    first = lax.axis_index("section") == 0
+    keep = outer(left, jnp.where(first, first_right, second_right))
+    return (keep + swapped(given).astype(FLOAT)).astype(HALF)
+
+
 def section_half(left, first_right, second_right):
-    first = lax.axis_index("section") == 0
-    give = outer(left, jnp.where(first, second_right, first_right)).astype(HALF)
-    keep = outer(left, jnp.where(first, first_right, second_right))
-    return (keep + swapped(give).astype(FLOAT)).astype(HALF)
+    given = half_to_give(left, first_right, second_right)
+    return half_to_keep(left, first_right, second_right, given)
 
 
 def row_share(values):
@@ -834,9 +780,34 @@
     inner = gate_norm.shape[1]
     state = conv_state.shape[2]
     wide = -(-inner // LANES) * LANES
+    layers = range(2)
 
     def pair(own, other):
         return (jnp.where(first, own, other), jnp.where(first, other, own))
+
+    tokens_now = lax.dynamic_index_in_dim(tokens, section_now, 0, keepdims=False)
+    grad_now = lax.dynamic_index_in_dim(cotangent, section_now, 0, keepdims=False)
+    wide_tokens = joined(spread(tokens_now.astype(HALF)))
+
+    halves = (
+        jnp.concatenate([widened(proj_gate[0], wide), proj_state[0]], axis=1),
+        jnp.concatenate([widened(proj_input[0], wide), widened(proj_step[0], state)], axis=1),
+    )
+    keep, give = jnp.where(first, *halves), jnp.where(first, *halves[::-1])
+    mine = pair(keep, swapped(give))
+    mine = [lax.all_gather(half, "row", axis=0, tiled=True) for half in mine]
+    proj = [pair(half, swapped(half)) for half in mine]
+
+    def both_layers(weight):
+        whole = lax.all_gather(weight, ("section", "row"), axis=0, tiled=True)
+        return whole.reshape(2, n_row * weight.shape[0], weight.shape[1])
+
+    proj_out = both_layers(widened(proj_output[0], wide))
+    gate_all = lax.all_gather(expert_gate[0, 0], "section")
+    up_all = lax.all_gather(expert_up[0, 0], "section")
+    down_all = lax.all_gather(expert_down[0, 0], "section")
+    shared = both_layers(jnp.concatenate([shared_gate[0], shared_up[0], shared_down[0]], axis=1))
+    experts = [(gate_all[s], up_all[s], down_all[s]) for s in layers]
 
     small_in = (
         norm_in[0],
@@ -848,38 +819,13 @@
     )
     vector = flat(small_in)
     small_all = [unflat(part, [v.shape for v in small_in]) for part in pair(vector, swapped(vector))]
-
-    def both_layers(weight):
-        whole = lax.all_gather(weight, ("section", "row"), axis=0, tiled=True)
-        return whole.reshape(2, n_row * weight.shape[0], weight.shape[1])
-
-    proj = both_layers(
-        jnp.concatenate(
-            [
-                widened(proj_gate[0], wide),
-                widened(proj_input[0], wide),
-                proj_state[0],
-                widened(proj_step[0], LANES),
-            ],
-            axis=1,
-        )
-    )
-    proj_out = both_layers(widened(proj_output[0], wide))
-    gate_all = lax.all_gather(expert_gate[0, 0], "section")
-    up_all = lax.all_gather(expert_up[0, 0], "section")
-    down_all = lax.all_gather(expert_down[0, 0], "section")
-    shared = both_layers(jnp.concatenate([shared_gate[0], shared_up[0], shared_down[0]], axis=1))
-    dense = [
-        (proj[s], proj_out[s], shared[s], gate_all[s], up_all[s], down_all[s]) for s in range(2)
-    ]
+    norm_ins = [part[0] for part in small_all]
+    norm_mids = [part[1] for part in small_all]
 
     meta = jnp.concatenate([routes.astype(FLOAT), gates], axis=3)[0]
     keep = lax.dynamic_index_in_dim(meta, section_now, 0, keepdims=False)
     give = lax.dynamic_index_in_dim(meta, 1 - section_now, 0, keepdims=False)
     meta = jnp.concatenate(pair(keep, swapped(give)), axis=1)
-
-    def tables_once(scaled):
-        return route_tables(spread(after(meta, scaled)), top, capacity, 2)
 
     lengths = lax.dynamic_slice(
         doc_lengths, (section_now, row_now, 0), (1, 1, doc_lengths.shape[2])
@@ -893,76 +839,200 @@
     label_row = labels.astype(FLOAT)[None]
     place = turn()
     mixers = [
-        (conv_in, conv_st, step_row, wide_row, marks, label_row, place, heads)
+        (conv_in, conv_st, step_row, wide_row, marks, label_row, place)
         for _, _, conv_in, conv_st, step_row, wide_row in small_all
     ]
-    params = [part[:2] for part in small_all]
-
-    resid = lax.dynamic_index_in_dim(tokens, section_now, 0, keepdims=False)
-    grad = lax.dynamic_index_in_dim(cotangent, section_now, 0, keepdims=False)
-    outputs, stored = [], []
-    tables = tables_once
-    for s in range(2):
-        resid, saved, tables = layer_forward(
-            resid, params[s], dense[s], mixers[s], tables if s == 0 else both_tables[1:]
+
+    def mix_in(s, wide_in):
+        pre = [project(wide_in, half) for half in proj[s]]
+        return pre, *mixer_forward(pre, heads, wide, mixers[s])
+
+    def mix_out(s, resid, scaled, total_part):
+        mixed, _ = line_shares([scaled], [proj_out[s]])
+        total = gathered_sum([block_of(total_part, back) for back in range(groups())])
+        rr = lax.rsqrt(total / DI + EPS)
+        return resid + mixed * rr, mixed, rr
+
+    wide_in_0 = rms_norm(wide_tokens.astype(FLOAT), norm_ins[0]).astype(HALF)
+    pre_0, y_0, scaled_0, total_0 = mix_in(0, wide_in_0)
+    grad_blocks = spread(after(grad_now.astype(HALF), wide_in_0))
+    tables = route_tables(spread(after(meta, scaled_0)), top, capacity, 2)
+    plain = [[table[0] for table in tables[s]] for s in layers]
+    scaling = [[table[1] for table in tables[s]] for s in layers]
+    middle_0, mixed_0, rr_0 = mix_out(0, tokens_now, scaled_0, total_0)
+    kept_0, kept_s_0 = {}, {}
+
+    def expert_0(index, rows):
+        kept_0[index], answer = expert_forward(rows, experts[0])
+        return answer
+
+    def beside_0(index, block, result):
+        kept_s_0[index] = shared_forward(block, shared[0])
+        return home_part(scaling[0][index], result, kept_s_0[index][2], shared[0])
+
+    parts, rows_0, mids_0 = through_experts(
+        rms_norm(middle_0, norm_mids[0]).astype(HALF), plain[0], expert_0, beside_0
+    )
+    out_0 = middle_0 + gathered_sum(parts)
+
+    wide_in_1 = joined(spread(rms_norm(out_0, norm_ins[1]).astype(HALF)))
+    grad_tokens = [joined([grad_blocks[back] for back in chunk]) for chunk in chunks()]
+    grad_rows_1 = [
+        to_experts(project(table, after(block, out_0)))
+        for table, block in zip(scaling[1], grad_tokens)
+    ]
+    pre_1, y_1, scaled_1, total_1 = mix_in(1, wide_in_1)
+    scaled_1 = after(scaled_1, *grad_rows_1)
+    middle_1, mixed_1, rr_1 = mix_out(1, out_0, scaled_1, total_1)
+
+    kept_1, kept_s_1, grads_1, grads_s_1, answers_1 = {}, {}, {}, {}, {}
+
+    def expert_1(index, rows):
+        kept_1[index], answers_1[index] = expert_forward(rows, experts[1])
+        grads_1[index], back = expert_backward(grad_rows_1[index], kept_1[index], experts[1])
+        return back
+
+    def beside_1(index, block, result):
+        kept_s_1[index] = shared_forward(block, shared[1])
+        grads_s_1[index], part = shared_backward(grad_tokens[index], kept_s_1[index], shared[1])
+        return (part + outer(plain[1][index], result)).astype(HALF)
+
+    parts, rows_1, mids_1 = through_experts(
+        rms_norm(middle_1, norm_mids[1]).astype(HALF), plain[1], expert_1, beside_1
+    )
+    order = range(len(chunks()))
+    answers = [to_experts(after(answers_1[index], parts[-1])) for index in order]
+
+    def listed(kept):
+        return [kept[index] for index in order]
+
+    def mixer_back(s, grad_middle, along, rr, saved, weight_grads, last):
+        wide_in, pre, y, scaled = saved
+        wide_mix = joined(spread(grad_middle.astype(HALF)))
+        sides = joined(spread(jnp.concatenate([rr, along], axis=1)))
+        wide_mix = after(wide_mix, weight_grads)
+        grad_scaled = project(wide_mix, proj_out[s])
+        *grad_pre, wide_grads, grad_conv_input, grad_conv_state, step_grads = mixer_backward(
+            pre, y, grad_scaled, sides, heads, mixers[s]
         )
-        outputs.append(resid)
-        stored.append(saved)
-        if s == 0:
-            both_tables = tables
+        ends = [part[:, :wide] for part in grad_pre]
+        if last:
+            given = half_to_give(wide_in, *ends)
+            grad_in, whole = line_shares([after(part, given) for part in grad_pre], proj[s])
+        else:
+            grad_in, whole = line_shares(grad_pre, proj[s])
+            given = half_to_give(after(wide_in, whole), *ends)
+        grad_proj = half_to_keep(after(wide_in, whole), *ends, given)
+        mix_rr = (after(wide_mix, grad_proj) * sides[:, :1]).astype(HALF)
+        grad_proj_out = section_half(mix_rr, *two_halves(scaled))
+        tail = jnp.concatenate([grad_pre[0][:, wide:], grad_pre[1][:, wide : wide + LANES]], axis=1)
+        grad_tail = outer(after(wide_in, grad_proj), tail).astype(HALF)
+        rest = (grad_conv_state, grad_conv_input, wide_grads, step_grads)
+        return wide_mix, grad_in, grad_proj, grad_proj_out, grad_tail, rest
+
+    def resid_back(resid, norm, grad_normed, grad_middle):
+        _, pull_in = jax.vjp(rms_norm, resid, norm)
+        grad_resid, grad_norm = pull_in(grad_normed)
+        return grad_resid + grad_middle, grad_norm
+
+    def row_sums(value):
+        return lax.psum_scatter(value, "row", scatter_dimension=0, tiled=True)
 
     def own_layer(first_value, second_value):
         keep = jnp.where(first, first_value, second_value)
         give = jnp.where(first, second_value, first_value).astype(HALF)
         return keep.astype(FLOAT) + swapped(give).astype(FLOAT)
 
-    def row_sums(value):
-        return lax.psum_scatter(value, "row", scatter_dimension=0, tiled=True)
+    grad_middle, along, grad_norm_mid_1 = middle_backward(
+        gathered_sum(parts), grad_now, middle_1, mixed_1, norm_mids[1]
+    )
+    expert_grads_1, shared_grads_1 = weight_sums(
+        rows_1,
+        grad_rows_1,
+        listed(kept_1),
+        listed(grads_1),
+        mids_1,
+        grad_tokens,
+        listed(kept_s_1),
+        listed(grads_s_1),
+    )
+    expert_grads_1 = [grad.astype(HALF) for grad in expert_grads_1]
+    wide_mix, grad_in, grad_proj_1, grad_out_1, grad_tail_1, rest_1 = mixer_back(
+        1,
+        grad_middle,
+        along,
+        rr_1,
+        (wide_in_1, pre_1, y_1, scaled_1),
+        (expert_grads_1, shared_grads_1),
+        False,
+    )
+    grad_1, grad_norm_in_1 = resid_back(out_0, norm_ins[1], grad_in, grad_middle)
+    home = [
+        home_part(scaling[1][index], answers[index], kept_s_1[index][2], shared[1])
+        for index in order
+    ]
+    home = [after(part, wide_mix) for part in home]
+    out_1 = middle_1 + gathered_sum(to_blocks(home))
+    sums_1 = [row_sums(value) for value in (*shared_grads_1, grad_out_1, grad_proj_1)]
+
+    grads_0, grads_s_0 = {}, {}
+
+    def expert_back_0(index, rows):
+        grads_0[index], back = expert_backward(rows, kept_0[index], experts[0])
+        return back
+
+    def beside_back_0(index, block, result):
+        grads_s_0[index], part = shared_backward(block, kept_s_0[index], shared[0])
+        return (part + outer(plain[0][index], result)).astype(HALF)
+
+    parts, grad_rows_0, grad_tokens_0 = through_experts(
+        grad_1.astype(HALF), scaling[0], expert_back_0, beside_back_0
+    )
+    grad_middle, along, grad_norm_mid_0 = middle_backward(
+        gathered_sum(parts), grad_1, middle_0, mixed_0, norm_mids[0]
+    )
+    expert_grads_0, shared_grads_0 = weight_sums(
+        rows_0,
+        grad_rows_0,
+        listed(kept_0),
+        listed(grads_0),
+        mids_0,
+        grad_tokens_0,
+        listed(kept_s_0),
+        listed(grads_s_0),
+    )
+    expert_out = [
+        own_layer(a.astype(HALF), b) for a, b in zip(expert_grads_0, expert_grads_1)
+    ]
+    sums_0 = [row_sums(value) for value in shared_grads_0]
+    wide_mix, grad_in, grad_proj_0, grad_out_0, grad_tail_0, rest_0 = mixer_back(
+        0,
+        grad_middle,
+        along,
+        rr_0,
+        (wide_in_0, pre_0, y_0, scaled_0),
+        (expert_out, shared_grads_0),
+        True,
+    )
+    grad_0, grad_norm_in_0 = resid_back(tokens_now, norm_ins[0], grad_in, grad_middle)
+    sums_0 = [*sums_0, row_sums(grad_out_0), row_share(grad_proj_0)]
 
     def own_halves(first_value, second_value):
         keep = jnp.where(first, first_value, second_value)
         give = jnp.where(first, second_value, first_value)
         return pair(keep, swapped(give))
 
-    held = {}
-
-    def keep_first(expert_grads):
-        held["experts"] = [grad.astype(HALF) for grad in expert_grads]
-        return held["experts"]
-
-    def settle(expert_grads):
-        return [
-            own_layer(a.astype(HALF), b).astype(FLOAT)
-            for a, b in zip(expert_grads, held["experts"])
-        ]
-
-    grads = [None, None]
-    backs = [None, None]
-    sums = [None, None]
-    tails = [None, None]
-    for s in (1, 0):
-        grad, small, (grad_proj, *others), tails[s], expert_out = layer_backward(
-            grad,
-            stored[s],
-            params[s],
-            dense[s],
-            mixers[s],
-            both_tables[s],
-            keep_first if s else settle,
-        )
-        backs[s] = grad
-        grads[s] = small
-        sums[s] = [
-            row_sums(grad_proj) if s else row_share(grad_proj),
-            *[row_sums(value) for value in others],
-        ]
-    tail = row_share(own_layer(tails[0], tails[1]).astype(HALF))
+    tail = row_share(own_layer(grad_tail_0, grad_tail_1).astype(HALF))
     state_grad = col_sum(tail[:, :state])
-    grad_gates, grad_out, grad_shared, grad_down = [own_halves(a, b) for a, b in zip(*sums)]
+    grad_shared, grad_down, grad_out, grad_ends = [own_halves(a, b) for a, b in zip(sums_0, sums_1)]
     grad_out, grad_down = [jnp.concatenate(both, axis=1) for both in (grad_out, grad_down)]
 
-    shapes = [part.shape for part in grads[0]]
-    vector = own_layer(flat(grads[0]), flat(grads[1]))
+    smalls = (
+        (grad_norm_in_0, grad_norm_mid_0, *rest_0),
+        (grad_norm_in_1, grad_norm_mid_1, *rest_1),
+    )
+    shapes = [part.shape for part in smalls[0]]
+    vector = own_layer(flat(smalls[0]), flat(smalls[1]))
     lines = [shifted(vector[None], "row", back) for back in range(n_row)]
     vector = jnp.sum(in_order(lines, "row"), axis=0)
     common = 2 * width + conv_state.shape[1] * state
@@ -989,11 +1059,11 @@
         return value.astype(FLOAT)[None]
 
     return (
-        per_micro(outputs[0], outputs[1]),
-        per_micro(backs[0], backs[1]),
+        per_micro(out_0, out_1),
+        per_micro(grad_0, grad_1),
         out_norm_in[None],
-        out(grad_gates[0][:, :inner]),
-        out(grad_gates[1][:, :inner]),
+        out(grad_ends[0][:, :inner]),
+        out(grad_ends[1][:, :inner]),
         out(state_grad),
         out(tail[:, state : state + heads]),
         out_step[:1, :heads],

time: 1270 us -> 1260 us (level)
  matrix products: 375 us -> 317 us
  other arithmetic: 55.4 us -> 79.4 us
  waiting for transfers between devices: 440 us -> 460 us
    dot_general x52 -> x42, matrix products: 137 us -> 89.3 us  [project_back(): lax.dot_general(left, right, (((1,), (1,)), ((), ())), preferred_element_...]
    all_to_all x24, waiting for transfers between devices: 115 us -> 74.3 us  [to_experts(): lax.all_to_all(rows.astype(HALF), 'row', split_axis=0, concat_axis=0, til...]
    all_gather x0 -> x2, waiting for transfers between devices: none -> 35.6 us  [shards(): mine = [lax.all_gather(half, 'row', axis=0, tiled=True) for half in mine]]
    all_gather x3 -> x2, waiting for transfers between devices: 15.5 us -> 50.6 us  [both_layers(): whole = lax.all_gather(weight, ('section', 'row'), axis=0, tiled=True)]
    dot_general x55 -> x57, matrix products: 132 us -> 130 us  [project(): return jnp.dot(left, right, preferred_element_type=FLOAT)]
    unnamed x522 -> x600, local copies, waits for them, and re-layouts: 26 us -> 28.2 us
  transfers between devices with their start and end apart: 139 -> 143, of which waited for: 58 -> 67; matrix products, arithmetic and copies ran while one was open for 35% -> 33% of each run, Pallas kernels for 4% -> 5%
where the time goes in v4:
time: 1260 us; the launch traced here: 1250 us
  waiting for transfers between devices  460 us (37%)
  matrix products  317 us (25%)
  starting transfers between devices  259 us (21%)
  other arithmetic  79.4 us (6%)
  Pallas kernels  61 us (5%)
  local copies, waits for them, and re-layouts  51.5 us (4%)
  between operations  18.3 us (1%)
    ppermute x81, waiting for transfers between devices, shifted(): lax.ppermute(block, axis, [(i, (i + distance) % count) for i in range(cou...  291 us
    ppermute x81, starting transfers between devices, shifted(): lax.ppermute(block, axis, [(i, (i + distance) % count) for i in range(cou...  156 us
    dot_general x57, matrix products, project(): return jnp.dot(left, right, preferred_element_type=FLOAT)  130 us
    dot_general x36, matrix products, outer(): lax.dot_general(left, right, (((0,), (0,)), ((), ())), preferred_element_...  98 us
    all_to_all x24, starting transfers between devices, to_experts(): lax.all_to_all(rows.astype(HALF), 'row', split_axis=0, concat_axis=0, til...  96.1 us
    dot_general x42, matrix products, project_back(): lax.dot_general(left, right, (((1,), (1,)), ((), ())), preferred_element_...  89.3 us
    all_to_all x24, waiting for transfers between devices, to_experts(): lax.all_to_all(rows.astype(HALF), 'row', split_axis=0, concat_axis=0, til...  74.3 us
    all_gather x2, waiting for transfers between devices, both_layers(): whole = lax.all_gather(weight, ('section', 'row'), axis=0, tiled=True)  50.6 us
  transfers between devices with their start and end apart: 143, of which 67 were waited for; matrix products, arithmetic and copies ran while one was open for 33% of the time, Pallas kernels for 5%

profile of v4, /device:TPU:0, one launch (start us, length us, event | category | flops | bytes accessed | tf_op | source)
XLA Modules:
  0.0 1245.6 jit_solution(18335512650582347677)
XLA Ops:
  27.5 33.1 %all-gather.12.cloned.1.call-done = bf16[1536,1024]{1,0:T(8,128)(2,1)} async-done(((bf16[384,1024]{1,0:T(8,128)(2,1)}), bf16[1536,1024]{1,0:T(8,128)(2,1)}) %all-gather.12.cloned.1.call-update) | async-done | bytes 3145744 | tf_op jit(solution)/shard_map/all_gather | solution.py:798
  70.5 8.4 collective-permute-done.26
  87.2 16.5 %collective-permute-done.28 = bf16[128,1536]{1,0:T(8,128)(2,1)S(1)} collective-permute-done((bf16[128,1536]{1,0:T(8,128)(2,1)S(1)}, bf16[128,1536]{1,0:T(8,128)(2,1)S(1)}, u32[]{:S(2)}, u32[]{:S(2)}) %collective-permute-start.28) | collective-permute-done | bytes 393248 | tf_op jit(solution)/shard_map/ppermute | solution.py:26
  107.0 41.4 %all-gather.14.cloned.1.call-done = bf16[3072,768]{1,0:T(8,128)(2,1)} async-done(((bf16[384,768]{1,0:T(8,128)(2,1)}), bf16[3072,768]{1,0:T(8,128)(2,1)}) %all-gather.14.cloned.1.call-update) | async-done | bytes 4718608 | tf_op jit(solution)/shard_map/all_gather | solution.py:802
  161.0 12.4 mixer_forward.2
  180.0 9.1 all-gather.18.cloned.1.call-done
  212.5 15.5 %collective-permute-done.7 = bf16[128,1536]{1,0:T(8,128)(2,1)S(1)} collective-permute-done((bf16[128,1536]{1,0:T(8,128)(2,1)}, bf16[128,1536]{1,0:T(8,128)(2,1)S(1)}, u32[]{:S(2)}, u32[]{:S(2)}) %collective-permute-start.7) | collective-permute-done | bytes 393248 | tf_op jit(solution)/shard_map/ppermute | solution.py:26
  240.4 8.7 collective-permute-start.15
  289.9 14.2 %collective-permute-done.18 = bf16[128,1536]{1,0:T(8,128)(2,1)S(1)} collective-permute-done((bf16[128,1536]{1,0:T(8,128)(2,1)}, bf16[128,1536]{1,0:T(8,128)(2,1)S(1)}, u32[]{:S(2)}, u32[]{:S(2)}) %collective-permute-start.18) | collective-permute-done | bytes 393248 | tf_op jit(solution)/shard_map/ppermute | solution.py:26
  352.6 9.3 all-to-all-done.3
  380.8 7.5 collective-permute-done.19
  410.8 20.6 %collective-permute-done.23 = bf16[128,1536]{1,0:T(8,128)(2,1)} collective-permute-done((bf16[128,1536]{1,0:T(8,128)(2,1)S(1)}, bf16[128,1536]{1,0:T(8,128)(2,1)}, u32[]{:S(2)}, u32[]{:S(2)}) %collective-permute-start.23) | collective-permute-done | bytes 393248 | tf_op jit(solution)/shard_map/ppermute | solution.py:26
  445.8 12.0 mixer_forward.3
  485.0 13.4 %collective-permute-done.30 = bf16[128,1536]{1,0:T(8,128)(2,1)S(1)} collective-permute-done((bf16[128,1536]{1,0:T(8,128)(2,1)S(1)}, bf16[128,1536]{1,0:T(8,128)(2,1)S(1)}, u32[]{:S(2)}, u32[]{:S(2)}) %collective-permute-start.30) | collective-permute-done | bytes 393248 | tf_op jit(solution)/shard_map/ppermute | solution.py:26
  500.6 8.9 collective-permute-start.35
  663.6 8.2 collective-permute-done.38
  708.9 12.9 %collective-permute-done.42 = bf16[128,1536]{1,0:T(8,128)(2,1)} collective-permute-done((bf16[128,1536]{1,0:T(8,128)(2,1)}, bf16[128,1536]{1,0:T(8,128)(2,1)}, u32[]{:S(2)}, u32[]{:S(2)}) %collective-permute-start.42) | collective-permute-done | bytes 393248 | tf_op jit(solution)/shard_map/ppermute | solution.py:26
  728.0 18.2 %mixer_backward.2 = (bf16[512,1024]{1,0:T(8,128)(2,1)S(1)}, bf16[512,1024]{1,0:T(8,128)(2,1)S(1)}, f32[2,768]{1,0:T(2,128)S(1)}, f32[4,768]{1,0:T(4,128)S(1)}, f...) custom-call(f32[512,1024]{1,0:T(8,128)} %copy-done.3, f32[512,1024]{1,0:T(8,128)} %fusion.52.pre_other_in_ref, ...), custom_call_target="tpu_custom_call" | custom-call | tf_op jit(solution)/shard_map/mixer_backward/pallas_call | solution.py:542
  770.7 15.8 %collective-permute-done.46 = bf16[128,1536]{1,0:T(8,128)(2,1)S(1)} collective-permute-done((bf16[128,1536]{1,0:T(8,128)(2,1)S(1)}, bf16[128,1536]{1,0:T(8,128)(2,1)S(1)}, u32[]{:S(2)}, u32[]{:S(2)}) %collective-permute-start.46) | collective-permute-done | bytes 393248 | tf_op jit(solution)/shard_map/ppermute | solution.py:26
  788.0 14.7 %collective-permute-done.54 = bf16[128,1536]{1,0:T(8,128)(2,1)S(1)} collective-permute-done((bf16[128,1536]{1,0:T(8,128)(2,1)S(1)}, bf16[128,1536]{1,0:T(8,128)(2,1)S(1)}, u32[]{:S(2)}, u32[]{:S(2)}) %collective-permute-start.54) | collective-permute-done | bytes 393248 | tf_op jit(solution)/shard_map/ppermute | solution.py:26
  806.2 7.7 collective-permute-start.56
  852.7 7.9 collective-permute-done.58
  950.9 7.4 all-to-all-done.23
  996.5 9.3 collective-permute-done.60
  1005.8 7.7 collective-permute-done.59
  1032.5 13.0 %collective-permute-done.72 = f32[128,2]{0,1:T(2,128)S(1)} collective-permute-done((f32[128,2]{0,1:T(2,128)S(1)}, f32[128,2]{0,1:T(2,128)S(1)}, u32[]{:S(2)}, u32[]{:S(2)}) %collective-permute-start.72) | collective-permute-done | bytes 1056 | tf_op jit(solution)/shard_map/ppermute | solution.py:26
  1045.4 9.0 collective-permute-start.70
  1063.6 18.5 %mixer_backward.3 = (bf16[512,1024]{1,0:T(8,128)(2,1)S(1)}, bf16[512,1024]{1,0:T(8,128)(2,1)S(1)}, f32[2,768]{1,0:T(2,128)S(1)}, f32[4,768]{1,0:T(4,128)S(1)}, f...) custom-call(f32[512,1024]{1,0:T(8,128)} %copy-done.2, f32[512,1024]{1,0:T(8,128)} %fusion.49.pre_other_in_ref, ...), custom_call_target="tpu_custom_call" | custom-call | tf_op jit(solution)/shard_map/mixer_backward/pallas_call | solution.py:542
  1105.9 15.9 %collective-permute-done.74 = bf16[128,1536]{1,0:T(8,128)(2,1)} collective-permute-done((bf16[128,1536]{1,0:T(8,128)(2,1)}, bf16[128,1536]{1,0:T(8,128)(2,1)}, u32[]{:S(2)}, u32[]{:S(2)}) %collective-permute-start.74) | collective-permute-done | bytes 393248 | tf_op jit(solution)/shard_map/ppermute | solution.py:26
  1134.0 8.5 collective-permute-start.81
  1179.4 7.1 collective-permute-done.87
  1192.4 11.1 collective-permute-done.85
  (1191 shorter events, 803.5 us)
Async XLA Ops:
  7.2 53.4 %all-gather.12.cloned.1.call-start = ((), (), s32[]{:S(2)}) async-start(), calls=%async_computation.31 | async-start | bytes 3932160 | tf_op jit(solution)/shard_map/all_gather | solution.py:798
  13.9 93.2 %all-gather.16.cloned.1.call-start = ((), (), s32[]{:S(2)}) async-start(), calls=%async_computation.33 | async-start | bytes 3932160 | tf_op jit(solution)/shard_map/all_gather | solution.py:798
  14.6 133.8 %all-gather.14.cloned.1.call-start = ((), (), s32[]{:S(2)}) async-start(), calls=%async_computation.32 | async-start | bytes 5308416 | tf_op jit(solution)/shard_map/all_gather | solution.py:802
  15.6 173.6 %all-gather.18.cloned.1.call-start = ((), (), s32[]{:S(2)}) async-start(), calls=%async_computation.41 | async-start | bytes 5308416 | tf_op jit(solution)/shard_map/all_gather | solution.py:802
  16.3 234.3 %all-gather.20.cloned.1.call-start = ((), (), s32[]{:S(2)}) async-start(), calls=%async_computation.42 | async-start | bytes 4718592 | tf_op jit(solution)/shard_map/all_gather | solution.py:806
  16.9 236.0 %all-gather.22.cloned.1.call-start = ((), (), s32[]{:S(2)}) async-start(), calls=%async_computation.43 | async-start | bytes 4718592 | tf_op jit(solution)/shard_map/all_gather | solution.py:807
  17.4 238.4 %all-gather.24.cloned.1.call-start = ((), (), s32[]{:S(2)}) async-start(), calls=%async_computation.44 | async-start | bytes 4718592 | tf_op jit(solution)/shard_map/all_gather | solution.py:808
  17.6 43.3 %collective-permute-start.2 = (bf16[128,1536]{1,0:T(8,128)(2,1)S(1)}, bf16[128,1536]{1,0:T(8,128)(2,1)S(1)}, u32[]{:S(2)}, u32[]{:S(2)}) collective-permute-start(bf16[128,1536]{1,0:T(8,128)(2,1)S(1)} %bitcast_convert_fusion.1), channel_id=1, source_target_pairs={{0,3},{1,0},{2,1},{3,2},{4,7},{5,4},{6,5},{7,6},{8,11},{9,8},{10,9... | collective-permute-start | bytes 1179656 | tf_op jit(solution)/shard_map/ppermute | solution.py:26
  22.6 38.3 %collective-permute-start.1 = (bf16[128,1536]{1,0:T(8,128)(2,1)S(1)}, bf16[128,1536]{1,0:T(8,128)(2,1)}, u32[]{:S(2)}, u32[]{:S(2)}) collective-permute-start(bf16[128,1536]{1,0:T(8,128)(2,1)S(1)} %bitcast_convert_fusion.1), channel_id=1, source_target_pairs={{0,2},{1,3},{2,0},{3,1},{4,6},{5,7},{6,4},{7,5},{8,10},{9,11},{10,... | collective-permute-start | bytes 1179656 | tf_op jit(solution)/shard_map/ppermute | solution.py:26
  22.6 38.3 %collective-permute-start = (bf16[128,1536]{1,0:T(8,128)(2,1)S(1)}, bf16[128,1536]{1,0:T(8,128)(2,1)}, u32[]{:S(2)}, u32[]{:S(2)}) collective-permute-start(bf16[128,1536]{1,0:T(8,128)(2,1)S(1)} %bitcast_convert_fusion.1), channel_id=1, source_target_pairs={{0,1},{1,2},{2,3},{3,0},{4,5},{5,6},{6,7},{7,4},{8,9},{9,10},{10,1... | collective-permute-start | bytes 1179656 | tf_op jit(solution)/shard_map/ppermute | solution.py:26
  60.6 89.9 %collective-permute-start.5 = (bf16[1536,1024]{1,0:T(8,128)(2,1)}, bf16[1536,1024]{1,0:T(8,128)(2,1)}, u32[]{:S(2)}, u32[]{:S(2)}) collective-permute-start(bf16[1536,1024]{1,0:T(8,128)(2,1)} %all-gather.12.cloned.1.call-done), channel_id=1, source_target_pairs={{0,16},{16,0},{1,17},{17,1},{2,18},{18,2},{3,19},{19,3},{4,20},{20... | collective-permute-start | bytes 9437192 | tf_op jit(solution)/shard_map/ppermute | solution.py:30
  107.0 303.7 %collective-permute-start.25 = (bf16[1536,1024]{1,0:T(8,128)(2,1)}, bf16[1536,1024]{1,0:T(8,128)(2,1)}, u32[]{:S(2)}, u32[]{:S(2)}) collective-permute-start(bf16[1536,1024]{1,0:T(8,128)(2,1)} %all-gather.16.cloned.1.call-done), channel_id=1, source_target_pairs={{0,16},{16,0},{1,17},{17,1},{2,18},{18,2},{3,19},{19,3},{4,20},{20... | collective-permute-start | bytes 9437192 | tf_op jit(solution)/shard_map/ppermute | solution.py:30
  569.4 110.9 %collective-permute-start.44 = (bf16[1536,256]{1,0:T(8,128)(2,1)}, bf16[1536,256]{1,0:T(8,128)(2,1)}, u32[]{:S(2)}, u32[]{:S(2)}) collective-permute-start(bf16[1536,256]{1,0:T(8,128)(2,1)} %convolution_convert_fusion.22), channel_id=1, source_target_pairs={{0,16},{16,0},{1,17},{17,1},{2,18},{18,2},{3,19},{19,3},{4,20},{20... | collective-permute-start | bytes 2359304 | tf_op jit(solution)/shard_map/ppermute | solution.py:30
  606.7 388.6 %reduce-scatter.20.cloned.1.call-start = ((), (), s32[]{:S(2)}) async-start(), calls=%async_computation.40 | async-start | bytes 491520 | tf_op jit(solution)/shard_map/reduce_scatter | solution.py:939
  701.5 51.6 %all-to-all-start.16 = ((bf16[4,128,1536]{2,1,0:T(8,128)(2,1)}), bf16[4,128,1536]{2,1,0:T(8,128)(2,1)}, u32[]{:S(2)}, u32[]{:S(2)}) async-start(bf16[4,128,1536]{2,1,0:T(8,128)(2,1)} %bitcast.456), calls=%async_computation.16 | async-start | bytes 3145728 | tf_op jit(solution)/shard_map/all_to_all | solution.py:140
  760.9 41.8 %collective-permute-start.54 = (bf16[128,1536]{1,0:T(8,128)(2,1)S(1)}, bf16[128,1536]{1,0:T(8,128)(2,1)S(1)}, u32[]{:S(2)}, u32[]{:S(2)}) collective-permute-start(bf16[128,1536]{1,0:T(8,128)(2,1)S(1)} %get-tuple-element.304), channel_id=1, source_target_pairs={{0,2},{1,3},{2,0},{3,1},{4,6},{5,7},{6,4},{7,5},{8,10},{9,11},{10,... | collective-permute-start | bytes 1179656 | tf_op jit(solution)/shard_map/ppermute | solution.py:26
  761.5 41.2 %collective-permute-start.53 = (bf16[128,1536]{1,0:T(8,128)(2,1)S(1)}, bf16[128,1536]{1,0:T(8,128)(2,1)S(1)}, u32[]{:S(2)}, u32[]{:S(2)}) collective-permute-start(bf16[128,1536]{1,0:T(8,128)(2,1)S(1)} %get-tuple-element.302), channel_id=1, source_target_pairs={{0,3},{1,0},{2,1},{3,2},{4,7},{5,4},{6,5},{7,6},{8,11},{9,8},{10,9... | collective-permute-start | bytes 1179656 | tf_op jit(solution)/shard_map/ppermute | solution.py:26
  839.7 155.6 %reduce-scatter.18.cloned.1.call-start = ((), (), s32[]{:S(2)}) async-start(), calls=%async_computation.39 | async-start | bytes 491520 | tf_op jit(solution)/shard_map/reduce_scatter | solution.py:939
  867.3 189.6 %reduce-scatter.16.cloned.1.call-start = ((), (), s32[]{:S(2)}) async-start(), calls=%async_computation.38 | async-start | bytes 983040 | tf_op jit(solution)/shard_map/reduce_scatter | solution.py:939
  870.0 186.9 %reduce-scatter.14.cloned.1.call-start = ((), (), s32[]{:S(2)}) async-start(), calls=%async_computation.37 | async-start | bytes 983040 | tf_op jit(solution)/shard_map/reduce_scatter | solution.py:939
  893.7 295.0 %reduce-scatter.8.cloned.1.call-start = ((), (), s32[]{:S(2)}) async-start(), calls=%async_computation.34 | async-start | bytes 2949120 | tf_op jit(solution)/shard_map/reduce_scatter | solution.py:939
  905.3 82.8 %collective-permute-start.101 = (bf16[1536,384]{1,0:T(8,128)(2,1)}, bf16[1536,384]{1,0:T(8,128)(2,1)}, u32[]{:S(2)}, u32[]{:S(2)}) collective-permute-start(bf16[1536,384]{1,0:T(8,128)(2,1)} %convolution_convert_fusion.14), channel_id=1, source_target_pairs={{0,16},{16,0},{1,17},{17,1},{2,18},{18,2},{3,19},{19,3},{4,20},{20... | collective-permute-start | bytes 3538952 | tf_op jit(solution)/shard_map/ppermute | solution.py:30
  962.8 271.3 %reduce-scatter.12.cloned.1.call-start = ((), (), s32[]{:S(2)}) async-start(), calls=%async_computation.36 | async-start | bytes 1474560 | tf_op jit(solution)/shard_map/reduce_scatter | solution.py:939
  969.2 50.6 %collective-permute-start.65 = (bf16[1536,512]{1,0:T(8,128)(2,1)}, bf16[1536,512]{1,0:T(8,128)(2,1)}, u32[]{:S(2)}, u32[]{:S(2)}) collective-permute-start(bf16[1536,512]{1,0:T(8,128)(2,1)} %get-tuple-element.421), channel_id=1, source_target_pairs={{0,16},{16,0},{1,17},{17,1},{2,18},{18,2},{3,19},{19,3},{4,20},{20... | collective-permute-start | bytes 4718600 | tf_op jit(solution)/shard_map/ppermute | solution.py:30
  969.3 55.6 %collective-permute-start.66 = (bf16[1536,512]{1,0:T(8,128)(2,1)}, bf16[1536,512]{1,0:T(8,128)(2,1)}, u32[]{:S(2)}, u32[]{:S(2)}) collective-permute-start(bf16[1536,512]{1,0:T(8,128)(2,1)} %get-tuple-element.423), channel_id=1, source_target_pairs={{0,16},{16,0},{1,17},{17,1},{2,18},{18,2},{3,19},{19,3},{4,20},{20... | collective-permute-start | bytes 4718600 | tf_op jit(solution)/shard_map/ppermute | solution.py:30
  995.3 238.8 %reduce-scatter.10.cloned.1.call-start = ((), (), s32[]{:S(2)}) async-start(), calls=%async_computation.35 | async-start | bytes 1474560 | tf_op jit(solution)/shard_map/reduce_scatter | solution.py:939
  1017.5 41.0 %collective-permute-start.64 = (bf16[128,1536]{1,0:T(8,128)(2,1)S(1)}, bf16[128,1536]{1,0:T(8,128)(2,1)}, u32[]{:S(2)}, u32[]{:S(2)}) collective-permute-start(bf16[128,1536]{1,0:T(8,128)(2,1)S(1)} %convert_element_type.791), channel_id=1, source_target_pairs={{0,3},{1,0},{2,1},{3,2},{4,7},{5,4},{6,5},{7,6},{8,11},{9,8},{10,9... | collective-permute-start | bytes 1179656 | tf_op jit(solution)/shard_map/ppermute | solution.py:26
  1019.8 38.6 %collective-permute-start.63 = (bf16[128,1536]{1,0:T(8,128)(2,1)S(1)}, bf16[128,1536]{1,0:T(8,128)(2,1)}, u32[]{:S(2)}, u32[]{:S(2)}) collective-permute-start(bf16[128,1536]{1,0:T(8,128)(2,1)S(1)} %convert_element_type.791), channel_id=1, source_target_pairs={{0,2},{1,3},{2,0},{3,1},{4,6},{5,7},{6,4},{7,5},{8,10},{9,11},{10,... | collective-permute-start | bytes 1179656 | tf_op jit(solution)/shard_map/ppermute | solution.py:26
  1019.9 38.6 %collective-permute-start.62 = (bf16[128,1536]{1,0:T(8,128)(2,1)S(1)}, bf16[128,1536]{1,0:T(8,128)(2,1)}, u32[]{:S(2)}, u32[]{:S(2)}) collective-permute-start(bf16[128,1536]{1,0:T(8,128)(2,1)S(1)} %convert_element_type.791), channel_id=1, source_target_pairs={{0,1},{1,2},{2,3},{3,0},{4,5},{5,6},{6,7},{7,4},{8,9},{9,10},{10,1... | collective-permute-start | bytes 1179656 | tf_op jit(solution)/shard_map/ppermute | solution.py:26
  1056.7 38.8 %collective-permute-start.104 = (bf16[384,128]{1,0:T(8,128)(2,1)S(1)}, bf16[384,128]{1,0:T(8,128)(2,1)}, u32[]{:S(2)}, u32[]{:S(2)}) collective-permute-start(bf16[384,128]{1,0:T(8,128)(2,1)S(1)} %broadcast_select_fusion.27), channel_id=1, source_target_pairs={{0,16},{16,0},{1,17},{17,1},{2,18},{18,2},{3,19},{19,3},{4,20},{20... | collective-permute-start | bytes 294920 | tf_op jit(solution)/shard_map/ppermute | solution.py:30
  1057.9 39.4 %collective-permute-start.103 = (bf16[384,256]{1,0:T(8,128)(2,1)S(1)}, bf16[384,256]{1,0:T(8,128)(2,1)S(1)}, u32[]{:S(2)}, u32[]{:S(2)}) collective-permute-start(bf16[384,256]{1,0:T(8,128)(2,1)S(1)} %broadcast_select_fusion.25), channel_id=1, source_target_pairs={{0,16},{16,0},{1,17},{17,1},{2,18},{18,2},{3,19},{19,3},{4,20},{20... | collective-permute-start | bytes 589832 | tf_op jit(solution)/shard_map/ppermute | solution.py:30
  1098.2 52.2 %collective-permute-start.84 = (bf16[1536,768]{1,0:T(8,128)(2,1)}, bf16[1536,768]{1,0:T(8,128)(2,1)}, u32[]{:S(2)}, u32[]{:S(2)}) collective-permute-start(bf16[1536,768]{1,0:T(8,128)(2,1)} %convolution_convert_fusion.1), channel_id=1, source_target_pairs={{0,16},{16,0},{1,17},{17,1},{2,18},{18,2},{3,19},{19,3},{4,20},{20... | collective-permute-start | bytes 7077896 | tf_op jit(solution)/shard_map/ppermute | solution.py:30
  (395 other events, 5500.1 us)
Sparse Core Ops, SparseCore 0:
  14.0 46.5 all-gather.11
  63.0 43.9 all-gather.15
  109.5 38.9 all-gather.13
  150.2 38.9 all-gather.17
  190.5 12.1 all-gather.19
  204.1 13.2 all-gather.21
  219.0 13.2 all-gather.23
  610.3 32.6 reduce-scatter.19
  867.4 23.6 reduce-scatter.17
  893.8 40.6 reduce-scatter.15
  937.4 41.5 reduce-scatter.13
  981.9 36.4 reduce-scatter.7
  1021.3 28.5 reduce-scatter.11
  1174.3 45.4 reduce-scatter.9

commit v5 on v4

--- a/solution.py
+++ b/solution.py
@@ -68,14 +68,14 @@
 
 
 def chunks():
-    count = groups()
-    return {1: [(0,)], 2: [(0,), (1,)], 3: [(0,), (1, 2)], 4: [(0,), (1, 3), (2,)]}[count]
-
-
-def spread(block):
+    return [tuple(range(groups()))]
+
+
+def spread(block, meanwhile=()):
     if groups() == 1:
         return [lax.all_gather(block, "col", axis=0, tiled=True)]
-    return [shifted(block, "col", back) for back in range(groups())]
+    received = [shifted(block, "col", back) for back in range(1, groups())]
+    return [block, *after(received, meanwhile)]
 
 
 def joined(blocks):
@@ -92,13 +92,35 @@
     return lax.dynamic_slice_in_dim(line, start, count * rows, axis=0)
 
 
-def gathered_sum(parts):
+def gathered_sum(parts, meanwhile=()):
     if len(parts) == 1:
         return lax.psum_scatter(parts[0], "col", scatter_dimension=0, tiled=True).astype(FLOAT)
-    total = parts[0].astype(FLOAT)
-    for back in range(1, len(parts)):
-        total = total + shifted(parts[back], "col", -back).astype(FLOAT)
-    return total
+    received = [shifted(part, "col", -back) for back, part in enumerate(parts) if back]
+    received = after(received, meanwhile)
+    return sum([part.astype(FLOAT) for part in received], parts[0].astype(FLOAT))
+
+
+def gathered_sum_in_turn(parts, meanwhile=()):
+    count = len(parts)
+    if count == 1:
+        return gathered_sum(parts)
+
+    def sent(values, section):
+        at = section * count
+        return [
+            lax.ppermute(
+                value,
+                ("section", "col"),
+                [(at + i, at + (i - back) % count) for i in range(count)],
+            )
+            for back, value in enumerate(values, 1)
+        ]
+
+    first = after(sent(parts[1:], 0), meanwhile)
+    done = sum(part[:8, :LANES] for part in first)
+    go = lax.ppermute(done, "section", [(0, 1)])
+    second = sent(after(parts[1:], go), 1)
+    return sum([part.astype(FLOAT) for part in (*first, *second)], parts[0].astype(FLOAT))
 
 
 def block_of(values, back):
@@ -579,39 +601,20 @@
 
 
 def through_experts(block, tables, expert, beside):
-    if groups() < 4:
-        blocks = spread(block)
-        tokens = [joined([blocks[back] for back in chunk]) for chunk in chunks()]
-        arrived = [to_experts(project(table, each)) for table, each in zip(tables, tokens)]
-        answers = [to_experts(expert(index, rows)) for index, rows in enumerate(arrived)]
-        made = [beside(*each) for each in zip(range(len(tokens)), tokens, answers)]
-        return to_blocks(made), arrived, tokens
-    near, far = shifted(block, "col", 1), shifted(block, "col", 3)
-    rows = to_experts(project(tables[0], block))
-    answer = expert(0, rows)
-    answered = to_experts(answer)
-    near, far = after(near, answer), after(far, answer)
-    last = shifted(after(block, near, far), "col", 2)
-    near = jnp.concatenate([near, far], axis=0)
-    sent = project(tables[1], near).astype(HALF)
-    rows_near = to_experts(sent)
-    part = beside(0, block, answered)
-    last = after(last, sent, part)
-    sent = project(tables[2], last).astype(HALF)
-    rows_last = to_experts(sent)
-    answer = expert(1, after(rows_near, sent))
-    answered = to_experts(answer)
-    answer = expert(2, after(rows_last, answer))
-    answered_last = to_experts(answer)
-    part_near = beside(1, near, after(answered, answer))
-    part_last = beside(2, last, answered_last)
-    parts = to_blocks([part, part_near, part_last])
-    return parts, [rows, rows_near, rows_last], [block, near, last]
-
-
-def line_shares(values, weights):
-    whole = sum(project_back(value, weight) for value, weight in zip(values, weights)).astype(HALF)
-    return gathered_sum([block_of(whole, back) for back in range(groups())]), whole
+    blocks = spread(block)
+    tokens = [joined([blocks[back] for back in chunk]) for chunk in chunks()]
+    arrived = [to_experts(project(table, each)) for table, each in zip(tables, tokens)]
+    answers = [to_experts(expert(index, rows)) for index, rows in enumerate(arrived)]
+    made = [beside(*each) for each in zip(range(len(tokens)), tokens, answers)]
+    return to_blocks(made), arrived, tokens
+
+
+def line_product(values, weights):
+    return sum(project_back(value, weight) for value, weight in zip(values, weights)).astype(HALF)
+
+
+def line_blocks(whole):
+    return [block_of(whole, back) for back in range(groups())]
 
 
 def expert_forward(rows, experts):
@@ -656,15 +659,15 @@
 def weight_sums(rows_in, rows_out, kept, grads, tokens_in, tokens_out, kept_s, grads_s):
     rows_in, rows_out = joined(rows_in), joined(rows_out)
     experts = (
-        outer(rows_in, joined([each[0] for each in grads])),
-        outer(rows_in, joined([each[1] for each in grads])),
-        outer(joined([each[2] for each in kept]), rows_out),
+        outer(rows_in, joined([each[0] for each in grads])).astype(HALF),
+        outer(rows_in, joined([each[1] for each in grads])).astype(HALF),
+        outer(joined([each[2] for each in kept]), rows_out).astype(HALF),
     )
     tokens_in, tokens_out = joined(tokens_in), joined(tokens_out)
     pairs = [joined([each[at] for each in grads_s]) for at in range(2)]
     act_s = joined([each[2] for each in kept_s])
-    shared = (section_half(tokens_in, *pairs), section_half(tokens_out, *two_halves(act_s)))
-    return experts, shared
+    shared = ((tokens_in, *pairs), (tokens_out, *two_halves(act_s)))
+    return experts, [(*each, swapped(half_to_give(*each))) for each in shared]
 
 
 def middle_backward(grad_normed, grad_out, middle, mixed, norm_mid):
@@ -688,23 +691,20 @@
 def half_to_keep(left, first_right, second_right, given):
     first = lax.axis_index("section") == 0
     keep = outer(left, jnp.where(first, first_right, second_right))
-    return (keep + swapped(given).astype(FLOAT)).astype(HALF)
-
-
-def section_half(left, first_right, second_right):
-    given = half_to_give(left, first_right, second_right)
-    return half_to_keep(left, first_right, second_right, given)
-
-
-def row_share(values):
+    return (keep + given.astype(FLOAT)).astype(HALF)
+
+
+def row_pieces(values):
     n_row = lax.axis_size("row")
     rows = values.shape[0] // n_row
-    total = None
-    for ahead in range(n_row):
-        index = lax.rem(lax.axis_index("row") + ahead, n_row)
-        part = lax.dynamic_slice_in_dim(values, index * rows, rows, axis=0)
-        part = shifted(part, "row", ahead).astype(FLOAT)
-        total = part if total is None else total + part
+    index = [lax.rem(lax.axis_index("row") + ahead, n_row) * rows for ahead in range(n_row)]
+    return [lax.dynamic_slice_in_dim(values, at, rows, axis=0) for at in index]
+
+
+def row_total(pieces, meanwhile=()):
+    received = [shifted(piece, "row", ahead) for ahead, piece in enumerate(pieces) if ahead]
+    received = after(received, meanwhile)
+    total = sum([piece.astype(FLOAT) for piece in received], pieces[0].astype(FLOAT))
     return total.astype(HALF)
 
 
@@ -795,8 +795,12 @@
     )
     keep, give = jnp.where(first, *halves), jnp.where(first, *halves[::-1])
     mine = pair(keep, swapped(give))
-    mine = [lax.all_gather(half, "row", axis=0, tiled=True) for half in mine]
-    proj = [pair(half, swapped(half)) for half in mine]
+
+    def both_halves(half):
+        whole = lax.all_gather(half, ("section", "row"), axis=0, tiled=True)
+        return whole.reshape(2, n_row * half.shape[0], half.shape[1])
+
+    proj = [both_halves(mine[0])]
 
     def both_layers(weight):
         whole = lax.all_gather(weight, ("section", "row"), axis=0, tiled=True)
@@ -847,9 +851,10 @@
         pre = [project(wide_in, half) for half in proj[s]]
         return pre, *mixer_forward(pre, heads, wide, mixers[s])
 
-    def mix_out(s, resid, scaled, total_part):
-        mixed, _ = line_shares([scaled], [proj_out[s]])
-        total = gathered_sum([block_of(total_part, back) for back in range(groups())])
+    def mix_out(s, resid, scaled, total_part, meanwhile, gathered):
+        parts = line_blocks(line_product([scaled], [proj_out[s]]))
+        mixed = gathered(parts, meanwhile)
+        total = gathered_sum(line_blocks(total_part), meanwhile)
         rr = lax.rsqrt(total / DI + EPS)
         return resid + mixed * rr, mixed, rr
 
@@ -859,7 +864,10 @@
     tables = route_tables(spread(after(meta, scaled_0)), top, capacity, 2)
     plain = [[table[0] for table in tables[s]] for s in layers]
     scaling = [[table[1] for table in tables[s]] for s in layers]
-    middle_0, mixed_0, rr_0 = mix_out(0, tokens_now, scaled_0, total_0)
+    proj.append(both_halves(after(mine[1], scaled_0)))
+    middle_0, mixed_0, rr_0 = mix_out(
+        0, tokens_now, scaled_0, total_0, tables, gathered_sum_in_turn
+    )
     kept_0, kept_s_0 = {}, {}
 
     def expert_0(index, rows):
@@ -876,14 +884,14 @@
     out_0 = middle_0 + gathered_sum(parts)
 
     wide_in_1 = joined(spread(rms_norm(out_0, norm_ins[1]).astype(HALF)))
+    grad_blocks = after(grad_blocks, out_0)
     grad_tokens = [joined([grad_blocks[back] for back in chunk]) for chunk in chunks()]
     grad_rows_1 = [
-        to_experts(project(table, after(block, out_0)))
-        for table, block in zip(scaling[1], grad_tokens)
+        to_experts(project(table, block)) for table, block in zip(scaling[1], grad_tokens)
     ]
     pre_1, y_1, scaled_1, total_1 = mix_in(1, wide_in_1)
     scaled_1 = after(scaled_1, *grad_rows_1)
-    middle_1, mixed_1, rr_1 = mix_out(1, out_0, scaled_1, total_1)
+    middle_1, mixed_1, rr_1 = mix_out(1, out_0, scaled_1, total_1, (), gathered_sum)
 
     kept_1, kept_s_1, grads_1, grads_s_1, answers_1 = {}, {}, {}, {}, {}
 
@@ -906,11 +914,10 @@
     def listed(kept):
         return [kept[index] for index in order]
 
-    def mixer_back(s, grad_middle, along, rr, saved, weight_grads, last):
+    def mixer_back(s, grad_middle, along, rr, saved, meanwhile, last):
         wide_in, pre, y, scaled = saved
-        wide_mix = joined(spread(grad_middle.astype(HALF)))
-        sides = joined(spread(jnp.concatenate([rr, along], axis=1)))
-        wide_mix = after(wide_mix, weight_grads)
+        wide_mix = joined(spread(grad_middle.astype(HALF), meanwhile))
+        sides = joined(spread(jnp.concatenate([rr, along], axis=1), meanwhile))
         grad_scaled = project(wide_mix, proj_out[s])
         *grad_pre, wide_grads, grad_conv_input, grad_conv_state, step_grads = mixer_backward(
             pre, y, grad_scaled, sides, heads, mixers[s]
@@ -918,16 +925,27 @@
         ends = [part[:, :wide] for part in grad_pre]
         if last:
             given = half_to_give(wide_in, *ends)
-            grad_in, whole = line_shares([after(part, given) for part in grad_pre], proj[s])
+            whole = line_product([after(part, given) for part in grad_pre], proj[s])
         else:
-            grad_in, whole = line_shares(grad_pre, proj[s])
+            whole = line_product(grad_pre, proj[s])
             given = half_to_give(after(wide_in, whole), *ends)
-        grad_proj = half_to_keep(after(wide_in, whole), *ends, given)
-        mix_rr = (after(wide_mix, grad_proj) * sides[:, :1]).astype(HALF)
-        grad_proj_out = section_half(mix_rr, *two_halves(scaled))
+        grad_proj = (after(wide_in, whole), *ends, swapped(given))
+        mix_rr = (after(wide_mix, whole, given) * sides[:, :1]).astype(HALF)
+        halves = two_halves(scaled)
+        given_out = half_to_give(mix_rr, *halves)
+        grad_proj_out = (mix_rr, *halves, swapped(given_out))
         tail = jnp.concatenate([grad_pre[0][:, wide:], grad_pre[1][:, wide : wide + LANES]], axis=1)
-        grad_tail = outer(after(wide_in, grad_proj), tail).astype(HALF)
+        grad_tail = outer(after(wide_in, given_out), tail).astype(HALF)
         rest = (grad_conv_state, grad_conv_input, wide_grads, step_grads)
+        if last:
+            grad_proj = half_to_keep(*grad_proj)
+            meanwhile = row_pieces(grad_proj)
+            grad_proj_out = half_to_keep(*after(grad_proj_out, meanwhile))
+            grad_proj = row_total(meanwhile)
+            meanwhile = (meanwhile, grad_proj_out, grad_tail)
+        else:
+            meanwhile = (given, given_out, grad_tail)
+        grad_in = gathered_sum(line_blocks(whole), meanwhile)
         return wide_mix, grad_in, grad_proj, grad_proj_out, grad_tail, rest
 
     def resid_back(resid, norm, grad_normed, grad_middle):
@@ -938,10 +956,10 @@
     def row_sums(value):
         return lax.psum_scatter(value, "row", scatter_dimension=0, tiled=True)
 
-    def own_layer(first_value, second_value):
+    def own_layer(first_value, second_value, *ahead):
         keep = jnp.where(first, first_value, second_value)
         give = jnp.where(first, second_value, first_value).astype(HALF)
-        return keep.astype(FLOAT) + swapped(give).astype(FLOAT)
+        return keep.astype(FLOAT) + after(swapped(give), *ahead).astype(FLOAT)
 
     grad_middle, along, grad_norm_mid_1 = middle_backward(
         gathered_sum(parts), grad_now, middle_1, mixed_1, norm_mids[1]
@@ -956,14 +974,13 @@
         listed(kept_s_1),
         listed(grads_s_1),
     )
-    expert_grads_1 = [grad.astype(HALF) for grad in expert_grads_1]
     wide_mix, grad_in, grad_proj_1, grad_out_1, grad_tail_1, rest_1 = mixer_back(
         1,
         grad_middle,
         along,
         rr_1,
         (wide_in_1, pre_1, y_1, scaled_1),
-        (expert_grads_1, shared_grads_1),
+        expert_grads_1,
         False,
     )
     grad_1, grad_norm_in_1 = resid_back(out_0, norm_ins[1], grad_in, grad_middle)
@@ -972,8 +989,8 @@
         for index in order
     ]
     home = [after(part, wide_mix) for part in home]
-    out_1 = middle_1 + gathered_sum(to_blocks(home))
-    sums_1 = [row_sums(value) for value in (*shared_grads_1, grad_out_1, grad_proj_1)]
+    out_1 = middle_1 + gathered_sum(to_blocks(home), grad_in)
+    sums_1 = [half_to_keep(*after(made, grad_1)) for made in shared_grads_1]
 
     grads_0, grads_s_0 = {}, {}
 
@@ -988,9 +1005,15 @@
     parts, grad_rows_0, grad_tokens_0 = through_experts(
         grad_1.astype(HALF), scaling[0], expert_back_0, beside_back_0
     )
+    sums_1 = [
+        *sums_1,
+        half_to_keep(*after(grad_out_1, parts)),
+        half_to_keep(*after(grad_proj_1, parts)),
+    ]
     grad_middle, along, grad_norm_mid_0 = middle_backward(
-        gathered_sum(parts), grad_1, middle_0, mixed_0, norm_mids[0]
-    )
+        gathered_sum(parts, sums_1), grad_1, middle_0, mixed_0, norm_mids[0]
+    )
+    sums_1 = [row_sums(value) for value in sums_1]
     expert_grads_0, shared_grads_0 = weight_sums(
         rows_0,
         grad_rows_0,
@@ -1001,28 +1024,28 @@
         listed(kept_s_0),
         listed(grads_s_0),
     )
-    expert_out = [
-        own_layer(a.astype(HALF), b) for a, b in zip(expert_grads_0, expert_grads_1)
-    ]
-    sums_0 = [row_sums(value) for value in shared_grads_0]
     wide_mix, grad_in, grad_proj_0, grad_out_0, grad_tail_0, rest_0 = mixer_back(
         0,
         grad_middle,
         along,
         rr_0,
         (wide_in_0, pre_0, y_0, scaled_0),
-        (expert_out, shared_grads_0),
+        expert_grads_0,
         True,
     )
+    sums_0 = [row_sums(half_to_keep(*after(made, wide_mix))) for made in shared_grads_0]
     grad_0, grad_norm_in_0 = resid_back(tokens_now, norm_ins[0], grad_in, grad_middle)
-    sums_0 = [*sums_0, row_sums(grad_out_0), row_share(grad_proj_0)]
+    sums_0 = [*sums_0, row_sums(grad_out_0), grad_proj_0]
+    expert_out = [
+        own_layer(a, b, grad_out_0) for a, b in zip(expert_grads_0, expert_grads_1)
+    ]
 
     def own_halves(first_value, second_value):
         keep = jnp.where(first, first_value, second_value)
         give = jnp.where(first, second_value, first_value)
         return pair(keep, swapped(give))
 
-    tail = row_share(own_layer(grad_tail_0, grad_tail_1).astype(HALF))
+    tail = row_total(row_pieces(own_layer(grad_tail_0, grad_tail_1).astype(HALF)))
     state_grad = col_sum(tail[:, :state])
     grad_shared, grad_down, grad_out, grad_ends = [own_halves(a, b) for a, b in zip(sums_0, sums_1)]
     grad_out, grad_down = [jnp.concatenate(both, axis=1) for both in (grad_out, grad_down)]
@@ -1050,16 +1073,16 @@
         out_step,
     ) = unflat(jnp.concatenate([shared_sum, vector[common:]]), shapes)
 
-    def per_micro(first_value, second_value):
+    def per_micro(first_value, second_value, *ahead):
         keep = jnp.where(first, first_value, second_value)
-        other = swapped(jnp.where(first, second_value, first_value).astype(HALF)).astype(FLOAT)
-        return jnp.stack(pair(keep, other))[None]
+        other = swapped(jnp.where(first, second_value, first_value).astype(HALF))
+        return jnp.stack(pair(keep, after(other, *ahead).astype(FLOAT)))[None]
 
     def out(value):
         return value.astype(FLOAT)[None]
 
     return (
-        per_micro(out_0, out_1),
+        per_micro(out_0, out_1, grad_out_0),
         per_micro(grad_0, grad_1),
         out_norm_in[None],
         out(grad_ends[0][:, :inner]),

time: 1260 us -> 1260 us (level)
  waiting for transfers between devices: 460 us -> 575 us
  matrix products: 317 us -> 211 us
  blocking collectives: 0 us -> 40.6 us
  starting transfers between devices: 259 us -> 231 us
    ppermute x81 -> x78, waiting for transfers between devices: 291 us -> 385 us  [shifted(): lax.ppermute(block, axis, [(i, (i + distance) % count) for i in range(cou...]
    all_to_all x24 -> x7, waiting for transfers between devices: 74.3 us -> 158 us  [to_experts(): lax.all_to_all(rows.astype(HALF), 'row', split_axis=0, concat_axis=0, til...]
    all_to_all x24 -> x7, starting transfers between devices: 96.1 us -> 33.5 us  [to_experts(): lax.all_to_all(rows.astype(HALF), 'row', split_axis=0, concat_axis=0, til...]
    dot_general x57 -> x23, matrix products: 130 us -> 72.3 us  [project(): return jnp.dot(left, right, preferred_element_type=FLOAT)]
    all_to_all x0 -> x1, blocking collectives: none -> 40.6 us  [to_experts(): lax.all_to_all(rows.astype(HALF), 'row', split_axis=0, concat_axis=0, til...]
    dot_general x42 -> x18, matrix products: 89.3 us -> 52.1 us  [project_back(): lax.dot_general(left, right, (((1,), (1,)), ((), ())), preferred_element_...]
    all_gather x2, waiting for transfers between devices: 50.6 us -> 14 us  [both_layers(): whole = lax.all_gather(weight, ('section', 'row'), axis=0, tiled=True)]
    ppermute x0 -> x6, starting transfers between devices: none -> 31.8 us  [sent(): lax.ppermute(value, ('section', 'col'), [(at + i, at + (i - back) % count...]
  transfers between devices with their start and end apart: 143 -> 127, of which waited for: 67 -> 48; matrix products, arithmetic and copies ran while one was open for 33% -> 21% of each run, Pallas kernels for 5% -> 3%
where the time goes in v5:
time: 1260 us; the launch traced here: 1250 us
  waiting for transfers between devices  575 us (46%)
  starting transfers between devices  231 us (18%)
  matrix products  211 us (17%)
  other arithmetic  72.3 us (6%)
  Pallas kernels  60.8 us (5%)
  local copies, waits for them, and re-layouts  42.3 us (3%)
  blocking collectives  40.6 us (3%)
  between operations  17.8 us (1%)
    ppermute x78, waiting for transfers between devices, shifted(): lax.ppermute(block, axis, [(i, (i + distance) % count) for i in range(cou...  385 us
    ppermute x78, starting transfers between devices, shifted(): lax.ppermute(block, axis, [(i, (i + distance) % count) for i in range(cou...  159 us
    all_to_all x7, waiting for transfers between devices, to_experts(): lax.all_to_all(rows.astype(HALF), 'row', split_axis=0, concat_axis=0, til...  158 us
    dot_general x28, matrix products, outer(): lax.dot_general(left, right, (((0,), (0,)), ((), ())), preferred_element_...  86 us
    dot_general x23, matrix products, project(): return jnp.dot(left, right, preferred_element_type=FLOAT)  72.3 us
    dot_general x18, matrix products, project_back(): lax.dot_general(left, right, (((1,), (1,)), ((), ())), preferred_element_...  52.1 us
    all_to_all x1, blocking collectives, to_experts(): lax.all_to_all(rows.astype(HALF), 'row', split_axis=0, concat_axis=0, til...  40.6 us
    pallas_call x2, Pallas kernels, mixer_backward(): whole_call(kernel, 5 + len(mixer), (jax.ShapeDtypeStruct(pre[0].shape, HA...  36.4 us
  transfers between devices with their start and end apart: 127, of which 48 were waited for; matrix products, arithmetic and copies ran while one was open for 21% of the time, Pallas kernels for 3%

profile of v5, /device:TPU:0, one launch (start us, length us, event | category | flops | bytes accessed | tf_op | source)
XLA Modules:
  0.0 1250.8 jit_solution(13576073984670749237)
XLA Ops:
  31.8 16.4 %collective-permute-done.1 = bf16[128,1536]{1,0:T(8,128)(2,1)S(1)} collective-permute-done((bf16[128,1536]{1,0:T(8,128)(2,1)S(1)}, bf16[128,1536]{1,0:T(8,128)(2,1)S(1)}, u32[]{:S(2)}, u32[]{:S(2)}) %collective-permute-start.1) | collective-permute-done | bytes 393248 | tf_op jit(solution)/shard_map/ppermute | solution.py:26
  70.0 12.5 mixer_forward.2
  88.9 14.0 %all-gather.18.cloned.1.call-done = bf16[1,3072,768]{2,1,0:T(8,128)(2,1)} async-done(((bf16[1,384,768]{2,1,0:T(8,128)(2,1)}), bf16[1,3072,768]{2,1,0:T(8,128)(2,1)}) %all-gather.18.cloned.1.call-update) | async-done | bytes 4718608 | tf_op jit(solution)/shard_map/all_gather | solution.py:806
  128.7 22.6 %collective-permute-start.7 = (bf16[128,1536]{1,0:T(8,128)(2,1)S(1)}, bf16[128,1536]{1,0:T(8,128)(2,1)S(1)}, u32[]{:S(2)}, u32[]{:S(2)}) collective-permute-start(bf16[128,1536]{1,0:T(8,128)(2,1)S(1)} %copy-done.147), channel_id=1, source_target_pairs={{0,1},{1,2},{2,3},{3,0},{4,5},{5,6},{6,7},{7,4},{8,9},{9,10},{10,1... | collective-permute-start | bytes 1179656 | tf_op jit(solution)/shard_map/ppermute | solution.py:111
  192.9 41.0 %all-to-all-done = bf16[4,256,1536]{2,1,0:T(8,128)(2,1)} async-done(((bf16[4,256,1536]{2,1,0:T(8,128)(2,1)}), bf16[4,256,1536]{2,1,0:T(8,128)(2,1)}, u32[]{:S(2)}, u32[]{:S(2)}) %all-to-all-start) | async-done | bytes 3145760 | tf_op jit(solution)/shard_map/all_to_all | solution.py:162
  273.7 24.0 %all-to-all-done.1 = bf16[4,256,1536]{2,1,0:T(8,128)(2,1)} async-done(((bf16[4,256,1536]{2,1,0:T(8,128)(2,1)}), bf16[4,256,1536]{2,1,0:T(8,128)(2,1)}, u32[]{:S(2)}, u32[]{:S(2)}) %all-to-all-start.1) | async-done | bytes 3145760 | tf_op jit(solution)/shard_map/all_to_all | solution.py:162
  316.7 24.9 %collective-permute-done.22 = bf16[128,1536]{1,0:T(8,128)(2,1)S(1)} collective-permute-done((bf16[128,1536]{1,0:T(8,128)(2,1)S(1)}, bf16[128,1536]{1,0:T(8,128)(2,1)S(1)}, u32[]{:S(2)}, u32[]{:S(2)}) %collective-permute-start.22) | collective-permute-done | bytes 393248 | tf_op jit(solution)/shard_map/ppermute | solution.py:26
  367.8 14.0 %collective-permute-done.25 = bf16[128,1536]{1,0:T(8,128)(2,1)S(1)} collective-permute-done((bf16[128,1536]{1,0:T(8,128)(2,1)S(1)}, bf16[128,1536]{1,0:T(8,128)(2,1)S(1)}, u32[]{:S(2)}, u32[]{:S(2)}) %collective-permute-start.25) | collective-permute-done | bytes 393248 | tf_op jit(solution)/shard_map/ppermute | solution.py:26
  389.0 12.0 mixer_forward.3
  421.0 21.1 %collective-permute-done.33 = f32[128,1]{1,0:T(8,128)S(1)} collective-permute-done((f32[128,1]{1,0:T(8,128)S(1)}, f32[128,1]{1,0:T(8,128)S(1)}, u32[]{:S(2)}, u32[]{:S(2)}) %collective-permute-start.33) | collective-permute-done | bytes 544 | tf_op jit(solution)/shard_map/ppermute | solution.py:26
  442.1 12.9 %collective-permute-start.35 = (f32[128,1]{1,0:T(8,128)S(1)}, f32[128,1]{1,0:T(8,128)S(1)}, u32[]{:S(2)}, u32[]{:S(2)}) collective-permute-start(f32[128,1]{1,0:T(8,128)S(1)} %get-tuple-element.488), channel_id=1, source_target_pairs={{0,1},{1,2},{2,3},{3,0},{4,5},{5,6},{6,7},{7,4},{8,9},{9,10},{10,1... | collective-permute-start | bytes 1544 | tf_op jit(solution)/shard_map/ppermute | solution.py:26
  471.9 12.7 %collective-permute-done.37 = bf16[128,1536]{1,0:T(8,128)(2,1)S(1)} collective-permute-done((bf16[128,1536]{1,0:T(8,128)(2,1)S(1)}, bf16[128,1536]{1,0:T(8,128)(2,1)S(1)}, u32[]{:S(2)}, u32[]{:S(2)}) %collective-permute-start.37) | collective-permute-done | bytes 393248 | tf_op jit(solution)/shard_map/ppermute | solution.py:26
  486.5 40.6 %all_to_all.96 = bf16[4,256,1536]{2,1,0:T(8,128)(2,1)S(1)} all-to-all(bf16[4,256,1536]{2,1,0:T(8,128)(2,1)S(1)} %bitcast.278), channel_id=1, replica_groups=mesh['section'=2,'row'=4,'col'=4] {'row'}, dimensions={0} | all-to-all | bytes 6291456 | tf_op jit(solution)/shard_map/all_to_all | solution.py:162
  560.2 22.6 %all-to-all-done.4 = bf16[4,256,1536]{2,1,0:T(8,128)(2,1)} async-done(((bf16[4,256,1536]{2,1,0:T(8,128)(2,1)}), bf16[4,256,1536]{2,1,0:T(8,128)(2,1)}, u32[]{:S(2)}, u32[]{:S(2)}) %all-to-all-start.4) | async-done | bytes 3145760 | tf_op jit(solution)/shard_map/all_to_all | solution.py:162
  589.2 10.1 collective-permute-start.40
  606.2 26.5 %collective-permute-done.40 = bf16[128,1536]{1,0:T(8,128)(2,1)S(1)} collective-permute-done((bf16[128,1536]{1,0:T(8,128)(2,1)S(1)}, bf16[128,1536]{1,0:T(8,128)(2,1)S(1)}, u32[]{:S(2)}, u32[]{:S(2)}) %collective-permute-start.40) | collective-permute-done | bytes 393248 | tf_op jit(solution)/shard_map/ppermute | solution.py:26
  651.8 22.5 %collective-permute-done.49 = f32[128,2]{0,1:T(2,128)S(1)} collective-permute-done((f32[128,2]{0,1:T(2,128)S(1)}, f32[128,2]{0,1:T(2,128)S(1)}, u32[]{:S(2)}, u32[]{:S(2)}) %collective-permute-start.49) | collective-permute-done | bytes 1056 | tf_op jit(solution)/shard_map/ppermute | solution.py:26
  677.9 18.1 %mixer_backward.2 = (bf16[512,1024]{1,0:T(8,128)(2,1)S(1)}, bf16[512,1024]{1,0:T(8,128)(2,1)S(1)}, f32[2,768]{1,0:T(2,128)S(1)}, f32[4,768]{1,0:T(4,128)S(1)}, f...) custom-call(f32[512,1024]{1,0:T(8,128)} %copy-done.3, f32[512,1024]{1,0:T(8,128)} %fusion.14.pre_other_in_ref, ...), custom_call_target="tpu_custom_call" | custom-call | tf_op jit(solution)/shard_map/mixer_backward/pallas_call | solution.py:564
  710.7 25.6 %collective-permute-done.52 = bf16[128,1536]{1,0:T(8,128)(2,1)S(1)} collective-permute-done((bf16[128,1536]{1,0:T(8,128)(2,1)S(1)}, bf16[128,1536]{1,0:T(8,128)(2,1)S(1)}, u32[]{:S(2)}, u32[]{:S(2)}) %collective-permute-start.52) | collective-permute-done | bytes 393248 | tf_op jit(solution)/shard_map/ppermute | solution.py:26
  742.3 10.1 collective-permute-done.55
  752.4 15.0 %collective-permute-done.56 = bf16[128,1536]{1,0:T(8,128)(2,1)S(1)} collective-permute-done((bf16[128,1536]{1,0:T(8,128)(2,1)S(1)}, bf16[128,1536]{1,0:T(8,128)(2,1)S(1)}, u32[]{:S(2)}, u32[]{:S(2)}) %collective-permute-start.56) | collective-permute-done | bytes 393248 | tf_op jit(solution)/shard_map/ppermute | solution.py:26
  788.4 24.0 %all-to-all-done.6 = bf16[4,256,1536]{2,1,0:T(8,128)(2,1)} async-done(((bf16[4,256,1536]{2,1,0:T(8,128)(2,1)}), bf16[4,256,1536]{2,1,0:T(8,128)(2,1)}, u32[]{:S(2)}, u32[]{:S(2)}) %all-to-all-start.6) | async-done | bytes 3145760 | tf_op jit(solution)/shard_map/all_to_all | solution.py:162
  851.3 13.6 %all-to-all-done.7 = bf16[4,256,1536]{2,1,0:T(8,128)(2,1)} async-done(((bf16[4,256,1536]{2,1,0:T(8,128)(2,1)}), bf16[4,256,1536]{2,1,0:T(8,128)(2,1)}, u32[]{:S(2)}, u32[]{:S(2)}) %all-to-all-start.7) | async-done | bytes 3145760 | tf_op jit(solution)/shard_map/all_to_all | solution.py:162
  873.0 10.4 collective-permute-start.58
  893.4 23.7 %collective-permute-done.59 = bf16[128,1536]{1,0:T(8,128)(2,1)} collective-permute-done((bf16[128,1536]{1,0:T(8,128)(2,1)}, bf16[128,1536]{1,0:T(8,128)(2,1)}, u32[]{:S(2)}, u32[]{:S(2)}) %collective-permute-start.59) | collective-permute-done | bytes 393248 | tf_op jit(solution)/shard_map/ppermute | solution.py:26
  935.9 13.9 %collective-permute-done.66 = bf16[128,1536]{1,0:T(8,128)(2,1)S(1)} collective-permute-done((bf16[128,1536]{1,0:T(8,128)(2,1)S(1)}, bf16[128,1536]{1,0:T(8,128)(2,1)S(1)}, u32[]{:S(2)}, u32[]{:S(2)}) %collective-permute-start.66) | collective-permute-done | bytes 393248 | tf_op jit(solution)/shard_map/ppermute | solution.py:26
  971.3 32.4 %all-to-all-done.5 = bf16[4,256,1536]{2,1,0:T(8,128)(2,1)} async-done(((bf16[4,256,1536]{2,1,0:T(8,128)(2,1)}), bf16[4,256,1536]{2,1,0:T(8,128)(2,1)}, u32[]{:S(2)}, u32[]{:S(2)}) %all-to-all-start.5) | async-done | bytes 3145760 | tf_op jit(solution)/shard_map/all_to_all | solution.py:162
  1032.4 19.6 %collective-permute-done.46 = bf16[128,1536]{1,0:T(8,128)(2,1)S(1)} collective-permute-done((bf16[128,1536]{1,0:T(8,128)(2,1)S(1)}, bf16[128,1536]{1,0:T(8,128)(2,1)S(1)}, u32[]{:S(2)}, u32[]{:S(2)}) %collective-permute-start.46) | collective-permute-done | bytes 393248 | tf_op jit(solution)/shard_map/ppermute | solution.py:26
  1055.9 18.2 %mixer_backward.3 = (bf16[512,1024]{1,0:T(8,128)(2,1)S(1)}, bf16[512,1024]{1,0:T(8,128)(2,1)S(1)}, f32[2,768]{1,0:T(2,128)S(1)}, f32[4,768]{1,0:T(4,128)S(1)}, f...) custom-call(f32[512,1024]{1,0:T(8,128)} %copy-done.2, f32[512,1024]{1,0:T(8,128)} %fusion.22.pre_other_in_ref, ...), custom_call_target="tpu_custom_call" | custom-call | tf_op jit(solution)/shard_map/mixer_backward/pallas_call | solution.py:564
  1100.7 11.9 collective-permute-done.89
  1145.5 15.3 %collective-permute-done.84 = bf16[384,768]{1,0:T(8,128)(2,1)S(1)} collective-permute-done((bf16[384,768]{1,0:T(8,128)(2,1)S(1)}, bf16[384,768]{1,0:T(8,128)(2,1)S(1)}, u32[]{:S(2)}, u32[]{:S(2)}) %collective-permute-start.84) | collective-permute-done | bytes 589856 | tf_op jit(solution)/shard_map/ppermute | solution.py:26
  1181.3 17.8 %collective-permute-done.74 = bf16[128,1536]{1,0:T(8,128)(2,1)S(1)} collective-permute-done((bf16[128,1536]{1,0:T(8,128)(2,1)}, bf16[128,1536]{1,0:T(8,128)(2,1)S(1)}, u32[]{:S(2)}, u32[]{:S(2)}) %collective-permute-start.74) | collective-permute-done | bytes 393248 | tf_op jit(solution)/shard_map/ppermute | solution.py:26
  (942 shorter events, 612.8 us)
Async XLA Ops:
  7.2 54.9 %all-gather.12.cloned.1.call-start = ((), (), s32[]{:S(2)}) async-start(), calls=%async_computation.15 | async-start | bytes 7077888 | tf_op jit(solution)/shard_map/all_gather | solution.py:800
  13.8 89.1 %all-gather.18.cloned.1.call-start = ((), (), s32[]{:S(2)}) async-start(), calls=%async_computation.25 | async-start | bytes 5308416 | tf_op jit(solution)/shard_map/all_gather | solution.py:806
  14.6 178.3 %all-gather.20.cloned.1.call-start = ((), (), s32[]{:S(2)}) async-start(), calls=%async_computation.26 | async-start | bytes 4718592 | tf_op jit(solution)/shard_map/all_gather | solution.py:810
  15.5 223.9 %all-gather.22.cloned.1.call-start = ((), (), s32[]{:S(2)}) async-start(), calls=%async_computation.27 | async-start | bytes 4718592 | tf_op jit(solution)/shard_map/all_gather | solution.py:811
  16.1 229.6 %all-gather.24.cloned.1.call-start = ((), (), s32[]{:S(2)}) async-start(), calls=%async_computation.28 | async-start | bytes 4718592 | tf_op jit(solution)/shard_map/all_gather | solution.py:812
  16.6 251.9 %all-gather.14.cloned.1.call-start = ((), (), s32[]{:S(2)}) async-start(), calls=%async_computation.16 | async-start | bytes 5308416 | tf_op jit(solution)/shard_map/all_gather | solution.py:806
  108.3 44.4 %collective-permute-start.5 = (bf16[128,1536]{1,0:T(8,128)(2,1)}, bf16[128,1536]{1,0:T(8,128)(2,1)S(1)}, u32[]{:S(2)}, u32[]{:S(2)}) collective-permute-start(bf16[128,1536]{1,0:T(8,128)(2,1)} %get-tuple-element.172), channel_id=1, source_target_pairs={{0,3},{1,0},{2,1},{3,2},{4,7},{5,4},{6,5},{7,6},{8,11},{9,8},{10,9... | collective-permute-start | bytes 1179656 | tf_op jit(solution)/shard_map/ppermute | solution.py:111
  113.5 43.0 %collective-permute-start.6 = (bf16[128,1536]{1,0:T(8,128)(2,1)}, bf16[128,1536]{1,0:T(8,128)(2,1)S(1)}, u32[]{:S(2)}, u32[]{:S(2)}) collective-permute-start(bf16[128,1536]{1,0:T(8,128)(2,1)} %get-tuple-element.173), channel_id=1, source_target_pairs={{0,2},{1,3},{2,0},{3,1},{4,6},{5,7},{6,4},{7,5},{8,10},{9,11},{10,... | collective-permute-start | bytes 1179656 | tf_op jit(solution)/shard_map/ppermute | solution.py:111
  187.4 46.5 %all-to-all-start = ((bf16[4,256,1536]{2,1,0:T(8,128)(2,1)}), bf16[4,256,1536]{2,1,0:T(8,128)(2,1)}, u32[]{:S(2)}, u32[]{:S(2)}) async-start(bf16[4,256,1536]{2,1,0:T(8,128)(2,1)} %bitcast.277), calls=%async_computation | async-start | bytes 6291456 | tf_op jit(solution)/shard_map/all_to_all | solution.py:162
  192.1 189.7 %all-gather.16.cloned.1.call-start = ((), (), s32[]{:S(2)}) async-start(), calls=%async_computation.17 | async-start | bytes 7077888 | tf_op jit(solution)/shard_map/all_gather | solution.py:800
  251.0 46.7 %all-to-all-start.1 = ((bf16[4,256,1536]{2,1,0:T(8,128)(2,1)}), bf16[4,256,1536]{2,1,0:T(8,128)(2,1)}, u32[]{:S(2)}, u32[]{:S(2)}) async-start(bf16[4,256,1536]{2,1,0:T(8,128)(2,1)} %bitcast.276), calls=%async_computation.1 | async-start | bytes 6291456 | tf_op jit(solution)/shard_map/all_to_all | solution.py:162
  257.0 51.4 %collective-permute-start.27 = (bf16[128,1536]{1,0:T(8,128)(2,1)S(1)}, bf16[128,1536]{1,0:T(8,128)(2,1)}, u32[]{:S(2)}, u32[]{:S(2)}) collective-permute-start(bf16[128,1536]{1,0:T(8,128)(2,1)S(1)} %bitcast_convert_fusion), channel_id=1, source_target_pairs={{0,1},{1,2},{2,3},{3,0},{4,5},{5,6},{6,7},{7,4},{8,9},{9,10},{10,1... | collective-permute-start | bytes 1179656 | tf_op jit(solution)/shard_map/ppermute | solution.py:26
  266.0 42.4 %collective-permute-start.28 = (bf16[128,1536]{1,0:T(8,128)(2,1)S(1)}, bf16[128,1536]{1,0:T(8,128)(2,1)}, u32[]{:S(2)}, u32[]{:S(2)}) collective-permute-start(bf16[128,1536]{1,0:T(8,128)(2,1)S(1)} %bitcast_convert_fusion), channel_id=1, source_target_pairs={{0,2},{1,3},{2,0},{3,1},{4,6},{5,7},{6,4},{7,5},{8,10},{9,11},{10,... | collective-permute-start | bytes 1179656 | tf_op jit(solution)/shard_map/ppermute | solution.py:26
  266.8 41.6 %collective-permute-start.29 = (bf16[128,1536]{1,0:T(8,128)(2,1)S(1)}, bf16[128,1536]{1,0:T(8,128)(2,1)}, u32[]{:S(2)}, u32[]{:S(2)}) collective-permute-start(bf16[128,1536]{1,0:T(8,128)(2,1)S(1)} %bitcast_convert_fusion), channel_id=1, source_target_pairs={{0,3},{1,0},{2,1},{3,2},{4,7},{5,4},{6,5},{7,6},{8,11},{9,8},{10,9... | collective-permute-start | bytes 1179656 | tf_op jit(solution)/shard_map/ppermute | solution.py:26
  348.9 53.3 %all-to-all-start.2 = ((bf16[4,256,1536]{2,1,0:T(8,128)(2,1)}), bf16[4,256,1536]{2,1,0:T(8,128)(2,1)}, u32[]{:S(2)}, u32[]{:S(2)}) async-start(bf16[4,256,1536]{2,1,0:T(8,128)(2,1)} %bitcast.275), calls=%async_computation.2 | async-start | bytes 6291456 | tf_op jit(solution)/shard_map/all_to_all | solution.py:162
  405.9 51.0 %collective-permute-start.30 = (bf16[128,1536]{1,0:T(8,128)(2,1)S(1)}, bf16[128,1536]{1,0:T(8,128)(2,1)S(1)}, u32[]{:S(2)}, u32[]{:S(2)}) collective-permute-start(bf16[128,1536]{1,0:T(8,128)(2,1)S(1)} %get-tuple-element.457), channel_id=1, source_target_pairs={{0,3},{1,0},{2,1},{3,2},{4,7},{5,4},{6,5},{7,6},{8,11},{9,8},{10,9... | collective-permute-start | bytes 1179656 | tf_op jit(solution)/shard_map/ppermute | solution.py:26
  589.2 43.5 %collective-permute-start.40 = (bf16[128,1536]{1,0:T(8,128)(2,1)S(1)}, bf16[128,1536]{1,0:T(8,128)(2,1)S(1)}, u32[]{:S(2)}, u32[]{:S(2)}) collective-permute-start(bf16[128,1536]{1,0:T(8,128)(2,1)S(1)} %get-tuple-element.452), channel_id=1, source_target_pairs={{0,2},{1,3},{2,0},{3,1},{4,6},{5,7},{6,4},{7,5},{8,10},{9,11},{10,... | collective-permute-start | bytes 1179656 | tf_op jit(solution)/shard_map/ppermute | solution.py:26
  771.0 41.4 %all-to-all-start.6 = ((bf16[4,256,1536]{2,1,0:T(8,128)(2,1)}), bf16[4,256,1536]{2,1,0:T(8,128)(2,1)}, u32[]{:S(2)}, u32[]{:S(2)}) async-start(bf16[4,256,1536]{2,1,0:T(8,128)(2,1)} %bitcast.274), calls=%async_computation.6 | async-start | bytes 6291456 | tf_op jit(solution)/shard_map/all_to_all | solution.py:162
  775.7 316.7 %reduce-scatter.20.cloned.1.call-start = ((), (), s32[]{:S(2)}) async-start(), calls=%async_computation.24 | async-start | bytes 491520 | tf_op jit(solution)/shard_map/reduce_scatter | solution.py:957
  783.6 104.9 %collective-permute-start.63 = (bf16[1536,384]{1,0:T(8,128)(2,1)}, bf16[1536,384]{1,0:T(8,128)(2,1)}, u32[]{:S(2)}, u32[]{:S(2)}) collective-permute-start(bf16[1536,384]{1,0:T(8,128)(2,1)} %convolution_convert_fusion.19), channel_id=1, source_target_pairs={{0,16},{16,0},{1,17},{17,1},{2,18},{18,2},{3,19},{19,3},{4,20},{20... | collective-permute-start | bytes 3538952 | tf_op jit(solution)/shard_map/ppermute | solution.py:30
  785.6 97.9 %collective-permute-start.64 = (bf16[1536,768]{1,0:T(8,128)(2,1)}, bf16[1536,768]{1,0:T(8,128)(2,1)}, u32[]{:S(2)}, u32[]{:S(2)}) collective-permute-start(bf16[1536,768]{1,0:T(8,128)(2,1)} %convolution_convert_fusion.7), channel_id=1, source_target_pairs={{0,16},{16,0},{1,17},{17,1},{2,18},{18,2},{3,19},{19,3},{4,20},{20... | collective-permute-start | bytes 7077896 | tf_op jit(solution)/shard_map/ppermute | solution.py:30
  829.3 263.0 %reduce-scatter.18.cloned.1.call-start = ((), (), s32[]{:S(2)}) async-start(), calls=%async_computation.23 | async-start | bytes 491520 | tf_op jit(solution)/shard_map/reduce_scatter | solution.py:957
  834.2 117.6 %collective-permute-start.104 = (bf16[1536,128]{1,0:T(8,128)(2,1)}, bf16[1536,128]{1,0:T(8,128)(2,1)}, u32[]{:S(2)}, u32[]{:S(2)}) collective-permute-start(bf16[1536,128]{1,0:T(8,128)(2,1)} %convolution_convert_fusion.22), channel_id=1, source_target_pairs={{0,16},{16,0},{1,17},{17,1},{2,18},{18,2},{3,19},{19,3},{4,20},{20... | collective-permute-start | bytes 1179656 | tf_op jit(solution)/shard_map/ppermute | solution.py:30
  959.5 44.3 %all-to-all-start.5 = ((bf16[4,256,1536]{2,1,0:T(8,128)(2,1)}), bf16[4,256,1536]{2,1,0:T(8,128)(2,1)}, u32[]{:S(2)}, u32[]{:S(2)}) async-start(bf16[4,256,1536]{2,1,0:T(8,128)(2,1)} %bitcast.51), calls=%async_computation.5 | async-start | bytes 6291456 | tf_op jit(solution)/shard_map/all_to_all | solution.py:162
  964.3 168.1 %reduce-scatter.16.cloned.1.call-start = ((), (), s32[]{:S(2)}) async-start(), calls=%async_computation.22 | async-start | bytes 983040 | tf_op jit(solution)/shard_map/reduce_scatter | solution.py:957
  964.9 167.5 %reduce-scatter.14.cloned.1.call-start = ((), (), s32[]{:S(2)}) async-start(), calls=%async_computation.21 | async-start | bytes 983040 | tf_op jit(solution)/shard_map/reduce_scatter | solution.py:957
  969.5 204.5 %reduce-scatter.8.cloned.1.call-start = ((), (), s32[]{:S(2)}) async-start(), calls=%async_computation.18 | async-start | bytes 2949120 | tf_op jit(solution)/shard_map/reduce_scatter | solution.py:957
  1009.3 229.4 %reduce-scatter.12.cloned.1.call-start = ((), (), s32[]{:S(2)}) async-start(), calls=%async_computation.20 | async-start | bytes 1474560 | tf_op jit(solution)/shard_map/reduce_scatter | solution.py:957
  1089.1 149.7 %reduce-scatter.10.cloned.1.call-start = ((), (), s32[]{:S(2)}) async-start(), calls=%async_computation.19 | async-start | bytes 1474560 | tf_op jit(solution)/shard_map/reduce_scatter | solution.py:957
  1089.3 87.9 %collective-permute-start.71 = (bf16[1536,384]{1,0:T(8,128)(2,1)}, bf16[1536,384]{1,0:T(8,128)(2,1)}, u32[]{:S(2)}, u32[]{:S(2)}) collective-permute-start(bf16[1536,384]{1,0:T(8,128)(2,1)} %convolution_convert_fusion.17), channel_id=1, source_target_pairs={{0,16},{16,0},{1,17},{17,1},{2,18},{18,2},{3,19},{19,3},{4,20},{20... | collective-permute-start | bytes 3538952 | tf_op jit(solution)/shard_map/ppermute | solution.py:30
  1089.9 46.8 %collective-permute-start.72 = (bf16[1536,768]{1,0:T(8,128)(2,1)}, bf16[1536,768]{1,0:T(8,128)(2,1)}, u32[]{:S(2)}, u32[]{:S(2)}) collective-permute-start(bf16[1536,768]{1,0:T(8,128)(2,1)} %convolution_convert_fusion.6), channel_id=1, source_target_pairs={{0,16},{16,0},{1,17},{17,1},{2,18},{18,2},{3,19},{19,3},{4,20},{20... | collective-permute-start | bytes 7077896 | tf_op jit(solution)/shard_map/ppermute | solution.py:30
  1144.5 59.9 %collective-permute-start.54 = (bf16[128,1536]{1,0:T(8,128)(2,1)}, bf16[128,1536]{1,0:T(8,128)(2,1)}, u32[]{:S(2)}, u32[]{:S(2)}) collective-permute-start(bf16[128,1536]{1,0:T(8,128)(2,1)} %select_convert_fusion.2), channel_id=1, source_target_pairs={{0,16},{16,0},{1,17},{17,1},{2,18},{18,2},{3,19},{19,3},{4,20},{20... | collective-permute-start | bytes 1179656 | tf_op jit(solution)/shard_map/ppermute | solution.py:30
  (307 other events, 5242.9 us)
Sparse Core Ops, SparseCore 0:
  13.9 48.1 all-gather.11
  64.0 38.9 all-gather.17
  104.5 12.1 all-gather.19
  118.1 13.2 all-gather.21
  132.8 13.2 all-gather.23
  148.4 40.0 all-gather.13
  195.4 92.9 all-gather.15
  788.5 41.5 reduce-scatter.19
  954.4 46.4 reduce-scatter.17
  1003.7 34.1 reduce-scatter.15
  1040.7 26.0 reduce-scatter.13
  1070.3 49.3 reduce-scatter.7
  1122.7 39.4 reduce-scatter.11
  1208.3 27.4 reduce-scatter.9

commit v6 on v5

--- a/solution.py
+++ b/solution.py
@@ -92,35 +92,18 @@
     return lax.dynamic_slice_in_dim(line, start, count * rows, axis=0)
 
 
+def sent_home(parts):
+    return [shifted(part, "col", -back) for back, part in enumerate(parts) if back]
+
+
 def gathered_sum(parts, meanwhile=()):
     if len(parts) == 1:
         return lax.psum_scatter(parts[0], "col", scatter_dimension=0, tiled=True).astype(FLOAT)
-    received = [shifted(part, "col", -back) for back, part in enumerate(parts) if back]
-    received = after(received, meanwhile)
-    return sum([part.astype(FLOAT) for part in received], parts[0].astype(FLOAT))
-
-
-def gathered_sum_in_turn(parts, meanwhile=()):
-    count = len(parts)
-    if count == 1:
-        return gathered_sum(parts)
-
-    def sent(values, section):
-        at = section * count
-        return [
-            lax.ppermute(
-                value,
-                ("section", "col"),
-                [(at + i, at + (i - back) % count) for i in range(count)],
-            )
-            for back, value in enumerate(values, 1)
-        ]
-
-    first = after(sent(parts[1:], 0), meanwhile)
-    done = sum(part[:8, :LANES] for part in first)
-    go = lax.ppermute(done, "section", [(0, 1)])
-    second = sent(after(parts[1:], go), 1)
-    return sum([part.astype(FLOAT) for part in (*first, *second)], parts[0].astype(FLOAT))
+    return total_of(parts[0], after(sent_home(parts), meanwhile))
+
+
+def total_of(own, received):
+    return sum([part.astype(FLOAT) for part in received], own.astype(FLOAT))
 
 
 def block_of(values, back):
@@ -600,13 +583,16 @@
     return parts
 
 
-def through_experts(block, tables, expert, beside):
+def through_experts(block, tables, expert, beside, aside=None):
     blocks = spread(block)
     tokens = [joined([blocks[back] for back in chunk]) for chunk in chunks()]
     arrived = [to_experts(project(table, each)) for table, each in zip(tables, tokens)]
-    answers = [to_experts(expert(index, rows)) for index, rows in enumerate(arrived)]
+    answers = [expert(index, rows) for index, rows in enumerate(arrived)]
+    if aside is not None:
+        answers = after(answers, aside(tokens))
+    answers = [to_experts(rows) for rows in answers]
     made = [beside(*each) for each in zip(range(len(tokens)), tokens, answers)]
-    return to_blocks(made), arrived, tokens
+    return to_blocks(made), arrived, tokens, answers
 
 
 def line_product(values, weights):
@@ -694,33 +680,15 @@
     return (keep + given.astype(FLOAT)).astype(HALF)
 
 
-def row_pieces(values):
-    n_row = lax.axis_size("row")
-    rows = values.shape[0] // n_row
-    index = [lax.rem(lax.axis_index("row") + ahead, n_row) * rows for ahead in range(n_row)]
+def row_pieces(values, axis="row"):
+    count = lax.axis_size(axis)
+    rows = values.shape[0] // count
+    index = [lax.rem(lax.axis_index(axis) + ahead, count) * rows for ahead in range(count)]
     return [lax.dynamic_slice_in_dim(values, at, rows, axis=0) for at in index]
 
 
-def row_total(pieces, meanwhile=()):
-    received = [shifted(piece, "row", ahead) for ahead, piece in enumerate(pieces) if ahead]
-    received = after(received, meanwhile)
-    total = sum([piece.astype(FLOAT) for piece in received], pieces[0].astype(FLOAT))
-    return total.astype(HALF)
-
-
-def col_sum(values):
-    n_col = lax.axis_size("col")
-    if groups() == 1:
-        return lax.psum(values, "col")
-    rows = values.shape[0] // n_col
-    total = None
-    for ahead in range(n_col):
-        index = lax.rem(lax.axis_index("col") + ahead, n_col)
-        part = lax.dynamic_slice_in_dim(values, index * rows, rows, axis=0)
-        part = shifted(part, "col", ahead).astype(FLOAT)
-        total = part if total is None else total + part
-    total = total.astype(values.dtype)
-    return in_order([shifted(total, "col", back) for back in range(n_col)], "col")
+def row_received(pieces, axis="row"):
+    return [shifted(piece, axis, ahead) for ahead, piece in enumerate(pieces) if ahead]
 
 
 def flat(parts):
@@ -851,24 +819,20 @@
         pre = [project(wide_in, half) for half in proj[s]]
         return pre, *mixer_forward(pre, heads, wide, mixers[s])
 
-    def mix_out(s, resid, scaled, total_part, meanwhile, gathered):
-        parts = line_blocks(line_product([scaled], [proj_out[s]]))
-        mixed = gathered(parts, meanwhile)
-        total = gathered_sum(line_blocks(total_part), meanwhile)
+    def mix_out(s, resid, scaled, total_part, meanwhile):
+        total = gathered_sum(line_blocks(total_part))
+        whole = after(line_product([scaled], [proj_out[s]]), total)
+        mixed = gathered_sum(line_blocks(whole), meanwhile)
         rr = lax.rsqrt(total / DI + EPS)
         return resid + mixed * rr, mixed, rr
 
     wide_in_0 = rms_norm(wide_tokens.astype(FLOAT), norm_ins[0]).astype(HALF)
     pre_0, y_0, scaled_0, total_0 = mix_in(0, wide_in_0)
-    grad_blocks = spread(after(grad_now.astype(HALF), wide_in_0))
     tables = route_tables(spread(after(meta, scaled_0)), top, capacity, 2)
     plain = [[table[0] for table in tables[s]] for s in layers]
     scaling = [[table[1] for table in tables[s]] for s in layers]
-    proj.append(both_halves(after(mine[1], scaled_0)))
-    middle_0, mixed_0, rr_0 = mix_out(
-        0, tokens_now, scaled_0, total_0, tables, gathered_sum_in_turn
-    )
-    kept_0, kept_s_0 = {}, {}
+    middle_0, mixed_0, rr_0 = mix_out(0, tokens_now, scaled_0, total_0, tables)
+    kept_0, kept_s_0, grad_blocks = {}, {}, []
 
     def expert_0(index, rows):
         kept_0[index], answer = expert_forward(rows, experts[0])
@@ -878,9 +842,14 @@
         kept_s_0[index] = shared_forward(block, shared[0])
         return home_part(scaling[0][index], result, kept_s_0[index][2], shared[0])
 
-    parts, rows_0, mids_0 = through_experts(
-        rms_norm(middle_0, norm_mids[0]).astype(HALF), plain[0], expert_0, beside_0
-    )
+    def aside_0(blocks):
+        grad_blocks.extend(spread(after(grad_now.astype(HALF), blocks)))
+        return grad_blocks
+
+    parts, rows_0, mids_0, answers = through_experts(
+        rms_norm(middle_0, norm_mids[0]).astype(HALF), plain[0], expert_0, beside_0, aside_0
+    )
+    proj.append(both_halves(after(mine[1], answers)))
     out_0 = middle_0 + gathered_sum(parts)
 
     wide_in_1 = joined(spread(rms_norm(out_0, norm_ins[1]).astype(HALF)))
@@ -891,7 +860,7 @@
     ]
     pre_1, y_1, scaled_1, total_1 = mix_in(1, wide_in_1)
     scaled_1 = after(scaled_1, *grad_rows_1)
-    middle_1, mixed_1, rr_1 = mix_out(1, out_0, scaled_1, total_1, (), gathered_sum)
+    middle_1, mixed_1, rr_1 = mix_out(1, out_0, scaled_1, total_1, ())
 
     kept_1, kept_s_1, grads_1, grads_s_1, answers_1 = {}, {}, {}, {}, {}
 
@@ -905,7 +874,7 @@
         grads_s_1[index], part = shared_backward(grad_tokens[index], kept_s_1[index], shared[1])
         return (part + outer(plain[1][index], result)).astype(HALF)
 
-    parts, rows_1, mids_1 = through_experts(
+    parts, rows_1, mids_1, _ = through_experts(
         rms_norm(middle_1, norm_mids[1]).astype(HALF), plain[1], expert_1, beside_1
     )
     order = range(len(chunks()))
@@ -914,39 +883,19 @@
     def listed(kept):
         return [kept[index] for index in order]
 
-    def mixer_back(s, grad_middle, along, rr, saved, meanwhile, last):
+    def mixer_back(s, grad_middle, along, rr, saved, meanwhile):
         wide_in, pre, y, scaled = saved
+        sides = joined(spread(jnp.concatenate([rr, along], axis=1), meanwhile))
         wide_mix = joined(spread(grad_middle.astype(HALF), meanwhile))
-        sides = joined(spread(jnp.concatenate([rr, along], axis=1), meanwhile))
         grad_scaled = project(wide_mix, proj_out[s])
         *grad_pre, wide_grads, grad_conv_input, grad_conv_state, step_grads = mixer_backward(
             pre, y, grad_scaled, sides, heads, mixers[s]
         )
         ends = [part[:, :wide] for part in grad_pre]
-        if last:
-            given = half_to_give(wide_in, *ends)
-            whole = line_product([after(part, given) for part in grad_pre], proj[s])
-        else:
-            whole = line_product(grad_pre, proj[s])
-            given = half_to_give(after(wide_in, whole), *ends)
-        grad_proj = (after(wide_in, whole), *ends, swapped(given))
-        mix_rr = (after(wide_mix, whole, given) * sides[:, :1]).astype(HALF)
-        halves = two_halves(scaled)
-        given_out = half_to_give(mix_rr, *halves)
-        grad_proj_out = (mix_rr, *halves, swapped(given_out))
         tail = jnp.concatenate([grad_pre[0][:, wide:], grad_pre[1][:, wide : wide + LANES]], axis=1)
-        grad_tail = outer(after(wide_in, given_out), tail).astype(HALF)
+        mix_rr = (wide_mix * sides[:, :1]).astype(HALF)
         rest = (grad_conv_state, grad_conv_input, wide_grads, step_grads)
-        if last:
-            grad_proj = half_to_keep(*grad_proj)
-            meanwhile = row_pieces(grad_proj)
-            grad_proj_out = half_to_keep(*after(grad_proj_out, meanwhile))
-            grad_proj = row_total(meanwhile)
-            meanwhile = (meanwhile, grad_proj_out, grad_tail)
-        else:
-            meanwhile = (given, given_out, grad_tail)
-        grad_in = gathered_sum(line_blocks(whole), meanwhile)
-        return wide_mix, grad_in, grad_proj, grad_proj_out, grad_tail, rest
+        return wide_mix, grad_pre, (wide_in, *ends), (mix_rr, *two_halves(scaled)), tail, rest
 
     def resid_back(resid, norm, grad_normed, grad_middle):
         _, pull_in = jax.vjp(rms_norm, resid, norm)
@@ -956,13 +905,13 @@
     def row_sums(value):
         return lax.psum_scatter(value, "row", scatter_dimension=0, tiled=True)
 
-    def own_layer(first_value, second_value, *ahead):
+    def own_layer(first_value, second_value):
         keep = jnp.where(first, first_value, second_value)
         give = jnp.where(first, second_value, first_value).astype(HALF)
-        return keep.astype(FLOAT) + after(swapped(give), *ahead).astype(FLOAT)
+        return keep.astype(FLOAT), swapped(give)
 
     grad_middle, along, grad_norm_mid_1 = middle_backward(
-        gathered_sum(parts), grad_now, middle_1, mixed_1, norm_mids[1]
+        gathered_sum(parts, answers), grad_now, middle_1, mixed_1, norm_mids[1]
     )
     expert_grads_1, shared_grads_1 = weight_sums(
         rows_1,
@@ -974,25 +923,29 @@
         listed(kept_s_1),
         listed(grads_s_1),
     )
-    wide_mix, grad_in, grad_proj_1, grad_out_1, grad_tail_1, rest_1 = mixer_back(
+    home = [
+        home_part(scaling[1][index], answers[index], kept_s_1[index][2], shared[1])
+        for index in order
+    ]
+    _, grad_pre, to_proj, to_out, tail, rest_1 = mixer_back(
         1,
         grad_middle,
         along,
         rr_1,
         (wide_in_1, pre_1, y_1, scaled_1),
-        expert_grads_1,
-        False,
-    )
+        (expert_grads_1, home),
+    )
+    whole = line_product(grad_pre, proj[1])
+    given = half_to_give(*after(to_proj, whole))
+    given_out = half_to_give(*after(to_out, given))
+    grad_proj_1 = (*to_proj, swapped(given))
+    grad_out_1 = (*to_out, swapped(given_out))
+    grad_tail_1 = outer(after(wide_in_1, given_out), tail).astype(HALF)
+    grad_in = gathered_sum(line_blocks(whole), (given, given_out, grad_tail_1))
     grad_1, grad_norm_in_1 = resid_back(out_0, norm_ins[1], grad_in, grad_middle)
-    home = [
-        home_part(scaling[1][index], answers[index], kept_s_1[index][2], shared[1])
-        for index in order
-    ]
-    home = [after(part, wide_mix) for part in home]
-    out_1 = middle_1 + gathered_sum(to_blocks(home), grad_in)
     sums_1 = [half_to_keep(*after(made, grad_1)) for made in shared_grads_1]
 
-    grads_0, grads_s_0 = {}, {}
+    grads_0, grads_s_0, out_parts = {}, {}, []
 
     def expert_back_0(index, rows):
         grads_0[index], back = expert_backward(rows, kept_0[index], experts[0])
@@ -1002,18 +955,24 @@
         grads_s_0[index], part = shared_backward(block, kept_s_0[index], shared[0])
         return (part + outer(plain[0][index], result)).astype(HALF)
 
-    parts, grad_rows_0, grad_tokens_0 = through_experts(
-        grad_1.astype(HALF), scaling[0], expert_back_0, beside_back_0
-    )
-    sums_1 = [
-        *sums_1,
-        half_to_keep(*after(grad_out_1, parts)),
-        half_to_keep(*after(grad_proj_1, parts)),
-    ]
+    def aside_back_0(blocks):
+        sums_1.extend(half_to_keep(*after(made, blocks)) for made in (grad_out_1, grad_proj_1))
+        out_parts.extend(to_blocks(after(home, blocks)))
+        if groups() > 1:
+            out_parts[1:] = after(sent_home(out_parts), sums_1)
+        return out_parts[1:]
+
+    parts, grad_rows_0, grad_tokens_0, _ = through_experts(
+        grad_1.astype(HALF), scaling[0], expert_back_0, beside_back_0, aside_back_0
+    )
+    if groups() > 1:
+        out_1 = middle_1 + total_of(out_parts[0], out_parts[1:])
+    else:
+        out_1 = middle_1 + gathered_sum(out_parts)
+    sums_1 = [row_sums(value) for value in sums_1]
     grad_middle, along, grad_norm_mid_0 = middle_backward(
-        gathered_sum(parts, sums_1), grad_1, middle_0, mixed_0, norm_mids[0]
-    )
-    sums_1 = [row_sums(value) for value in sums_1]
+        gathered_sum(parts, out_1), grad_1, middle_0, mixed_0, norm_mids[0]
+    )
     expert_grads_0, shared_grads_0 = weight_sums(
         rows_0,
         grad_rows_0,
@@ -1024,46 +983,95 @@
         listed(kept_s_0),
         listed(grads_s_0),
     )
-    wide_mix, grad_in, grad_proj_0, grad_out_0, grad_tail_0, rest_0 = mixer_back(
+    expert_out = [own_layer(a, b) for a, b in zip(expert_grads_0, expert_grads_1)]
+    wide_mix, grad_pre, to_proj, to_out, tail, rest_0 = mixer_back(
         0,
         grad_middle,
         along,
         rr_0,
         (wide_in_0, pre_0, y_0, scaled_0),
-        expert_grads_0,
-        True,
+        [part[0] for part in expert_out],
     )
     sums_0 = [row_sums(half_to_keep(*after(made, wide_mix))) for made in shared_grads_0]
-    grad_0, grad_norm_in_0 = resid_back(tokens_now, norm_ins[0], grad_in, grad_middle)
-    sums_0 = [*sums_0, row_sums(grad_out_0), grad_proj_0]
-    expert_out = [
-        own_layer(a, b, grad_out_0) for a, b in zip(expert_grads_0, expert_grads_1)
+
+    given = half_to_give(*to_proj)
+    whole = line_product(after(grad_pre, given), proj[0])
+    given_out = half_to_give(*after(to_out, whole))
+    grad_tail_0 = outer(after(wide_in_0, given_out), tail).astype(HALF)
+    tail_keep, tail_other = own_layer(grad_tail_0, grad_tail_1)
+    wide_x = wide_tokens.astype(FLOAT)
+    wide_r = lax.rsqrt(jnp.mean(wide_x * wide_x, axis=1, keepdims=True) + EPS)
+    grad_norm_in_0 = jnp.sum(whole.astype(FLOAT) * wide_x * wide_r, axis=0)
+    smalls = (
+        (grad_norm_in_0, grad_norm_mid_0, *rest_0),
+        (grad_norm_in_1, grad_norm_mid_1, *rest_1),
+    )
+    shapes = [part.shape for part in smalls[0]]
+    small_keep, small_other = own_layer(flat(smalls[0]), flat(smalls[1]))
+    line_parts = line_blocks(whole)
+    if groups() > 1:
+        line_received = sent_home(line_parts)
+    to_proj, to_out, tail_own, small_own = after(
+        (
+            (*to_proj, swapped(given)),
+            (*to_out, swapped(given_out)),
+            (tail_keep, tail_other),
+            (small_keep, small_other),
+        ),
+        grad_tail_0,
+    )
+    proj_pieces = row_pieces(half_to_keep(*to_proj))
+    out_pieces = row_pieces(half_to_keep(*to_out))
+    tail_pieces = row_pieces((tail_own[0] + tail_own[1].astype(FLOAT)).astype(HALF))
+    vector = small_own[0] + small_own[1].astype(FLOAT)
+    proj_received, out_received, tail_received = [
+        row_received(pieces) for pieces in (proj_pieces, out_pieces, tail_pieces)
     ]
+    lines = [shifted(vector[None], "row", back) for back in range(n_row)]
+    expert_out = [keep + other.astype(FLOAT) for keep, other in after(expert_out, proj_pieces)]
+    if groups() > 1:
+        line_received, proj_received, out_received, tail_received, lines, sums_0 = after(
+            (line_received, proj_received, out_received, tail_received, lines, sums_0), expert_out
+        )
+        grad_in = total_of(line_parts[0], line_received)
+    else:
+        grad_in = gathered_sum(line_parts)
+    grad_proj_0 = total_of(proj_pieces[0], proj_received).astype(HALF)
+    grad_out_0 = total_of(out_pieces[0], out_received).astype(HALF)
+    tail = total_of(tail_pieces[0], tail_received).astype(HALF)
+    vector = jnp.sum(in_order(lines, "row"), axis=0)
+    grad_0, _ = resid_back(tokens_now, norm_ins[0], grad_in, grad_middle)
+    sums_0 = [*sums_0, grad_out_0, grad_proj_0]
 
     def own_halves(first_value, second_value):
         keep = jnp.where(first, first_value, second_value)
         give = jnp.where(first, second_value, first_value)
-        return pair(keep, swapped(give))
-
-    tail = row_total(row_pieces(own_layer(grad_tail_0, grad_tail_1).astype(HALF)))
-    state_grad = col_sum(tail[:, :state])
-    grad_shared, grad_down, grad_out, grad_ends = [own_halves(a, b) for a, b in zip(sums_0, sums_1)]
-    grad_out, grad_down = [jnp.concatenate(both, axis=1) for both in (grad_out, grad_down)]
-
-    smalls = (
-        (grad_norm_in_0, grad_norm_mid_0, *rest_0),
-        (grad_norm_in_1, grad_norm_mid_1, *rest_1),
-    )
-    shapes = [part.shape for part in smalls[0]]
-    vector = own_layer(flat(smalls[0]), flat(smalls[1]))
-    lines = [shifted(vector[None], "row", back) for back in range(n_row)]
-    vector = jnp.sum(in_order(lines, "row"), axis=0)
+        return keep, swapped(give)
+
+    def per_micro(first_value, second_value):
+        keep = jnp.where(first, first_value, second_value)
+        return keep, swapped(jnp.where(first, second_value, first_value).astype(HALF))
+
+    halves = [own_halves(a, b) for a, b in zip(sums_0, sums_1)]
+    outs, in_grads = per_micro(out_0, after(out_1, grad_in)), per_micro(grad_0, grad_1)
     common = 2 * width + conv_state.shape[1] * state
+    state_grad = tail[:, :state]
     if groups() > 1:
+        state_pieces = row_pieces(state_grad, "col")
+        state_received = row_received(state_pieces, "col")
         lines = [shifted(vector[None, :common], "col", back) for back in range(n_col)]
+        state_received, lines, halves, outs, in_grads = after(
+            (state_received, lines, halves, outs, in_grads)
+        )
+        state_grad = total_of(state_pieces[0], state_received).astype(HALF)
+        state_grad = in_order([shifted(state_grad, "col", back) for back in range(n_col)], "col")
         shared_sum = jnp.sum(in_order(lines, "col"), axis=0)
     else:
+        state_grad = lax.psum(state_grad, "col")
         shared_sum = lax.psum(vector[:common], "col")
+    halves = [pair(*half) for half in halves]
+    grad_shared, grad_down, grad_out, grad_ends = halves
+    grad_out, grad_down = [jnp.concatenate(both, axis=1) for both in (grad_out, grad_down)]
     (
         out_norm_in,
         out_norm_mid,
@@ -1073,17 +1081,15 @@
         out_step,
     ) = unflat(jnp.concatenate([shared_sum, vector[common:]]), shapes)
 
-    def per_micro(first_value, second_value, *ahead):
-        keep = jnp.where(first, first_value, second_value)
-        other = swapped(jnp.where(first, second_value, first_value).astype(HALF))
-        return jnp.stack(pair(keep, after(other, *ahead).astype(FLOAT)))[None]
+    def stacked(keep, other):
+        return jnp.stack(pair(keep, other.astype(FLOAT)))[None]
 
     def out(value):
         return value.astype(FLOAT)[None]
 
     return (
-        per_micro(out_0, out_1, grad_out_0),
-        per_micro(grad_0, grad_1),
+        stacked(*outs),
+        stacked(*in_grads),
         out_norm_in[None],
         out(grad_ends[0][:, :inner]),
         out(grad_ends[1][:, :inner]),

time: 1260 us -> 1260 us (level)
  matrix products: 211 us -> 228 us
  starting transfers between devices: 231 us -> 215 us
    all_to_all x7, waiting for transfers between devices: 158 us -> 71.1 us  [to_experts(): lax.all_to_all(rows.astype(HALF), 'row', split_axis=0, concat_axis=0, til...]
    reduce_scatter x7 -> x6, waiting for transfers between devices: 0.01 us -> 43.4 us  [row_sums(): return lax.psum_scatter(value, 'row', scatter_dimension=0, tiled=True)]
    ppermute x78 -> x84, waiting for transfers between devices: 385 us -> 420 us  [shifted(): lax.ppermute(block, axis, [(i, (i + distance) % count) for i in range(cou...]
    ppermute x6 -> x0, starting transfers between devices: 31.8 us -> none  [sent(): lax.ppermute(value, ('section', 'col'), [(at + i, at + (i - back) % count...]
    ppermute x78 -> x84, starting transfers between devices: 159 us -> 176 us  [shifted(): lax.ppermute(block, axis, [(i, (i + distance) % count) for i in range(cou...]
  transfers between devices with their start and end apart: 127 -> 126, of which waited for: 48 -> 49; matrix products, arithmetic and copies ran while one was open for 21% -> 21% of each run, Pallas kernels for 3% -> 3%
where the time goes in v6:
time: 1260 us; the launch traced here: 1250 us
  waiting for transfers between devices  566 us (45%)
  matrix products  228 us (18%)
  starting transfers between devices  215 us (17%)
  other arithmetic  70 us (6%)
  Pallas kernels  60.9 us (5%)
  blocking collectives  52.3 us (4%)
  local copies, waits for them, and re-layouts  39.8 us (3%)
  between operations  17.8 us (1%)
    ppermute x84, waiting for transfers between devices, shifted(): lax.ppermute(block, axis, [(i, (i + distance) % count) for i in range(cou...  420 us
    ppermute x84, starting transfers between devices, shifted(): lax.ppermute(block, axis, [(i, (i + distance) % count) for i in range(cou...  176 us
    dot_general x28, matrix products, outer(): lax.dot_general(left, right, (((0,), (0,)), ((), ())), preferred_element_...  92.6 us
    dot_general x23, matrix products, project(): return jnp.dot(left, right, preferred_element_type=FLOAT)  77.3 us
    all_to_all x7, waiting for transfers between devices, to_experts(): lax.all_to_all(rows.astype(HALF), 'row', split_axis=0, concat_axis=0, til...  71.1 us
    dot_general x18, matrix products, project_back(): lax.dot_general(left, right, (((1,), (1,)), ((), ())), preferred_element_...  58.1 us
    all_to_all x1, blocking collectives, to_experts(): lax.all_to_all(rows.astype(HALF), 'row', split_axis=0, concat_axis=0, til...  52.3 us
    reduce_scatter x6, waiting for transfers between devices, row_sums(): return lax.psum_scatter(value, 'row', scatter_dimension=0, tiled=True)  43.4 us
  transfers between devices with their start and end apart: 126, of which 49 were waited for; matrix products, arithmetic and copies ran while one was open for 21% of the time, Pallas kernels for 3%

profile of v6, /device:TPU:0, one launch (start us, length us, event | category | flops | bytes accessed | tf_op | source)
XLA Modules:
  0.0 1250.4 jit_solution(12351870815492217511)
XLA Ops:
  31.8 16.4 %collective-permute-done.1 = bf16[128,1536]{1,0:T(8,128)(2,1)S(1)} collective-permute-done((bf16[128,1536]{1,0:T(8,128)(2,1)S(1)}, bf16[128,1536]{1,0:T(8,128)(2,1)S(1)}, u32[]{:S(2)}, u32[]{:S(2)}) %collective-permute-start.1) | collective-permute-done | bytes 393248 | tf_op jit(solution)/shard_map/ppermute | solution.py:26
  69.9 12.4 mixer_forward.2
  90.0 12.9 %all-gather.18.cloned.1.call-done = bf16[1,3072,768]{2,1,0:T(8,128)(2,1)} async-done(((bf16[1,384,768]{2,1,0:T(8,128)(2,1)}), bf16[1,3072,768]{2,1,0:T(8,128)(2,1)}) %all-gather.18.cloned.1.call-update) | async-done | bytes 4718608 | tf_op jit(solution)/shard_map/all_gather | solution.py:774
  123.6 22.6 %collective-permute-done.9 = bf16[128,1536]{1,0:T(8,128)(2,1)S(1)} collective-permute-done((bf16[128,1536]{1,0:T(8,128)(2,1)}, bf16[128,1536]{1,0:T(8,128)(2,1)S(1)}, u32[]{:S(2)}, u32[]{:S(2)}) %collective-permute-start.9) | collective-permute-done | bytes 393248 | tf_op jit(solution)/shard_map/ppermute | solution.py:26
  162.8 15.1 %collective-permute-done.16 = bf16[128,1536]{1,0:T(8,128)(2,1)S(1)} collective-permute-done((bf16[128,1536]{1,0:T(8,128)(2,1)S(1)}, bf16[128,1536]{1,0:T(8,128)(2,1)S(1)}, u32[]{:S(2)}, u32[]{:S(2)}) %collective-permute-start.16) | collective-permute-done | bytes 393248 | tf_op jit(solution)/shard_map/ppermute | solution.py:26
  210.0 15.1 %collective-permute-done.19 = bf16[128,1536]{1,0:T(8,128)(2,1)S(1)} collective-permute-done((bf16[128,1536]{1,0:T(8,128)(2,1)S(1)}, bf16[128,1536]{1,0:T(8,128)(2,1)S(1)}, u32[]{:S(2)}, u32[]{:S(2)}) %collective-permute-start.19) | collective-permute-done | bytes 393248 | tf_op jit(solution)/shard_map/ppermute | solution.py:26
  241.2 52.3 %all_to_all.96 = bf16[4,256,1536]{2,1,0:T(8,128)(2,1)} all-to-all(bf16[4,256,1536]{2,1,0:T(8,128)(2,1)S(1)} %bitcast.267), channel_id=1, replica_groups=mesh['section'=2,'row'=4,'col'=4] {'row'}, dimensions={0} | all-to-all | bytes 6291456 | tf_op jit(solution)/shard_map/all_to_all | solution.py:145
  321.4 23.9 %collective-permute-done.22 = bf16[128,1536]{1,0:T(8,128)(2,1)S(1)} collective-permute-done((bf16[128,1536]{1,0:T(8,128)(2,1)S(1)}, bf16[128,1536]{1,0:T(8,128)(2,1)S(1)}, u32[]{:S(2)}, u32[]{:S(2)}) %collective-permute-start.22) | collective-permute-done | bytes 393248 | tf_op jit(solution)/shard_map/ppermute | solution.py:26
  359.5 10.0 collective-permute-done.24
  369.5 13.4 %collective-permute-done.25 = bf16[128,1536]{1,0:T(8,128)(2,1)S(1)} collective-permute-done((bf16[128,1536]{1,0:T(8,128)(2,1)S(1)}, bf16[128,1536]{1,0:T(8,128)(2,1)S(1)}, u32[]{:S(2)}, u32[]{:S(2)}) %collective-permute-start.25) | collective-permute-done | bytes 393248 | tf_op jit(solution)/shard_map/ppermute | solution.py:26
  391.8 11.9 mixer_forward.3
  431.9 23.9 %collective-permute-done.31 = bf16[128,1536]{1,0:T(8,128)(2,1)S(1)} collective-permute-done((bf16[128,1536]{1,0:T(8,128)(2,1)S(1)}, bf16[128,1536]{1,0:T(8,128)(2,1)S(1)}, u32[]{:S(2)}, u32[]{:S(2)}) %collective-permute-start.31) | collective-permute-done | bytes 393248 | tf_op jit(solution)/shard_map/ppermute | solution.py:26
  470.4 13.0 %collective-permute-done.34 = bf16[128,1536]{1,0:T(8,128)(2,1)S(1)} collective-permute-done((bf16[128,1536]{1,0:T(8,128)(2,1)S(1)}, bf16[128,1536]{1,0:T(8,128)(2,1)S(1)}, u32[]{:S(2)}, u32[]{:S(2)}) %collective-permute-start.34) | collective-permute-done | bytes 393248 | tf_op jit(solution)/shard_map/ppermute | solution.py:26
  497.1 31.0 %all-to-all-done.3 = bf16[4,256,1536]{2,1,0:T(8,128)(2,1)} async-done(((bf16[4,256,1536]{2,1,0:T(8,128)(2,1)}), bf16[4,256,1536]{2,1,0:T(8,128)(2,1)}, u32[]{:S(2)}, u32[]{:S(2)}) %all-to-all-start.3) | async-done | bytes 3145760 | tf_op jit(solution)/shard_map/all_to_all | solution.py:145
  561.9 21.9 %all-to-all-done.4 = bf16[4,256,1536]{2,1,0:T(8,128)(2,1)} async-done(((bf16[4,256,1536]{2,1,0:T(8,128)(2,1)}), bf16[4,256,1536]{2,1,0:T(8,128)(2,1)}, u32[]{:S(2)}, u32[]{:S(2)}) %all-to-all-start.4) | async-done | bytes 3145760 | tf_op jit(solution)/shard_map/all_to_all | solution.py:145
  628.0 10.7 collective-permute-done.36
  638.7 17.4 %collective-permute-done.37 = bf16[128,1536]{1,0:T(8,128)(2,1)} collective-permute-done((bf16[128,1536]{1,0:T(8,128)(2,1)S(1)}, bf16[128,1536]{1,0:T(8,128)(2,1)}, u32[]{:S(2)}, u32[]{:S(2)}) %collective-permute-start.37) | collective-permute-done | bytes 393248 | tf_op jit(solution)/shard_map/ppermute | solution.py:26
  671.0 20.3 %collective-permute-done.42 = f32[128,2]{0,1:T(2,128)S(1)} collective-permute-done((f32[128,2]{0,1:T(2,128)S(1)}, f32[128,2]{0,1:T(2,128)S(1)}, u32[]{:S(2)}, u32[]{:S(2)}) %collective-permute-start.42) | collective-permute-done | bytes 1056 | tf_op jit(solution)/shard_map/ppermute | solution.py:26
  702.7 18.3 %mixer_backward.2 = (bf16[512,1024]{1,0:T(8,128)(2,1)S(1)}, bf16[512,1024]{1,0:T(8,128)(2,1)S(1)}, f32[2,768]{1,0:T(2,128)S(1)}, f32[4,768]{1,0:T(4,128)S(1)}, f...) custom-call(f32[512,1024]{1,0:T(8,128)} %copy-done.3, f32[512,1024]{1,0:T(8,128)} %fusion.16.pre_other_in_ref, ...), custom_call_target="tpu_custom_call" | custom-call | tf_op jit(solution)/shard_map/mixer_backward/pallas_call | solution.py:547
  742.5 22.4 %collective-permute-done.46 = bf16[128,1536]{1,0:T(8,128)(2,1)S(1)} collective-permute-done((bf16[128,1536]{1,0:T(8,128)(2,1)S(1)}, bf16[128,1536]{1,0:T(8,128)(2,1)S(1)}, u32[]{:S(2)}, u32[]{:S(2)}) %collective-permute-start.46) | collective-permute-done | bytes 393248 | tf_op jit(solution)/shard_map/ppermute | solution.py:26
  779.8 14.0 %collective-permute-done.49 = bf16[128,1536]{1,0:T(8,128)(2,1)S(1)} collective-permute-done((bf16[128,1536]{1,0:T(8,128)(2,1)S(1)}, bf16[128,1536]{1,0:T(8,128)(2,1)S(1)}, u32[]{:S(2)}, u32[]{:S(2)}) %collective-permute-start.49) | collective-permute-done | bytes 393248 | tf_op jit(solution)/shard_map/ppermute | solution.py:26
  812.9 10.9 collective-permute-start.51
  833.6 24.8 %collective-permute-done.52 = bf16[128,1536]{1,0:T(8,128)(2,1)} collective-permute-done((bf16[128,1536]{1,0:T(8,128)(2,1)}, bf16[128,1536]{1,0:T(8,128)(2,1)}, u32[]{:S(2)}, u32[]{:S(2)}) %collective-permute-start.52) | collective-permute-done | bytes 393248 | tf_op jit(solution)/shard_map/ppermute | solution.py:26
  893.9 18.2 %all-to-all-done.7 = bf16[4,256,1536]{2,1,0:T(8,128)(2,1)} async-done(((bf16[4,256,1536]{2,1,0:T(8,128)(2,1)}), bf16[4,256,1536]{2,1,0:T(8,128)(2,1)}, u32[]{:S(2)}, u32[]{:S(2)}) %all-to-all-start.7) | async-done | bytes 3145760 | tf_op jit(solution)/shard_map/all_to_all | solution.py:145
  928.8 25.5 %collective-permute-done.59 = bf16[128,1536]{1,0:T(8,128)(2,1)S(1)} collective-permute-done((bf16[128,1536]{1,0:T(8,128)(2,1)S(1)}, bf16[128,1536]{1,0:T(8,128)(2,1)S(1)}, u32[]{:S(2)}, u32[]{:S(2)}) %collective-permute-start.59) | collective-permute-done | bytes 393248 | tf_op jit(solution)/shard_map/ppermute | solution.py:26
  970.8 14.4 %collective-permute-done.62 = bf16[128,1536]{1,0:T(8,128)(2,1)S(1)} collective-permute-done((bf16[128,1536]{1,0:T(8,128)(2,1)S(1)}, bf16[128,1536]{1,0:T(8,128)(2,1)S(1)}, u32[]{:S(2)}, u32[]{:S(2)}) %collective-permute-start.62) | collective-permute-done | bytes 393248 | tf_op jit(solution)/shard_map/ppermute | solution.py:26
  1011.7 18.3 %mixer_backward.3 = (bf16[512,1024]{1,0:T(8,128)(2,1)S(1)}, bf16[512,1024]{1,0:T(8,128)(2,1)S(1)}, f32[2,768]{1,0:T(2,128)S(1)}, f32[4,768]{1,0:T(4,128)S(1)}, f...) custom-call(f32[512,1024]{1,0:T(8,128)} %copy-done.2, f32[512,1024]{1,0:T(8,128)} %fusion.24.pre_other_in_ref, ...), custom_call_target="tpu_custom_call" | custom-call | tf_op jit(solution)/shard_map/mixer_backward/pallas_call | solution.py:547
  1072.2 14.9 %collective-permute-done.72 = bf16[128,1536]{1,0:T(8,128)(2,1)S(1)} collective-permute-done((bf16[128,1536]{1,0:T(8,128)(2,1)S(1)}, bf16[128,1536]{1,0:T(8,128)(2,1)S(1)}, u32[]{:S(2)}, u32[]{:S(2)}) %collective-permute-start.72) | collective-permute-done | bytes 393248 | tf_op jit(solution)/shard_map/ppermute | solution.py:26
  1110.3 15.6 %collective-permute-start.81 = (bf16[384,384]{1,0:T(8,128)(2,1)}, bf16[384,384]{1,0:T(8,128)(2,1)}, u32[]{:S(2)}, u32[]{:S(2)}) collective-permute-start(bf16[384,384]{1,0:T(8,128)(2,1)} %get-tuple-element.560), channel_id=1, source_target_pairs={{0,8},{4,12},{8,0},{12,4},{1,9},{5,13},{9,1},{13,5},{2,10},{6,14},... | collective-permute-start | bytes 884744 | tf_op jit(solution)/shard_map/ppermute | solution.py:26
  1129.5 17.4 %collective-permute-done.81 = bf16[384,384]{1,0:T(8,128)(2,1)} collective-permute-done((bf16[384,384]{1,0:T(8,128)(2,1)}, bf16[384,384]{1,0:T(8,128)(2,1)}, u32[]{:S(2)}, u32[]{:S(2)}) %collective-permute-start.81) | collective-permute-done | bytes 294944 | tf_op jit(solution)/shard_map/ppermute | solution.py:26
  1165.6 20.1 %reduce-scatter.17.cloned.1.call-done = bf16[384,768]{1,0:T(8,128)(2,1)} async-done(((bf16[1536,768]{1,0:T(8,128)(2,1)}), bf16[384,768]{1,0:T(8,128)(2,1)}) %reduce-scatter.17.cloned.1.call-update) | async-done | bytes 589840 | tf_op jit(solution)/shard_map/reduce_scatter | solution.py:906
  1189.8 23.2 %reduce-scatter.13.cloned.1.call-done = bf16[384,128]{1,0:T(8,128)(2,1)} async-done(((bf16[1536,128]{1,0:T(8,128)(2,1)}), bf16[384,128]{1,0:T(8,128)(2,1)}) %reduce-scatter.13.cloned.1.call-update) | async-done | bytes 98320 | tf_op jit(solution)/shard_map/reduce_scatter | solution.py:906
  (978 shorter events, 630.3 us)
Async XLA Ops:
  7.2 54.9 %all-gather.12.cloned.1.call-start = ((), (), s32[]{:S(2)}) async-start(), calls=%async_computation.14 | async-start | bytes 7077888 | tf_op jit(solution)/shard_map/all_gather | solution.py:768
  13.8 89.1 %all-gather.18.cloned.1.call-start = ((), (), s32[]{:S(2)}) async-start(), calls=%async_computation.23 | async-start | bytes 5308416 | tf_op jit(solution)/shard_map/all_gather | solution.py:774
  14.6 211.3 %all-gather.20.cloned.1.call-start = ((), (), s32[]{:S(2)}) async-start(), calls=%async_computation.24 | async-start | bytes 4718592 | tf_op jit(solution)/shard_map/all_gather | solution.py:778
  15.5 215.8 %all-gather.22.cloned.1.call-start = ((), (), s32[]{:S(2)}) async-start(), calls=%async_computation.25 | async-start | bytes 4718592 | tf_op jit(solution)/shard_map/all_gather | solution.py:779
  16.1 221.5 %all-gather.24.cloned.1.call-start = ((), (), s32[]{:S(2)}) async-start(), calls=%async_computation.26 | async-start | bytes 4718592 | tf_op jit(solution)/shard_map/all_gather | solution.py:780
  16.6 276.9 %all-gather.14.cloned.1.call-start = ((), (), s32[]{:S(2)}) async-start(), calls=%async_computation.15 | async-start | bytes 5308416 | tf_op jit(solution)/shard_map/all_gather | solution.py:774
  181.5 44.4 %all-to-all-start = ((bf16[4,256,1536]{2,1,0:T(8,128)(2,1)}), bf16[4,256,1536]{2,1,0:T(8,128)(2,1)}, u32[]{:S(2)}, u32[]{:S(2)}) async-start(bf16[4,256,1536]{2,1,0:T(8,128)(2,1)} %bitcast.264), calls=%async_computation | async-start | bytes 6291456 | tf_op jit(solution)/shard_map/all_to_all | solution.py:145
  186.3 198.2 %all-gather.16.cloned.1.call-start = ((), (), s32[]{:S(2)}) async-start(), calls=%async_computation.16 | async-start | bytes 7077888 | tf_op jit(solution)/shard_map/all_gather | solution.py:768
  350.7 54.2 %all-to-all-start.2 = ((bf16[4,256,1536]{2,1,0:T(8,128)(2,1)}), bf16[4,256,1536]{2,1,0:T(8,128)(2,1)}, u32[]{:S(2)}, u32[]{:S(2)}) async-start(bf16[4,256,1536]{2,1,0:T(8,128)(2,1)} %bitcast.263), calls=%async_computation.2 | async-start | bytes 6291456 | tf_op jit(solution)/shard_map/all_to_all | solution.py:145
  486.9 41.2 %all-to-all-start.3 = ((bf16[4,256,1536]{2,1,0:T(8,128)(2,1)}), bf16[4,256,1536]{2,1,0:T(8,128)(2,1)}, u32[]{:S(2)}, u32[]{:S(2)}) async-start(bf16[4,256,1536]{2,1,0:T(8,128)(2,1)} %bitcast.266), calls=%async_computation.3 | async-start | bytes 6291456 | tf_op jit(solution)/shard_map/all_to_all | solution.py:145
  543.3 40.5 %all-to-all-start.4 = ((bf16[4,256,1536]{2,1,0:T(8,128)(2,1)}), bf16[4,256,1536]{2,1,0:T(8,128)(2,1)}, u32[]{:S(2)}, u32[]{:S(2)}) async-start(bf16[4,256,1536]{2,1,0:T(8,128)(2,1)} %bitcast.260), calls=%async_computation.4 | async-start | bytes 6291456 | tf_op jit(solution)/shard_map/all_to_all | solution.py:145
  591.9 64.2 %all-to-all-start.5 = ((bf16[4,256,1536]{2,1,0:T(8,128)(2,1)}), bf16[4,256,1536]{2,1,0:T(8,128)(2,1)}, u32[]{:S(2)}, u32[]{:S(2)}) async-start(bf16[4,256,1536]{2,1,0:T(8,128)(2,1)} %bitcast.262), calls=%async_computation.5 | async-start | bytes 6291456 | tf_op jit(solution)/shard_map/all_to_all | solution.py:145
  611.5 44.6 %collective-permute-start.38 = (bf16[128,1536]{1,0:T(8,128)(2,1)S(1)}, bf16[128,1536]{1,0:T(8,128)(2,1)S(1)}, u32[]{:S(2)}, u32[]{:S(2)}) collective-permute-start(bf16[128,1536]{1,0:T(8,128)(2,1)S(1)} %copy-done.142), channel_id=1, source_target_pairs={{0,1},{1,2},{2,3},{3,0},{4,5},{5,6},{6,7},{7,4},{8,9},{9,10},{10,1... | collective-permute-start | bytes 1179656 | tf_op jit(solution)/shard_map/ppermute | solution.py:26
  779.8 48.1 %collective-permute-start.57 = (bf16[1536,768]{1,0:T(8,128)(2,1)}, bf16[1536,768]{1,0:T(8,128)(2,1)}, u32[]{:S(2)}, u32[]{:S(2)}) collective-permute-start(bf16[1536,768]{1,0:T(8,128)(2,1)} %convolution_convert_fusion.7), channel_id=1, source_target_pairs={{0,16},{16,0},{1,17},{17,1},{2,18},{18,2},{3,19},{19,3},{4,20},{20... | collective-permute-start | bytes 7077896 | tf_op jit(solution)/shard_map/ppermute | solution.py:30
  797.4 61.0 %all-to-all-start.6 = ((bf16[4,256,1536]{2,1,0:T(8,128)(2,1)}), bf16[4,256,1536]{2,1,0:T(8,128)(2,1)}, u32[]{:S(2)}, u32[]{:S(2)}) async-start(bf16[4,256,1536]{2,1,0:T(8,128)(2,1)} %bitcast.261), calls=%async_computation.6 | async-start | bytes 6291456 | tf_op jit(solution)/shard_map/all_to_all | solution.py:145
  870.9 41.2 %all-to-all-start.7 = ((bf16[4,256,1536]{2,1,0:T(8,128)(2,1)}), bf16[4,256,1536]{2,1,0:T(8,128)(2,1)}, u32[]{:S(2)}, u32[]{:S(2)}) async-start(bf16[4,256,1536]{2,1,0:T(8,128)(2,1)} %bitcast.259), calls=%async_computation.7 | async-start | bytes 6291456 | tf_op jit(solution)/shard_map/all_to_all | solution.py:145
  875.5 254.0 %reduce-scatter.9.cloned.1.call-start = ((), (), s32[]{:S(2)}) async-start(), calls=%async_computation.18 | async-start | bytes 491520 | tf_op jit(solution)/shard_map/reduce_scatter | solution.py:906
  879.8 108.7 %collective-permute-start.86 = (bf16[1536,256]{1,0:T(8,128)(2,1)}, bf16[1536,256]{1,0:T(8,128)(2,1)}, u32[]{:S(2)}, u32[]{:S(2)}) collective-permute-start(bf16[1536,256]{1,0:T(8,128)(2,1)} %convolution_convert_fusion.20), channel_id=1, source_target_pairs={{0,16},{16,0},{1,17},{17,1},{2,18},{18,2},{3,19},{19,3},{4,20},{20... | collective-permute-start | bytes 2359304 | tf_op jit(solution)/shard_map/ppermute | solution.py:30
  881.2 104.8 %collective-permute-start.87 = (bf16[1536,128]{1,0:T(8,128)(2,1)}, bf16[1536,128]{1,0:T(8,128)(2,1)}, u32[]{:S(2)}, u32[]{:S(2)}) collective-permute-start(bf16[1536,128]{1,0:T(8,128)(2,1)} %convolution_convert_fusion.22), channel_id=1, source_target_pairs={{0,16},{16,0},{1,17},{17,1},{2,18},{18,2},{3,19},{19,3},{4,20},{20... | collective-permute-start | bytes 1179656 | tf_op jit(solution)/shard_map/ppermute | solution.py:30
  988.5 141.0 %reduce-scatter.7.cloned.1.call-start = ((), (), s32[]{:S(2)}) async-start(), calls=%async_computation.17 | async-start | bytes 983040 | tf_op jit(solution)/shard_map/reduce_scatter | solution.py:906
  991.8 169.0 %reduce-scatter.15.cloned.1.call-start = ((), (), s32[]{:S(2)}) async-start(), calls=%async_computation.21 | async-start | bytes 1474560 | tf_op jit(solution)/shard_map/reduce_scatter | solution.py:906
  992.4 171.5 %reduce-scatter.11.cloned.1.call-start = ((), (), s32[]{:S(2)}) async-start(), calls=%async_computation.19 | async-start | bytes 983040 | tf_op jit(solution)/shard_map/reduce_scatter | solution.py:906
  993.1 192.6 %reduce-scatter.17.cloned.1.call-start = ((), (), s32[]{:S(2)}) async-start(), calls=%async_computation.22 | async-start | bytes 2949120 | tf_op jit(solution)/shard_map/reduce_scatter | solution.py:906
  994.4 218.6 %reduce-scatter.13.cloned.1.call-start = ((), (), s32[]{:S(2)}) async-start(), calls=%async_computation.20 | async-start | bytes 491520 | tf_op jit(solution)/shard_map/reduce_scatter | solution.py:906
  1093.9 53.2 %collective-permute-start.74 = (bf16[384,768]{1,0:T(8,128)(2,1)}, bf16[384,768]{1,0:T(8,128)(2,1)S(1)}, u32[]{:S(2)}, u32[]{:S(2)}) collective-permute-start(bf16[384,768]{1,0:T(8,128)(2,1)} %get-tuple-element.522), channel_id=1, source_target_pairs={{0,4},{4,8},{8,12},{12,0},{1,5},{5,9},{9,13},{13,1},{2,6},{6,10},{... | collective-permute-start | bytes 1769480 | tf_op jit(solution)/shard_map/ppermute | solution.py:26
  1102.2 44.8 %collective-permute-start.75 = (bf16[384,768]{1,0:T(8,128)(2,1)}, bf16[384,768]{1,0:T(8,128)(2,1)}, u32[]{:S(2)}, u32[]{:S(2)}) collective-permute-start(bf16[384,768]{1,0:T(8,128)(2,1)} %get-tuple-element.521), channel_id=1, source_target_pairs={{0,8},{4,12},{8,0},{12,4},{1,9},{5,13},{9,1},{13,5},{2,10},{6,14},... | collective-permute-start | bytes 1769480 | tf_op jit(solution)/shard_map/ppermute | solution.py:26
  1108.6 39.3 %collective-permute-start.76 = (bf16[384,768]{1,0:T(8,128)(2,1)}, bf16[384,768]{1,0:T(8,128)(2,1)}, u32[]{:S(2)}, u32[]{:S(2)}) collective-permute-start(bf16[384,768]{1,0:T(8,128)(2,1)} %get-tuple-element.520), channel_id=1, source_target_pairs={{0,12},{4,0},{8,4},{12,8},{1,13},{5,1},{9,5},{13,9},{2,14},{6,2},{... | collective-permute-start | bytes 1769480 | tf_op jit(solution)/shard_map/ppermute | solution.py:26
  1148.5 66.1 %collective-permute-start.94 = (f32[1,4096]{1,0:T(1,128)S(1)}, f32[1,4096]{1,0:T(1,128)S(1)}, u32[]{:S(2)}, u32[]{:S(2)}) collective-permute-start(f32[1,4096]{1,0:T(1,128)S(1)} %bitcast.289), channel_id=1, source_target_pairs={{0,1},{1,2},{2,3},{3,0},{4,5},{5,6},{6,7},{7,4},{8,9},{9,10},{10,1... | collective-permute-start | bytes 49160 | tf_op jit(solution)/shard_map/ppermute | solution.py:26
  1148.5 69.4 %collective-permute-start.95 = (f32[1,4096]{1,0:T(1,128)S(1)}, f32[1,4096]{1,0:T(1,128)S(1)}, u32[]{:S(2)}, u32[]{:S(2)}) collective-permute-start(f32[1,4096]{1,0:T(1,128)S(1)} %bitcast.290), channel_id=1, source_target_pairs={{0,2},{1,3},{2,0},{3,1},{4,6},{5,7},{6,4},{7,5},{8,10},{9,11},{10,... | collective-permute-start | bytes 49160 | tf_op jit(solution)/shard_map/ppermute | solution.py:26
  1148.6 69.3 %collective-permute-start.96 = (f32[1,4096]{1,0:T(1,128)S(1)}, f32[1,4096]{1,0:T(1,128)}, u32[]{:S(2)}, u32[]{:S(2)}) collective-permute-start(f32[1,4096]{1,0:T(1,128)S(1)} %bitcast.291), channel_id=1, source_target_pairs={{0,3},{1,0},{2,1},{3,2},{4,7},{5,4},{6,5},{7,6},{8,11},{9,8},{10,9... | collective-permute-start | bytes 49160 | tf_op jit(solution)/shard_map/ppermute | solution.py:26
  1157.5 61.0 %collective-permute-start.91 = (bf16[96,256]{1,0:T(8,128)(2,1)}, bf16[96,256]{1,0:T(8,128)(2,1)}, u32[]{:S(2)}, u32[]{:S(2)}) collective-permute-start(bf16[96,256]{1,0:T(8,128)(2,1)} %get-tuple-element.598), channel_id=1, source_target_pairs={{0,1},{1,2},{2,3},{3,0},{4,5},{5,6},{6,7},{7,4},{8,9},{9,10},{10,1... | collective-permute-start | bytes 147464 | tf_op jit(solution)/shard_map/ppermute | solution.py:26
  1158.2 60.3 %collective-permute-start.92 = (bf16[96,256]{1,0:T(8,128)(2,1)}, bf16[96,256]{1,0:T(8,128)(2,1)}, u32[]{:S(2)}, u32[]{:S(2)}) collective-permute-start(bf16[96,256]{1,0:T(8,128)(2,1)} %get-tuple-element.597), channel_id=1, source_target_pairs={{0,2},{1,3},{2,0},{3,1},{4,6},{5,7},{6,4},{7,5},{8,10},{9,11},{10,... | collective-permute-start | bytes 147464 | tf_op jit(solution)/shard_map/ppermute | solution.py:26
  (323 other events, 5058.2 us)
Sparse Core Ops, SparseCore 0:
  13.9 48.1 all-gather.11
  64.0 38.9 all-gather.17
  104.5 12.1 all-gather.19
  118.1 13.2 all-gather.21
  132.8 13.2 all-gather.23
  148.4 40.0 all-gather.13
  293.7 50.7 all-gather.15
  988.6 30.3 reduce-scatter.8
  1021.9 26.0 reduce-scatter.6
  1051.4 29.2 reduce-scatter.14
  1083.6 48.5 reduce-scatter.10
  1135.1 50.5 reduce-scatter.16
  1188.5 24.4 reduce-scatter.12

commit v7 on v6

--- a/solution.py
+++ b/solution.py
@@ -62,87 +62,71 @@
     return sigma * (1.0 + value * (1.0 - sigma))
 
 
-def groups():
+def spread(block):
     count = lax.axis_size("col")
-    return count if count <= 4 else 1
-
-
-def chunks():
-    return [tuple(range(groups()))]
-
-
-def spread(block, meanwhile=()):
-    if groups() == 1:
-        return [lax.all_gather(block, "col", axis=0, tiled=True)]
-    received = [shifted(block, "col", back) for back in range(1, groups())]
-    return [block, *after(received, meanwhile)]
-
-
-def joined(blocks):
-    return blocks[0] if len(blocks) == 1 else jnp.concatenate(blocks, axis=0)
-
-
-def in_order(blocks, axis):
-    count = len(blocks)
-    if count == 1:
-        return blocks[0]
-    rows = blocks[0].shape[0]
-    line = jnp.concatenate(blocks[::-1] + blocks[:0:-1], axis=0)
-    start = (count - 1 - lax.axis_index(axis)) * rows
-    return lax.dynamic_slice_in_dim(line, start, count * rows, axis=0)
-
-
-def sent_home(parts):
-    return [shifted(part, "col", -back) for back, part in enumerate(parts) if back]
-
-
-def gathered_sum(parts, meanwhile=()):
-    if len(parts) == 1:
-        return lax.psum_scatter(parts[0], "col", scatter_dimension=0, tiled=True).astype(FLOAT)
-    return total_of(parts[0], after(sent_home(parts), meanwhile))
-
-
-def total_of(own, received):
-    return sum([part.astype(FLOAT) for part in received], own.astype(FLOAT))
-
-
-def block_of(values, back):
-    rows = values.shape[0] // groups()
-    return values[back * rows : (back + 1) * rows]
-
-
-def turn():
-    place = lax.axis_index("col") if groups() > 1 else jnp.int32(0)
-    return place.astype(jnp.int32).reshape(1)
-
-
-def route_tables(blocks, top, capacity, layers):
+    if count > 4:
+        return lax.all_gather(block, "col", axis=0, tiled=True)
+    return exchanged(jnp.tile(block, (count, 1)), "col")
+
+
+def exchanged(rows, axis):
+    return lax.all_to_all(rows, axis, split_axis=0, concat_axis=0, tiled=True)
+
+
+def summed(rows, axis):
+    count = lax.axis_size(axis)
+    rows = rows.reshape(count, rows.shape[0] // count, rows.shape[1])
+    return sum(rows[index].astype(FLOAT) for index in range(count))
+
+
+def sent_home(rows):
+    if lax.axis_size("col") > 4:
+        return lax.psum_scatter(rows, "col", scatter_dimension=0, tiled=True)
+    return exchanged(rows, "col")
+
+
+def added_up(received):
+    if lax.axis_size("col") > 4:
+        return received.astype(FLOAT)
+    return summed(received, "col")
+
+
+def gathered_sum(rows, meanwhile=()):
+    return added_up(after(sent_home(rows), meanwhile))
+
+
+def as_halves(columns):
+    high = lax.reduce_precision(columns, 8, 7)
+    both = jnp.concatenate([high, columns - high], axis=1).astype(HALF)
+    return jnp.pad(both, ((0, 0), (0, LANES - both.shape[1])))
+
+
+def from_halves(tile, count):
+    return tile[:, :count].astype(FLOAT) + tile[:, count : 2 * count].astype(FLOAT)
+
+
+def route_tables(meta, top, capacity, layers):
     n_row, n_col = lax.axis_size("row"), lax.axis_size("col")
     experts = (jnp.arange(n_row) * n_col + lax.axis_index("col")).astype(FLOAT)
-    tables = [[] for _ in range(layers)]
-    for chunk in chunks():
-        now = joined([blocks[back] for back in chunk])
-        count = now.shape[0]
-        slots = len(chunk) * (n_col // groups()) * capacity
-        now = now.reshape(count, layers, 2, top).transpose(1, 2, 3, 0)
-        match = now[:, None, 0] == experts[None, :, None, None]
-        hit = jnp.any(match, axis=2)
-        weight = jnp.sum(jnp.where(match, now[:, None, 1], 0.0), axis=2)
-        order = jnp.arange(count, dtype=jnp.int32)
-        triangle = (order[:, None] <= order[None, :]).astype(HALF)
-        place = project(hit.astype(HALF).reshape(-1, count), triangle).reshape(hit.shape)
-        slot = jnp.arange(1, slots + 1, dtype=jnp.int32).astype(FLOAT)
-        chosen = (place[:, :, None, :] == slot[:, None]) & hit[:, :, None, :]
-        shape = (layers, n_row * slots, count)
-        plain = chosen.astype(HALF).reshape(shape)
-        scaled = jnp.where(chosen, weight[:, :, None, :], 0.0).astype(HALF).reshape(shape)
-        for s in range(layers):
-            tables[s].append((plain[s], scaled[s]))
-    return tables
+    count = meta.shape[0]
+    slots = n_col * capacity
+    meta = meta.reshape(count, layers, 2, top).transpose(1, 2, 3, 0)
+    match = meta[:, None, 0] == experts[None, :, None, None]
+    hit = jnp.any(match, axis=2)
+    weight = jnp.sum(jnp.where(match, meta[:, None, 1], 0.0), axis=2)
+    order = jnp.arange(count, dtype=jnp.int32)
+    triangle = (order[:, None] <= order[None, :]).astype(HALF)
+    place = project(hit.astype(HALF).reshape(-1, count), triangle).reshape(hit.shape)
+    slot = jnp.arange(1, slots + 1, dtype=jnp.int32).astype(FLOAT)
+    chosen = (place[:, :, None, :] == slot[:, None]) & hit[:, :, None, :]
+    shape = (layers, n_row * slots, count)
+    plain = chosen.astype(HALF).reshape(shape)
+    scaled = jnp.where(chosen, weight[:, :, None, :], 0.0).astype(HALF).reshape(shape)
+    return [(plain[s], scaled[s]) for s in range(layers)]
 
 
 def to_experts(rows):
-    return lax.all_to_all(rows.astype(HALF), "row", split_axis=0, concat_axis=0, tiled=True)
+    return exchanged(rows.astype(HALF), "row")
 
 
 def summed_rows(values, reverse):
@@ -201,41 +185,19 @@
     return result
 
 
-def copy_in_order(source_ref, target_ref, place_ref, parts):
-    if parts == 1:
-        return source_ref
-    rows = source_ref.shape[0] // parts
-    for index in range(parts):
-        target_ref[index * rows : (index + 1) * rows, :] = source_ref[
-            block_rows(index, rows, place_ref, parts), :
-        ]
-    return target_ref
-
-
-def block_rows(index, rows, place_ref, parts):
-    if parts == 1:
-        return slice(0, rows)
-    back = lax.rem(place_ref[0] - index + parts, parts)
-    return pl.ds(pl.multiple_of(back * rows, rows), rows)
-
-
 def mixer_forward_kernel(
     heads,
-    parts,
-    pre_in_ref,
-    pre_other_in_ref,
+    pre_ref,
+    pre_other_ref,
     conv_input_ref,
     conv_state_ref,
     step_row_ref,
     wide_row_ref,
     marks_ref,
     labels_ref,
-    place_ref,
     y_ref,
     scaled_ref,
     total_ref,
-    pre_ref,
-    pre_other_ref,
     x_ref,
     dosed_ref,
     keys_ref,
@@ -245,8 +207,6 @@
     states = conv_state_ref.shape[1] // 2
     state_at, step_at = wide, wide
     head_width = HEAD
-    pre_ref = copy_in_order(pre_in_ref, pre_ref, place_ref, parts)
-    pre_other_ref = copy_in_order(pre_other_in_ref, pre_other_ref, place_ref, parts)
     _, sizes, rate = step_sizes(pre_other_ref[:, step_at : step_at + LANES], step_row_ref)
     running = summed_rows(sizes * rate, False)
     running_t = running.T
@@ -306,44 +266,31 @@
         gate = pre_ref[:, columns]
         gated = y * gate * sigmoid(gate)
         y_ref[:, columns] = y
-        scaled = (gated * wide_row_ref[0:1, columns]).astype(HALF)
-        each = length // parts
-        for index in range(parts):
-            block_at = block_rows(index, each, place_ref, parts)
-            scaled_ref[block_at, columns] = scaled[index * each : (index + 1) * each]
+        scaled_ref[:, columns] = (gated * wide_row_ref[0:1, columns]).astype(HALF)
         total = total + jnp.sum(gated * gated, axis=1, keepdims=True)
-    each = length // parts
-    for index in range(parts):
-        block_at = block_rows(index, each, place_ref, parts)
-        total_ref[block_at, :] = total[index * each : (index + 1) * each]
+    total_ref[...] = total
 
 
 def mixer_backward_kernel(
     heads,
-    parts,
     inner_all,
-    pre_in_ref,
-    pre_other_in_ref,
+    pre_ref,
+    pre_other_ref,
     y_ref,
-    grad_in_ref,
-    sides_in_ref,
+    grad_ref,
+    sides_ref,
     conv_input_ref,
     conv_state_ref,
     step_row_ref,
     wide_row_ref,
     marks_ref,
     labels_ref,
-    place_ref,
     grad_pre_ref,
     grad_pre_other_ref,
     wide_grad_ref,
     conv_input_grad_ref,
     conv_state_grad_ref,
     step_grad_ref,
-    pre_ref,
-    pre_other_ref,
-    grad_ref,
-    sides_ref,
     x_ref,
     dosed_ref,
     dose_ref,
@@ -358,18 +305,6 @@
     states = conv_state_ref.shape[1] // 2
     state_at, step_at = wide, wide
     head_width = HEAD
-    each = length // parts
-    pre_ref = copy_in_order(pre_in_ref, pre_ref, place_ref, parts)
-    pre_other_ref = copy_in_order(pre_other_in_ref, pre_other_ref, place_ref, parts)
-    grad_ref = copy_in_order(grad_in_ref, grad_ref, place_ref, parts)
-    sides_ref = copy_in_order(sides_in_ref, sides_ref, place_ref, parts)
-
-    def put(target_ref, value, start):
-        for index in range(parts):
-            target_ref[block_rows(index, each, place_ref, parts), start : start + LANES] = value[
-                index * each : (index + 1) * each
-            ]
-
     shifted_pre, sizes, rate = step_sizes(pre_other_ref[:, step_at : step_at + LANES], step_row_ref)
     running = summed_rows(sizes * rate, False)
     running_t = running.T
@@ -389,7 +324,7 @@
         wide_grad_ref[0:1, columns] = jnp.sum(grad * normed, axis=0, keepdims=True)
         grad_gated = rr * gain * grad - gated * pull
         slope = sigma * (1.0 + gate * (1.0 - sigma))
-        put(grad_pre_ref, (grad_gated * y * slope).astype(HALF), start)
+        grad_pre_ref[:, start : start + LANES] = (grad_gated * y * slope).astype(HALF)
         dy = grad_gated * silu
         dy_ref[:, columns] = dy
         conv = conv_rows(
@@ -477,7 +412,7 @@
             marks_ref,
             conv_input_grad_ref,
         )
-        put(grad_pre_other_ref, grad_in.astype(HALF), start)
+        grad_pre_other_ref[:, start : start + LANES] = grad_in.astype(HALF)
     for start in range(0, 2 * states, LANES):
         columns = slice(start, start + LANES)
         grad_in = conv_rows_back(
@@ -488,26 +423,19 @@
             marks_ref,
             conv_state_grad_ref,
         )
-        put(grad_pre_ref, grad_in.astype(HALF), state_at + start)
+        grad_pre_ref[:, state_at + start : state_at + start + LANES] = grad_in.astype(HALF)
     crossing = summed_rows(balance, True)
     grad_step = (direct + rate * crossing) * sigmoid(shifted_pre)
-    put(grad_pre_other_ref, grad_step.astype(HALF), step_at)
+    grad_pre_other_ref[:, step_at : step_at + LANES] = grad_step.astype(HALF)
     for start in range(step_at + LANES, grad_pre_other_ref.shape[1], LANES):
-        put(grad_pre_other_ref, jnp.zeros((length, LANES), HALF), start)
+        grad_pre_other_ref[:, start : start + LANES] = jnp.zeros((length, LANES), HALF)
     step_grad_ref[0:1, :] = jnp.sum(grad_step, axis=0, keepdims=True)
     step_grad_ref[1:2, :] = rate * jnp.sum(sizes * crossing, axis=0, keepdims=True)
 
 
-def ordered_copy(shape):
-    return pltpu.VMEM(shape if groups() > 1 else (8, LANES), FLOAT)
-
-
-def whole_call(kernel, inputs, results, scratch, name):
-    whole = pl.BlockSpec(memory_space=pltpu.VMEM)
-    place = pl.BlockSpec(memory_space=pltpu.SMEM)
+def whole_call(kernel, results, scratch, name):
     return pl.pallas_call(
         kernel,
-        in_specs=[whole] * (inputs - 1) + [place],
         out_shape=results,
         scratch_shapes=scratch,
         compiler_params=pltpu.CompilerParams(vmem_limit_bytes=VMEM_BYTES),
@@ -517,19 +445,16 @@
 
 def mixer_forward(pre, heads, wide, mixer):
     length = pre[0].shape[0]
-    kernel = functools.partial(mixer_forward_kernel, heads, groups())
+    kernel = functools.partial(mixer_forward_kernel, heads)
     states = mixer[1].shape[1] // 2
     return whole_call(
         kernel,
-        2 + len(mixer),
         (
             jax.ShapeDtypeStruct((length, wide), FLOAT),
             jax.ShapeDtypeStruct((length, wide), HALF),
             jax.ShapeDtypeStruct((length, 1), FLOAT),
         ),
         [
-            ordered_copy(pre[0].shape),
-            ordered_copy(pre[1].shape),
             pltpu.VMEM((length, wide), FLOAT),
             pltpu.VMEM((length, wide), HALF),
             pltpu.VMEM((length, states), HALF),
@@ -541,12 +466,11 @@
 
 def mixer_backward(pre, y, grad, sides, heads, mixer):
     length, wide = y.shape
-    kernel = functools.partial(mixer_backward_kernel, heads, groups(), DI)
+    kernel = functools.partial(mixer_backward_kernel, heads, DI)
     double = mixer[1].shape[1]
     square = pltpu.VMEM((length, wide), FLOAT)
     return whole_call(
         kernel,
-        5 + len(mixer),
         (
             jax.ShapeDtypeStruct(pre[0].shape, HALF),
             jax.ShapeDtypeStruct(pre[1].shape, HALF),
@@ -556,10 +480,6 @@
             jax.ShapeDtypeStruct((2, LANES), FLOAT),
         ),
         [
-            ordered_copy(pre[0].shape),
-            ordered_copy(pre[1].shape),
-            ordered_copy(y.shape),
-            ordered_copy(sides.shape),
             square,
             pltpu.VMEM((length, wide), HALF),
             square,
@@ -574,33 +494,18 @@
     )(*pre, y, grad, sides, *mixer)
 
 
-def to_blocks(per_chunk):
-    parts = [None] * groups()
-    for chunk, part in zip(chunks(), per_chunk):
-        rows_each = part.shape[0] // len(chunk)
-        for at, back in enumerate(chunk):
-            parts[back] = part[at * rows_each : (at + 1) * rows_each]
-    return parts
-
-
-def through_experts(block, tables, expert, beside, aside=None):
-    blocks = spread(block)
-    tokens = [joined([blocks[back] for back in chunk]) for chunk in chunks()]
-    arrived = [to_experts(project(table, each)) for table, each in zip(tables, tokens)]
-    answers = [expert(index, rows) for index, rows in enumerate(arrived)]
+def through_experts(block, table, expert, beside, aside=None):
+    tokens = spread(block)
+    arrived = to_experts(project(table, tokens))
+    answer = expert(arrived)
     if aside is not None:
-        answers = after(answers, aside(tokens))
-    answers = [to_experts(rows) for rows in answers]
-    made = [beside(*each) for each in zip(range(len(tokens)), tokens, answers)]
-    return to_blocks(made), arrived, tokens, answers
+        answer = after(answer, aside(tokens))
+    answer = to_experts(answer)
+    return beside(tokens, answer), arrived, tokens
 
 
 def line_product(values, weights):
     return sum(project_back(value, weight) for value, weight in zip(values, weights)).astype(HALF)
-
-
-def line_blocks(whole):
-    return [block_of(whole, back) for back in range(groups())]
 
 
 def expert_forward(rows, experts):
@@ -643,16 +548,12 @@
 
 
 def weight_sums(rows_in, rows_out, kept, grads, tokens_in, tokens_out, kept_s, grads_s):
-    rows_in, rows_out = joined(rows_in), joined(rows_out)
     experts = (
-        outer(rows_in, joined([each[0] for each in grads])).astype(HALF),
-        outer(rows_in, joined([each[1] for each in grads])).astype(HALF),
-        outer(joined([each[2] for each in kept]), rows_out).astype(HALF),
-    )
-    tokens_in, tokens_out = joined(tokens_in), joined(tokens_out)
-    pairs = [joined([each[at] for each in grads_s]) for at in range(2)]
-    act_s = joined([each[2] for each in kept_s])
-    shared = ((tokens_in, *pairs), (tokens_out, *two_halves(act_s)))
+        outer(rows_in, grads[0]).astype(HALF),
+        outer(rows_in, grads[1]).astype(HALF),
+        outer(kept[2], rows_out).astype(HALF),
+    )
+    shared = ((tokens_in, *grads_s), (tokens_out, *two_halves(kept_s[2])))
     return experts, [(*each, swapped(half_to_give(*each))) for each in shared]
 
 
@@ -678,17 +579,6 @@
     first = lax.axis_index("section") == 0
     keep = outer(left, jnp.where(first, first_right, second_right))
     return (keep + given.astype(FLOAT)).astype(HALF)
-
-
-def row_pieces(values, axis="row"):
-    count = lax.axis_size(axis)
-    rows = values.shape[0] // count
-    index = [lax.rem(lax.axis_index(axis) + ahead, count) * rows for ahead in range(count)]
-    return [lax.dynamic_slice_in_dim(values, at, rows, axis=0) for at in index]
-
-
-def row_received(pieces, axis="row"):
-    return [shifted(piece, axis, ahead) for ahead, piece in enumerate(pieces) if ahead]
 
 
 def flat(parts):
@@ -755,7 +645,7 @@
 
     tokens_now = lax.dynamic_index_in_dim(tokens, section_now, 0, keepdims=False)
     grad_now = lax.dynamic_index_in_dim(cotangent, section_now, 0, keepdims=False)
-    wide_tokens = joined(spread(tokens_now.astype(HALF)))
+    wide_tokens = spread(tokens_now.astype(HALF))
 
     halves = (
         jnp.concatenate([widened(proj_gate[0], wide), proj_state[0]], axis=1),
@@ -809,9 +699,8 @@
         marks.append((prior == labels).astype(FLOAT))
     marks = jnp.stack(marks, axis=1)
     label_row = labels.astype(FLOAT)[None]
-    place = turn()
     mixers = [
-        (conv_in, conv_st, step_row, wide_row, marks, label_row, place)
+        (conv_in, conv_st, step_row, wide_row, marks, label_row)
         for _, _, conv_in, conv_st, step_row, wide_row in small_all
     ]
 
@@ -820,73 +709,66 @@
         return pre, *mixer_forward(pre, heads, wide, mixers[s])
 
     def mix_out(s, resid, scaled, total_part, meanwhile):
-        total = gathered_sum(line_blocks(total_part))
-        whole = after(line_product([scaled], [proj_out[s]]), total)
-        mixed = gathered_sum(line_blocks(whole), meanwhile)
+        whole = line_product([scaled], [proj_out[s]])
+        sums = gathered_sum(jnp.concatenate([whole, as_halves(total_part)], axis=1), meanwhile)
+        mixed, total = sums[:, :width], from_halves(sums[:, width:], 1)
         rr = lax.rsqrt(total / DI + EPS)
         return resid + mixed * rr, mixed, rr
 
     wide_in_0 = rms_norm(wide_tokens.astype(FLOAT), norm_ins[0]).astype(HALF)
     pre_0, y_0, scaled_0, total_0 = mix_in(0, wide_in_0)
     tables = route_tables(spread(after(meta, scaled_0)), top, capacity, 2)
-    plain = [[table[0] for table in tables[s]] for s in layers]
-    scaling = [[table[1] for table in tables[s]] for s in layers]
+    plain = [table[0] for table in tables]
+    scaling = [table[1] for table in tables]
     middle_0, mixed_0, rr_0 = mix_out(0, tokens_now, scaled_0, total_0, tables)
-    kept_0, kept_s_0, grad_blocks = {}, {}, []
-
-    def expert_0(index, rows):
-        kept_0[index], answer = expert_forward(rows, experts[0])
+    kept = {}
+
+    def expert_0(rows):
+        kept["rows 0"], answer = expert_forward(rows, experts[0])
         return answer
 
-    def beside_0(index, block, result):
-        kept_s_0[index] = shared_forward(block, shared[0])
-        return home_part(scaling[0][index], result, kept_s_0[index][2], shared[0])
+    def beside_0(block, result):
+        kept["shared 0"] = shared_forward(block, shared[0])
+        return home_part(scaling[0], result, kept["shared 0"][2], shared[0])
 
     def aside_0(blocks):
-        grad_blocks.extend(spread(after(grad_now.astype(HALF), blocks)))
-        return grad_blocks
-
-    parts, rows_0, mids_0, answers = through_experts(
+        kept["grads"] = spread(after(grad_now.astype(HALF), blocks))
+        return kept["grads"]
+
+    parts, rows_0, mids_0 = through_experts(
         rms_norm(middle_0, norm_mids[0]).astype(HALF), plain[0], expert_0, beside_0, aside_0
     )
-    proj.append(both_halves(after(mine[1], answers)))
+    proj.append(both_halves(after(mine[1], parts)))
     out_0 = middle_0 + gathered_sum(parts)
 
-    wide_in_1 = joined(spread(rms_norm(out_0, norm_ins[1]).astype(HALF)))
-    grad_blocks = after(grad_blocks, out_0)
-    grad_tokens = [joined([grad_blocks[back] for back in chunk]) for chunk in chunks()]
-    grad_rows_1 = [
-        to_experts(project(table, block)) for table, block in zip(scaling[1], grad_tokens)
-    ]
+    wide_in_1 = spread(rms_norm(out_0, norm_ins[1]).astype(HALF))
+    grad_tokens_1 = after(kept["grads"], out_0)
+    grad_rows_1 = to_experts(project(scaling[1], grad_tokens_1))
     pre_1, y_1, scaled_1, total_1 = mix_in(1, wide_in_1)
-    scaled_1 = after(scaled_1, *grad_rows_1)
+    scaled_1 = after(scaled_1, grad_rows_1)
     middle_1, mixed_1, rr_1 = mix_out(1, out_0, scaled_1, total_1, ())
 
-    kept_1, kept_s_1, grads_1, grads_s_1, answers_1 = {}, {}, {}, {}, {}
-
-    def expert_1(index, rows):
-        kept_1[index], answers_1[index] = expert_forward(rows, experts[1])
-        grads_1[index], back = expert_backward(grad_rows_1[index], kept_1[index], experts[1])
+    def expert_1(rows):
+        kept["rows 1"], kept["answer 1"] = expert_forward(rows, experts[1])
+        kept["grads 1"], back = expert_backward(grad_rows_1, kept["rows 1"], experts[1])
         return back
 
-    def beside_1(index, block, result):
-        kept_s_1[index] = shared_forward(block, shared[1])
-        grads_s_1[index], part = shared_backward(grad_tokens[index], kept_s_1[index], shared[1])
-        return (part + outer(plain[1][index], result)).astype(HALF)
-
-    parts, rows_1, mids_1, _ = through_experts(
+    def beside_1(block, result):
+        kept["shared 1"] = shared_forward(block, shared[1])
+        kept["shared grads 1"], part = shared_backward(grad_tokens_1, kept["shared 1"], shared[1])
+        return (part + outer(plain[1], result)).astype(HALF)
+
+    parts, rows_1, mids_1 = through_experts(
         rms_norm(middle_1, norm_mids[1]).astype(HALF), plain[1], expert_1, beside_1
     )
-    order = range(len(chunks()))
-    answers = [to_experts(after(answers_1[index], parts[-1])) for index in order]
-
-    def listed(kept):
-        return [kept[index] for index in order]
+    answer_1 = to_experts(after(kept["answer 1"], parts))
 
     def mixer_back(s, grad_middle, along, rr, saved, meanwhile):
         wide_in, pre, y, scaled = saved
-        sides = joined(spread(jnp.concatenate([rr, along], axis=1), meanwhile))
-        wide_mix = joined(spread(grad_middle.astype(HALF), meanwhile))
+        sides = as_halves(jnp.concatenate([rr, along], axis=1))
+        payload = spread(jnp.concatenate([grad_middle.astype(HALF), sides], axis=1))
+        payload = after(payload, meanwhile)
+        wide_mix, sides = payload[:, :width], from_halves(payload[:, width:], 2)
         grad_scaled = project(wide_mix, proj_out[s])
         *grad_pre, wide_grads, grad_conv_input, grad_conv_state, step_grads = mixer_backward(
             pre, y, grad_scaled, sides, heads, mixers[s]
@@ -895,45 +777,45 @@
         tail = jnp.concatenate([grad_pre[0][:, wide:], grad_pre[1][:, wide : wide + LANES]], axis=1)
         mix_rr = (wide_mix * sides[:, :1]).astype(HALF)
         rest = (grad_conv_state, grad_conv_input, wide_grads, step_grads)
-        return wide_mix, grad_pre, (wide_in, *ends), (mix_rr, *two_halves(scaled)), tail, rest
+        return grad_pre, (wide_in, *ends), (mix_rr, *two_halves(scaled)), tail, rest
 
     def resid_back(resid, norm, grad_normed, grad_middle):
         _, pull_in = jax.vjp(rms_norm, resid, norm)
         grad_resid, grad_norm = pull_in(grad_normed)
         return grad_resid + grad_middle, grad_norm
 
-    def row_sums(value):
-        return lax.psum_scatter(value, "row", scatter_dimension=0, tiled=True)
-
     def own_layer(first_value, second_value):
         keep = jnp.where(first, first_value, second_value)
         give = jnp.where(first, second_value, first_value).astype(HALF)
         return keep.astype(FLOAT), swapped(give)
 
+    def row_sent(values):
+        return exchanged(values, "row")
+
+    def row_total(received):
+        return summed(received, "row").astype(HALF)
+
     grad_middle, along, grad_norm_mid_1 = middle_backward(
-        gathered_sum(parts, answers), grad_now, middle_1, mixed_1, norm_mids[1]
+        gathered_sum(parts, answer_1), grad_now, middle_1, mixed_1, norm_mids[1]
     )
     expert_grads_1, shared_grads_1 = weight_sums(
         rows_1,
         grad_rows_1,
-        listed(kept_1),
-        listed(grads_1),
+        kept["rows 1"],
+        kept["grads 1"],
         mids_1,
-        grad_tokens,
-        listed(kept_s_1),
-        listed(grads_s_1),
-    )
-    home = [
-        home_part(scaling[1][index], answers[index], kept_s_1[index][2], shared[1])
-        for index in order
-    ]
-    _, grad_pre, to_proj, to_out, tail, rest_1 = mixer_back(
+        grad_tokens_1,
+        kept["shared 1"],
+        kept["shared grads 1"],
+    )
+    home = home_part(scaling[1], answer_1, kept["shared 1"][2], shared[1])
+    grad_pre, to_proj, to_out, tail, rest_1 = mixer_back(
         1,
         grad_middle,
         along,
         rr_1,
         (wide_in_1, pre_1, y_1, scaled_1),
-        (expert_grads_1, home),
+        (expert_grads_1, home, [made[-1] for made in shared_grads_1]),
     )
     whole = line_product(grad_pre, proj[1])
     given = half_to_give(*after(to_proj, whole))
@@ -941,64 +823,66 @@
     grad_proj_1 = (*to_proj, swapped(given))
     grad_out_1 = (*to_out, swapped(given_out))
     grad_tail_1 = outer(after(wide_in_1, given_out), tail).astype(HALF)
-    grad_in = gathered_sum(line_blocks(whole), (given, given_out, grad_tail_1))
+    shared_sent_1 = [row_sent(half_to_keep(*after(made, whole))) for made in shared_grads_1]
+    grad_in = gathered_sum(whole, (given, given_out, grad_tail_1, shared_sent_1))
     grad_1, grad_norm_in_1 = resid_back(out_0, norm_ins[1], grad_in, grad_middle)
-    sums_1 = [half_to_keep(*after(made, grad_1)) for made in shared_grads_1]
-
-    grads_0, grads_s_0, out_parts = {}, {}, []
-
-    def expert_back_0(index, rows):
-        grads_0[index], back = expert_backward(rows, kept_0[index], experts[0])
+
+    def expert_back_0(rows):
+        kept["grads 0"], back = expert_backward(rows, kept["rows 0"], experts[0])
         return back
 
-    def beside_back_0(index, block, result):
-        grads_s_0[index], part = shared_backward(block, kept_s_0[index], shared[0])
-        return (part + outer(plain[0][index], result)).astype(HALF)
+    def beside_back_0(block, result):
+        kept["shared grads 0"], part = shared_backward(block, kept["shared 0"], shared[0])
+        return (part + outer(plain[0], result)).astype(HALF)
 
     def aside_back_0(blocks):
-        sums_1.extend(half_to_keep(*after(made, blocks)) for made in (grad_out_1, grad_proj_1))
-        out_parts.extend(to_blocks(after(home, blocks)))
-        if groups() > 1:
-            out_parts[1:] = after(sent_home(out_parts), sums_1)
-        return out_parts[1:]
-
-    parts, grad_rows_0, grad_tokens_0, _ = through_experts(
+        sums = [half_to_keep(*after(made, blocks)) for made in (grad_out_1, grad_proj_1)]
+        kept["sums 1"] = sums
+        kept["home"] = after(sent_home(after(home, blocks)), sums)
+        return kept["home"]
+
+    parts, grad_rows_0, grad_tokens_0 = through_experts(
         grad_1.astype(HALF), scaling[0], expert_back_0, beside_back_0, aside_back_0
     )
-    if groups() > 1:
-        out_1 = middle_1 + total_of(out_parts[0], out_parts[1:])
-    else:
-        out_1 = middle_1 + gathered_sum(out_parts)
-    sums_1 = [row_sums(value) for value in sums_1]
+    out_1 = middle_1 + added_up(kept["home"])
+    mixer_sent_1 = [row_sent(after(made, parts)) for made in kept["sums 1"]]
     grad_middle, along, grad_norm_mid_0 = middle_backward(
-        gathered_sum(parts, out_1), grad_1, middle_0, mixed_0, norm_mids[0]
+        gathered_sum(parts, (out_1, mixer_sent_1)), grad_1, middle_0, mixed_0, norm_mids[0]
     )
     expert_grads_0, shared_grads_0 = weight_sums(
         rows_0,
         grad_rows_0,
-        listed(kept_0),
-        listed(grads_0),
+        kept["rows 0"],
+        kept["grads 0"],
         mids_0,
         grad_tokens_0,
-        listed(kept_s_0),
-        listed(grads_s_0),
+        kept["shared 0"],
+        kept["shared grads 0"],
     )
     expert_out = [own_layer(a, b) for a, b in zip(expert_grads_0, expert_grads_1)]
-    wide_mix, grad_pre, to_proj, to_out, tail, rest_0 = mixer_back(
+    sums_1 = [row_total(received) for received in (*shared_sent_1, *mixer_sent_1)]
+    grad_pre, to_proj, to_out, tail, rest_0 = mixer_back(
         0,
         grad_middle,
         along,
         rr_0,
         (wide_in_0, pre_0, y_0, scaled_0),
-        [part[0] for part in expert_out],
-    )
-    sums_0 = [row_sums(half_to_keep(*after(made, wide_mix))) for made in shared_grads_0]
-
+        ([part[0] for part in expert_out], [made[-1] for made in shared_grads_0], sums_1),
+    )
+
+    def row_sums(value):
+        return lax.psum_scatter(value, "row", scatter_dimension=0, tiled=True)
+
+    sums_0 = [row_sums(half_to_keep(*after(made, to_out[0]))) for made in shared_grads_0]
     given = half_to_give(*to_proj)
     whole = line_product(after(grad_pre, given), proj[0])
+    line_received = sent_home(whole)
+    proj_sent = row_sent(half_to_keep(*after((*to_proj, swapped(given)), whole)))
     given_out = half_to_give(*after(to_out, whole))
+    sums_0.append(row_sums(half_to_keep(*after((*to_out, swapped(given_out)), proj_sent[:8]))))
     grad_tail_0 = outer(after(wide_in_0, given_out), tail).astype(HALF)
     tail_keep, tail_other = own_layer(grad_tail_0, grad_tail_1)
+    tail_sent = row_sent((tail_keep + tail_other.astype(FLOAT)).astype(HALF))
     wide_x = wide_tokens.astype(FLOAT)
     wide_r = lax.rsqrt(jnp.mean(wide_x * wide_x, axis=1, keepdims=True) + EPS)
     grad_norm_in_0 = jnp.sum(whole.astype(FLOAT) * wide_x * wide_r, axis=0)
@@ -1008,40 +892,17 @@
     )
     shapes = [part.shape for part in smalls[0]]
     small_keep, small_other = own_layer(flat(smalls[0]), flat(smalls[1]))
-    line_parts = line_blocks(whole)
-    if groups() > 1:
-        line_received = sent_home(line_parts)
-    to_proj, to_out, tail_own, small_own = after(
-        (
-            (*to_proj, swapped(given)),
-            (*to_out, swapped(given_out)),
-            (tail_keep, tail_other),
-            (small_keep, small_other),
-        ),
-        grad_tail_0,
-    )
-    proj_pieces = row_pieces(half_to_keep(*to_proj))
-    out_pieces = row_pieces(half_to_keep(*to_out))
-    tail_pieces = row_pieces((tail_own[0] + tail_own[1].astype(FLOAT)).astype(HALF))
-    vector = small_own[0] + small_own[1].astype(FLOAT)
-    proj_received, out_received, tail_received = [
-        row_received(pieces) for pieces in (proj_pieces, out_pieces, tail_pieces)
-    ]
-    lines = [shifted(vector[None], "row", back) for back in range(n_row)]
-    expert_out = [keep + other.astype(FLOAT) for keep, other in after(expert_out, proj_pieces)]
-    if groups() > 1:
-        line_received, proj_received, out_received, tail_received, lines, sums_0 = after(
-            (line_received, proj_received, out_received, tail_received, lines, sums_0), expert_out
-        )
-        grad_in = total_of(line_parts[0], line_received)
-    else:
-        grad_in = gathered_sum(line_parts)
-    grad_proj_0 = total_of(proj_pieces[0], proj_received).astype(HALF)
-    grad_out_0 = total_of(out_pieces[0], out_received).astype(HALF)
-    tail = total_of(tail_pieces[0], tail_received).astype(HALF)
-    vector = jnp.sum(in_order(lines, "row"), axis=0)
+    vector = small_keep + small_other.astype(FLOAT)
+    lines = row_sent(jnp.tile(vector[None], (n_row, 1)))
+    expert_out = [keep + other.astype(FLOAT) for keep, other in after(expert_out, given_out)]
+    line_received, proj_sent, tail_sent, lines = after(
+        (line_received, proj_sent, tail_sent, lines), expert_out
+    )
+    grad_in = added_up(line_received)
+    sums_0.append(row_total(proj_sent))
+    tail = row_total(tail_sent)
+    vector = jnp.sum(lines, axis=0)
     grad_0, _ = resid_back(tokens_now, norm_ins[0], grad_in, grad_middle)
-    sums_0 = [*sums_0, grad_out_0, grad_proj_0]
 
     def own_halves(first_value, second_value):
         keep = jnp.where(first, first_value, second_value)
@@ -1056,16 +917,14 @@
     outs, in_grads = per_micro(out_0, after(out_1, grad_in)), per_micro(grad_0, grad_1)
     common = 2 * width + conv_state.shape[1] * state
     state_grad = tail[:, :state]
-    if groups() > 1:
-        state_pieces = row_pieces(state_grad, "col")
-        state_received = row_received(state_pieces, "col")
-        lines = [shifted(vector[None, :common], "col", back) for back in range(n_col)]
-        state_received, lines, halves, outs, in_grads = after(
-            (state_received, lines, halves, outs, in_grads)
+    if n_col <= 4:
+        state_sent = exchanged(state_grad, "col")
+        lines = exchanged(jnp.tile(vector[None, :common], (n_col, 1)), "col")
+        state_sent, lines, halves, outs, in_grads = after(
+            (state_sent, lines, halves, outs, in_grads)
         )
-        state_grad = total_of(state_pieces[0], state_received).astype(HALF)
-        state_grad = in_order([shifted(state_grad, "col", back) for back in range(n_col)], "col")
-        shared_sum = jnp.sum(in_order(lines, "col"), axis=0)
+        state_grad = spread(summed(state_sent, "col").astype(HALF))
+        shared_sum = jnp.sum(lines, axis=0)
     else:
         state_grad = lax.psum(state_grad, "col")
         shared_sum = lax.psum(vector[:common], "col")

time: 1260 us -> 1420 us (1.13)
  waiting for transfers between devices: 566 us -> 657 us
  blocking collectives: 52.3 us -> 138 us
  starting transfers between devices: 215 us -> 143 us
  local copies, waits for them, and re-layouts: 39.8 us -> 64.4 us
  matrix products: 228 us -> 250 us
    all_to_all x7 -> x31, waiting for transfers between devices: 71.1 us -> 615 us  [exchanged(): return lax.all_to_all(rows, axis, split_axis=0, concat_axis=0, tiled=True)]
    ppermute x84 -> x0, waiting for transfers between devices: 420 us -> none  [shifted(): lax.ppermute(block, axis, [(i, (i + distance) % count) for i in range(cou...]
    ppermute x84 -> x0, starting transfers between devices: 176 us -> none  [shifted(): lax.ppermute(block, axis, [(i, (i + distance) % count) for i in range(cou...]
    all_to_all x7 -> x31, starting transfers between devices: 33 us -> 136 us  [exchanged(): return lax.all_to_all(rows, axis, split_axis=0, concat_axis=0, tiled=True)]
    all_to_all x1 -> x4, blocking collectives: 52.3 us -> 138 us  [exchanged(): return lax.all_to_all(rows, axis, split_axis=0, concat_axis=0, tiled=True)]
    all_to_all x0 -> x9, local copies, waits for them, and re-layouts: none -> 20 us  [exchanged(): return lax.all_to_all(rows, axis, split_axis=0, concat_axis=0, tiled=True)]
    reduce_scatter x6 -> x3, waiting for transfers between devices: 43.4 us -> 28.5 us  [row_sums(): return lax.psum_scatter(value, 'row', scatter_dimension=0, tiled=True)]
  transfers between devices with their start and end apart: 126 -> 63, of which waited for: 49 -> 32; matrix products, arithmetic and copies ran while one was open for 21% -> 21% of each run, Pallas kernels for 3% -> 2%
where the time goes in v7:
time: 1420 us; the launch traced here: 1410 us
  waiting for transfers between devices  657 us (46%)
  matrix products  250 us (18%)
  starting transfers between devices  143 us (10%)
  blocking collectives  138 us (10%)
  other arithmetic  78.7 us (6%)
  local copies, waits for them, and re-layouts  64.4 us (5%)
  Pallas kernels  58.9 us (4%)
  between operations  17.6 us (1%)
    all_to_all x31, waiting for transfers between devices, exchanged(): return lax.all_to_all(rows, axis, split_axis=0, concat_axis=0, tiled=True)  615 us
    all_to_all x4, blocking collectives, exchanged(): return lax.all_to_all(rows, axis, split_axis=0, concat_axis=0, tiled=True)  138 us
    all_to_all x31, starting transfers between devices, exchanged(): return lax.all_to_all(rows, axis, split_axis=0, concat_axis=0, tiled=True)  136 us
    dot_general x28, matrix products, outer(): lax.dot_general(left, right, (((0,), (0,)), ((), ())), preferred_element_...  98.1 us
    dot_general x23, matrix products, project(): return jnp.dot(left, right, preferred_element_type=FLOAT)  84.9 us
    dot_general x18, matrix products, project_back(): lax.dot_general(left, right, (((1,), (1,)), ((), ())), preferred_element_...  67.1 us
    pallas_call x2, Pallas kernels, mixer_backward(): whole_call(kernel, (jax.ShapeDtypeStruct(pre[0].shape, HALF), jax.ShapeDt...  35.6 us
    reduce_scatter x3, waiting for transfers between devices, row_sums(): return lax.psum_scatter(value, 'row', scatter_dimension=0, tiled=True)  28.5 us
  transfers between devices with their start and end apart: 63, of which 32 were waited for; matrix products, arithmetic and copies ran while one was open for 21% of the time, Pallas kernels for 2%

profile of v7, /device:TPU:0, one launch (start us, length us, event | category | flops | bytes accessed | tf_op | source)
XLA Modules:
  0.0 1407.7 jit_solution(11657744882183126452)
XLA Ops:
  27.9 35.2 %all-to-all-done = bf16[4,128,1536]{2,1,0:T(8,128)(2,1)} async-done(((bf16[4,128,1536]{2,1,0:T(8,128)(2,1)}), bf16[4,128,1536]{2,1,0:T(8,128)(2,1)}, u32[]{:S(2)}, u32[]{:S(2)}) %all-to-all-start) | async-done | bytes 1572896 | tf_op jit(solution)/shard_map/all_to_all | solution.py:73
  79.0 11.7 mixer_forward.2
  115.8 36.5 %all-to-all-done.1 = bf16[4,128,1664]{2,1,0:T(8,128)(2,1)} async-done(((bf16[4,128,1664]{2,1,0:T(8,128)(2,1)}), bf16[4,128,1664]{2,1,0:T(8,128)(2,1)}, u32[]{:S(2)}, u32[]{:S(2)}) %all-to-all-start.1) | async-done | bytes 1703968 | tf_op jit(solution)/shard_map/all_to_all | solution.py:73
  167.4 33.4 %all-to-all-done.3 = bf16[4,128,1536]{2,1,0:T(8,128)(2,1)} async-done(((bf16[4,128,1536]{2,1,0:T(8,128)(2,1)}), bf16[4,128,1536]{2,1,0:T(8,128)(2,1)}, u32[]{:S(2)}, u32[]{:S(2)}) %all-to-all-start.3) | async-done | bytes 1572896 | tf_op jit(solution)/shard_map/all_to_all | solution.py:73
  210.9 35.2 %all-to-all-done.4 = bf16[4,256,1536]{2,1,0:T(8,128)(2,1)} async-done(((bf16[4,256,1536]{2,1,0:T(8,128)(2,1)}), bf16[4,256,1536]{2,1,0:T(8,128)(2,1)}, u32[]{:S(2)}, u32[]{:S(2)}) %all-to-all-start.4) | async-done | bytes 3145760 | tf_op jit(solution)/shard_map/all_to_all | solution.py:73
  269.2 19.4 %all-to-all-done.5 = bf16[4,128,1536]{2,1,0:T(8,128)(2,1)} async-done(((bf16[4,128,1536]{2,1,0:T(8,128)(2,1)}), bf16[4,128,1536]{2,1,0:T(8,128)(2,1)}, u32[]{:S(2)}, u32[]{:S(2)}) %all-to-all-start.5) | async-done | bytes 1572896 | tf_op jit(solution)/shard_map/all_to_all | solution.py:73
  298.7 30.2 %all-to-all-done.6 = bf16[4,256,1536]{2,1,0:T(8,128)(2,1)} async-done(((bf16[4,256,1536]{2,1,0:T(8,128)(2,1)}), bf16[4,256,1536]{2,1,0:T(8,128)(2,1)}, u32[]{:S(2)}, u32[]{:S(2)}) %all-to-all-start.6) | async-done | bytes 3145760 | tf_op jit(solution)/shard_map/all_to_all | solution.py:73
  340.0 36.5 %all-to-all-done.7 = bf16[4,128,1536]{2,1,0:T(8,128)(2,1)} async-done(((bf16[4,128,1536]{2,1,0:T(8,128)(2,1)}), bf16[4,128,1536]{2,1,0:T(8,128)(2,1)}, u32[]{:S(2)}, u32[]{:S(2)}) %all-to-all-start.7) | async-done | bytes 1572896 | tf_op jit(solution)/shard_map/all_to_all | solution.py:73
  391.2 31.2 %all-to-all-done.8 = bf16[4,128,1536]{2,1,0:T(8,128)(2,1)S(1)} async-done(((bf16[4,128,1536]{2,1,0:T(8,128)(2,1)}), bf16[4,128,1536]{2,1,0:T(8,128)(2,1)S(1)}, u32[]{:S(2)}, u32[]{:S(2)}) %all-to-all-start.8) | async-done | bytes 1572896 | tf_op jit(solution)/shard_map/all_to_all | solution.py:73
  436.3 11.5 mixer_forward.3
  449.1 14.8 %all-to-all-done.9 = bf16[4,256,1536]{2,1,0:T(8,128)(2,1)} async-done(((bf16[4,256,1536]{2,1,0:T(8,128)(2,1)}), bf16[4,256,1536]{2,1,0:T(8,128)(2,1)}, u32[]{:S(2)}, u32[]{:S(2)}) %all-to-all-start.9) | async-done | bytes 3145760 | tf_op jit(solution)/shard_map/all_to_all | solution.py:73
  467.5 41.7 %all_to_all.363 = bf16[4,128,1664]{2,1,0:T(8,128)(2,1)S(1)} all-to-all(bf16[4,128,1664]{2,1,0:T(8,128)(2,1)S(1)} %bitcast.357), channel_id=1, replica_groups=mesh['section'=2,'row'=4,'col'=4] {'col'}, dimensions={0} | all-to-all | bytes 3407872 | tf_op jit(solution)/shard_map/all_to_all | solution.py:73
  514.0 39.1 %all_to_all.364 = bf16[4,128,1536]{2,1,0:T(8,128)(2,1)S(1)} all-to-all(bf16[4,128,1536]{2,1,0:T(8,128)(2,1)S(1)} %tile.29), channel_id=1, replica_groups=mesh['section'=2,'row'=4,'col'=4] {'col'}, dimensions={0} | all-to-all | bytes 3145728 | tf_op jit(solution)/shard_map/all_to_all | solution.py:73
  566.8 29.7 %all-to-all-done.12 = bf16[4,256,1536]{2,1,0:T(8,128)(2,1)} async-done(((bf16[4,256,1536]{2,1,0:T(8,128)(2,1)}), bf16[4,256,1536]{2,1,0:T(8,128)(2,1)}, u32[]{:S(2)}, u32[]{:S(2)}) %all-to-all-start.12) | async-done | bytes 3145760 | tf_op jit(solution)/shard_map/all_to_all | solution.py:73
  626.4 26.0 %all-to-all-done.13 = bf16[4,256,1536]{2,1,0:T(8,128)(2,1)} async-done(((bf16[4,256,1536]{2,1,0:T(8,128)(2,1)}), bf16[4,256,1536]{2,1,0:T(8,128)(2,1)}, u32[]{:S(2)}, u32[]{:S(2)}) %all-to-all-start.13) | async-done | bytes 3145760 | tf_op jit(solution)/shard_map/all_to_all | solution.py:73
  668.8 31.3 %all-to-all-done.14 = bf16[4,128,1536]{2,1,0:T(8,128)(2,1)} async-done(((bf16[4,128,1536]{2,1,0:T(8,128)(2,1)}), bf16[4,128,1536]{2,1,0:T(8,128)(2,1)}, u32[]{:S(2)}, u32[]{:S(2)}) %all-to-all-start.14) | async-done | bytes 1572896 | tf_op jit(solution)/shard_map/all_to_all | solution.py:73
  710.5 30.0 %all-to-all-done.15 = bf16[4,256,1536]{2,1,0:T(8,128)(2,1)} async-done(((bf16[4,256,1536]{2,1,0:T(8,128)(2,1)}), bf16[4,256,1536]{2,1,0:T(8,128)(2,1)}, u32[]{:S(2)}, u32[]{:S(2)}) %all-to-all-start.15) | async-done | bytes 3145760 | tf_op jit(solution)/shard_map/all_to_all | solution.py:73
  773.1 15.2 %all-to-all-done.16 = bf16[4,128,1664]{2,1,0:T(8,128)(2,1)S(1)} async-done(((bf16[4,128,1664]{2,1,0:T(8,128)(2,1)}), bf16[4,128,1664]{2,1,0:T(8,128)(2,1)S(1)}, u32[]{:S(2)}, u32[]{:S(2)}) %all-to-all-start.16) | async-done | bytes 1703968 | tf_op jit(solution)/shard_map/all_to_all | solution.py:73
  792.1 17.8 %mixer_backward.2 = (bf16[512,1024]{1,0:T(8,128)(2,1)S(1)}, bf16[512,1024]{1,0:T(8,128)(2,1)S(1)}, f32[2,768]{1,0:T(2,128)S(1)}, f32[4,768]{1,0:T(4,128)S(1)}, f...) custom-call(f32[512,1024]{1,0:T(8,128)} %copy-done.3, f32[512,1024]{1,0:T(8,128)} %fusion.18.pre_other_ref, ...), custom_call_target="tpu_custom_call" | custom-call | tf_op jit(solution)/shard_map/mixer_backward/pallas_call | solution.py:472
  831.4 26.9 %all-to-all-done.17 = bf16[4,128,1536]{2,1,0:T(8,128)(2,1)} async-done(((bf16[4,128,1536]{2,1,0:T(8,128)(2,1)}), bf16[4,128,1536]{2,1,0:T(8,128)(2,1)}, u32[]{:S(2)}, u32[]{:S(2)}) %all-to-all-start.17) | async-done | bytes 1572896 | tf_op jit(solution)/shard_map/all_to_all | solution.py:73
  862.7 39.1 %all_to_all.365 = bf16[4,128,1536]{2,1,0:T(8,128)(2,1)S(1)} all-to-all(bf16[4,128,1536]{2,1,0:T(8,128)(2,1)S(1)} %tile.31), channel_id=1, replica_groups=mesh['section'=2,'row'=4,'col'=4] {'col'}, dimensions={0} | all-to-all | bytes 3145728 | tf_op jit(solution)/shard_map/all_to_all | solution.py:73
  910.7 34.6 %all-to-all-done.19 = bf16[4,256,1536]{2,1,0:T(8,128)(2,1)} async-done(((bf16[4,256,1536]{2,1,0:T(8,128)(2,1)}), bf16[4,256,1536]{2,1,0:T(8,128)(2,1)}, u32[]{:S(2)}, u32[]{:S(2)}) %all-to-all-start.19) | async-done | bytes 3145760 | tf_op jit(solution)/shard_map/all_to_all | solution.py:73
  972.1 14.2 %all-to-all-done.20 = bf16[4,128,1536]{2,1,0:T(8,128)(2,1)} async-done(((bf16[4,128,1536]{2,1,0:T(8,128)(2,1)}), bf16[4,128,1536]{2,1,0:T(8,128)(2,1)}, u32[]{:S(2)}, u32[]{:S(2)}) %all-to-all-start.20) | async-done | bytes 1572896 | tf_op jit(solution)/shard_map/all_to_all | solution.py:73
  1014.2 26.3 %all-to-all-done.21 = bf16[4,256,1536]{2,1,0:T(8,128)(2,1)} async-done(((bf16[4,256,1536]{2,1,0:T(8,128)(2,1)}), bf16[4,256,1536]{2,1,0:T(8,128)(2,1)}, u32[]{:S(2)}, u32[]{:S(2)}) %all-to-all-start.21) | async-done | bytes 3145760 | tf_op jit(solution)/shard_map/all_to_all | solution.py:73
  1055.1 18.2 %all_to_all.366 = bf16[4,384,384]{2,1,0:T(8,128)(2,1)} all-to-all(bf16[4,384,384]{2,1,0:T(8,128)(2,1)S(1)} %bitcast.392), channel_id=1, replica_groups=mesh['section'=2,'row'=4,'col'=4] {'row'}, dimensions={0} | all-to-all | bytes 2359296 | tf_op jit(solution)/shard_map/all_to_all | solution.py:73
  1079.6 33.2 %all-to-all-done.22 = bf16[4,128,1536]{2,1,0:T(8,128)(2,1)} async-done(((bf16[4,128,1536]{2,1,0:T(8,128)(2,1)}), bf16[4,128,1536]{2,1,0:T(8,128)(2,1)}, u32[]{:S(2)}, u32[]{:S(2)}) %all-to-all-start.22) | async-done | bytes 1572896 | tf_op jit(solution)/shard_map/all_to_all | solution.py:73
  1126.7 18.0 %all-to-all-done.27 = bf16[4,384,768]{2,1,0:T(8,128)(2,1)} async-done(((bf16[4,384,768]{2,1,0:T(8,128)(2,1)}), bf16[4,384,768]{2,1,0:T(8,128)(2,1)}, u32[]{:S(2)}, u32[]{:S(2)}) %all-to-all-start.27) | async-done | bytes 2359328 | tf_op jit(solution)/shard_map/all_to_all | solution.py:73
  1172.0 16.8 %all-to-all-done.23 = bf16[4,128,1664]{2,1,0:T(8,128)(2,1)S(1)} async-done(((bf16[4,128,1664]{2,1,0:T(8,128)(2,1)}), bf16[4,128,1664]{2,1,0:T(8,128)(2,1)S(1)}, u32[]{:S(2)}, u32[]{:S(2)}) %all-to-all-start.23) | async-done | bytes 1703968 | tf_op jit(solution)/shard_map/all_to_all | solution.py:73
  1192.6 17.8 %mixer_backward.3 = (bf16[512,1024]{1,0:T(8,128)(2,1)S(1)}, bf16[512,1024]{1,0:T(8,128)(2,1)S(1)}, f32[2,768]{1,0:T(2,128)S(1)}, f32[4,768]{1,0:T(4,128)S(1)}, f...) custom-call(f32[512,1024]{1,0:T(8,128)} %copy-done.2, f32[512,1024]{1,0:T(8,128)} %fusion.26.pre_other_ref, ...), custom_call_target="tpu_custom_call" | custom-call | tf_op jit(solution)/shard_map/mixer_backward/pallas_call | solution.py:472
  1245.4 11.6 all-to-all-done.30
  1278.2 19.6 %all-to-all-done.28 = bf16[4,128,1536]{2,1,0:T(8,128)(2,1)} async-done(((bf16[4,128,1536]{2,1,0:T(8,128)(2,1)}), bf16[4,128,1536]{2,1,0:T(8,128)(2,1)}, u32[]{:S(2)}, u32[]{:S(2)}) %all-to-all-start.28) | async-done | bytes 1572896 | tf_op jit(solution)/shard_map/all_to_all | solution.py:73
  1317.1 28.5 %reduce-scatter.8.cloned.1.call-done = bf16[384,384]{1,0:T(8,128)(2,1)} async-done(((bf16[1536,384]{1,0:T(8,128)(2,1)}), bf16[384,384]{1,0:T(8,128)(2,1)}) %reduce-scatter.8.cloned.1.call-update) | async-done | bytes 294928 | tf_op jit(solution)/shard_map/reduce_scatter | solution.py:874
  (753 shorter events, 558.8 us)
Async XLA Ops:
  7.2 63.6 %all-gather.12.cloned.1.call-start = ((), (), s32[]{:S(2)}) async-start(), calls=%async_computation.38 | async-start | bytes 7077888 | tf_op jit(solution)/shard_map/all_gather | solution.py:658
  13.8 89.1 %all-gather.18.cloned.1.call-start = ((), (), s32[]{:S(2)}) async-start(), calls=%async_computation.44 | async-start | bytes 5308416 | tf_op jit(solution)/shard_map/all_gather | solution.py:664
  14.6 237.5 %all-gather.20.cloned.1.call-start = ((), (), s32[]{:S(2)}) async-start(), calls=%async_computation.45 | async-start | bytes 4718592 | tf_op jit(solution)/shard_map/all_gather | solution.py:668
  19.3 43.8 %all-to-all-start = ((bf16[4,128,1536]{2,1,0:T(8,128)(2,1)}), bf16[4,128,1536]{2,1,0:T(8,128)(2,1)}, u32[]{:S(2)}, u32[]{:S(2)}) async-start(bf16[4,128,1536]{2,1,0:T(8,128)(2,1)} %tile.24), calls=%async_computation | async-start | bytes 3145728 | tf_op jit(solution)/shard_map/all_to_all | solution.py:73
  25.7 231.9 %all-gather.22.cloned.1.call-start = ((), (), s32[]{:S(2)}) async-start(), calls=%async_computation.46 | async-start | bytes 4718592 | tf_op jit(solution)/shard_map/all_gather | solution.py:669
  107.4 44.9 %all-to-all-start.1 = ((bf16[4,128,1664]{2,1,0:T(8,128)(2,1)}), bf16[4,128,1664]{2,1,0:T(8,128)(2,1)}, u32[]{:S(2)}, u32[]{:S(2)}) async-start(bf16[4,128,1664]{2,1,0:T(8,128)(2,1)} %bitcast.356), calls=%async_computation.1 | async-start | bytes 3407872 | tf_op jit(solution)/shard_map/all_to_all | solution.py:73
  112.0 151.9 %all-gather.24.cloned.1.call-start = ((), (), s32[]{:S(2)}) async-start(), calls=%async_computation.47 | async-start | bytes 4718592 | tf_op jit(solution)/shard_map/all_gather | solution.py:670
  159.7 41.0 %all-to-all-start.3 = ((bf16[4,128,1536]{2,1,0:T(8,128)(2,1)}), bf16[4,128,1536]{2,1,0:T(8,128)(2,1)}, u32[]{:S(2)}, u32[]{:S(2)}) async-start(bf16[4,128,1536]{2,1,0:T(8,128)(2,1)} %tile.26), calls=%async_computation.3 | async-start | bytes 3145728 | tf_op jit(solution)/shard_map/all_to_all | solution.py:73
  164.1 129.2 %all-gather.14.cloned.1.call-start = ((), (), s32[]{:S(2)}) async-start(), calls=%async_computation.39 | async-start | bytes 5308416 | tf_op jit(solution)/shard_map/all_gather | solution.py:664
  205.6 40.5 %all-to-all-start.4 = ((bf16[4,256,1536]{2,1,0:T(8,128)(2,1)}), bf16[4,256,1536]{2,1,0:T(8,128)(2,1)}, u32[]{:S(2)}, u32[]{:S(2)}) async-start(bf16[4,256,1536]{2,1,0:T(8,128)(2,1)} %bitcast.368), calls=%async_computation.4 | async-start | bytes 6291456 | tf_op jit(solution)/shard_map/all_to_all | solution.py:73
  247.3 41.2 %all-to-all-start.5 = ((bf16[4,128,1536]{2,1,0:T(8,128)(2,1)}), bf16[4,128,1536]{2,1,0:T(8,128)(2,1)}, u32[]{:S(2)}, u32[]{:S(2)}) async-start(bf16[4,128,1536]{2,1,0:T(8,128)(2,1)} %tile.27), calls=%async_computation.5 | async-start | bytes 3145728 | tf_op jit(solution)/shard_map/all_to_all | solution.py:73
  288.6 40.3 %all-to-all-start.6 = ((bf16[4,256,1536]{2,1,0:T(8,128)(2,1)}), bf16[4,256,1536]{2,1,0:T(8,128)(2,1)}, u32[]{:S(2)}, u32[]{:S(2)}) async-start(bf16[4,256,1536]{2,1,0:T(8,128)(2,1)} %bitcast.365), calls=%async_computation.6 | async-start | bytes 6291456 | tf_op jit(solution)/shard_map/all_to_all | solution.py:73
  293.2 135.3 %all-gather.16.cloned.1.call-start = ((), (), s32[]{:S(2)}) async-start(), calls=%async_computation.40 | async-start | bytes 7077888 | tf_op jit(solution)/shard_map/all_gather | solution.py:658
  335.6 40.9 %all-to-all-start.7 = ((bf16[4,128,1536]{2,1,0:T(8,128)(2,1)}), bf16[4,128,1536]{2,1,0:T(8,128)(2,1)}, u32[]{:S(2)}, u32[]{:S(2)}) async-start(bf16[4,128,1536]{2,1,0:T(8,128)(2,1)} %bitcast.360), calls=%async_computation.7 | async-start | bytes 3145728 | tf_op jit(solution)/shard_map/all_to_all | solution.py:73
  423.6 40.3 %all-to-all-start.9 = ((bf16[4,256,1536]{2,1,0:T(8,128)(2,1)}), bf16[4,256,1536]{2,1,0:T(8,128)(2,1)}, u32[]{:S(2)}, u32[]{:S(2)}) async-start(bf16[4,256,1536]{2,1,0:T(8,128)(2,1)} %bitcast.364), calls=%async_computation.9 | async-start | bytes 6291456 | tf_op jit(solution)/shard_map/all_to_all | solution.py:73
  611.8 40.7 %all-to-all-start.13 = ((bf16[4,256,1536]{2,1,0:T(8,128)(2,1)}), bf16[4,256,1536]{2,1,0:T(8,128)(2,1)}, u32[]{:S(2)}, u32[]{:S(2)}) async-start(bf16[4,256,1536]{2,1,0:T(8,128)(2,1)} %bitcast.349), calls=%async_computation.13 | async-start | bytes 6291456 | tf_op jit(solution)/shard_map/all_to_all | solution.py:73
  659.3 40.9 %all-to-all-start.14 = ((bf16[4,128,1536]{2,1,0:T(8,128)(2,1)}), bf16[4,128,1536]{2,1,0:T(8,128)(2,1)}, u32[]{:S(2)}, u32[]{:S(2)}) async-start(bf16[4,128,1536]{2,1,0:T(8,128)(2,1)} %bitcast.362), calls=%async_computation.14 | async-start | bytes 3145728 | tf_op jit(solution)/shard_map/all_to_all | solution.py:73
  700.1 40.3 %all-to-all-start.15 = ((bf16[4,256,1536]{2,1,0:T(8,128)(2,1)}), bf16[4,256,1536]{2,1,0:T(8,128)(2,1)}, u32[]{:S(2)}, u32[]{:S(2)}) async-start(bf16[4,256,1536]{2,1,0:T(8,128)(2,1)} %bitcast.367), calls=%async_computation.15 | async-start | bytes 6291456 | tf_op jit(solution)/shard_map/all_to_all | solution.py:73
  707.8 65.3 %collective-permute-start.3 = (bf16[1536,256]{1,0:T(8,128)(2,1)}, bf16[1536,256]{1,0:T(8,128)(2,1)}, u32[]{:S(2)}, u32[]{:S(2)}) collective-permute-start(bf16[1536,256]{1,0:T(8,128)(2,1)} %convolution_convert_fusion.21), channel_id=1, source_target_pairs={{0,16},{16,0},{1,17},{17,1},{2,18},{18,2},{3,19},{19,3},{4,20},{20... | collective-permute-start | bytes 2359304 | tf_op jit(solution)/shard_map/ppermute | solution.py:30
  745.5 42.8 %all-to-all-start.16 = ((bf16[4,128,1664]{2,1,0:T(8,128)(2,1)}), bf16[4,128,1664]{2,1,0:T(8,128)(2,1)S(1)}, u32[]{:S(2)}, u32[]{:S(2)}) async-start(bf16[4,128,1664]{2,1,0:T(8,128)(2,1)} %tile.30), calls=%async_computation.16 | async-start | bytes 3407872 | tf_op jit(solution)/shard_map/all_to_all | solution.py:73
  817.2 41.0 %all-to-all-start.17 = ((bf16[4,128,1536]{2,1,0:T(8,128)(2,1)}), bf16[4,128,1536]{2,1,0:T(8,128)(2,1)}, u32[]{:S(2)}, u32[]{:S(2)}) async-start(bf16[4,128,1536]{2,1,0:T(8,128)(2,1)} %bitcast.389), calls=%async_computation.17 | async-start | bytes 3145728 | tf_op jit(solution)/shard_map/all_to_all | solution.py:73
  910.1 42.8 %collective-permute-start.6 = (bf16[1536,768]{1,0:T(8,128)(2,1)}, bf16[1536,768]{1,0:T(8,128)(2,1)}, u32[]{:S(2)}, u32[]{:S(2)}) collective-permute-start(bf16[1536,768]{1,0:T(8,128)(2,1)} %convolution_convert_fusion.7), channel_id=1, source_target_pairs={{0,16},{16,0},{1,17},{17,1},{2,18},{18,2},{3,19},{19,3},{4,20},{20... | collective-permute-start | bytes 7077896 | tf_op jit(solution)/shard_map/ppermute | solution.py:30
  910.2 42.7 %collective-permute-start.5 = (bf16[1536,384]{1,0:T(8,128)(2,1)}, bf16[1536,384]{1,0:T(8,128)(2,1)}, u32[]{:S(2)}, u32[]{:S(2)}) collective-permute-start(bf16[1536,384]{1,0:T(8,128)(2,1)} %convolution_convert_fusion.19), channel_id=1, source_target_pairs={{0,16},{16,0},{1,17},{17,1},{2,18},{18,2},{3,19},{19,3},{4,20},{20... | collective-permute-start | bytes 3538952 | tf_op jit(solution)/shard_map/ppermute | solution.py:30
  945.3 41.0 %all-to-all-start.20 = ((bf16[4,128,1536]{2,1,0:T(8,128)(2,1)}), bf16[4,128,1536]{2,1,0:T(8,128)(2,1)}, u32[]{:S(2)}, u32[]{:S(2)}) async-start(bf16[4,128,1536]{2,1,0:T(8,128)(2,1)} %bitcast.359), calls=%async_computation.20 | async-start | bytes 3145728 | tf_op jit(solution)/shard_map/all_to_all | solution.py:73
  1000.2 40.3 %all-to-all-start.21 = ((bf16[4,256,1536]{2,1,0:T(8,128)(2,1)}), bf16[4,256,1536]{2,1,0:T(8,128)(2,1)}, u32[]{:S(2)}, u32[]{:S(2)}) async-start(bf16[4,256,1536]{2,1,0:T(8,128)(2,1)} %bitcast.348), calls=%async_computation.21 | async-start | bytes 6291456 | tf_op jit(solution)/shard_map/all_to_all | solution.py:73
  1146.0 42.8 %all-to-all-start.23 = ((bf16[4,128,1664]{2,1,0:T(8,128)(2,1)}), bf16[4,128,1664]{2,1,0:T(8,128)(2,1)S(1)}, u32[]{:S(2)}, u32[]{:S(2)}) async-start(bf16[4,128,1664]{2,1,0:T(8,128)(2,1)} %tile.32), calls=%async_computation.23 | async-start | bytes 3407872 | tf_op jit(solution)/shard_map/all_to_all | solution.py:73
  1241.3 70.5 %reduce-scatter.6.cloned.1.call-start = ((), (), s32[]{:S(2)}) async-start(), calls=%async_computation.42 | async-start | bytes 491520 | tf_op jit(solution)/shard_map/reduce_scatter | solution.py:874
  1257.0 40.8 %all-to-all-start.28 = ((bf16[4,128,1536]{2,1,0:T(8,128)(2,1)}), bf16[4,128,1536]{2,1,0:T(8,128)(2,1)}, u32[]{:S(2)}, u32[]{:S(2)}) async-start(bf16[4,128,1536]{2,1,0:T(8,128)(2,1)} %bitcast.388), calls=%async_computation.28 | async-start | bytes 3145728 | tf_op jit(solution)/shard_map/all_to_all | solution.py:73
  1261.4 52.1 %reduce-scatter.4.cloned.1.call-start = ((), (), s32[]{:S(2)}) async-start(), calls=%async_computation.41 | async-start | bytes 983040 | tf_op jit(solution)/shard_map/reduce_scatter | solution.py:874
  1264.7 80.9 %reduce-scatter.8.cloned.1.call-start = ((), (), s32[]{:S(2)}) async-start(), calls=%async_computation.43 | async-start | bytes 1474560 | tf_op jit(solution)/shard_map/reduce_scatter | solution.py:874
  1297.8 50.0 %all-to-all-start.29 = ((bf16[4,384,768]{2,1,0:T(8,128)(2,1)}), bf16[4,384,768]{2,1,0:T(8,128)(2,1)}, u32[]{:S(2)}, u32[]{:S(2)}) async-start(bf16[4,384,768]{2,1,0:T(8,128)(2,1)} %bitcast.92), calls=%async_computation.29 | async-start | bytes 4718592 | tf_op jit(solution)/shard_map/all_to_all | solution.py:73
  1313.4 62.4 %collective-permute-start.16 = (bf16[384,128]{1,0:T(8,128)(2,1)}, bf16[384,128]{1,0:T(8,128)(2,1)}, u32[]{:S(2)}, u32[]{:S(2)}) collective-permute-start(bf16[384,128]{1,0:T(8,128)(2,1)} %get-tuple-element.392), channel_id=1, source_target_pairs={{0,16},{16,0},{1,17},{17,1},{2,18},{18,2},{3,19},{19,3},{4,20},{20... | collective-permute-start | bytes 294920 | tf_op jit(solution)/shard_map/ppermute | solution.py:30
  (204 other events, 3282.2 us)
Sparse Core Ops, SparseCore 0:
  14.0 48.1 all-gather.11
  64.0 38.9 all-gather.17
  104.5 12.1 all-gather.19
  118.1 13.2 all-gather.21
  132.8 13.2 all-gather.23
  167.1 39.3 all-gather.13
  335.7 42.7 all-gather.15
  1245.5 23.9 reduce-scatter.5
  1272.4 26.0 reduce-scatter.3
  1301.8 43.7 reduce-scatter.7

commit v8 on v7

--- a/solution.py
+++ b/solution.py
@@ -62,37 +62,46 @@
     return sigma * (1.0 + value * (1.0 - sigma))
 
 
-def spread(block):
+def groups():
     count = lax.axis_size("col")
-    if count > 4:
+    return count if count <= 4 else 1
+
+
+def spread(block, meanwhile=()):
+    if groups() == 1:
         return lax.all_gather(block, "col", axis=0, tiled=True)
-    return exchanged(jnp.tile(block, (count, 1)), "col")
+    received = [shifted(block, "col", back) for back in range(1, groups())]
+    return jnp.concatenate([block, *after(received, meanwhile)], axis=0)
+
+
+def in_order(blocks, axis):
+    count = len(blocks)
+    if count == 1:
+        return blocks[0]
+    rows = blocks[0].shape[0]
+    line = jnp.concatenate(blocks[::-1] + blocks[:0:-1], axis=0)
+    start = (count - 1 - lax.axis_index(axis)) * rows
+    return lax.dynamic_slice_in_dim(line, start, count * rows, axis=0)
+
+
+def sent_home(rows):
+    if groups() == 1:
+        return lax.psum_scatter(rows, "col", scatter_dimension=0, tiled=True)
+    return [shifted(block_of(rows, back), "col", -back) for back in range(1, groups())]
+
+
+def added_up(rows, received):
+    if groups() == 1:
+        return received.astype(FLOAT)
+    return sum([part.astype(FLOAT) for part in received], block_of(rows, 0).astype(FLOAT))
+
+
+def gathered_sum(rows, meanwhile=()):
+    return added_up(rows, after(sent_home(rows), meanwhile))
 
 
 def exchanged(rows, axis):
     return lax.all_to_all(rows, axis, split_axis=0, concat_axis=0, tiled=True)
-
-
-def summed(rows, axis):
-    count = lax.axis_size(axis)
-    rows = rows.reshape(count, rows.shape[0] // count, rows.shape[1])
-    return sum(rows[index].astype(FLOAT) for index in range(count))
-
-
-def sent_home(rows):
-    if lax.axis_size("col") > 4:
-        return lax.psum_scatter(rows, "col", scatter_dimension=0, tiled=True)
-    return exchanged(rows, "col")
-
-
-def added_up(received):
-    if lax.axis_size("col") > 4:
-        return received.astype(FLOAT)
-    return summed(received, "col")
-
-
-def gathered_sum(rows, meanwhile=()):
-    return added_up(after(sent_home(rows), meanwhile))
 
 
 def as_halves(columns):
@@ -103,6 +112,16 @@
 
 def from_halves(tile, count):
     return tile[:, :count].astype(FLOAT) + tile[:, count : 2 * count].astype(FLOAT)
+
+
+def block_of(values, back):
+    rows = values.shape[0] // groups()
+    return values[back * rows : (back + 1) * rows]
+
+
+def turn():
+    place = lax.axis_index("col") if groups() > 1 else jnp.int32(0)
+    return place.astype(jnp.int32).reshape(1)
 
 
 def route_tables(meta, top, capacity, layers):
@@ -185,19 +204,41 @@
     return result
 
 
+def copy_in_order(source_ref, target_ref, place_ref, parts):
+    if parts == 1:
+        return source_ref
+    rows = source_ref.shape[0] // parts
+    for index in range(parts):
+        target_ref[index * rows : (index + 1) * rows, :] = source_ref[
+            block_rows(index, rows, place_ref, parts), :
+        ]
+    return target_ref
+
+
+def block_rows(index, rows, place_ref, parts):
+    if parts == 1:
+        return slice(0, rows)
+    back = lax.rem(place_ref[0] - index + parts, parts)
+    return pl.ds(pl.multiple_of(back * rows, rows), rows)
+
+
 def mixer_forward_kernel(
     heads,
-    pre_ref,
-    pre_other_ref,
+    parts,
+    pre_in_ref,
+    pre_other_in_ref,
     conv_input_ref,
     conv_state_ref,
     step_row_ref,
     wide_row_ref,
     marks_ref,
     labels_ref,
+    place_ref,
     y_ref,
     scaled_ref,
     total_ref,
+    pre_ref,
+    pre_other_ref,
     x_ref,
     dosed_ref,
     keys_ref,
@@ -207,6 +248,8 @@
     states = conv_state_ref.shape[1] // 2
     state_at, step_at = wide, wide
     head_width = HEAD
+    pre_ref = copy_in_order(pre_in_ref, pre_ref, place_ref, parts)
+    pre_other_ref = copy_in_order(pre_other_in_ref, pre_other_ref, place_ref, parts)
     _, sizes, rate = step_sizes(pre_other_ref[:, step_at : step_at + LANES], step_row_ref)
     running = summed_rows(sizes * rate, False)
     running_t = running.T
@@ -266,31 +309,44 @@
         gate = pre_ref[:, columns]
         gated = y * gate * sigmoid(gate)
         y_ref[:, columns] = y
-        scaled_ref[:, columns] = (gated * wide_row_ref[0:1, columns]).astype(HALF)
+        scaled = (gated * wide_row_ref[0:1, columns]).astype(HALF)
+        each = length // parts
+        for index in range(parts):
+            block_at = block_rows(index, each, place_ref, parts)
+            scaled_ref[block_at, columns] = scaled[index * each : (index + 1) * each]
         total = total + jnp.sum(gated * gated, axis=1, keepdims=True)
-    total_ref[...] = total
+    each = length // parts
+    for index in range(parts):
+        block_at = block_rows(index, each, place_ref, parts)
+        total_ref[block_at, :] = total[index * each : (index + 1) * each]
 
 
 def mixer_backward_kernel(
     heads,
+    parts,
     inner_all,
-    pre_ref,
-    pre_other_ref,
+    pre_in_ref,
+    pre_other_in_ref,
     y_ref,
-    grad_ref,
-    sides_ref,
+    grad_in_ref,
+    sides_in_ref,
     conv_input_ref,
     conv_state_ref,
     step_row_ref,
     wide_row_ref,
     marks_ref,
     labels_ref,
+    place_ref,
     grad_pre_ref,
     grad_pre_other_ref,
     wide_grad_ref,
     conv_input_grad_ref,
     conv_state_grad_ref,
     step_grad_ref,
+    pre_ref,
+    pre_other_ref,
+    grad_ref,
+    sides_ref,
     x_ref,
     dosed_ref,
     dose_ref,
@@ -305,6 +361,18 @@
     states = conv_state_ref.shape[1] // 2
     state_at, step_at = wide, wide
     head_width = HEAD
+    each = length // parts
+    pre_ref = copy_in_order(pre_in_ref, pre_ref, place_ref, parts)
+    pre_other_ref = copy_in_order(pre_other_in_ref, pre_other_ref, place_ref, parts)
+    grad_ref = copy_in_order(grad_in_ref, grad_ref, place_ref, parts)
+    sides_ref = copy_in_order(sides_in_ref, sides_ref, place_ref, parts)
+
+    def put(target_ref, value, start):
+        for index in range(parts):
+            target_ref[block_rows(index, each, place_ref, parts), start : start + LANES] = value[
+                index * each : (index + 1) * each
+            ]
+
     shifted_pre, sizes, rate = step_sizes(pre_other_ref[:, step_at : step_at + LANES], step_row_ref)
     running = summed_rows(sizes * rate, False)
     running_t = running.T
@@ -324,7 +392,7 @@
         wide_grad_ref[0:1, columns] = jnp.sum(grad * normed, axis=0, keepdims=True)
         grad_gated = rr * gain * grad - gated * pull
         slope = sigma * (1.0 + gate * (1.0 - sigma))
-        grad_pre_ref[:, start : start + LANES] = (grad_gated * y * slope).astype(HALF)
+        put(grad_pre_ref, (grad_gated * y * slope).astype(HALF), start)
         dy = grad_gated * silu
         dy_ref[:, columns] = dy
         conv = conv_rows(
@@ -412,7 +480,7 @@
             marks_ref,
             conv_input_grad_ref,
         )
-        grad_pre_other_ref[:, start : start + LANES] = grad_in.astype(HALF)
+        put(grad_pre_other_ref, grad_in.astype(HALF), start)
     for start in range(0, 2 * states, LANES):
         columns = slice(start, start + LANES)
         grad_in = conv_rows_back(
@@ -423,19 +491,26 @@
             marks_ref,
             conv_state_grad_ref,
         )
-        grad_pre_ref[:, state_at + start : state_at + start + LANES] = grad_in.astype(HALF)
+        put(grad_pre_ref, grad_in.astype(HALF), state_at + start)
     crossing = summed_rows(balance, True)
     grad_step = (direct + rate * crossing) * sigmoid(shifted_pre)
-    grad_pre_other_ref[:, step_at : step_at + LANES] = grad_step.astype(HALF)
+    put(grad_pre_other_ref, grad_step.astype(HALF), step_at)
     for start in range(step_at + LANES, grad_pre_other_ref.shape[1], LANES):
-        grad_pre_other_ref[:, start : start + LANES] = jnp.zeros((length, LANES), HALF)
+        put(grad_pre_other_ref, jnp.zeros((length, LANES), HALF), start)
     step_grad_ref[0:1, :] = jnp.sum(grad_step, axis=0, keepdims=True)
     step_grad_ref[1:2, :] = rate * jnp.sum(sizes * crossing, axis=0, keepdims=True)
 
 
-def whole_call(kernel, results, scratch, name):
+def ordered_copy(shape):
+    return pltpu.VMEM(shape if groups() > 1 else (8, LANES), FLOAT)
+
+
+def whole_call(kernel, inputs, results, scratch, name):
+    whole = pl.BlockSpec(memory_space=pltpu.VMEM)
+    place = pl.BlockSpec(memory_space=pltpu.SMEM)
     return pl.pallas_call(
         kernel,
+        in_specs=[whole] * (inputs - 1) + [place],
         out_shape=results,
         scratch_shapes=scratch,
         compiler_params=pltpu.CompilerParams(vmem_limit_bytes=VMEM_BYTES),
@@ -445,16 +520,19 @@
 
 def mixer_forward(pre, heads, wide, mixer):
     length = pre[0].shape[0]
-    kernel = functools.partial(mixer_forward_kernel, heads)
+    kernel = functools.partial(mixer_forward_kernel, heads, groups())
     states = mixer[1].shape[1] // 2
     return whole_call(
         kernel,
+        2 + len(mixer),
         (
             jax.ShapeDtypeStruct((length, wide), FLOAT),
             jax.ShapeDtypeStruct((length, wide), HALF),
             jax.ShapeDtypeStruct((length, 1), FLOAT),
         ),
         [
+            ordered_copy(pre[0].shape),
+            ordered_copy(pre[1].shape),
             pltpu.VMEM((length, wide), FLOAT),
             pltpu.VMEM((length, wide), HALF),
             pltpu.VMEM((length, states), HALF),
@@ -466,11 +544,12 @@
 
 def mixer_backward(pre, y, grad, sides, heads, mixer):
     length, wide = y.shape
-    kernel = functools.partial(mixer_backward_kernel, heads, DI)
+    kernel = functools.partial(mixer_backward_kernel, heads, groups(), DI)
     double = mixer[1].shape[1]
     square = pltpu.VMEM((length, wide), FLOAT)
     return whole_call(
         kernel,
+        5 + len(mixer),
         (
             jax.ShapeDtypeStruct(pre[0].shape, HALF),
             jax.ShapeDtypeStruct(pre[1].shape, HALF),
@@ -480,6 +559,10 @@
             jax.ShapeDtypeStruct((2, LANES), FLOAT),
         ),
         [
+            ordered_copy(pre[0].shape),
+            ordered_copy(pre[1].shape),
+            ordered_copy(y.shape),
+            ordered_copy(sides.shape),
             square,
             pltpu.VMEM((length, wide), HALF),
             square,
@@ -494,14 +577,15 @@
     )(*pre, y, grad, sides, *mixer)
 
 
-def through_experts(block, table, expert, beside, aside=None):
+def through_experts(block, table, expert, own, beside, aside=None):
     tokens = spread(block)
     arrived = to_experts(project(table, tokens))
     answer = expert(arrived)
     if aside is not None:
         answer = after(answer, aside(tokens))
-    answer = to_experts(answer)
-    return beside(tokens, answer), arrived, tokens
+    answered = to_experts(answer)
+    answered = after(answered, own(after(tokens, answer), after(arrived, answer)))
+    return beside(answered), arrived, tokens
 
 
 def line_product(values, weights):
@@ -579,6 +663,21 @@
     first = lax.axis_index("section") == 0
     keep = outer(left, jnp.where(first, first_right, second_right))
     return (keep + given.astype(FLOAT)).astype(HALF)
+
+
+def row_pieces(values, axis="row"):
+    count = lax.axis_size(axis)
+    rows = values.shape[0] // count
+    index = [lax.rem(lax.axis_index(axis) + ahead, count) * rows for ahead in range(count)]
+    return [lax.dynamic_slice_in_dim(values, at, rows, axis=0) for at in index]
+
+
+def total_of(own, received):
+    return sum([part.astype(FLOAT) for part in received], own.astype(FLOAT))
+
+
+def row_received(pieces, axis="row"):
+    return [shifted(piece, axis, ahead) for ahead, piece in enumerate(pieces) if ahead]
 
 
 def flat(parts):
@@ -699,8 +798,9 @@
         marks.append((prior == labels).astype(FLOAT))
     marks = jnp.stack(marks, axis=1)
     label_row = labels.astype(FLOAT)[None]
+    place = turn()
     mixers = [
-        (conv_in, conv_st, step_row, wide_row, marks, label_row)
+        (conv_in, conv_st, step_row, wide_row, marks, label_row, place)
         for _, _, conv_in, conv_st, step_row, wide_row in small_all
     ]
 
@@ -727,8 +827,11 @@
         kept["rows 0"], answer = expert_forward(rows, experts[0])
         return answer
 
-    def beside_0(block, result):
+    def own_0(block, rows):
         kept["shared 0"] = shared_forward(block, shared[0])
+        return kept["shared 0"]
+
+    def beside_0(result):
         return home_part(scaling[0], result, kept["shared 0"][2], shared[0])
 
     def aside_0(blocks):
@@ -736,7 +839,7 @@
         return kept["grads"]
 
     parts, rows_0, mids_0 = through_experts(
-        rms_norm(middle_0, norm_mids[0]).astype(HALF), plain[0], expert_0, beside_0, aside_0
+        rms_norm(middle_0, norm_mids[0]).astype(HALF), plain[0], expert_0, own_0, beside_0, aside_0
     )
     proj.append(both_halves(after(mine[1], parts)))
     out_0 = middle_0 + gathered_sum(parts)
@@ -753,21 +856,38 @@
         kept["grads 1"], back = expert_backward(grad_rows_1, kept["rows 1"], experts[1])
         return back
 
-    def beside_1(block, result):
+    def own_1(block, rows):
         kept["shared 1"] = shared_forward(block, shared[1])
-        kept["shared grads 1"], part = shared_backward(grad_tokens_1, kept["shared 1"], shared[1])
-        return (part + outer(plain[1], result)).astype(HALF)
+        kept["shared grads 1"], kept["part 1"] = shared_backward(
+            grad_tokens_1, kept["shared 1"], shared[1]
+        )
+        kept["sums 1"] = weight_sums(
+            rows,
+            grad_rows_1,
+            kept["rows 1"],
+            kept["grads 1"],
+            block,
+            grad_tokens_1,
+            kept["shared 1"],
+            kept["shared grads 1"],
+        )
+        experts_1, shared_1 = kept["sums 1"]
+        return experts_1, [made[-1] for made in shared_1]
+
+    def beside_1(result):
+        return (kept["part 1"] + outer(plain[1], result)).astype(HALF)
 
     parts, rows_1, mids_1 = through_experts(
-        rms_norm(middle_1, norm_mids[1]).astype(HALF), plain[1], expert_1, beside_1
+        rms_norm(middle_1, norm_mids[1]).astype(HALF), plain[1], expert_1, own_1, beside_1
     )
     answer_1 = to_experts(after(kept["answer 1"], parts))
 
     def mixer_back(s, grad_middle, along, rr, saved, meanwhile):
         wide_in, pre, y, scaled = saved
         sides = as_halves(jnp.concatenate([rr, along], axis=1))
-        payload = spread(jnp.concatenate([grad_middle.astype(HALF), sides], axis=1))
-        payload = after(payload, meanwhile)
+        payload = spread(
+            jnp.concatenate([grad_middle.astype(HALF), sides], axis=1), meanwhile
+        )
         wide_mix, sides = payload[:, :width], from_halves(payload[:, width:], 2)
         grad_scaled = project(wide_mix, proj_out[s])
         *grad_pre, wide_grads, grad_conv_input, grad_conv_state, step_grads = mixer_backward(
@@ -789,25 +909,13 @@
         give = jnp.where(first, second_value, first_value).astype(HALF)
         return keep.astype(FLOAT), swapped(give)
 
-    def row_sent(values):
-        return exchanged(values, "row")
-
-    def row_total(received):
-        return summed(received, "row").astype(HALF)
+    def row_sums(value):
+        return lax.psum_scatter(value, "row", scatter_dimension=0, tiled=True)
 
     grad_middle, along, grad_norm_mid_1 = middle_backward(
         gathered_sum(parts, answer_1), grad_now, middle_1, mixed_1, norm_mids[1]
     )
-    expert_grads_1, shared_grads_1 = weight_sums(
-        rows_1,
-        grad_rows_1,
-        kept["rows 1"],
-        kept["grads 1"],
-        mids_1,
-        grad_tokens_1,
-        kept["shared 1"],
-        kept["shared grads 1"],
-    )
+    expert_grads_1, shared_grads_1 = kept["sums 1"]
     home = home_part(scaling[1], answer_1, kept["shared 1"][2], shared[1])
     grad_pre, to_proj, to_out, tail, rest_1 = mixer_back(
         1,
@@ -815,74 +923,81 @@
         along,
         rr_1,
         (wide_in_1, pre_1, y_1, scaled_1),
-        (expert_grads_1, home, [made[-1] for made in shared_grads_1]),
+        home,
     )
     whole = line_product(grad_pre, proj[1])
-    given = half_to_give(*after(to_proj, whole))
-    given_out = half_to_give(*after(to_out, given))
-    grad_proj_1 = (*to_proj, swapped(given))
-    grad_out_1 = (*to_out, swapped(given_out))
-    grad_tail_1 = outer(after(wide_in_1, given_out), tail).astype(HALF)
-    shared_sent_1 = [row_sent(half_to_keep(*after(made, whole))) for made in shared_grads_1]
-    grad_in = gathered_sum(whole, (given, given_out, grad_tail_1, shared_sent_1))
+    grad_in = gathered_sum(whole)
     grad_1, grad_norm_in_1 = resid_back(out_0, norm_ins[1], grad_in, grad_middle)
+
+    def aside_back_0(blocks):
+        own_proj, own_out, own_tail = after((to_proj, to_out, tail), blocks)
+        given, given_out = half_to_give(*own_proj), half_to_give(*own_out)
+        made = (*shared_grads_1, (*own_out, swapped(given_out)), (*own_proj, swapped(given)))
+        made = [half_to_keep(*each) for each in after(made, (given, given_out))]
+        kept["sent 1"] = [row_sums(each) for each in made]
+        kept["tail 1"] = outer(own_proj[0], own_tail).astype(HALF)
+        kept["home"] = home
+        if groups() > 1:
+            kept["home"] = in_order([block_of(home, back) for back in range(groups())], "col")
+        kept["home"] = lax.psum_scatter(
+            after(kept["home"], made), "col", scatter_dimension=0, tiled=True
+        )
+        return made, kept["tail 1"]
 
     def expert_back_0(rows):
         kept["grads 0"], back = expert_backward(rows, kept["rows 0"], experts[0])
         return back
 
-    def beside_back_0(block, result):
-        kept["shared grads 0"], part = shared_backward(block, kept["shared 0"], shared[0])
-        return (part + outer(plain[0], result)).astype(HALF)
-
-    def aside_back_0(blocks):
-        sums = [half_to_keep(*after(made, blocks)) for made in (grad_out_1, grad_proj_1)]
-        kept["sums 1"] = sums
-        kept["home"] = after(sent_home(after(home, blocks)), sums)
-        return kept["home"]
+    def own_back_0(block, rows):
+        kept["shared grads 0"], kept["part 0"] = shared_backward(block, kept["shared 0"], shared[0])
+        kept["sums 0"] = weight_sums(
+            rows_0,
+            rows,
+            kept["rows 0"],
+            kept["grads 0"],
+            mids_0,
+            block,
+            kept["shared 0"],
+            kept["shared grads 0"],
+        )
+        experts_0, shared_0 = kept["sums 0"]
+        return experts_0, [made[-1] for made in shared_0]
+
+    def beside_back_0(result):
+        return (kept["part 0"] + outer(plain[0], result)).astype(HALF)
 
     parts, grad_rows_0, grad_tokens_0 = through_experts(
-        grad_1.astype(HALF), scaling[0], expert_back_0, beside_back_0, aside_back_0
-    )
-    out_1 = middle_1 + added_up(kept["home"])
-    mixer_sent_1 = [row_sent(after(made, parts)) for made in kept["sums 1"]]
+        grad_1.astype(HALF), scaling[0], expert_back_0, own_back_0, beside_back_0, aside_back_0
+    )
+    sums_1, grad_tail_1 = kept["sent 1"], kept["tail 1"]
     grad_middle, along, grad_norm_mid_0 = middle_backward(
-        gathered_sum(parts, (out_1, mixer_sent_1)), grad_1, middle_0, mixed_0, norm_mids[0]
-    )
-    expert_grads_0, shared_grads_0 = weight_sums(
-        rows_0,
-        grad_rows_0,
-        kept["rows 0"],
-        kept["grads 0"],
-        mids_0,
-        grad_tokens_0,
-        kept["shared 0"],
-        kept["shared grads 0"],
-    )
+        gathered_sum(parts), grad_1, middle_0, mixed_0, norm_mids[0]
+    )
+    expert_grads_0, shared_grads_0 = kept["sums 0"]
+    shared_sums_0 = [half_to_keep(*after(made, parts)) for made in shared_grads_0]
+    sums_0 = [row_sums(made) for made in shared_sums_0]
     expert_out = [own_layer(a, b) for a, b in zip(expert_grads_0, expert_grads_1)]
-    sums_1 = [row_total(received) for received in (*shared_sent_1, *mixer_sent_1)]
     grad_pre, to_proj, to_out, tail, rest_0 = mixer_back(
         0,
         grad_middle,
         along,
         rr_0,
         (wide_in_0, pre_0, y_0, scaled_0),
-        ([part[0] for part in expert_out], [made[-1] for made in shared_grads_0], sums_1),
-    )
-
-    def row_sums(value):
-        return lax.psum_scatter(value, "row", scatter_dimension=0, tiled=True)
-
-    sums_0 = [row_sums(half_to_keep(*after(made, to_out[0]))) for made in shared_grads_0]
+        ([part[0] for part in expert_out], shared_sums_0, sums_1),
+    )
+
     given = half_to_give(*to_proj)
     whole = line_product(after(grad_pre, given), proj[0])
     line_received = sent_home(whole)
-    proj_sent = row_sent(half_to_keep(*after((*to_proj, swapped(given)), whole)))
-    given_out = half_to_give(*after(to_out, whole))
-    sums_0.append(row_sums(half_to_keep(*after((*to_out, swapped(given_out)), proj_sent[:8]))))
+    proj_half = half_to_keep(*after((*to_proj, swapped(given)), whole))
+    proj_sums = row_sums(proj_half)
+    given_out = half_to_give(*after(to_out, proj_half))
     grad_tail_0 = outer(after(wide_in_0, given_out), tail).astype(HALF)
+    out_half = half_to_keep(*after((*to_out, swapped(given_out)), grad_tail_0))
+    sums_0.append(row_sums(out_half))
     tail_keep, tail_other = own_layer(grad_tail_0, grad_tail_1)
-    tail_sent = row_sent((tail_keep + tail_other.astype(FLOAT)).astype(HALF))
+    tail_pieces = row_pieces((tail_keep + tail_other.astype(FLOAT)).astype(HALF))
+    tail_received = row_received(tail_pieces)
     wide_x = wide_tokens.astype(FLOAT)
     wide_r = lax.rsqrt(jnp.mean(wide_x * wide_x, axis=1, keepdims=True) + EPS)
     grad_norm_in_0 = jnp.sum(whole.astype(FLOAT) * wide_x * wide_r, axis=0)
@@ -893,16 +1008,15 @@
     shapes = [part.shape for part in smalls[0]]
     small_keep, small_other = own_layer(flat(smalls[0]), flat(smalls[1]))
     vector = small_keep + small_other.astype(FLOAT)
-    lines = row_sent(jnp.tile(vector[None], (n_row, 1)))
-    expert_out = [keep + other.astype(FLOAT) for keep, other in after(expert_out, given_out)]
-    line_received, proj_sent, tail_sent, lines = after(
-        (line_received, proj_sent, tail_sent, lines), expert_out
-    )
-    grad_in = added_up(line_received)
-    sums_0.append(row_total(proj_sent))
-    tail = row_total(tail_sent)
-    vector = jnp.sum(lines, axis=0)
+    lines = [shifted(vector[None], "row", back) for back in range(n_row)]
+    expert_out = [keep + other.astype(FLOAT) for keep, other in after(expert_out, out_half)]
+    line_received, tail_received, lines = after((line_received, tail_received, lines), expert_out)
+    grad_in = added_up(whole, line_received)
+    sums_0.append(proj_sums)
+    tail = total_of(tail_pieces[0], tail_received).astype(HALF)
+    vector = jnp.sum(in_order(lines, "row"), axis=0)
     grad_0, _ = resid_back(tokens_now, norm_ins[0], grad_in, grad_middle)
+    out_1 = middle_1 + kept["home"].astype(FLOAT)
 
     def own_halves(first_value, second_value):
         keep = jnp.where(first, first_value, second_value)
@@ -917,14 +1031,14 @@
     outs, in_grads = per_micro(out_0, after(out_1, grad_in)), per_micro(grad_0, grad_1)
     common = 2 * width + conv_state.shape[1] * state
     state_grad = tail[:, :state]
-    if n_col <= 4:
-        state_sent = exchanged(state_grad, "col")
-        lines = exchanged(jnp.tile(vector[None, :common], (n_col, 1)), "col")
-        state_sent, lines, halves, outs, in_grads = after(
-            (state_sent, lines, halves, outs, in_grads)
-        )
-        state_grad = spread(summed(state_sent, "col").astype(HALF))
-        shared_sum = jnp.sum(lines, axis=0)
+    if groups() > 1:
+        state_pieces = row_pieces(state_grad, "col")
+        state_received = row_received(state_pieces, "col")
+        lines = [shifted(vector[None, :common], "col", back) for back in range(n_col)]
+        state_received, lines, outs, in_grads = after((state_received, lines, outs, in_grads))
+        state_grad = total_of(state_pieces[0], state_received).astype(HALF)
+        state_grad = in_order([shifted(state_grad, "col", back) for back in range(n_col)], "col")
+        shared_sum = jnp.sum(in_order(lines, "col"), axis=0)
     else:
         state_grad = lax.psum(state_grad, "col")
         shared_sum = lax.psum(vector[:common], "col")

time: 1420 us -> 1210 us (0.85)
  blocking collectives: 138 us -> 0 us
  waiting for transfers between devices: 657 us -> 567 us
  starting transfers between devices: 143 us -> 183 us
  other arithmetic: 78.7 us -> 62.7 us
    all_to_all x31 -> x8, waiting for transfers between devices: 615 us -> 108 us  [exchanged(): return lax.all_to_all(rows, axis, split_axis=0, concat_axis=0, tiled=True)]
    ppermute x0 -> x63, waiting for transfers between devices: none -> 395 us  [shifted(): lax.ppermute(block, axis, [(i, (i + distance) % count) for i in range(cou...]
    all_to_all x4 -> x0, blocking collectives: 138 us -> none  [exchanged(): return lax.all_to_all(rows, axis, split_axis=0, concat_axis=0, tiled=True)]
    ppermute x0 -> x63, starting transfers between devices: none -> 137 us  [shifted(): lax.ppermute(block, axis, [(i, (i + distance) % count) for i in range(cou...]
    all_to_all x31 -> x8, starting transfers between devices: 136 us -> 37.9 us  [exchanged(): return lax.all_to_all(rows, axis, split_axis=0, concat_axis=0, tiled=True)]
    all_to_all x9 -> x0, local copies, waits for them, and re-layouts: 20 us -> none  [exchanged(): return lax.all_to_all(rows, axis, split_axis=0, concat_axis=0, tiled=True)]
    reduce_scatter x3 -> x8, waiting for transfers between devices: 28.5 us -> 31 us  [row_sums(): return lax.psum_scatter(value, 'row', scatter_dimension=0, tiled=True)]
  transfers between devices with their start and end apart: 63 -> 109, of which waited for: 32 -> 43; matrix products, arithmetic and copies ran while one was open for 21% -> 24% of each run, Pallas kernels for 2% -> 4%
where the time goes in v8:
time: 1210 us; the launch traced here: 1190 us
  waiting for transfers between devices  567 us (47%)
  matrix products  250 us (21%)
  starting transfers between devices  183 us (15%)
  other arithmetic  62.7 us (5%)
  Pallas kernels  59.4 us (5%)
  local copies, waits for them, and re-layouts  54.6 us (5%)
  between operations  17.4 us (1%)
    ppermute x63, waiting for transfers between devices, shifted(): lax.ppermute(block, axis, [(i, (i + distance) % count) for i in range(cou...  395 us
    ppermute x63, starting transfers between devices, shifted(): lax.ppermute(block, axis, [(i, (i + distance) % count) for i in range(cou...  137 us
    all_to_all x8, waiting for transfers between devices, exchanged(): return lax.all_to_all(rows, axis, split_axis=0, concat_axis=0, tiled=True)  108 us
    dot_general x28, matrix products, outer(): lax.dot_general(left, right, (((0,), (0,)), ((), ())), preferred_element_...  106 us
    dot_general x23, matrix products, project(): return jnp.dot(left, right, preferred_element_type=FLOAT)  82.2 us
    dot_general x18, matrix products, project_back(): lax.dot_general(left, right, (((1,), (1,)), ((), ())), preferred_element_...  61.8 us
    all_to_all x8, starting transfers between devices, exchanged(): return lax.all_to_all(rows, axis, split_axis=0, concat_axis=0, tiled=True)  37.9 us
    pallas_call x2, Pallas kernels, mixer_backward(): whole_call(kernel, 5 + len(mixer), (jax.ShapeDtypeStruct(pre[0].shape, HA...  34.4 us
  transfers between devices with their start and end apart: 109, of which 43 were waited for; matrix products, arithmetic and copies ran while one was open for 24% of the time, Pallas kernels for 4%

profile of v8, /device:TPU:0, one launch (start us, length us, event | category | flops | bytes accessed | tf_op | source)
XLA Modules:
  0.0 1193.9 jit_solution(13260508134451397964)
XLA Ops:
  32.9 16.4 %collective-permute-done.1 = bf16[128,1536]{1,0:T(8,128)(2,1)S(1)} collective-permute-done((bf16[128,1536]{1,0:T(8,128)(2,1)S(1)}, bf16[128,1536]{1,0:T(8,128)(2,1)S(1)}, u32[]{:S(2)}, u32[]{:S(2)}) %collective-permute-start.1) | collective-permute-done | bytes 393248 | tf_op jit(solution)/shard_map/ppermute | solution.py:26
  51.6 10.5 all-gather.12.cloned.1.call-done
  69.3 12.7 %mixer_forward.2 = (f32[512,768]{1,0:T(8,128)S(1)}, bf16[512,768]{1,0:T(8,128)(2,1)S(1)}, f32[512,1]{1,0:T(8,128)S(1)}) custom-call(f32[512,1024]{1,0:T(8,128)S(1)} %fusion.25.pre_in_ref, f32[512,1024]{1,0:T(8,128)} %fusion.22.pre_other_in_ref, f32[4,768]{1,0:T(4,128)S(1)} %reshape.420.conv_input_ref, f32[4,256]{1,0:T(4,128)S(1)} %slice.465.conv_state_ref, ...), custom_call_target="tpu_custom_call" | custom-call | tf_op jit(solution)/shard_map/mixer_forward/pallas_call | solution.py:525
  87.8 15.2 %all-gather.18.cloned.1.call-done = bf16[1,3072,768]{2,1,0:T(8,128)(2,1)} async-done(((bf16[1,384,768]{2,1,0:T(8,128)(2,1)}), bf16[1,3072,768]{2,1,0:T(8,128)(2,1)}) %all-gather.18.cloned.1.call-update) | async-done | bytes 4718608 | tf_op jit(solution)/shard_map/all_gather | solution.py:763
  121.1 26.7 %collective-permute-done.6 = bf16[128,1664]{1,0:T(8,128)(2,1)} collective-permute-done((bf16[128,1664]{1,0:T(8,128)(2,1)}, bf16[128,1664]{1,0:T(8,128)(2,1)}, u32[]{:S(2)}, u32[]{:S(2)}) %collective-permute-start.6) | collective-permute-done | bytes 426016 | tf_op jit(solution)/shard_map/ppermute | solution.py:26
  165.3 15.4 %collective-permute-done.13 = bf16[128,1536]{1,0:T(8,128)(2,1)S(1)} collective-permute-done((bf16[128,1536]{1,0:T(8,128)(2,1)S(1)}, bf16[128,1536]{1,0:T(8,128)(2,1)S(1)}, u32[]{:S(2)}, u32[]{:S(2)}) %collective-permute-start.13) | collective-permute-done | bytes 393248 | tf_op jit(solution)/shard_map/ppermute | solution.py:26
  212.5 14.6 %collective-permute-done.16 = bf16[128,1536]{1,0:T(8,128)(2,1)S(1)} collective-permute-done((bf16[128,1536]{1,0:T(8,128)(2,1)S(1)}, bf16[128,1536]{1,0:T(8,128)(2,1)S(1)}, u32[]{:S(2)}, u32[]{:S(2)}) %collective-permute-start.16) | collective-permute-done | bytes 393248 | tf_op jit(solution)/shard_map/ppermute | solution.py:26
  256.8 31.1 %all-to-all-done.1 = bf16[4,256,1536]{2,1,0:T(8,128)(2,1)} async-done(((bf16[4,256,1536]{2,1,0:T(8,128)(2,1)}), bf16[4,256,1536]{2,1,0:T(8,128)(2,1)}, u32[]{:S(2)}, u32[]{:S(2)}) %all-to-all-start.1) | async-done | bytes 3145760 | tf_op jit(solution)/shard_map/all_to_all | solution.py:104
  315.1 25.1 %collective-permute-done.19 = bf16[128,1536]{1,0:T(8,128)(2,1)S(1)} collective-permute-done((bf16[128,1536]{1,0:T(8,128)(2,1)S(1)}, bf16[128,1536]{1,0:T(8,128)(2,1)S(1)}, u32[]{:S(2)}, u32[]{:S(2)}) %collective-permute-start.19) | collective-permute-done | bytes 393248 | tf_op jit(solution)/shard_map/ppermute | solution.py:26
  356.3 9.9 collective-permute-done.21
  366.2 14.3 %collective-permute-done.22 = bf16[128,1536]{1,0:T(8,128)(2,1)S(1)} collective-permute-done((bf16[128,1536]{1,0:T(8,128)(2,1)S(1)}, bf16[128,1536]{1,0:T(8,128)(2,1)S(1)}, u32[]{:S(2)}, u32[]{:S(2)}) %collective-permute-start.22) | collective-permute-done | bytes 393248 | tf_op jit(solution)/shard_map/ppermute | solution.py:26
  389.8 12.3 %mixer_forward.3 = (f32[512,768]{1,0:T(8,128)S(1)}, bf16[512,768]{1,0:T(8,128)(2,1)S(1)}, f32[512,1]{1,0:T(8,128)S(1)}) custom-call(f32[512,1024]{1,0:T(8,128)S(1)} %fusion.18.pre_in_ref, f32[512,1024]{1,0:T(8,128)} %fusion.14.pre_other_in_ref, f32[4,768]{1,0:T(4,128)S(1)} %reshape.425.conv_input_ref, f32[4,256]{1,0:T(4,128)S(1)} %slice.500.conv_state_ref, ...), custom_call_target="tpu_custom_call" | custom-call | tf_op jit(solution)/shard_map/mixer_forward/pallas_call | solution.py:525
  417.7 9.7 collective-permute-done.24
  427.4 26.2 %collective-permute-done.25 = bf16[128,1664]{1,0:T(8,128)(2,1)S(1)} collective-permute-done((bf16[128,1664]{1,0:T(8,128)(2,1)S(1)}, bf16[128,1664]{1,0:T(8,128)(2,1)S(1)}, u32[]{:S(2)}, u32[]{:S(2)}) %collective-permute-start.25) | collective-permute-done | bytes 426016 | tf_op jit(solution)/shard_map/ppermute | solution.py:26
  459.2 10.0 collective-permute-done.27
  469.2 14.1 %collective-permute-done.28 = bf16[128,1536]{1,0:T(8,128)(2,1)S(1)} collective-permute-done((bf16[128,1536]{1,0:T(8,128)(2,1)S(1)}, bf16[128,1536]{1,0:T(8,128)(2,1)S(1)}, u32[]{:S(2)}, u32[]{:S(2)}) %collective-permute-start.28) | collective-permute-done | bytes 393248 | tf_op jit(solution)/shard_map/ppermute | solution.py:26
  501.0 26.1 %all-to-all-done.3 = bf16[4,256,1536]{2,1,0:T(8,128)(2,1)} async-done(((bf16[4,256,1536]{2,1,0:T(8,128)(2,1)}), bf16[4,256,1536]{2,1,0:T(8,128)(2,1)}, u32[]{:S(2)}, u32[]{:S(2)}) %all-to-all-start.3) | async-done | bytes 3145760 | tf_op jit(solution)/shard_map/all_to_all | solution.py:104
  579.2 12.7 %all-to-all-done.4 = bf16[4,256,1536]{2,1,0:T(8,128)(2,1)} async-done(((bf16[4,256,1536]{2,1,0:T(8,128)(2,1)}), bf16[4,256,1536]{2,1,0:T(8,128)(2,1)}, u32[]{:S(2)}, u32[]{:S(2)}) %all-to-all-start.4) | async-done | bytes 3145760 | tf_op jit(solution)/shard_map/all_to_all | solution.py:104
  624.3 25.0 %collective-permute-done.33 = bf16[128,1536]{1,0:T(8,128)(2,1)} collective-permute-done((bf16[128,1536]{1,0:T(8,128)(2,1)}, bf16[128,1536]{1,0:T(8,128)(2,1)}, u32[]{:S(2)}, u32[]{:S(2)}) %collective-permute-start.33) | collective-permute-done | bytes 393248 | tf_op jit(solution)/shard_map/ppermute | solution.py:26
  668.8 15.6 %collective-permute-done.36 = bf16[128,1664]{1,0:T(8,128)(2,1)S(1)} collective-permute-done((bf16[128,1664]{1,0:T(8,128)(2,1)S(1)}, bf16[128,1664]{1,0:T(8,128)(2,1)S(1)}, u32[]{:S(2)}, u32[]{:S(2)}) %collective-permute-start.36) | collective-permute-done | bytes 426016 | tf_op jit(solution)/shard_map/ppermute | solution.py:26
  686.1 17.1 %mixer_backward.2 = (bf16[512,1024]{1,0:T(8,128)(2,1)S(1)}, bf16[512,1024]{1,0:T(8,128)(2,1)S(1)}, f32[2,768]{1,0:T(2,128)S(1)}, f32[4,768]{1,0:T(4,128)S(1)}, f...) custom-call(f32[512,1024]{1,0:T(8,128)} %copy-done.3, f32[512,1024]{1,0:T(8,128)} %fusion.14.pre_other_in_ref, ...), custom_call_target="tpu_custom_call" | custom-call | tf_op jit(solution)/shard_map/mixer_backward/pallas_call | solution.py:550
  710.8 9.8 collective-permute-start.38
  730.2 24.2 %collective-permute-done.39 = bf16[128,1536]{1,0:T(8,128)(2,1)S(1)} collective-permute-done((bf16[128,1536]{1,0:T(8,128)(2,1)S(1)}, bf16[128,1536]{1,0:T(8,128)(2,1)S(1)}, u32[]{:S(2)}, u32[]{:S(2)}) %collective-permute-start.39) | collective-permute-done | bytes 393248 | tf_op jit(solution)/shard_map/ppermute | solution.py:26
  770.1 14.1 %collective-permute-done.42 = bf16[128,1536]{1,0:T(8,128)(2,1)S(1)} collective-permute-done((bf16[128,1536]{1,0:T(8,128)(2,1)S(1)}, bf16[128,1536]{1,0:T(8,128)(2,1)S(1)}, u32[]{:S(2)}, u32[]{:S(2)}) %collective-permute-start.42) | collective-permute-done | bytes 393248 | tf_op jit(solution)/shard_map/ppermute | solution.py:26
  833.0 19.8 %all-to-all-done.6 = bf16[4,256,1536]{2,1,0:T(8,128)(2,1)} async-done(((bf16[4,256,1536]{2,1,0:T(8,128)(2,1)}), bf16[4,256,1536]{2,1,0:T(8,128)(2,1)}, u32[]{:S(2)}, u32[]{:S(2)}) %all-to-all-start.6) | async-done | bytes 3145760 | tf_op jit(solution)/shard_map/all_to_all | solution.py:104
  900.1 18.3 %all-to-all-done.7 = bf16[4,256,1536]{2,1,0:T(8,128)(2,1)} async-done(((bf16[4,256,1536]{2,1,0:T(8,128)(2,1)}), bf16[4,256,1536]{2,1,0:T(8,128)(2,1)}, u32[]{:S(2)}, u32[]{:S(2)}) %all-to-all-start.7) | async-done | bytes 3145760 | tf_op jit(solution)/shard_map/all_to_all | solution.py:104
  928.9 15.0 %collective-permute-start.48 = (bf16[128,1536]{1,0:T(8,128)(2,1)}, bf16[128,1536]{1,0:T(8,128)(2,1)S(1)}, u32[]{:S(2)}, u32[]{:S(2)}) collective-permute-start(bf16[128,1536]{1,0:T(8,128)(2,1)} %get-tuple-element.489), channel_id=1, source_target_pairs={{0,3},{1,0},{2,1},{3,2},{4,7},{5,4},{6,5},{7,6},{8,11},{9,8},{10,9... | collective-permute-start | bytes 1179656 | tf_op jit(solution)/shard_map/ppermute | solution.py:26
  953.9 23.6 %collective-permute-done.49 = bf16[128,1536]{1,0:T(8,128)(2,1)S(1)} collective-permute-done((bf16[128,1536]{1,0:T(8,128)(2,1)}, bf16[128,1536]{1,0:T(8,128)(2,1)S(1)}, u32[]{:S(2)}, u32[]{:S(2)}) %collective-permute-start.49) | collective-permute-done | bytes 393248 | tf_op jit(solution)/shard_map/ppermute | solution.py:26
  997.1 21.2 %collective-permute-done.52 = bf16[128,1664]{1,0:T(8,128)(2,1)S(1)} collective-permute-done((bf16[128,1664]{1,0:T(8,128)(2,1)}, bf16[128,1664]{1,0:T(8,128)(2,1)S(1)}, u32[]{:S(2)}, u32[]{:S(2)}) %collective-permute-start.52) | collective-permute-done | bytes 426016 | tf_op jit(solution)/shard_map/ppermute | solution.py:26
  1022.4 17.3 %mixer_backward.3 = (bf16[512,1024]{1,0:T(8,128)(2,1)S(1)}, bf16[512,1024]{1,0:T(8,128)(2,1)S(1)}, f32[2,768]{1,0:T(2,128)S(1)}, f32[4,768]{1,0:T(4,128)S(1)}, f...) custom-call(f32[512,1024]{1,0:T(8,128)} %copy-done.2, f32[512,1024]{1,0:T(8,128)} %fusion.22.pre_other_in_ref, ...), custom_call_target="tpu_custom_call" | custom-call | tf_op jit(solution)/shard_map/mixer_backward/pallas_call | solution.py:550
  1068.2 28.6 %reduce-scatter.24.cloned.1.call-done = bf16[384,256]{1,0:T(8,128)(2,1)} async-done(((bf16[1536,256]{1,0:T(8,128)(2,1)}), bf16[384,256]{1,0:T(8,128)(2,1)}) %reduce-scatter.24.cloned.1.call-update) | async-done | bytes 196624 | tf_op jit(solution)/shard_map/reduce_scatter | solution.py:913
  1134.0 13.1 %collective-permute-done.57 = bf16[128,1536]{1,0:T(8,128)(2,1)} collective-permute-done((bf16[128,1536]{1,0:T(8,128)(2,1)}, bf16[128,1536]{1,0:T(8,128)(2,1)}, u32[]{:S(2)}, u32[]{:S(2)}) %collective-permute-start.57) | collective-permute-done | bytes 393248 | tf_op jit(solution)/shard_map/ppermute | solution.py:26
  (893 shorter events, 611.0 us)
Async XLA Ops:
  7.2 54.9 %all-gather.12.cloned.1.call-start = ((), (), s32[]{:S(2)}) async-start(), calls=%async_computation.17 | async-start | bytes 7077888 | tf_op jit(solution)/shard_map/all_gather | solution.py:757
  13.8 89.1 %all-gather.18.cloned.1.call-start = ((), (), s32[]{:S(2)}) async-start(), calls=%async_computation.29 | async-start | bytes 5308416 | tf_op jit(solution)/shard_map/all_gather | solution.py:763
  14.6 214.8 %all-gather.20.cloned.1.call-start = ((), (), s32[]{:S(2)}) async-start(), calls=%async_computation.30 | async-start | bytes 4718592 | tf_op jit(solution)/shard_map/all_gather | solution.py:767
  15.5 219.4 %all-gather.22.cloned.1.call-start = ((), (), s32[]{:S(2)}) async-start(), calls=%async_computation.31 | async-start | bytes 4718592 | tf_op jit(solution)/shard_map/all_gather | solution.py:768
  16.0 225.5 %all-gather.24.cloned.1.call-start = ((), (), s32[]{:S(2)}) async-start(), calls=%async_computation.32 | async-start | bytes 4718592 | tf_op jit(solution)/shard_map/all_gather | solution.py:769
  16.6 234.8 %all-gather.14.cloned.1.call-start = ((), (), s32[]{:S(2)}) async-start(), calls=%async_computation.18 | async-start | bytes 5308416 | tf_op jit(solution)/shard_map/all_gather | solution.py:763
  110.5 37.3 %collective-permute-start.6 = (bf16[128,1664]{1,0:T(8,128)(2,1)}, bf16[128,1664]{1,0:T(8,128)(2,1)}, u32[]{:S(2)}, u32[]{:S(2)}) collective-permute-start(bf16[128,1664]{1,0:T(8,128)(2,1)} %get-tuple-element.483), channel_id=1, source_target_pairs={{0,2},{1,3},{2,0},{3,1},{4,6},{5,7},{6,4},{7,5},{8,10},{9,11},{10,... | collective-permute-start | bytes 1277960 | tf_op jit(solution)/shard_map/ppermute | solution.py:26
  110.5 37.3 %collective-permute-start.7 = (bf16[128,1664]{1,0:T(8,128)(2,1)}, bf16[128,1664]{1,0:T(8,128)(2,1)}, u32[]{:S(2)}, u32[]{:S(2)}) collective-permute-start(bf16[128,1664]{1,0:T(8,128)(2,1)} %get-tuple-element.481), channel_id=1, source_target_pairs={{0,1},{1,2},{2,3},{3,0},{4,5},{5,6},{6,7},{7,4},{8,9},{9,10},{10,1... | collective-permute-start | bytes 1277960 | tf_op jit(solution)/shard_map/ppermute | solution.py:26
  184.1 45.3 %all-to-all-start = ((bf16[4,256,1536]{2,1,0:T(8,128)(2,1)}), bf16[4,256,1536]{2,1,0:T(8,128)(2,1)}, u32[]{:S(2)}, u32[]{:S(2)}) async-start(bf16[4,256,1536]{2,1,0:T(8,128)(2,1)} %bitcast.267), calls=%async_computation | async-start | bytes 6291456 | tf_op jit(solution)/shard_map/all_to_all | solution.py:104
  246.7 41.2 %all-to-all-start.1 = ((bf16[4,256,1536]{2,1,0:T(8,128)(2,1)}), bf16[4,256,1536]{2,1,0:T(8,128)(2,1)}, u32[]{:S(2)}, u32[]{:S(2)}) async-start(bf16[4,256,1536]{2,1,0:T(8,128)(2,1)} %bitcast.268), calls=%async_computation.1 | async-start | bytes 6291456 | tf_op jit(solution)/shard_map/all_to_all | solution.py:104
  251.3 129.2 %all-gather.16.cloned.1.call-start = ((), (), s32[]{:S(2)}) async-start(), calls=%async_computation.19 | async-start | bytes 7077888 | tf_op jit(solution)/shard_map/all_gather | solution.py:757
  346.8 57.4 %all-to-all-start.2 = ((bf16[4,256,1536]{2,1,0:T(8,128)(2,1)}), bf16[4,256,1536]{2,1,0:T(8,128)(2,1)}, u32[]{:S(2)}, u32[]{:S(2)}) async-start(bf16[4,256,1536]{2,1,0:T(8,128)(2,1)} %bitcast.265), calls=%async_computation.2 | async-start | bytes 6291456 | tf_op jit(solution)/shard_map/all_to_all | solution.py:104
  417.1 36.5 %collective-permute-start.25 = (bf16[128,1664]{1,0:T(8,128)(2,1)S(1)}, bf16[128,1664]{1,0:T(8,128)(2,1)S(1)}, u32[]{:S(2)}, u32[]{:S(2)}) collective-permute-start(bf16[128,1664]{1,0:T(8,128)(2,1)S(1)} %get-tuple-element.480), channel_id=1, source_target_pairs={{0,2},{1,3},{2,0},{3,1},{4,6},{5,7},{6,4},{7,5},{8,10},{9,11},{10,... | collective-permute-start | bytes 1277960 | tf_op jit(solution)/shard_map/ppermute | solution.py:26
  417.4 36.2 %collective-permute-start.26 = (bf16[128,1664]{1,0:T(8,128)(2,1)S(1)}, bf16[128,1664]{1,0:T(8,128)(2,1)S(1)}, u32[]{:S(2)}, u32[]{:S(2)}) collective-permute-start(bf16[128,1664]{1,0:T(8,128)(2,1)S(1)} %get-tuple-element.478), channel_id=1, source_target_pairs={{0,1},{1,2},{2,3},{3,0},{4,5},{5,6},{6,7},{7,4},{8,9},{9,10},{10,1... | collective-permute-start | bytes 1277960 | tf_op jit(solution)/shard_map/ppermute | solution.py:26
  486.8 40.3 %all-to-all-start.3 = ((bf16[4,256,1536]{2,1,0:T(8,128)(2,1)}), bf16[4,256,1536]{2,1,0:T(8,128)(2,1)}, u32[]{:S(2)}, u32[]{:S(2)}) async-start(bf16[4,256,1536]{2,1,0:T(8,128)(2,1)} %bitcast.269), calls=%async_computation.3 | async-start | bytes 6291456 | tf_op jit(solution)/shard_map/all_to_all | solution.py:104
  550.3 41.7 %all-to-all-start.4 = ((bf16[4,256,1536]{2,1,0:T(8,128)(2,1)}), bf16[4,256,1536]{2,1,0:T(8,128)(2,1)}, u32[]{:S(2)}, u32[]{:S(2)}) async-start(bf16[4,256,1536]{2,1,0:T(8,128)(2,1)} %bitcast.263), calls=%async_computation.4 | async-start | bytes 6291456 | tf_op jit(solution)/shard_map/all_to_all | solution.py:104
  597.9 51.3 %all-to-all-start.5 = ((bf16[4,256,1536]{2,1,0:T(8,128)(2,1)}), bf16[4,256,1536]{2,1,0:T(8,128)(2,1)}, u32[]{:S(2)}, u32[]{:S(2)}) async-start(bf16[4,256,1536]{2,1,0:T(8,128)(2,1)} %bitcast.264), calls=%async_computation.5 | async-start | bytes 6291456 | tf_op jit(solution)/shard_map/all_to_all | solution.py:104
  602.6 388.5 %reduce-scatter.12.cloned.1.call-start = ((), (), s32[]{:S(2)}) async-start(), calls=%async_computation.21 | async-start | bytes 491520 | tf_op jit(solution)/shard_map/reduce_scatter | solution.py:913
  796.7 194.4 %reduce-scatter.10.cloned.1.call-start = ((), (), s32[]{:S(2)}) async-start(), calls=%async_computation.20 | async-start | bytes 983040 | tf_op jit(solution)/shard_map/reduce_scatter | solution.py:913
  810.2 42.6 %all-to-all-start.6 = ((bf16[4,256,1536]{2,1,0:T(8,128)(2,1)}), bf16[4,256,1536]{2,1,0:T(8,128)(2,1)}, u32[]{:S(2)}, u32[]{:S(2)}) async-start(bf16[4,256,1536]{2,1,0:T(8,128)(2,1)} %bitcast.266), calls=%async_computation.6 | async-start | bytes 6291456 | tf_op jit(solution)/shard_map/all_to_all | solution.py:104
  815.0 176.1 %reduce-scatter.14.cloned.1.call-start = ((), (), s32[]{:S(2)}) async-start(), calls=%async_computation.22 | async-start | bytes 1474560 | tf_op jit(solution)/shard_map/reduce_scatter | solution.py:913
  818.9 199.4 %reduce-scatter.16.cloned.1.call-start = ((), (), s32[]{:S(2)}) async-start(), calls=%async_computation.23 | async-start | bytes 2949120 | tf_op jit(solution)/shard_map/reduce_scatter | solution.py:913
  870.6 47.7 %all-to-all-start.7 = ((bf16[4,256,1536]{2,1,0:T(8,128)(2,1)}), bf16[4,256,1536]{2,1,0:T(8,128)(2,1)}, u32[]{:S(2)}, u32[]{:S(2)}) async-start(bf16[4,256,1536]{2,1,0:T(8,128)(2,1)} %bitcast.262), calls=%async_computation.7 | async-start | bytes 6291456 | tf_op jit(solution)/shard_map/all_to_all | solution.py:104
  875.3 168.5 %reduce-scatter.26.cloned.1.call-start = ((), (), s32[]{:S(2)}) async-start(), calls=%async_computation.28 | async-start | bytes 491520 | tf_op jit(solution)/shard_map/reduce_scatter | solution.py:913
  926.6 137.9 %reduce-scatter.18.cloned.1.call-start = ((), (), s32[]{:S(2)}) async-start(), calls=%async_computation.24 | async-start | bytes 1966080 | tf_op jit(solution)/shard_map/reduce_scatter | solution.py:942
  947.3 149.5 %reduce-scatter.24.cloned.1.call-start = ((), (), s32[]{:S(2)}) async-start(), calls=%async_computation.27 | async-start | bytes 983040 | tf_op jit(solution)/shard_map/reduce_scatter | solution.py:913
  1042.6 70.0 %collective-permute-start.68 = (bf16[512,1536]{1,0:T(8,128)(2,1)}, bf16[512,1536]{1,0:T(8,128)(2,1)}, u32[]{:S(2)}, u32[]{:S(2)}) collective-permute-start(bf16[512,1536]{1,0:T(8,128)(2,1)} %get-tuple-element.466), channel_id=1, source_target_pairs={{0,16},{16,0},{1,17},{17,1},{2,18},{18,2},{3,19},{19,3},{4,20},{20... | collective-permute-start | bytes 4718600 | tf_op jit(solution)/shard_map/ppermute | solution.py:30
  1043.2 70.9 %collective-permute-start.67 = (bf16[1536,512]{1,0:T(8,128)(2,1)}, bf16[1536,512]{1,0:T(8,128)(2,1)}, u32[]{:S(2)}, u32[]{:S(2)}) collective-permute-start(bf16[1536,512]{1,0:T(8,128)(2,1)} %get-tuple-element.468), channel_id=1, source_target_pairs={{0,16},{16,0},{1,17},{17,1},{2,18},{18,2},{3,19},{19,3},{4,20},{20... | collective-permute-start | bytes 4718600 | tf_op jit(solution)/shard_map/ppermute | solution.py:30
  1043.2 71.5 %collective-permute-start.66 = (bf16[1536,512]{1,0:T(8,128)(2,1)}, bf16[1536,512]{1,0:T(8,128)(2,1)}, u32[]{:S(2)}, u32[]{:S(2)}) collective-permute-start(bf16[1536,512]{1,0:T(8,128)(2,1)} %get-tuple-element.470), channel_id=1, source_target_pairs={{0,16},{16,0},{1,17},{17,1},{2,18},{18,2},{3,19},{19,3},{4,20},{20... | collective-permute-start | bytes 4718600 | tf_op jit(solution)/shard_map/ppermute | solution.py:30
  1043.7 136.1 %reduce-scatter.22.cloned.1.call-start = ((), (), s32[]{:S(2)}) async-start(), calls=%async_computation.26 | async-start | bytes 1474560 | tf_op jit(solution)/shard_map/reduce_scatter | solution.py:913
  1064.5 37.6 %collective-permute-start.69 = (bf16[1536,384]{1,0:T(8,128)(2,1)}, bf16[1536,384]{1,0:T(8,128)(2,1)}, u32[]{:S(2)}, u32[]{:S(2)}) collective-permute-start(bf16[1536,384]{1,0:T(8,128)(2,1)} %convolution_convert_fusion.17), channel_id=1, source_target_pairs={{0,16},{16,0},{1,17},{17,1},{2,18},{18,2},{3,19},{19,3},{4,20},{20... | collective-permute-start | bytes 3538952 | tf_op jit(solution)/shard_map/ppermute | solution.py:30
  1105.5 76.9 %reduce-scatter.20.cloned.1.call-start = ((), (), s32[]{:S(2)}) async-start(), calls=%async_computation.25 | async-start | bytes 2949120 | tf_op jit(solution)/shard_map/reduce_scatter | solution.py:913
  (272 other events, 4190.1 us)
Sparse Core Ops, SparseCore 0:
  13.9 48.1 all-gather.11
  64.0 38.9 all-gather.17
  104.5 12.1 all-gather.19
  118.1 13.3 all-gather.21
  132.8 13.2 all-gather.23
  148.5 40.0 all-gather.13
  295.0 51.4 all-gather.15
  796.8 41.9 reduce-scatter.11
  841.7 33.0 reduce-scatter.9
  878.1 49.6 reduce-scatter.13
  930.9 40.5 reduce-scatter.15
  974.1 24.4 reduce-scatter.25
  1001.4 43.3 reduce-scatter.17
  1048.1 48.6 reduce-scatter.23
  1105.6 37.7 reduce-scatter.21
  1146.3 36.0 reduce-scatter.19

commit v9 on v8

--- a/solution.py
+++ b/solution.py
@@ -124,24 +124,40 @@
     return place.astype(jnp.int32).reshape(1)
 
 
+def chunk_of(rows, index):
+    if groups() == 1:
+        return rows
+    own = rows.shape[0] // groups()
+    return rows[own:] if index else rows[:own]
+
+
 def route_tables(meta, top, capacity, layers):
     n_row, n_col = lax.axis_size("row"), lax.axis_size("col")
-    experts = (jnp.arange(n_row) * n_col + lax.axis_index("col")).astype(FLOAT)
-    count = meta.shape[0]
-    slots = n_col * capacity
-    meta = meta.reshape(count, layers, 2, top).transpose(1, 2, 3, 0)
-    match = meta[:, None, 0] == experts[None, :, None, None]
-    hit = jnp.any(match, axis=2)
-    weight = jnp.sum(jnp.where(match, meta[:, None, 1], 0.0), axis=2)
-    order = jnp.arange(count, dtype=jnp.int32)
-    triangle = (order[:, None] <= order[None, :]).astype(HALF)
-    place = project(hit.astype(HALF).reshape(-1, count), triangle).reshape(hit.shape)
-    slot = jnp.arange(1, slots + 1, dtype=jnp.int32).astype(FLOAT)
-    chosen = (place[:, :, None, :] == slot[:, None]) & hit[:, :, None, :]
-    shape = (layers, n_row * slots, count)
-    plain = chosen.astype(HALF).reshape(shape)
-    scaled = jnp.where(chosen, weight[:, :, None, :], 0.0).astype(HALF).reshape(shape)
-    return [(plain[s], scaled[s]) for s in range(layers)]
+    place = jnp.arange(n_row)
+    tables = [[] for _ in range(layers)]
+    for index in range(min(groups(), 2)):
+        now = chunk_of(meta, index)
+        count = now.shape[0]
+        slots = count * n_col * capacity // meta.shape[0]
+        rows = place
+        if groups() > 1 and index == 0:
+            rows = lax.rem(lax.axis_index("row") + place, n_row)
+        experts = (rows * n_col + lax.axis_index("col")).astype(FLOAT)
+        now = now.reshape(count, layers, 2, top).transpose(1, 2, 3, 0)
+        match = now[:, None, 0] == experts[None, :, None, None]
+        hit = jnp.any(match, axis=2)
+        weight = jnp.sum(jnp.where(match, now[:, None, 1], 0.0), axis=2)
+        order = jnp.arange(count, dtype=jnp.int32)
+        triangle = (order[:, None] <= order[None, :]).astype(HALF)
+        rank = project(hit.astype(HALF).reshape(-1, count), triangle).reshape(hit.shape)
+        slot = jnp.arange(1, slots + 1, dtype=jnp.int32).astype(FLOAT)
+        chosen = (rank[:, :, None, :] == slot[:, None]) & hit[:, :, None, :]
+        shape = (layers, n_row * slots, count)
+        plain = chosen.astype(HALF).reshape(shape)
+        scaled = jnp.where(chosen, weight[:, :, None, :], 0.0).astype(HALF).reshape(shape)
+        for s in range(layers):
+            tables[s].append((plain[s], scaled[s]))
+    return tables
 
 
 def to_experts(rows):
@@ -577,15 +593,58 @@
     )(*pre, y, grad, sides, *mixer)
 
 
-def through_experts(block, table, expert, own, beside, aside=None):
-    tokens = spread(block)
-    arrived = to_experts(project(table, tokens))
-    answer = expert(arrived)
-    if aside is not None:
-        answer = after(answer, aside(tokens))
+def joined(parts):
+    return parts[0] if len(parts) == 1 else jnp.concatenate(parts, axis=0)
+
+
+def row_slices(rows):
+    count = lax.axis_size("row")
+    each = rows.shape[0] // count
+    return [rows[index * each : (index + 1) * each] for index in range(count)]
+
+
+def sent_ahead(rows):
+    shares = row_slices(rows)
+    return shares[0], [shifted(share, "row", ahead) for ahead, share in enumerate(shares) if ahead]
+
+
+def sent_back(rows):
+    shares = row_slices(rows)
+    return shares[0], [shifted(share, "row", -ahead) for ahead, share in enumerate(shares) if ahead]
+
+
+def through_experts(block, tables, expert, own, beside, aside=None):
+    if groups() == 1:
+        tokens = spread(block)
+        sent = project(tables[0], tokens).astype(HALF)
+        arrived = to_experts(sent)
+        answer = expert(0, arrived)
+        if aside is not None:
+            answer = after(answer, aside(after(tokens, sent)))
+        answered = to_experts(answer)
+        answered = after(answered, own(after(tokens, answer), after([arrived], answer)))
+        return gathered_sum(beside(0, answered)), [arrived], tokens
+    count = block.shape[0]
+    first, others = sent_ahead(project(tables[0], block).astype(HALF))
+    line = [shifted(block, "col", back) for back in range(1, groups())]
+    others, line = after((others, line))
+    tokens = jnp.concatenate([block, *line], axis=0)
+    rows_own = jnp.concatenate([first, *others], axis=0)
+    sent = project(tables[1], chunk_of(tokens, 1)).astype(HALF)
+    arrived = to_experts(sent)
+    answer_own = expert(0, after(rows_own, sent))
+    held = () if aside is None else aside(after(tokens, sent))
+    answer = after(expert(1, arrived), answer_own, held)
     answered = to_experts(answer)
-    answered = after(answered, own(after(tokens, answer), after(arrived, answer)))
-    return beside(answered), arrived, tokens
+    answered = after(answered, own(after(tokens, answer), after([rows_own, arrived], answer)))
+    part = beside(1, answered)
+    first, others = sent_back(answer_own)
+    line = [
+        shifted(part[at * count : (at + 1) * count], "col", -at - 1) for at in range(groups() - 1)
+    ]
+    others, line = after((others, line))
+    total = beside(0, jnp.concatenate([first, *others], axis=0)).astype(FLOAT)
+    return sum([each.astype(FLOAT) for each in line], total), [rows_own, arrived], tokens
 
 
 def line_product(values, weights):
@@ -626,16 +685,16 @@
     return (grad_gate, grad_lift), part
 
 
-def home_part(table, result, act_s, shared):
-    hidden = shared.shape[1] // 3
-    return (outer(table, result) + project_back(act_s, shared[:, 2 * hidden :])).astype(HALF)
+def home_part(act_s, shared):
+    return project_back(act_s, shared[:, 2 * (shared.shape[1] // 3) :])
 
 
 def weight_sums(rows_in, rows_out, kept, grads, tokens_in, tokens_out, kept_s, grads_s):
+    rows_in, rows_out = joined(rows_in), joined(rows_out)
     experts = (
-        outer(rows_in, grads[0]).astype(HALF),
-        outer(rows_in, grads[1]).astype(HALF),
-        outer(kept[2], rows_out).astype(HALF),
+        outer(rows_in, joined([grads[index][0] for index in grads])).astype(HALF),
+        outer(rows_in, joined([grads[index][1] for index in grads])).astype(HALF),
+        outer(joined([kept[index][2] for index in kept]), rows_out).astype(HALF),
     )
     shared = ((tokens_in, *grads_s), (tokens_out, *two_halves(kept_s[2])))
     return experts, [(*each, swapped(half_to_give(*each))) for each in shared]
@@ -757,13 +816,15 @@
         whole = lax.all_gather(half, ("section", "row"), axis=0, tiled=True)
         return whole.reshape(2, n_row * half.shape[0], half.shape[1])
 
-    proj = [both_halves(mine[0])]
-
     def both_layers(weight):
         whole = lax.all_gather(weight, ("section", "row"), axis=0, tiled=True)
         return whole.reshape(2, n_row * weight.shape[0], weight.shape[1])
 
-    proj_out = both_layers(widened(proj_output[0], wide))
+    proj = [both_halves(mine[0])]
+    halves = two_halves(widened(proj_output[0], wide))
+    keep, give = jnp.where(first, *halves), jnp.where(first, *halves[::-1])
+    mine_out = pair(keep, swapped(give))
+    proj_out = [both_halves(mine_out[0])]
     gate_all = lax.all_gather(expert_gate[0, 0], "section")
     up_all = lax.all_gather(expert_up[0, 0], "section")
     down_all = lax.all_gather(expert_down[0, 0], "section")
@@ -809,7 +870,7 @@
         return pre, *mixer_forward(pre, heads, wide, mixers[s])
 
     def mix_out(s, resid, scaled, total_part, meanwhile):
-        whole = line_product([scaled], [proj_out[s]])
+        whole = line_product(two_halves(scaled), proj_out[s])
         sums = gathered_sum(jnp.concatenate([whole, as_halves(total_part)], axis=1), meanwhile)
         mixed, total = sums[:, :width], from_halves(sums[:, width:], 1)
         rr = lax.rsqrt(total / DI + EPS)
@@ -818,46 +879,58 @@
     wide_in_0 = rms_norm(wide_tokens.astype(FLOAT), norm_ins[0]).astype(HALF)
     pre_0, y_0, scaled_0, total_0 = mix_in(0, wide_in_0)
     tables = route_tables(spread(after(meta, scaled_0)), top, capacity, 2)
-    plain = [table[0] for table in tables]
-    scaling = [table[1] for table in tables]
+    plain = [[table[0] for table in tables[s]] for s in layers]
+    scaling = [[table[1] for table in tables[s]] for s in layers]
     middle_0, mixed_0, rr_0 = mix_out(0, tokens_now, scaled_0, total_0, tables)
-    kept = {}
-
-    def expert_0(rows):
-        kept["rows 0"], answer = expert_forward(rows, experts[0])
+    kept = {name: {} for name in ("rows 0", "rows 1", "answer 1", "grads 0", "grads 1")}
+
+    def expert_0(index, rows):
+        kept["rows 0"][index], answer = expert_forward(rows, experts[0])
         return answer
 
-    def own_0(block, rows):
-        kept["shared 0"] = shared_forward(block, shared[0])
-        return kept["shared 0"]
-
-    def beside_0(result):
-        return home_part(scaling[0], result, kept["shared 0"][2], shared[0])
-
-    def aside_0(blocks):
-        kept["grads"] = spread(after(grad_now.astype(HALF), blocks))
+    def own_0(tokens_all, rows):
+        kept["shared 0"] = shared_forward(tokens_all, shared[0])
+        kept["part 0"] = home_part(kept["shared 0"][2], shared[0])
+        return kept["part 0"]
+
+    def beside_0(index, result):
+        part = outer(scaling[0][index], result) + chunk_of(kept["part 0"], index)
+        return part.astype(HALF)
+
+    def aside_0(tokens_all):
+        kept["grads"] = spread(after(grad_now.astype(HALF), tokens_all))
         return kept["grads"]
 
-    parts, rows_0, mids_0 = through_experts(
+    total, rows_0, mids_0 = through_experts(
         rms_norm(middle_0, norm_mids[0]).astype(HALF), plain[0], expert_0, own_0, beside_0, aside_0
     )
-    proj.append(both_halves(after(mine[1], parts)))
-    out_0 = middle_0 + gathered_sum(parts)
+    proj.append(both_halves(after(mine[1], kept["part 0"])))
+    proj_out.append(both_halves(after(mine_out[1], kept["part 0"])))
+    out_0 = middle_0 + total
 
     wide_in_1 = spread(rms_norm(out_0, norm_ins[1]).astype(HALF))
     grad_tokens_1 = after(kept["grads"], out_0)
-    grad_rows_1 = to_experts(project(scaling[1], grad_tokens_1))
+    grad_sent = [
+        project(table, chunk_of(grad_tokens_1, index)).astype(HALF)
+        for index, table in enumerate(scaling[1])
+    ]
+    grad_rows_1 = [to_experts(grad_sent[-1])]
+    if groups() > 1:
+        own_rows, others = sent_ahead(grad_sent[0])
+        grad_rows_1 = [jnp.concatenate([own_rows, *others], axis=0), *grad_rows_1]
     pre_1, y_1, scaled_1, total_1 = mix_in(1, wide_in_1)
     scaled_1 = after(scaled_1, grad_rows_1)
     middle_1, mixed_1, rr_1 = mix_out(1, out_0, scaled_1, total_1, ())
 
-    def expert_1(rows):
-        kept["rows 1"], kept["answer 1"] = expert_forward(rows, experts[1])
-        kept["grads 1"], back = expert_backward(grad_rows_1, kept["rows 1"], experts[1])
+    def expert_1(index, rows):
+        kept["rows 1"][index], kept["answer 1"][index] = expert_forward(rows, experts[1])
+        kept["grads 1"][index], back = expert_backward(
+            grad_rows_1[index], kept["rows 1"][index], experts[1]
+        )
         return back
 
-    def own_1(block, rows):
-        kept["shared 1"] = shared_forward(block, shared[1])
+    def own_1(tokens_all, rows):
+        kept["shared 1"] = shared_forward(tokens_all, shared[1])
         kept["shared grads 1"], kept["part 1"] = shared_backward(
             grad_tokens_1, kept["shared 1"], shared[1]
         )
@@ -866,21 +939,21 @@
             grad_rows_1,
             kept["rows 1"],
             kept["grads 1"],
-            block,
+            tokens_all,
             grad_tokens_1,
             kept["shared 1"],
             kept["shared grads 1"],
         )
         experts_1, shared_1 = kept["sums 1"]
-        return experts_1, [made[-1] for made in shared_1]
-
-    def beside_1(result):
-        return (kept["part 1"] + outer(plain[1], result)).astype(HALF)
-
-    parts, rows_1, mids_1 = through_experts(
+        return experts_1, kept["part 1"], [made[-1] for made in shared_1]
+
+    def beside_1(index, result):
+        part = outer(plain[1][index], result) + chunk_of(kept["part 1"], index)
+        return part.astype(HALF)
+
+    total, rows_1, mids_1 = through_experts(
         rms_norm(middle_1, norm_mids[1]).astype(HALF), plain[1], expert_1, own_1, beside_1
     )
-    answer_1 = to_experts(after(kept["answer 1"], parts))
 
     def mixer_back(s, grad_middle, along, rr, saved, meanwhile):
         wide_in, pre, y, scaled = saved
@@ -889,7 +962,8 @@
             jnp.concatenate([grad_middle.astype(HALF), sides], axis=1), meanwhile
         )
         wide_mix, sides = payload[:, :width], from_halves(payload[:, width:], 2)
-        grad_scaled = project(wide_mix, proj_out[s])
+        grad_scaled = [project(wide_mix, half) for half in proj_out[s]]
+        grad_scaled = jnp.concatenate(grad_scaled, axis=1)
         *grad_pre, wide_grads, grad_conv_input, grad_conv_state, step_grads = mixer_backward(
             pre, y, grad_scaled, sides, heads, mixers[s]
         )
@@ -913,68 +987,80 @@
         return lax.psum_scatter(value, "row", scatter_dimension=0, tiled=True)
 
     grad_middle, along, grad_norm_mid_1 = middle_backward(
-        gathered_sum(parts, answer_1), grad_now, middle_1, mixed_1, norm_mids[1]
+        total, grad_now, middle_1, mixed_1, norm_mids[1]
     )
     expert_grads_1, shared_grads_1 = kept["sums 1"]
-    home = home_part(scaling[1], answer_1, kept["shared 1"][2], shared[1])
+    answers = after([kept["answer 1"][index] for index in kept["answer 1"]], grad_middle)
+    answers_back = [to_experts(answers[-1])]
+    if groups() > 1:
+        own_rows, others = sent_back(answers[0])
+        answers_back = [jnp.concatenate([own_rows, *others], axis=0), *answers_back]
+    shared_made_1 = [half_to_keep(*made) for made in shared_grads_1]
     grad_pre, to_proj, to_out, tail, rest_1 = mixer_back(
         1,
         grad_middle,
         along,
         rr_1,
         (wide_in_1, pre_1, y_1, scaled_1),
-        home,
-    )
+        shared_made_1,
+    )
+    shared_sent_1 = [row_sums(each) for each in shared_made_1]
     whole = line_product(grad_pre, proj[1])
     grad_in = gathered_sum(whole)
     grad_1, grad_norm_in_1 = resid_back(out_0, norm_ins[1], grad_in, grad_middle)
 
-    def aside_back_0(blocks):
-        own_proj, own_out, own_tail = after((to_proj, to_out, tail), blocks)
+    def aside_back_0(tokens_all):
+        own_proj, own_out, own_tail = after((to_proj, to_out, tail), tokens_all)
         given, given_out = half_to_give(*own_proj), half_to_give(*own_out)
-        made = (*shared_grads_1, (*own_out, swapped(given_out)), (*own_proj, swapped(given)))
+        made = ((*own_out, swapped(given_out)), (*own_proj, swapped(given)))
         made = [half_to_keep(*each) for each in after(made, (given, given_out))]
-        kept["sent 1"] = [row_sums(each) for each in made]
+        kept["sent 1"] = [*shared_sent_1, *[row_sums(each) for each in made]]
         kept["tail 1"] = outer(own_proj[0], own_tail).astype(HALF)
-        kept["home"] = home
+        home = home_part(after(kept["shared 1"][2], made), shared[1])
+        home = [
+            (outer(scaling[1][index], answer) + chunk_of(home, index)).astype(HALF)
+            for index, answer in enumerate(answers_back)
+        ]
+        home = joined(home)
         if groups() > 1:
-            kept["home"] = in_order([block_of(home, back) for back in range(groups())], "col")
-        kept["home"] = lax.psum_scatter(
-            after(kept["home"], made), "col", scatter_dimension=0, tiled=True
-        )
-        return made, kept["tail 1"]
-
-    def expert_back_0(rows):
-        kept["grads 0"], back = expert_backward(rows, kept["rows 0"], experts[0])
+            home = in_order([block_of(home, back) for back in range(groups())], "col")
+        kept["home"] = lax.psum_scatter(home, "col", scatter_dimension=0, tiled=True)
+        return made, kept["tail 1"], home
+
+    def expert_back_0(index, rows):
+        kept["grads 0"][index], back = expert_backward(rows, kept["rows 0"][index], experts[0])
         return back
 
-    def own_back_0(block, rows):
-        kept["shared grads 0"], kept["part 0"] = shared_backward(block, kept["shared 0"], shared[0])
+    def own_back_0(tokens_all, rows):
+        kept["shared grads 0"], kept["part 0"] = shared_backward(
+            tokens_all, kept["shared 0"], shared[0]
+        )
         kept["sums 0"] = weight_sums(
             rows_0,
             rows,
             kept["rows 0"],
             kept["grads 0"],
             mids_0,
-            block,
+            tokens_all,
             kept["shared 0"],
             kept["shared grads 0"],
         )
         experts_0, shared_0 = kept["sums 0"]
-        return experts_0, [made[-1] for made in shared_0]
-
-    def beside_back_0(result):
-        return (kept["part 0"] + outer(plain[0], result)).astype(HALF)
-
-    parts, grad_rows_0, grad_tokens_0 = through_experts(
+        return experts_0, kept["part 0"], [made[-1] for made in shared_0]
+
+    def beside_back_0(index, result):
+        part = outer(plain[0][index], result) + chunk_of(kept["part 0"], index)
+        return part.astype(HALF)
+
+    total, grad_rows_0, grad_tokens_0 = through_experts(
         grad_1.astype(HALF), scaling[0], expert_back_0, own_back_0, beside_back_0, aside_back_0
     )
     sums_1, grad_tail_1 = kept["sent 1"], kept["tail 1"]
     grad_middle, along, grad_norm_mid_0 = middle_backward(
-        gathered_sum(parts), grad_1, middle_0, mixed_0, norm_mids[0]
+        total, grad_1, middle_0, mixed_0, norm_mids[0]
     )
     expert_grads_0, shared_grads_0 = kept["sums 0"]
-    shared_sums_0 = [half_to_keep(*after(made, parts)) for made in shared_grads_0]
+    shared_sums_0 = [half_to_keep(*after(made, total)) for made in shared_grads_0]
     sums_0 = [row_sums(made) for made in shared_sums_0]
     expert_out = [own_layer(a, b) for a, b in zip(expert_grads_0, expert_grads_1)]
     grad_pre, to_proj, to_out, tail, rest_0 = mixer_back(
@@ -988,13 +1074,15 @@
 
     given = half_to_give(*to_proj)
     whole = line_product(after(grad_pre, given), proj[0])
-    line_received = sent_home(whole)
     proj_half = half_to_keep(*after((*to_proj, swapped(given)), whole))
-    proj_sums = row_sums(proj_half)
+    proj_pieces = row_pieces(proj_half)
+    proj_received = row_received(proj_pieces)
+    line_received = sent_home(after(whole, proj_half))
     given_out = half_to_give(*after(to_out, proj_half))
     grad_tail_0 = outer(after(wide_in_0, given_out), tail).astype(HALF)
     out_half = half_to_keep(*after((*to_out, swapped(given_out)), grad_tail_0))
-    sums_0.append(row_sums(out_half))
+    out_pieces = row_pieces(out_half)
+    out_received = row_received(out_pieces)
     tail_keep, tail_other = own_layer(grad_tail_0, grad_tail_1)
     tail_pieces = row_pieces((tail_keep + tail_other.astype(FLOAT)).astype(HALF))
     tail_received = row_received(tail_pieces)
@@ -1009,10 +1097,14 @@
     small_keep, small_other = own_layer(flat(smalls[0]), flat(smalls[1]))
     vector = small_keep + small_other.astype(FLOAT)
     lines = [shifted(vector[None], "row", back) for back in range(n_row)]
-    expert_out = [keep + other.astype(FLOAT) for keep, other in after(expert_out, out_half)]
-    line_received, tail_received, lines = after((line_received, tail_received, lines), expert_out)
+    line_received, proj_received, out_received, tail_received, lines = after(
+        (line_received, proj_received, out_received, tail_received, lines)
+    )
     grad_in = added_up(whole, line_received)
-    sums_0.append(proj_sums)
+    sums_0.append(total_of(out_pieces[0], out_received).astype(HALF))
+    sums_0.append(total_of(proj_pieces[0], proj_received).astype(HALF))
+    sums_0, sums_1 = after((sums_0, sums_1), grad_in)
+    expert_out = [keep + other.astype(FLOAT) for keep, other in after(expert_out, grad_in)]
     tail = total_of(tail_pieces[0], tail_received).astype(HALF)
     vector = jnp.sum(in_order(lines, "row"), axis=0)
     grad_0, _ = resid_back(tokens_now, norm_ins[0], grad_in, grad_middle)

time: 1210 us -> 1200 us (level)
  waiting for transfers between devices: 567 us -> 476 us
  starting transfers between devices: 183 us -> 242 us
  other arithmetic: 62.7 us -> 82.2 us
  local copies, waits for them, and re-layouts: 54.6 us -> 73.2 us
  matrix products: 250 us -> 236 us
    ppermute x63 -> x93, starting transfers between devices: 137 us -> 200 us  [shifted(): lax.ppermute(block, axis, [(i, (i + distance) % count) for i in range(cou...]
    all_to_all x8, waiting for transfers between devices: 108 us -> 67.1 us  [exchanged(): return lax.all_to_all(rows, axis, split_axis=0, concat_axis=0, tiled=True)]
    reduce_scatter x8 -> x6, waiting for transfers between devices: 31 us -> 0.01 us  [row_sums(): return lax.psum_scatter(value, 'row', scatter_dimension=0, tiled=True)]
    dot_general x28 -> x32, matrix products: 106 us -> 90.1 us  [outer(): lax.dot_general(left, right, (((0,), (0,)), ((), ())), preferred_element_...]
    all_gather x2 -> x1, waiting for transfers between devices: 15.2 us -> 0.01 us  [both_layers(): whole = lax.all_gather(weight, ('section', 'row'), axis=0, tiled=True)]
    unnamed x425 -> x606, local copies, waits for them, and re-layouts: 26.6 us -> 32.3 us
    dot_general x18 -> x26, matrix products: 61.8 us -> 63 us  [project_back(): lax.dot_general(left, right, (((1,), (1,)), ((), ())), preferred_element_...]
    dot_general x23 -> x36, matrix products: 82.2 us -> 83.3 us  [project(): return jnp.dot(left, right, preferred_element_type=FLOAT)]
  transfers between devices with their start and end apart: 109 -> 139, of which waited for: 43 -> 53; matrix products, arithmetic and copies ran while one was open for 24% -> 29% of each run, Pallas kernels for 4% -> 5%
where the time goes in v9:
time: 1200 us; the launch traced here: 1190 us
  waiting for transfers between devices  476 us (40%)
  starting transfers between devices  242 us (20%)
  matrix products  236 us (20%)
  other arithmetic  82.2 us (7%)
  local copies, waits for them, and re-layouts  73.2 us (6%)
  Pallas kernels  61.8 us (5%)
  between operations  18.2 us (2%)
    ppermute x93, waiting for transfers between devices, shifted(): lax.ppermute(block, axis, [(i, (i + distance) % count) for i in range(cou...  395 us
    ppermute x93, starting transfers between devices, shifted(): lax.ppermute(block, axis, [(i, (i + distance) % count) for i in range(cou...  200 us
    dot_general x32, matrix products, outer(): lax.dot_general(left, right, (((0,), (0,)), ((), ())), preferred_element_...  90.1 us
    dot_general x36, matrix products, project(): return jnp.dot(left, right, preferred_element_type=FLOAT)  83.3 us
    all_to_all x8, waiting for transfers between devices, exchanged(): return lax.all_to_all(rows, axis, split_axis=0, concat_axis=0, tiled=True)  67.1 us
    dot_general x26, matrix products, project_back(): lax.dot_general(left, right, (((1,), (1,)), ((), ())), preferred_element_...  63 us
    pallas_call x2, Pallas kernels, mixer_backward(): whole_call(kernel, 5 + len(mixer), (jax.ShapeDtypeStruct(pre[0].shape, HA...  36.6 us
    all_to_all x8, starting transfers between devices, exchanged(): return lax.all_to_all(rows, axis, split_axis=0, concat_axis=0, tiled=True)  35.8 us
  transfers between devices with their start and end apart: 139, of which 53 were waited for; matrix products, arithmetic and copies ran while one was open for 29% of the time, Pallas kernels for 5%

profile of v9, /device:TPU:0, one launch (start us, length us, event | category | flops | bytes accessed | tf_op | source)
XLA Modules:
  0.0 1189.5 jit_solution(4810904469040647109)
XLA Ops:
  34.4 24.3 %collective-permute-done.1 = bf16[128,1536]{1,0:T(8,128)(2,1)S(1)} collective-permute-done((bf16[128,1536]{1,0:T(8,128)(2,1)S(1)}, bf16[128,1536]{1,0:T(8,128)(2,1)S(1)}, u32[]{:S(2)}, u32[]{:S(2)}) %collective-permute-start.1) | collective-permute-done | bytes 393248 | tf_op jit(solution)/shard_map/ppermute | solution.py:26
  69.2 13.2 %mixer_forward.2 = (f32[512,768]{1,0:T(8,128)S(1)}, bf16[512,768]{1,0:T(8,128)(2,1)S(1)}, f32[512,1]{1,0:T(8,128)S(1)}) custom-call(f32[512,1024]{1,0:T(8,128)S(1)} %fusion.34.pre_in_ref, f32[512,1024]{1,0:T(8,128)} %fusion.31.pre_other_in_ref, f32[4,768]{1,0:T(4,128)S(1)} %reshape.470.conv_input_ref, f32[4,256]{1,0:T(4,128)S(1)} %slice.613.conv_state_ref, ...), custom_call_target="tpu_custom_call" | custom-call | tf_op jit(solution)/shard_map/mixer_forward/pallas_call | solution.py:541
  105.5 8.2 collective-permute-done.9
  113.7 7.9 collective-permute-done.7
  121.5 18.8 %collective-permute-done.8 = bf16[128,1664]{1,0:T(8,128)(2,1)} collective-permute-done((bf16[128,1664]{1,0:T(8,128)(2,1)S(1)}, bf16[128,1664]{1,0:T(8,128)(2,1)}, u32[]{:S(2)}, u32[]{:S(2)}) %collective-permute-start.8) | collective-permute-done | bytes 426016 | tf_op jit(solution)/shard_map/ppermute | solution.py:26
  170.6 8.3 collective-permute-done.17
  185.8 25.0 %collective-permute-done.23 = bf16[128,1536]{1,0:T(8,128)(2,1)} collective-permute-done((bf16[128,1536]{1,0:T(8,128)(2,1)}, bf16[128,1536]{1,0:T(8,128)(2,1)}, u32[]{:S(2)}, u32[]{:S(2)}) %collective-permute-start.23) | collective-permute-done | bytes 393248 | tf_op jit(solution)/shard_map/ppermute | solution.py:26
  258.4 30.2 %all-to-all-done.1 = bf16[4,192,1536]{2,1,0:T(8,128)(2,1)} async-done(((bf16[4,192,1536]{2,1,0:T(8,128)(2,1)}), bf16[4,192,1536]{2,1,0:T(8,128)(2,1)}, u32[]{:S(2)}, u32[]{:S(2)}) %all-to-all-start.1) | async-done | bytes 2359328 | tf_op jit(solution)/shard_map/all_to_all | solution.py:104
  303.4 9.0 collective-permute-done.19
  312.4 6.4 collective-permute-done.26
  321.0 12.8 %collective-permute-start.30 = (bf16[128,1536]{1,0:T(8,128)(2,1)S(1)}, bf16[128,1536]{1,0:T(8,128)(2,1)S(1)}, u32[]{:S(2)}, u32[]{:S(2)}) collective-permute-start(bf16[128,1536]{1,0:T(8,128)(2,1)S(1)} %multiply_convert_fusion.9), channel_id=1, source_target_pairs={{0,3},{1,0},{2,1},{3,2},{4,7},{5,4},{6,5},{7,6},{8,11},{9,8},{10,9... | collective-permute-start | bytes 1179656 | tf_op jit(solution)/shard_map/ppermute | solution.py:26
  348.7 30.1 %collective-permute-done.31 = bf16[64,1536]{1,0:T(8,128)(2,1)S(1)} collective-permute-done((bf16[64,1536]{1,0:T(8,128)(2,1)S(1)}, bf16[64,1536]{1,0:T(8,128)(2,1)S(1)}, u32[]{:S(2)}, u32[]{:S(2)}) %collective-permute-start.31) | collective-permute-done | bytes 196640 | tf_op jit(solution)/shard_map/ppermute | solution.py:26
  395.0 12.0 %mixer_forward.3 = (f32[512,768]{1,0:T(8,128)S(1)}, bf16[512,768]{1,0:T(8,128)(2,1)S(1)}, f32[512,1]{1,0:T(8,128)S(1)}) custom-call(f32[512,1024]{1,0:T(8,128)S(1)} %fusion.27.pre_in_ref, f32[512,1024]{1,0:T(8,128)} %fusion.23.pre_other_in_ref, f32[4,768]{1,0:T(4,128)S(1)} %reshape.476.conv_input_ref, f32[4,256]{1,0:T(4,128)S(1)} %slice.665.conv_state_ref, ...), custom_call_target="tpu_custom_call" | custom-call | tf_op jit(solution)/shard_map/mixer_forward/pallas_call | solution.py:541
  427.1 6.1 collective-permute-done.34
  433.2 17.7 %collective-permute-done.35 = bf16[128,1664]{1,0:T(8,128)(2,1)S(1)} collective-permute-done((bf16[128,1664]{1,0:T(8,128)(2,1)S(1)}, bf16[128,1664]{1,0:T(8,128)(2,1)S(1)}, u32[]{:S(2)}, u32[]{:S(2)}) %collective-permute-start.35) | collective-permute-done | bytes 426016 | tf_op jit(solution)/shard_map/ppermute | solution.py:26
  468.3 17.9 %collective-permute-done.41 = bf16[128,1536]{1,0:T(8,128)(2,1)} collective-permute-done((bf16[128,1536]{1,0:T(8,128)(2,1)S(1)}, bf16[128,1536]{1,0:T(8,128)(2,1)}, u32[]{:S(2)}, u32[]{:S(2)}) %collective-permute-start.41) | collective-permute-done | bytes 393248 | tf_op jit(solution)/shard_map/ppermute | solution.py:26
  511.2 17.3 %all-to-all-done.3 = bf16[4,192,1536]{2,1,0:T(8,128)(2,1)} async-done(((bf16[4,192,1536]{2,1,0:T(8,128)(2,1)}), bf16[4,192,1536]{2,1,0:T(8,128)(2,1)}, u32[]{:S(2)}, u32[]{:S(2)}) %all-to-all-start.3) | async-done | bytes 2359328 | tf_op jit(solution)/shard_map/all_to_all | solution.py:104
  588.7 16.1 %collective-permute-done.49 = bf16[128,1536]{1,0:T(8,128)(2,1)} collective-permute-done((bf16[128,1536]{1,0:T(8,128)(2,1)}, bf16[128,1536]{1,0:T(8,128)(2,1)}, u32[]{:S(2)}, u32[]{:S(2)}) %collective-permute-start.49) | collective-permute-done | bytes 393248 | tf_op jit(solution)/shard_map/ppermute | solution.py:26
  610.2 9.1 collective-permute-start.53
  631.9 24.2 %collective-permute-done.52 = bf16[128,1664]{1,0:T(8,128)(2,1)S(1)} collective-permute-done((bf16[128,1664]{1,0:T(8,128)(2,1)}, bf16[128,1664]{1,0:T(8,128)(2,1)S(1)}, u32[]{:S(2)}, u32[]{:S(2)}) %collective-permute-start.52) | collective-permute-done | bytes 426016 | tf_op jit(solution)/shard_map/ppermute | solution.py:26
  662.2 18.3 %mixer_backward.2 = (bf16[512,1024]{1,0:T(8,128)(2,1)S(1)}, bf16[512,1024]{1,0:T(8,128)(2,1)S(1)}, f32[2,768]{1,0:T(2,128)S(1)}, f32[4,768]{1,0:T(4,128)S(1)}, f...) custom-call(f32[512,1024]{1,0:T(8,128)} %copy-done.3, f32[512,1024]{1,0:T(8,128)} %fusion.23.pre_other_in_ref, ...), custom_call_target="tpu_custom_call" | custom-call | tf_op jit(solution)/shard_map/mixer_backward/pallas_call | solution.py:566
  702.2 14.2 %collective-permute-done.55 = bf16[128,1536]{1,0:T(8,128)(2,1)S(1)} collective-permute-done((bf16[128,1536]{1,0:T(8,128)(2,1)S(1)}, bf16[128,1536]{1,0:T(8,128)(2,1)S(1)}, u32[]{:S(2)}, u32[]{:S(2)}) %collective-permute-start.55) | collective-permute-done | bytes 393248 | tf_op jit(solution)/shard_map/ppermute | solution.py:26
  727.0 9.7 collective-permute-start.62
  749.2 18.8 %collective-permute-done.61 = bf16[128,1536]{1,0:T(8,128)(2,1)S(1)} collective-permute-done((bf16[128,1536]{1,0:T(8,128)(2,1)S(1)}, bf16[128,1536]{1,0:T(8,128)(2,1)S(1)}, u32[]{:S(2)}, u32[]{:S(2)}) %collective-permute-start.61) | collective-permute-done | bytes 393248 | tf_op jit(solution)/shard_map/ppermute | solution.py:26
  810.0 18.5 %all-to-all-done.5 = bf16[4,192,1536]{2,1,0:T(8,128)(2,1)} async-done(((bf16[4,192,1536]{2,1,0:T(8,128)(2,1)}), bf16[4,192,1536]{2,1,0:T(8,128)(2,1)}, u32[]{:S(2)}, u32[]{:S(2)}) %all-to-all-start.5) | async-done | bytes 2359328 | tf_op jit(solution)/shard_map/all_to_all | solution.py:104
  876.4 7.1 collective-permute-start.75
  897.1 20.8 %collective-permute-done.74 = bf16[128,1536]{1,0:T(8,128)(2,1)} collective-permute-done((bf16[128,1536]{1,0:T(8,128)(2,1)}, bf16[128,1536]{1,0:T(8,128)(2,1)}, u32[]{:S(2)}, u32[]{:S(2)}) %collective-permute-start.74) | collective-permute-done | bytes 393248 | tf_op jit(solution)/shard_map/ppermute | solution.py:26
  927.8 25.1 %collective-permute-start.78 = (bf16[128,1664]{1,0:T(8,128)(2,1)}, bf16[128,1664]{1,0:T(8,128)(2,1)}, u32[]{:S(2)}, u32[]{:S(2)}) collective-permute-start(bf16[128,1664]{1,0:T(8,128)(2,1)} %pad_maximum_fusion.19), channel_id=1, source_target_pairs={{0,3},{1,0},{2,1},{3,2},{4,7},{5,4},{6,5},{7,6},{8,11},{9,8},{10,9... | collective-permute-start | bytes 1277960 | tf_op jit(solution)/shard_map/ppermute | solution.py:26
  963.5 20.1 %collective-permute-done.77 = bf16[128,1664]{1,0:T(8,128)(2,1)} collective-permute-done((bf16[128,1664]{1,0:T(8,128)(2,1)}, bf16[128,1664]{1,0:T(8,128)(2,1)}, u32[]{:S(2)}, u32[]{:S(2)}) %collective-permute-start.77) | collective-permute-done | bytes 426016 | tf_op jit(solution)/shard_map/ppermute | solution.py:26
  990.3 18.3 %mixer_backward.3 = (bf16[512,1024]{1,0:T(8,128)(2,1)S(1)}, bf16[512,1024]{1,0:T(8,128)(2,1)S(1)}, f32[2,768]{1,0:T(2,128)S(1)}, f32[4,768]{1,0:T(4,128)S(1)}, f...) custom-call(f32[512,1024]{1,0:T(8,128)} %copy-done.2, f32[512,1024]{1,0:T(8,128)} %fusion.31.pre_other_in_ref, ...), custom_call_target="tpu_custom_call" | custom-call | tf_op jit(solution)/shard_map/mixer_backward/pallas_call | solution.py:566
  1060.1 10.9 collective-permute-done.82
  1083.5 7.7 collective-permute-done.92
  (1185 shorter events, 667.2 us)
Async XLA Ops:
  7.2 54.9 %all-gather.12.cloned.1.call-start = ((), (), s32[]{:S(2)}) async-start(), calls=%async_computation.15 | async-start | bytes 7077888 | tf_op jit(solution)/shard_map/all_gather | solution.py:816
  13.8 79.8 %all-gather.14.cloned.1.call-start = ((), (), s32[]{:S(2)}) async-start(), calls=%async_computation.16 | async-start | bytes 2654208 | tf_op jit(solution)/shard_map/all_gather | solution.py:816
  16.5 199.1 %all-gather.22.cloned.1.call-start = ((), (), s32[]{:S(2)}) async-start(), calls=%async_computation.27 | async-start | bytes 4718592 | tf_op jit(solution)/shard_map/all_gather | solution.py:828
  17.4 201.3 %all-gather.24.cloned.1.call-start = ((), (), s32[]{:S(2)}) async-start(), calls=%async_computation.28 | async-start | bytes 4718592 | tf_op jit(solution)/shard_map/all_gather | solution.py:829
  18.0 203.9 %all-gather.26.cloned.1.call-start = ((), (), s32[]{:S(2)}) async-start(), calls=%async_computation.29 | async-start | bytes 4718592 | tf_op jit(solution)/shard_map/all_gather | solution.py:830
  18.6 215.5 %all-gather.16.cloned.1.call-start = ((), (), s32[]{:S(2)}) async-start(), calls=%async_computation.17 | async-start | bytes 5308416 | tf_op jit(solution)/shard_map/all_gather | solution.py:820
  185.4 200.6 %all-gather.18.cloned.1.call-start = ((), (), s32[]{:S(2)}) async-start(), calls=%async_computation.18 | async-start | bytes 7077888 | tf_op jit(solution)/shard_map/all_gather | solution.py:816
  243.3 45.2 %all-to-all-start.1 = ((bf16[4,192,1536]{2,1,0:T(8,128)(2,1)}), bf16[4,192,1536]{2,1,0:T(8,128)(2,1)}, u32[]{:S(2)}, u32[]{:S(2)}) async-start(bf16[4,192,1536]{2,1,0:T(8,128)(2,1)} %bitcast.310), calls=%async_computation.1 | async-start | bytes 4718592 | tf_op jit(solution)/shard_map/all_to_all | solution.py:104
  247.8 160.6 %all-gather.20.cloned.1.call-start = ((), (), s32[]{:S(2)}) async-start(), calls=%async_computation.19 | async-start | bytes 2654208 | tf_op jit(solution)/shard_map/all_gather | solution.py:816
  252.9 49.6 %collective-permute-start.21 = (bf16[64,1536]{1,0:T(8,128)(2,1)}, bf16[64,1536]{1,0:T(8,128)(2,1)}, u32[]{:S(2)}, u32[]{:S(2)}) collective-permute-start(bf16[64,1536]{1,0:T(8,128)(2,1)} %get-tuple-element.623), channel_id=1, source_target_pairs={{0,4},{4,8},{8,12},{12,0},{1,5},{5,9},{9,13},{13,1},{2,6},{6,10},{... | collective-permute-start | bytes 589832 | tf_op jit(solution)/shard_map/ppermute | solution.py:26
  254.8 48.6 %collective-permute-start.20 = (bf16[64,1536]{1,0:T(8,128)(2,1)}, bf16[64,1536]{1,0:T(8,128)(2,1)}, u32[]{:S(2)}, u32[]{:S(2)}) collective-permute-start(bf16[64,1536]{1,0:T(8,128)(2,1)} %get-tuple-element.624), channel_id=1, source_target_pairs={{0,8},{4,12},{8,0},{12,4},{1,9},{5,13},{9,1},{13,5},{2,10},{6,14},... | collective-permute-start | bytes 589832 | tf_op jit(solution)/shard_map/ppermute | solution.py:26
  321.0 65.0 %collective-permute-start.30 = (bf16[128,1536]{1,0:T(8,128)(2,1)S(1)}, bf16[128,1536]{1,0:T(8,128)(2,1)S(1)}, u32[]{:S(2)}, u32[]{:S(2)}) collective-permute-start(bf16[128,1536]{1,0:T(8,128)(2,1)S(1)} %multiply_convert_fusion.9), channel_id=1, source_target_pairs={{0,3},{1,0},{2,1},{3,2},{4,7},{5,4},{6,5},{7,6},{8,11},{9,8},{10,9... | collective-permute-start | bytes 1179656 | tf_op jit(solution)/shard_map/ppermute | solution.py:26
  333.8 52.2 %collective-permute-start.29 = (bf16[128,1536]{1,0:T(8,128)(2,1)S(1)}, bf16[128,1536]{1,0:T(8,128)(2,1)}, u32[]{:S(2)}, u32[]{:S(2)}) collective-permute-start(bf16[128,1536]{1,0:T(8,128)(2,1)S(1)} %multiply_convert_fusion.9), channel_id=1, source_target_pairs={{0,2},{1,3},{2,0},{3,1},{4,6},{5,7},{6,4},{7,5},{8,10},{9,11},{10,... | collective-permute-start | bytes 1179656 | tf_op jit(solution)/shard_map/ppermute | solution.py:26
  333.8 52.2 %collective-permute-start.28 = (bf16[128,1536]{1,0:T(8,128)(2,1)S(1)}, bf16[128,1536]{1,0:T(8,128)(2,1)}, u32[]{:S(2)}, u32[]{:S(2)}) collective-permute-start(bf16[128,1536]{1,0:T(8,128)(2,1)S(1)} %multiply_convert_fusion.9), channel_id=1, source_target_pairs={{0,1},{1,2},{2,3},{3,0},{4,5},{5,6},{6,7},{7,4},{8,9},{9,10},{10,1... | collective-permute-start | bytes 1179656 | tf_op jit(solution)/shard_map/ppermute | solution.py:26
  337.3 70.9 %all-to-all-start.2 = ((bf16[4,192,1536]{2,1,0:T(8,128)(2,1)}), bf16[4,192,1536]{2,1,0:T(8,128)(2,1)}, u32[]{:S(2)}, u32[]{:S(2)}) async-start(bf16[4,192,1536]{2,1,0:T(8,128)(2,1)} %bitcast.311), calls=%async_computation.2 | async-start | bytes 4718592 | tf_op jit(solution)/shard_map/all_to_all | solution.py:104
  505.3 76.5 %collective-permute-start.45 = (bf16[64,1536]{1,0:T(8,128)(2,1)}, bf16[64,1536]{1,0:T(8,128)(2,1)}, u32[]{:S(2)}, u32[]{:S(2)}) collective-permute-start(bf16[64,1536]{1,0:T(8,128)(2,1)} %get-tuple-element.610), channel_id=1, source_target_pairs={{0,4},{4,8},{8,12},{12,0},{1,5},{5,9},{9,13},{13,1},{2,6},{6,10},{... | collective-permute-start | bytes 589832 | tf_op jit(solution)/shard_map/ppermute | solution.py:26
  507.3 77.5 %collective-permute-start.44 = (bf16[64,1536]{1,0:T(8,128)(2,1)}, bf16[64,1536]{1,0:T(8,128)(2,1)}, u32[]{:S(2)}, u32[]{:S(2)}) collective-permute-start(bf16[64,1536]{1,0:T(8,128)(2,1)} %get-tuple-element.611), channel_id=1, source_target_pairs={{0,8},{4,12},{8,0},{12,4},{1,9},{5,13},{9,1},{13,5},{2,10},{6,14},... | collective-permute-start | bytes 589832 | tf_op jit(solution)/shard_map/ppermute | solution.py:26
  545.8 413.6 %reduce-scatter.10.cloned.1.call-start = ((), (), s32[]{:S(2)}) async-start(), calls=%async_computation.21 | async-start | bytes 491520 | tf_op jit(solution)/shard_map/reduce_scatter | solution.py:987
  584.7 374.7 %reduce-scatter.8.cloned.1.call-start = ((), (), s32[]{:S(2)}) async-start(), calls=%async_computation.20 | async-start | bytes 983040 | tf_op jit(solution)/shard_map/reduce_scatter | solution.py:987
  627.1 170.3 %all-to-all-start.6 = ((bf16[4,192,1536]{2,1,0:T(8,128)(2,1)}), bf16[4,192,1536]{2,1,0:T(8,128)(2,1)}, u32[]{:S(2)}, u32[]{:S(2)}) async-start(bf16[4,192,1536]{2,1,0:T(8,128)(2,1)} %bitcast.308), calls=%async_computation.6 | async-start | bytes 4718592 | tf_op jit(solution)/shard_map/all_to_all | solution.py:104
  631.7 327.7 %reduce-scatter.12.cloned.1.call-start = ((), (), s32[]{:S(2)}) async-start(), calls=%async_computation.22 | async-start | bytes 1474560 | tf_op jit(solution)/shard_map/reduce_scatter | solution.py:987
  694.3 82.0 %collective-permute-start.66 = (bf16[1536,384]{1,0:T(8,128)(2,1)}, bf16[1536,384]{1,0:T(8,128)(2,1)}, u32[]{:S(2)}, u32[]{:S(2)}) collective-permute-start(bf16[1536,384]{1,0:T(8,128)(2,1)} %convolution_convert_fusion.16), channel_id=1, source_target_pairs={{0,16},{16,0},{1,17},{17,1},{2,18},{18,2},{3,19},{19,3},{4,20},{20... | collective-permute-start | bytes 3538952 | tf_op jit(solution)/shard_map/ppermute | solution.py:30
  697.2 79.1 %collective-permute-start.67 = (bf16[1536,768]{1,0:T(8,128)(2,1)}, bf16[1536,768]{1,0:T(8,128)(2,1)}, u32[]{:S(2)}, u32[]{:S(2)}) collective-permute-start(bf16[1536,768]{1,0:T(8,128)(2,1)} %convolution_convert_fusion.2), channel_id=1, source_target_pairs={{0,16},{16,0},{1,17},{17,1},{2,18},{18,2},{3,19},{19,3},{4,20},{20... | collective-permute-start | bytes 7077896 | tf_op jit(solution)/shard_map/ppermute | solution.py:30
  746.3 59.9 %collective-permute-start.70 = (bf16[64,1536]{1,0:T(8,128)(2,1)}, bf16[64,1536]{1,0:T(8,128)(2,1)}, u32[]{:S(2)}, u32[]{:S(2)}) collective-permute-start(bf16[64,1536]{1,0:T(8,128)(2,1)} %get-tuple-element.600), channel_id=1, source_target_pairs={{0,4},{4,8},{8,12},{12,0},{1,5},{5,9},{9,13},{13,1},{2,6},{6,10},{... | collective-permute-start | bytes 589832 | tf_op jit(solution)/shard_map/ppermute | solution.py:26
  779.6 204.0 %reduce-scatter.14.cloned.1.call-start = ((), (), s32[]{:S(2)}) async-start(), calls=%async_computation.23 | async-start | bytes 2949120 | tf_op jit(solution)/shard_map/reduce_scatter | solution.py:987
  787.3 103.8 %collective-permute-start.65 = (bf16[64,1536]{1,0:T(8,128)(2,1)}, bf16[64,1536]{1,0:T(8,128)(2,1)}, u32[]{:S(2)}, u32[]{:S(2)}) collective-permute-start(bf16[64,1536]{1,0:T(8,128)(2,1)} %get-tuple-element.591), channel_id=1, source_target_pairs={{0,4},{4,8},{8,12},{12,0},{1,5},{5,9},{9,13},{13,1},{2,6},{6,10},{... | collective-permute-start | bytes 589832 | tf_op jit(solution)/shard_map/ppermute | solution.py:26
  843.6 258.8 %reduce-scatter.16.cloned.1.call-start = ((), (), s32[]{:S(2)}) async-start(), calls=%async_computation.24 | async-start | bytes 1966080 | tf_op jit(solution)/shard_map/reduce_scatter | solution.py:1027
  892.5 239.8 %reduce-scatter.20.cloned.1.call-start = ((), (), s32[]{:S(2)}) async-start(), calls=%async_computation.26 | async-start | bytes 491520 | tf_op jit(solution)/shard_map/reduce_scatter | solution.py:987
  1032.0 100.4 %reduce-scatter.18.cloned.1.call-start = ((), (), s32[]{:S(2)}) async-start(), calls=%async_computation.25 | async-start | bytes 983040 | tf_op jit(solution)/shard_map/reduce_scatter | solution.py:987
  1080.2 45.4 %collective-permute-start.113 = (bf16[512,1536]{1,0:T(8,128)(2,1)}, bf16[512,1536]{1,0:T(8,128)(2,1)}, u32[]{:S(2)}, u32[]{:S(2)}) collective-permute-start(bf16[512,1536]{1,0:T(8,128)(2,1)} %get-tuple-element.523), channel_id=1, source_target_pairs={{0,16},{16,0},{1,17},{17,1},{2,18},{18,2},{3,19},{19,3},{4,20},{20... | collective-permute-start | bytes 4718600 | tf_op jit(solution)/shard_map/ppermute | solution.py:30
  1110.6 46.8 %collective-permute-start.103 = (f32[1,4096]{1,0:T(1,128)}, f32[1,4096]{1,0:T(1,128)}, u32[]{:S(2)}, u32[]{:S(2)}) collective-permute-start(f32[1,4096]{1,0:T(1,128)} %bitcast.66), channel_id=1, source_target_pairs={{0,3},{1,0},{2,1},{3,2},{4,7},{5,4},{6,5},{7,6},{8,11},{9,8},{10,9... | collective-permute-start | bytes 49160 | tf_op jit(solution)/shard_map/ppermute | solution.py:26
  1115.4 45.9 %collective-permute-start.102 = (f32[1,4096]{1,0:T(1,128)}, f32[1,4096]{1,0:T(1,128)}, u32[]{:S(2)}, u32[]{:S(2)}) collective-permute-start(f32[1,4096]{1,0:T(1,128)} %bitcast.66), channel_id=1, source_target_pairs={{0,2},{1,3},{2,0},{3,1},{4,6},{5,7},{6,4},{7,5},{8,10},{9,11},{10,... | collective-permute-start | bytes 49160 | tf_op jit(solution)/shard_map/ppermute | solution.py:26
  (391 other events, 4668.1 us)
Sparse Core Ops, SparseCore 0:
  14.0 48.1 all-gather.11
  64.6 28.9 all-gather.13
  95.2 12.1 all-gather.21
  108.7 13.2 all-gather.23
  123.5 13.2 all-gather.25
  138.5 47.5 all-gather.15
  242.8 71.5 all-gather.17
  316.3 44.2 all-gather.19
  584.8 21.6 reduce-scatter.9
  627.3 38.5 reduce-scatter.7
  779.8 39.3 reduce-scatter.11
  822.1 56.9 reduce-scatter.13
  892.7 47.0 reduce-scatter.15
  1032.1 24.0 reduce-scatter.19
  1080.3 33.6 reduce-scatter.17

commit v10 on v9

--- a/solution.py
+++ b/solution.py
@@ -627,7 +627,7 @@
     count = block.shape[0]
     first, others = sent_ahead(project(tables[0], block).astype(HALF))
     line = [shifted(block, "col", back) for back in range(1, groups())]
-    others, line = after((others, line))
+    line = after(line, others)
     tokens = jnp.concatenate([block, *line], axis=0)
     rows_own = jnp.concatenate([first, *others], axis=0)
     sent = project(tables[1], chunk_of(tokens, 1)).astype(HALF)
@@ -737,6 +737,10 @@
 
 def row_received(pieces, axis="row"):
     return [shifted(piece, axis, ahead) for ahead, piece in enumerate(pieces) if ahead]
+
+
+class Kept:
+    pass
 
 
 def flat(parts):
@@ -803,7 +807,6 @@
 
     tokens_now = lax.dynamic_index_in_dim(tokens, section_now, 0, keepdims=False)
     grad_now = lax.dynamic_index_in_dim(cotangent, section_now, 0, keepdims=False)
-    wide_tokens = spread(tokens_now.astype(HALF))
 
     halves = (
         jnp.concatenate([widened(proj_gate[0], wide), proj_state[0]], axis=1),
@@ -825,11 +828,10 @@
     keep, give = jnp.where(first, *halves), jnp.where(first, *halves[::-1])
     mine_out = pair(keep, swapped(give))
     proj_out = [both_halves(mine_out[0])]
-    gate_all = lax.all_gather(expert_gate[0, 0], "section")
-    up_all = lax.all_gather(expert_up[0, 0], "section")
-    down_all = lax.all_gather(expert_down[0, 0], "section")
+    own_experts = (expert_gate[0, 0], expert_up[0, 0], expert_down[0, 0])
+    experts = list(zip(*[pair(weight, swapped(weight)) for weight in own_experts]))
+    wide_tokens = spread(tokens_now.astype(HALF), experts)
     shared = both_layers(jnp.concatenate([shared_gate[0], shared_up[0], shared_down[0]], axis=1))
-    experts = [(gate_all[s], up_all[s], down_all[s]) for s in layers]
 
     small_in = (
         norm_in[0],
@@ -878,38 +880,39 @@
 
     wide_in_0 = rms_norm(wide_tokens.astype(FLOAT), norm_ins[0]).astype(HALF)
     pre_0, y_0, scaled_0, total_0 = mix_in(0, wide_in_0)
+    proj.append(both_halves(after(mine[1], scaled_0)))
+    proj_out.append(both_halves(after(mine_out[1], scaled_0)))
     tables = route_tables(spread(after(meta, scaled_0)), top, capacity, 2)
     plain = [[table[0] for table in tables[s]] for s in layers]
     scaling = [[table[1] for table in tables[s]] for s in layers]
     middle_0, mixed_0, rr_0 = mix_out(0, tokens_now, scaled_0, total_0, tables)
-    kept = {name: {} for name in ("rows 0", "rows 1", "answer 1", "grads 0", "grads 1")}
+    kept = Kept()
+    kept.rows_0, kept.rows_1, kept.answer_1, kept.grads_0, kept.grads_1 = {}, {}, {}, {}, {}
 
     def expert_0(index, rows):
-        kept["rows 0"][index], answer = expert_forward(rows, experts[0])
+        kept.rows_0[index], answer = expert_forward(rows, experts[0])
         return answer
 
     def own_0(tokens_all, rows):
-        kept["shared 0"] = shared_forward(tokens_all, shared[0])
-        kept["part 0"] = home_part(kept["shared 0"][2], shared[0])
-        return kept["part 0"]
+        kept.shared_0 = shared_forward(tokens_all, shared[0])
+        kept.part_0 = home_part(kept.shared_0[2], shared[0])
+        return kept.part_0
 
     def beside_0(index, result):
-        part = outer(scaling[0][index], result) + chunk_of(kept["part 0"], index)
+        part = outer(scaling[0][index], result) + chunk_of(kept.part_0, index)
         return part.astype(HALF)
 
     def aside_0(tokens_all):
-        kept["grads"] = spread(after(grad_now.astype(HALF), tokens_all))
-        return kept["grads"]
+        kept.grads = spread(after(grad_now.astype(HALF), tokens_all))
+        return kept.grads
 
     total, rows_0, mids_0 = through_experts(
         rms_norm(middle_0, norm_mids[0]).astype(HALF), plain[0], expert_0, own_0, beside_0, aside_0
     )
-    proj.append(both_halves(after(mine[1], kept["part 0"])))
-    proj_out.append(both_halves(after(mine_out[1], kept["part 0"])))
     out_0 = middle_0 + total
 
     wide_in_1 = spread(rms_norm(out_0, norm_ins[1]).astype(HALF))
-    grad_tokens_1 = after(kept["grads"], out_0)
+    grad_tokens_1 = after(kept.grads, out_0)
     grad_sent = [
         project(table, chunk_of(grad_tokens_1, index)).astype(HALF)
         for index, table in enumerate(scaling[1])
@@ -917,38 +920,39 @@
     grad_rows_1 = [to_experts(grad_sent[-1])]
     if groups() > 1:
         own_rows, others = sent_ahead(grad_sent[0])
-        grad_rows_1 = [jnp.concatenate([own_rows, *others], axis=0), *grad_rows_1]
     pre_1, y_1, scaled_1, total_1 = mix_in(1, wide_in_1)
-    scaled_1 = after(scaled_1, grad_rows_1)
+    if groups() > 1:
+        own_rows = jnp.concatenate([own_rows, *after(others, scaled_1)], axis=0)
+        grad_rows_1 = [own_rows, *after(grad_rows_1, scaled_1)]
     middle_1, mixed_1, rr_1 = mix_out(1, out_0, scaled_1, total_1, ())
 
     def expert_1(index, rows):
-        kept["rows 1"][index], kept["answer 1"][index] = expert_forward(rows, experts[1])
-        kept["grads 1"][index], back = expert_backward(
-            grad_rows_1[index], kept["rows 1"][index], experts[1]
+        kept.rows_1[index], kept.answer_1[index] = expert_forward(rows, experts[1])
+        kept.grads_1[index], back = expert_backward(
+            grad_rows_1[index], kept.rows_1[index], experts[1]
         )
         return back
 
     def own_1(tokens_all, rows):
-        kept["shared 1"] = shared_forward(tokens_all, shared[1])
-        kept["shared grads 1"], kept["part 1"] = shared_backward(
-            grad_tokens_1, kept["shared 1"], shared[1]
-        )
-        kept["sums 1"] = weight_sums(
+        kept.shared_1 = shared_forward(tokens_all, shared[1])
+        kept.shared_grads_1, kept.part_1 = shared_backward(
+            grad_tokens_1, kept.shared_1, shared[1]
+        )
+        kept.sums_1 = weight_sums(
             rows,
             grad_rows_1,
-            kept["rows 1"],
-            kept["grads 1"],
+            kept.rows_1,
+            kept.grads_1,
             tokens_all,
             grad_tokens_1,
-            kept["shared 1"],
-            kept["shared grads 1"],
-        )
-        experts_1, shared_1 = kept["sums 1"]
-        return experts_1, kept["part 1"], [made[-1] for made in shared_1]
+            kept.shared_1,
+            kept.shared_grads_1,
+        )
+        experts_1, shared_1 = kept.sums_1
+        return experts_1, kept.part_1, [made[-1] for made in shared_1]
 
     def beside_1(index, result):
-        part = outer(plain[1][index], result) + chunk_of(kept["part 1"], index)
+        part = outer(plain[1][index], result) + chunk_of(kept.part_1, index)
         return part.astype(HALF)
 
     total, rows_1, mids_1 = through_experts(
@@ -989,8 +993,8 @@
     grad_middle, along, grad_norm_mid_1 = middle_backward(
         total, grad_now, middle_1, mixed_1, norm_mids[1]
     )
-    expert_grads_1, shared_grads_1 = kept["sums 1"]
-    answers = after([kept["answer 1"][index] for index in kept["answer 1"]], grad_middle)
+    expert_grads_1, shared_grads_1 = kept.sums_1
+    answers = after([kept.answer_1[index] for index in kept.answer_1], grad_middle)
     answers_back = [to_experts(answers[-1])]
     if groups() > 1:
         own_rows, others = sent_back(answers[0])
@@ -1010,13 +1014,7 @@
     grad_1, grad_norm_in_1 = resid_back(out_0, norm_ins[1], grad_in, grad_middle)
 
     def aside_back_0(tokens_all):
-        own_proj, own_out, own_tail = after((to_proj, to_out, tail), tokens_all)
-        given, given_out = half_to_give(*own_proj), half_to_give(*own_out)
-        made = ((*own_out, swapped(given_out)), (*own_proj, swapped(given)))
-        made = [half_to_keep(*each) for each in after(made, (given, given_out))]
-        kept["sent 1"] = [*shared_sent_1, *[row_sums(each) for each in made]]
-        kept["tail 1"] = outer(own_proj[0], own_tail).astype(HALF)
-        home = home_part(after(kept["shared 1"][2], made), shared[1])
+        home = home_part(after(kept.shared_1[2], tokens_all), shared[1])
         home = [
             (outer(scaling[1][index], answer) + chunk_of(home, index)).astype(HALF)
             for index, answer in enumerate(answers_back)
@@ -1024,42 +1022,48 @@
         home = joined(home)
         if groups() > 1:
             home = in_order([block_of(home, back) for back in range(groups())], "col")
-        kept["home"] = lax.psum_scatter(home, "col", scatter_dimension=0, tiled=True)
-        return made, kept["tail 1"], home
+        kept.home = lax.psum_scatter(home, "col", scatter_dimension=0, tiled=True)
+        own_proj, own_out, own_tail = after((to_proj, to_out, tail), home)
+        given, given_out = half_to_give(*own_proj), half_to_give(*own_out)
+        made = ((*own_out, swapped(given_out)), (*own_proj, swapped(given)))
+        made = [half_to_keep(*each) for each in after(made, (given, given_out))]
+        kept.sent_1 = [*shared_sent_1, *[row_sums(each) for each in made]]
+        kept.tail_1 = outer(own_proj[0], own_tail).astype(HALF)
+        return made, kept.tail_1
 
     def expert_back_0(index, rows):
-        kept["grads 0"][index], back = expert_backward(rows, kept["rows 0"][index], experts[0])
+        kept.grads_0[index], back = expert_backward(rows, kept.rows_0[index], experts[0])
         return back
 
     def own_back_0(tokens_all, rows):
-        kept["shared grads 0"], kept["part 0"] = shared_backward(
-            tokens_all, kept["shared 0"], shared[0]
-        )
-        kept["sums 0"] = weight_sums(
+        kept.shared_grads_0, kept.part_0 = shared_backward(
+            tokens_all, kept.shared_0, shared[0]
+        )
+        kept.sums_0 = weight_sums(
             rows_0,
             rows,
-            kept["rows 0"],
-            kept["grads 0"],
+            kept.rows_0,
+            kept.grads_0,
             mids_0,
             tokens_all,
-            kept["shared 0"],
-            kept["shared grads 0"],
-        )
-        experts_0, shared_0 = kept["sums 0"]
-        return experts_0, kept["part 0"], [made[-1] for made in shared_0]
+            kept.shared_0,
+            kept.shared_grads_0,
+        )
+        experts_0, shared_0 = kept.sums_0
+        return experts_0, kept.part_0, [made[-1] for made in shared_0]
 
     def beside_back_0(index, result):
-        part = outer(plain[0][index], result) + chunk_of(kept["part 0"], index)
+        part = outer(plain[0][index], result) + chunk_of(kept.part_0, index)
         return part.astype(HALF)
 
     total, grad_rows_0, grad_tokens_0 = through_experts(
         grad_1.astype(HALF), scaling[0], expert_back_0, own_back_0, beside_back_0, aside_back_0
     )
-    sums_1, grad_tail_1 = kept["sent 1"], kept["tail 1"]
+    sums_1, grad_tail_1 = kept.sent_1, kept.tail_1
     grad_middle, along, grad_norm_mid_0 = middle_backward(
         total, grad_1, middle_0, mixed_0, norm_mids[0]
     )
-    expert_grads_0, shared_grads_0 = kept["sums 0"]
+    expert_grads_0, shared_grads_0 = kept.sums_0
     shared_sums_0 = [half_to_keep(*after(made, total)) for made in shared_grads_0]
     sums_0 = [row_sums(made) for made in shared_sums_0]
     expert_out = [own_layer(a, b) for a, b in zip(expert_grads_0, expert_grads_1)]
@@ -1072,20 +1076,10 @@
         ([part[0] for part in expert_out], shared_sums_0, sums_1),
     )
 
-    given = half_to_give(*to_proj)
+    grad_tail_0 = outer(wide_in_0, tail).astype(HALF)
+    tail_keep, tail_other = own_layer(grad_tail_0, grad_tail_1)
+    given = half_to_give(*after(to_proj, grad_tail_0))
     whole = line_product(after(grad_pre, given), proj[0])
-    proj_half = half_to_keep(*after((*to_proj, swapped(given)), whole))
-    proj_pieces = row_pieces(proj_half)
-    proj_received = row_received(proj_pieces)
-    line_received = sent_home(after(whole, proj_half))
-    given_out = half_to_give(*after(to_out, proj_half))
-    grad_tail_0 = outer(after(wide_in_0, given_out), tail).astype(HALF)
-    out_half = half_to_keep(*after((*to_out, swapped(given_out)), grad_tail_0))
-    out_pieces = row_pieces(out_half)
-    out_received = row_received(out_pieces)
-    tail_keep, tail_other = own_layer(grad_tail_0, grad_tail_1)
-    tail_pieces = row_pieces((tail_keep + tail_other.astype(FLOAT)).astype(HALF))
-    tail_received = row_received(tail_pieces)
     wide_x = wide_tokens.astype(FLOAT)
     wide_r = lax.rsqrt(jnp.mean(wide_x * wide_x, axis=1, keepdims=True) + EPS)
     grad_norm_in_0 = jnp.sum(whole.astype(FLOAT) * wide_x * wide_r, axis=0)
@@ -1095,20 +1089,46 @@
     )
     shapes = [part.shape for part in smalls[0]]
     small_keep, small_other = own_layer(flat(smalls[0]), flat(smalls[1]))
+    tail_pieces = row_pieces((tail_keep + tail_other.astype(FLOAT)).astype(HALF))
     vector = small_keep + small_other.astype(FLOAT)
     lines = [shifted(vector[None], "row", back) for back in range(n_row)]
-    line_received, proj_received, out_received, tail_received, lines = after(
-        (line_received, proj_received, out_received, tail_received, lines)
-    )
+    tail_received = row_received(tail_pieces)
+    proj_half = half_to_keep(*after((*to_proj, swapped(given)), whole))
+    given_out = half_to_give(*after(to_out, proj_half))
+    tail_received, lines = after((tail_received, lines), (proj_half, given_out))
+    tail = total_of(tail_pieces[0], tail_received).astype(HALF)
+    vector = jnp.sum(in_order(lines, "row"), axis=0)
+    common = 2 * width + conv_state.shape[1] * state
+    state_grad = tail[:, :state]
+    line_received = sent_home(after(whole, proj_half))
+    proj_pieces = row_pieces(after(proj_half, tail))
+    proj_received = row_received(proj_pieces)
+    out_half = half_to_keep(*after((*to_out, swapped(given_out)), tail))
+    out_pieces = row_pieces(out_half)
+    out_received = row_received(out_pieces)
+    if groups() > 1:
+        state_pieces = row_pieces(state_grad, "col")
+        state_received = row_received(state_pieces, "col")
+        lines = [shifted(vector[None, :common], "col", back) for back in range(n_col)]
+        state_received, lines = after((state_received, lines), out_half)
+        shared_sum = jnp.sum(in_order(lines, "col"), axis=0)
+        state_grad = total_of(state_pieces[0], state_received).astype(HALF)
+        state_lines = [shifted(state_grad, "col", back) for back in range(n_col)]
+    else:
+        state_grad = lax.psum(state_grad, "col")
+        state_lines = [state_grad]
+        shared_sum = lax.psum(vector[:common], "col")
+    expert_out = [keep + other.astype(FLOAT) for keep, other in after(expert_out, out_half)]
+    state_lines, line_received, proj_received, out_received = after(
+        (state_lines, line_received, proj_received, out_received), expert_out
+    )
+    state_grad = in_order(state_lines, "col")
     grad_in = added_up(whole, line_received)
     sums_0.append(total_of(out_pieces[0], out_received).astype(HALF))
     sums_0.append(total_of(proj_pieces[0], proj_received).astype(HALF))
     sums_0, sums_1 = after((sums_0, sums_1), grad_in)
-    expert_out = [keep + other.astype(FLOAT) for keep, other in after(expert_out, grad_in)]
-    tail = total_of(tail_pieces[0], tail_received).astype(HALF)
-    vector = jnp.sum(in_order(lines, "row"), axis=0)
     grad_0, _ = resid_back(tokens_now, norm_ins[0], grad_in, grad_middle)
-    out_1 = middle_1 + kept["home"].astype(FLOAT)
+    out_1 = middle_1 + kept.home.astype(FLOAT)
 
     def own_halves(first_value, second_value):
         keep = jnp.where(first, first_value, second_value)
@@ -1121,19 +1141,6 @@
 
     halves = [own_halves(a, b) for a, b in zip(sums_0, sums_1)]
     outs, in_grads = per_micro(out_0, after(out_1, grad_in)), per_micro(grad_0, grad_1)
-    common = 2 * width + conv_state.shape[1] * state
-    state_grad = tail[:, :state]
-    if groups() > 1:
-        state_pieces = row_pieces(state_grad, "col")
-        state_received = row_received(state_pieces, "col")
-        lines = [shifted(vector[None, :common], "col", back) for back in range(n_col)]
-        state_received, lines, outs, in_grads = after((state_received, lines, outs, in_grads))
-        state_grad = total_of(state_pieces[0], state_received).astype(HALF)
-        state_grad = in_order([shifted(state_grad, "col", back) for back in range(n_col)], "col")
-        shared_sum = jnp.sum(in_order(lines, "col"), axis=0)
-    else:
-        state_grad = lax.psum(state_grad, "col")
-        shared_sum = lax.psum(vector[:common], "col")
     halves = [pair(*half) for half in halves]
     grad_shared, grad_down, grad_out, grad_ends = halves
     grad_out, grad_down = [jnp.concatenate(both, axis=1) for both in (grad_out, grad_down)]

time: 1200 us -> 1180 us (0.983)
  waiting for transfers between devices: 476 us -> 455 us
    ppermute x93, waiting for transfers between devices: 395 us -> 364 us  [shifted(): lax.ppermute(block, axis, [(i, (i + distance) % count) for i in range(cou...]
    all_to_all x8, waiting for transfers between devices: 67.1 us -> 81.9 us  [exchanged(): return lax.all_to_all(rows, axis, split_axis=0, concat_axis=0, tiled=True)]
    ppermute x93, starting transfers between devices: 200 us -> 186 us  [shifted(): lax.ppermute(block, axis, [(i, (i + distance) % count) for i in range(cou...]
    add x1 -> x4, other arithmetic: 1.08 us -> 13.1 us  [the longest x3 11 us: shards(): keep + other.astype(FLOAT)]
    unnamed x606 -> x622, local copies, waits for them, and re-layouts: 32.3 us -> 39.5 us
  transfers between devices with their start and end apart: 139 -> 139, of which waited for: 53 -> 52; matrix products, arithmetic and copies ran while one was open for 29% -> 31% of each run, Pallas kernels for 5% -> 5%
where the time goes in v10:
time: 1180 us; the launch traced here: 1170 us
  waiting for transfers between devices  455 us (39%)
  matrix products  238 us (20%)
  starting transfers between devices  231 us (20%)
  other arithmetic  84.4 us (7%)
  local copies, waits for them, and re-layouts  80.5 us (7%)
  Pallas kernels  61.6 us (5%)
  between operations  18.4 us (2%)
    ppermute x93, waiting for transfers between devices, shifted(): lax.ppermute(block, axis, [(i, (i + distance) % count) for i in range(cou...  364 us
    ppermute x93, starting transfers between devices, shifted(): lax.ppermute(block, axis, [(i, (i + distance) % count) for i in range(cou...  186 us
    dot_general x32, matrix products, outer(): lax.dot_general(left, right, (((0,), (0,)), ((), ())), preferred_element_...  89.1 us
    all_to_all x8, waiting for transfers between devices, exchanged(): return lax.all_to_all(rows, axis, split_axis=0, concat_axis=0, tiled=True)  81.9 us
    dot_general x36, matrix products, project(): return jnp.dot(left, right, preferred_element_type=FLOAT)  78.3 us
    dot_general x26, matrix products, project_back(): lax.dot_general(left, right, (((1,), (1,)), ((), ())), preferred_element_...  70.7 us
    unnamed x622, local copies, waits for them, and re-layouts  39.5 us
    all_to_all x8, starting transfers between devices, exchanged(): return lax.all_to_all(rows, axis, split_axis=0, concat_axis=0, tiled=True)  36.9 us
  transfers between devices with their start and end apart: 139, of which 52 were waited for; matrix products, arithmetic and copies ran while one was open for 31% of the time, Pallas kernels for 5%

profile of v10, /device:TPU:0, one launch (start us, length us, event | category | flops | bytes accessed | tf_op | source)
XLA Modules:
  0.0 1169.7 jit_solution(158043382809539664)
XLA Ops:
  40.2 17.6 %collective-permute-done.1 = bf16[128,1536]{1,0:T(8,128)(2,1)} collective-permute-done((bf16[128,1536]{1,0:T(8,128)(2,1)S(1)}, bf16[128,1536]{1,0:T(8,128)(2,1)}, u32[]{:S(2)}, u32[]{:S(2)}) %collective-permute-start.1) | collective-permute-done | bytes 393248 | tf_op jit(solution)/shard_map/ppermute | solution.py:26
  69.6 13.3 %mixer_forward.2 = (f32[512,768]{1,0:T(8,128)S(1)}, bf16[512,768]{1,0:T(8,128)(2,1)S(1)}, f32[512,1]{1,0:T(8,128)S(1)}) custom-call(f32[512,1024]{1,0:T(8,128)S(1)} %fusion.34.pre_in_ref, f32[512,1024]{1,0:T(8,128)} %fusion.31.pre_other_in_ref, f32[4,768]{1,0:T(4,128)S(1)} %reshape.470.conv_input_ref, f32[4,256]{1,0:T(4,128)S(1)} %slice.595.conv_state_ref, ...), custom_call_target="tpu_custom_call" | custom-call | tf_op jit(solution)/shard_map/mixer_forward/pallas_call | solution.py:541
  106.5 8.2 collective-permute-done.11
  122.5 18.8 %collective-permute-done.10 = bf16[128,1664]{1,0:T(8,128)(2,1)} collective-permute-done((bf16[128,1664]{1,0:T(8,128)(2,1)S(1)}, bf16[128,1664]{1,0:T(8,128)(2,1)}, u32[]{:S(2)}, u32[]{:S(2)}) %collective-permute-start.10) | collective-permute-done | bytes 426016 | tf_op jit(solution)/shard_map/ppermute | solution.py:26
  150.6 8.0 collective-permute-done.18
  168.8 11.5 collective-permute-done.20
  187.9 23.9 %collective-permute-done.26 = bf16[128,1536]{1,0:T(8,128)(2,1)} collective-permute-done((bf16[128,1536]{1,0:T(8,128)(2,1)}, bf16[128,1536]{1,0:T(8,128)(2,1)}, u32[]{:S(2)}, u32[]{:S(2)}) %collective-permute-start.26) | collective-permute-done | bytes 393248 | tf_op jit(solution)/shard_map/ppermute | solution.py:26
  248.3 18.9 %all-to-all-done.1 = bf16[4,192,1536]{2,1,0:T(8,128)(2,1)} async-done(((bf16[4,192,1536]{2,1,0:T(8,128)(2,1)}), bf16[4,192,1536]{2,1,0:T(8,128)(2,1)}, u32[]{:S(2)}, u32[]{:S(2)}) %all-to-all-start.1) | async-done | bytes 2359328 | tf_op jit(solution)/shard_map/all_to_all | solution.py:104
  271.9 12.7 %collective-permute-start.30 = (bf16[128,1536]{1,0:T(8,128)(2,1)}, bf16[128,1536]{1,0:T(8,128)(2,1)S(1)}, u32[]{:S(2)}, u32[]{:S(2)}) collective-permute-start(bf16[128,1536]{1,0:T(8,128)(2,1)} %get-tuple-element.567), channel_id=1, source_target_pairs={{0,1},{1,2},{2,3},{3,0},{4,5},{5,6},{6,7},{7,4},{8,9},{9,10},{10,1... | collective-permute-start | bytes 1179656 | tf_op jit(solution)/shard_map/ppermute | solution.py:26
  310.7 14.4 %collective-permute-start.33 = (bf16[128,1536]{1,0:T(8,128)(2,1)S(1)}, bf16[128,1536]{1,0:T(8,128)(2,1)S(1)}, u32[]{:S(2)}, u32[]{:S(2)}) collective-permute-start(bf16[128,1536]{1,0:T(8,128)(2,1)S(1)} %multiply_convert_fusion.9), channel_id=1, source_target_pairs={{0,3},{1,0},{2,1},{3,2},{4,7},{5,4},{6,5},{7,6},{8,11},{9,8},{10,9... | collective-permute-start | bytes 1179656 | tf_op jit(solution)/shard_map/ppermute | solution.py:26
  342.0 12.4 %collective-permute-done.32 = bf16[128,1536]{1,0:T(8,128)(2,1)} collective-permute-done((bf16[128,1536]{1,0:T(8,128)(2,1)S(1)}, bf16[128,1536]{1,0:T(8,128)(2,1)}, u32[]{:S(2)}, u32[]{:S(2)}) %collective-permute-start.32) | collective-permute-done | bytes 393248 | tf_op jit(solution)/shard_map/ppermute | solution.py:26
  363.5 12.0 %mixer_forward.3 = (f32[512,768]{1,0:T(8,128)S(1)}, bf16[512,768]{1,0:T(8,128)(2,1)S(1)}, f32[512,1]{1,0:T(8,128)S(1)}) custom-call(f32[512,1024]{1,0:T(8,128)S(1)} %fusion.27.pre_in_ref, f32[512,1024]{1,0:T(8,128)} %fusion.23.pre_other_in_ref, f32[4,768]{1,0:T(4,128)S(1)} %reshape.476.conv_input_ref, f32[4,256]{1,0:T(4,128)S(1)} %slice.644.conv_state_ref, ...), custom_call_target="tpu_custom_call" | custom-call | tf_op jit(solution)/shard_map/mixer_forward/pallas_call | solution.py:541
  404.7 16.0 %collective-permute-done.35 = bf16[128,1664]{1,0:T(8,128)(2,1)} collective-permute-done((bf16[128,1664]{1,0:T(8,128)(2,1)}, bf16[128,1664]{1,0:T(8,128)(2,1)}, u32[]{:S(2)}, u32[]{:S(2)}) %collective-permute-start.35) | collective-permute-done | bytes 426016 | tf_op jit(solution)/shard_map/ppermute | solution.py:26
  444.0 20.9 %collective-permute-done.41 = bf16[128,1536]{1,0:T(8,128)(2,1)S(1)} collective-permute-done((bf16[128,1536]{1,0:T(8,128)(2,1)S(1)}, bf16[128,1536]{1,0:T(8,128)(2,1)S(1)}, u32[]{:S(2)}, u32[]{:S(2)}) %collective-permute-start.41) | collective-permute-done | bytes 393248 | tf_op jit(solution)/shard_map/ppermute | solution.py:26
  481.8 17.7 %all-to-all-done.2 = bf16[4,192,1536]{2,1,0:T(8,128)(2,1)} async-done(((bf16[4,192,1536]{2,1,0:T(8,128)(2,1)}), bf16[4,192,1536]{2,1,0:T(8,128)(2,1)}, u32[]{:S(2)}, u32[]{:S(2)}) %all-to-all-start.2) | async-done | bytes 2359328 | tf_op jit(solution)/shard_map/all_to_all | solution.py:104
  563.5 13.0 %collective-permute-done.52 = bf16[128,1536]{1,0:T(8,128)(2,1)S(1)} collective-permute-done((bf16[128,1536]{1,0:T(8,128)(2,1)S(1)}, bf16[128,1536]{1,0:T(8,128)(2,1)S(1)}, u32[]{:S(2)}, u32[]{:S(2)}) %collective-permute-start.52) | collective-permute-done | bytes 393248 | tf_op jit(solution)/shard_map/ppermute | solution.py:26
  594.4 20.7 %all-to-all-done.5 = bf16[4,192,1536]{2,1,0:T(8,128)(2,1)} async-done(((bf16[4,192,1536]{2,1,0:T(8,128)(2,1)}), bf16[4,192,1536]{2,1,0:T(8,128)(2,1)}, u32[]{:S(2)}, u32[]{:S(2)}) %all-to-all-start.5) | async-done | bytes 2359328 | tf_op jit(solution)/shard_map/all_to_all | solution.py:104
  644.3 12.0 %collective-permute-start.59 = (bf16[128,1664]{1,0:T(8,128)(2,1)}, bf16[128,1664]{1,0:T(8,128)(2,1)S(1)}, u32[]{:S(2)}, u32[]{:S(2)}) collective-permute-start(bf16[128,1664]{1,0:T(8,128)(2,1)} %pad_maximum_fusion.17), channel_id=1, source_target_pairs={{0,3},{1,0},{2,1},{3,2},{4,7},{5,4},{6,5},{7,6},{8,11},{9,8},{10,9... | collective-permute-start | bytes 1277960 | tf_op jit(solution)/shard_map/ppermute | solution.py:26
  661.5 13.4 %collective-permute-done.59 = bf16[128,1664]{1,0:T(8,128)(2,1)S(1)} collective-permute-done((bf16[128,1664]{1,0:T(8,128)(2,1)}, bf16[128,1664]{1,0:T(8,128)(2,1)S(1)}, u32[]{:S(2)}, u32[]{:S(2)}) %collective-permute-start.59) | collective-permute-done | bytes 426016 | tf_op jit(solution)/shard_map/ppermute | solution.py:26
  674.9 29.4 %collective-permute-done.58 = bf16[128,1664]{1,0:T(8,128)(2,1)S(1)} collective-permute-done((bf16[128,1664]{1,0:T(8,128)(2,1)}, bf16[128,1664]{1,0:T(8,128)(2,1)S(1)}, u32[]{:S(2)}, u32[]{:S(2)}) %collective-permute-start.58) | collective-permute-done | bytes 426016 | tf_op jit(solution)/shard_map/ppermute | solution.py:26
  710.0 18.1 %mixer_backward.2 = (bf16[512,1024]{1,0:T(8,128)(2,1)S(1)}, bf16[512,1024]{1,0:T(8,128)(2,1)S(1)}, f32[2,768]{1,0:T(2,128)S(1)}, f32[4,768]{1,0:T(4,128)S(1)}, f...) custom-call(f32[512,1024]{1,0:T(8,128)} %copy-done.3, f32[512,1024]{1,0:T(8,128)} %fusion.23.pre_other_in_ref, ...), custom_call_target="tpu_custom_call" | custom-call | tf_op jit(solution)/shard_map/mixer_backward/pallas_call | solution.py:566
  743.8 8.6 collective-permute-done.62
  752.4 15.7 %collective-permute-done.61 = bf16[128,1536]{1,0:T(8,128)(2,1)S(1)} collective-permute-done((bf16[128,1536]{1,0:T(8,128)(2,1)S(1)}, bf16[128,1536]{1,0:T(8,128)(2,1)S(1)}, u32[]{:S(2)}, u32[]{:S(2)}) %collective-permute-start.61) | collective-permute-done | bytes 393248 | tf_op jit(solution)/shard_map/ppermute | solution.py:26
  792.3 23.7 %collective-permute-done.67 = bf16[128,1536]{1,0:T(8,128)(2,1)S(1)} collective-permute-done((bf16[128,1536]{1,0:T(8,128)(2,1)S(1)}, bf16[128,1536]{1,0:T(8,128)(2,1)S(1)}, u32[]{:S(2)}, u32[]{:S(2)}) %collective-permute-start.67) | collective-permute-done | bytes 393248 | tf_op jit(solution)/shard_map/ppermute | solution.py:26
  839.1 12.7 %all-to-all-done.6 = bf16[4,192,1536]{2,1,0:T(8,128)(2,1)} async-done(((bf16[4,192,1536]{2,1,0:T(8,128)(2,1)}), bf16[4,192,1536]{2,1,0:T(8,128)(2,1)}, u32[]{:S(2)}, u32[]{:S(2)}) %all-to-all-start.6) | async-done | bytes 2359328 | tf_op jit(solution)/shard_map/all_to_all | solution.py:104
  902.9 9.9 all-to-all-done.7
  930.5 14.9 %collective-permute-done.77 = bf16[128,1536]{1,0:T(8,128)(2,1)S(1)} collective-permute-done((bf16[128,1536]{1,0:T(8,128)(2,1)S(1)}, bf16[128,1536]{1,0:T(8,128)(2,1)S(1)}, u32[]{:S(2)}, u32[]{:S(2)}) %collective-permute-start.77) | collective-permute-done | bytes 393248 | tf_op jit(solution)/shard_map/ppermute | solution.py:26
  950.5 9.9 collective-permute-start.81
  971.1 27.2 %collective-permute-done.80 = bf16[128,1664]{1,0:T(8,128)(2,1)} collective-permute-done((bf16[128,1664]{1,0:T(8,128)(2,1)}, bf16[128,1664]{1,0:T(8,128)(2,1)}, u32[]{:S(2)}, u32[]{:S(2)}) %collective-permute-start.80) | collective-permute-done | bytes 426016 | tf_op jit(solution)/shard_map/ppermute | solution.py:26
  1004.9 18.2 %mixer_backward.3 = (bf16[512,1024]{1,0:T(8,128)(2,1)S(1)}, bf16[512,1024]{1,0:T(8,128)(2,1)S(1)}, f32[2,768]{1,0:T(2,128)S(1)}, f32[4,768]{1,0:T(4,128)S(1)}, f...) custom-call(f32[512,1024]{1,0:T(8,128)} %copy-done.2, f32[512,1024]{1,0:T(8,128)} %fusion.31.pre_other_in_ref, ...), custom_call_target="tpu_custom_call" | custom-call | tf_op jit(solution)/shard_map/mixer_backward/pallas_call | solution.py:566
  1100.5 14.3 %collective-permute-done.102 = bf16[128,1536]{1,0:T(8,128)(2,1)S(1)} collective-permute-done((bf16[128,1536]{1,0:T(8,128)(2,1)S(1)}, bf16[128,1536]{1,0:T(8,128)(2,1)S(1)}, u32[]{:S(2)}, u32[]{:S(2)}) %collective-permute-start.102) | collective-permute-done | bytes 393248 | tf_op jit(solution)/shard_map/ppermute | solution.py:26
  1114.8 8.9 collective-permute-start.100
  (1197 shorter events, 654.4 us)
Async XLA Ops:
  7.2 54.9 %all-gather.6.cloned.1.call-start = ((), (), s32[]{:S(2)}) async-start(), calls=%async_computation.15 | async-start | bytes 7077888 | tf_op jit(solution)/shard_map/all_gather | solution.py:819
  13.8 79.8 %all-gather.8.cloned.1.call-start = ((), (), s32[]{:S(2)}) async-start(), calls=%async_computation.16 | async-start | bytes 2654208 | tf_op jit(solution)/shard_map/all_gather | solution.py:819
  16.6 223.2 %all-gather.10.cloned.1.call-start = ((), (), s32[]{:S(2)}) async-start(), calls=%async_computation.17 | async-start | bytes 5308416 | tf_op jit(solution)/shard_map/all_gather | solution.py:823
  17.6 336.9 %all-gather.12.cloned.1.call-start = ((), (), s32[]{:S(2)}) async-start(), calls=%async_computation.18 | async-start | bytes 7077888 | tf_op jit(solution)/shard_map/all_gather | solution.py:819
  34.0 50.1 %collective-permute-start.12 = (f32[128,12]{0,1:T(8,128)S(1)}, f32[128,12]{0,1:T(8,128)S(1)}, u32[]{:S(2)}, u32[]{:S(2)}) collective-permute-start(f32[128,12]{0,1:T(8,128)S(1)} %fusion.282), channel_id=1, source_target_pairs={{0,16},{16,0},{1,17},{17,1},{2,18},{18,2},{3,19},{19,3},{4,20},{20... | collective-permute-start | bytes 18440 | tf_op jit(solution)/shard_map/ppermute | solution.py:30
  103.7 37.7 %collective-permute-start.10 = (bf16[128,1664]{1,0:T(8,128)(2,1)S(1)}, bf16[128,1664]{1,0:T(8,128)(2,1)}, u32[]{:S(2)}, u32[]{:S(2)}) collective-permute-start(bf16[128,1664]{1,0:T(8,128)(2,1)S(1)} %get-tuple-element.548), channel_id=1, source_target_pairs={{0,2},{1,3},{2,0},{3,1},{4,6},{5,7},{6,4},{7,5},{8,10},{9,11},{10,... | collective-permute-start | bytes 1277960 | tf_op jit(solution)/shard_map/ppermute | solution.py:26
  145.4 34.9 %collective-permute-start.20 = (bf16[128,1536]{1,0:T(8,128)(2,1)S(1)}, bf16[128,1536]{1,0:T(8,128)(2,1)S(1)}, u32[]{:S(2)}, u32[]{:S(2)}) collective-permute-start(bf16[128,1536]{1,0:T(8,128)(2,1)S(1)} %multiply_convert_fusion.10), channel_id=1, source_target_pairs={{0,2},{1,3},{2,0},{3,1},{4,6},{5,7},{6,4},{7,5},{8,10},{9,11},{10,... | collective-permute-start | bytes 1179656 | tf_op jit(solution)/shard_map/ppermute | solution.py:26
  145.4 34.9 %collective-permute-start.19 = (bf16[128,1536]{1,0:T(8,128)(2,1)S(1)}, bf16[128,1536]{1,0:T(8,128)(2,1)S(1)}, u32[]{:S(2)}, u32[]{:S(2)}) collective-permute-start(bf16[128,1536]{1,0:T(8,128)(2,1)S(1)} %multiply_convert_fusion.10), channel_id=1, source_target_pairs={{0,1},{1,2},{2,3},{3,0},{4,5},{5,6},{6,7},{7,4},{8,9},{9,10},{10,1... | collective-permute-start | bytes 1179656 | tf_op jit(solution)/shard_map/ppermute | solution.py:26
  165.2 46.6 %collective-permute-start.26 = (bf16[128,1536]{1,0:T(8,128)(2,1)}, bf16[128,1536]{1,0:T(8,128)(2,1)}, u32[]{:S(2)}, u32[]{:S(2)}) collective-permute-start(bf16[128,1536]{1,0:T(8,128)(2,1)} %bitcast_convert_fusion), channel_id=1, source_target_pairs={{0,2},{1,3},{2,0},{3,1},{4,6},{5,7},{6,4},{7,5},{8,10},{9,11},{10,... | collective-permute-start | bytes 1179656 | tf_op jit(solution)/shard_map/ppermute | solution.py:26
  168.0 43.8 %collective-permute-start.25 = (bf16[128,1536]{1,0:T(8,128)(2,1)}, bf16[128,1536]{1,0:T(8,128)(2,1)}, u32[]{:S(2)}, u32[]{:S(2)}) collective-permute-start(bf16[128,1536]{1,0:T(8,128)(2,1)} %bitcast_convert_fusion), channel_id=1, source_target_pairs={{0,1},{1,2},{2,3},{3,0},{4,5},{5,6},{6,7},{7,4},{8,9},{9,10},{10,1... | collective-permute-start | bytes 1179656 | tf_op jit(solution)/shard_map/ppermute | solution.py:26
  183.2 36.3 %all-to-all-start = ((bf16[4,192,1536]{2,1,0:T(8,128)(2,1)}), bf16[4,192,1536]{2,1,0:T(8,128)(2,1)}, u32[]{:S(2)}, u32[]{:S(2)}) async-start(bf16[4,192,1536]{2,1,0:T(8,128)(2,1)} %bitcast.295), calls=%async_computation | async-start | bytes 4718592 | tf_op jit(solution)/shard_map/all_to_all | solution.py:104
  230.3 36.9 %all-to-all-start.1 = ((bf16[4,192,1536]{2,1,0:T(8,128)(2,1)}), bf16[4,192,1536]{2,1,0:T(8,128)(2,1)}, u32[]{:S(2)}, u32[]{:S(2)}) async-start(bf16[4,192,1536]{2,1,0:T(8,128)(2,1)} %bitcast.293), calls=%async_computation.1 | async-start | bytes 4718592 | tf_op jit(solution)/shard_map/all_to_all | solution.py:104
  235.0 143.3 %all-gather.14.cloned.1.call-start = ((), (), s32[]{:S(2)}) async-start(), calls=%async_computation.19 | async-start | bytes 2654208 | tf_op jit(solution)/shard_map/all_gather | solution.py:819
  236.6 55.4 %collective-permute-start.24 = (bf16[64,1536]{1,0:T(8,128)(2,1)}, bf16[64,1536]{1,0:T(8,128)(2,1)}, u32[]{:S(2)}, u32[]{:S(2)}) collective-permute-start(bf16[64,1536]{1,0:T(8,128)(2,1)} %get-tuple-element.621), channel_id=1, source_target_pairs={{0,4},{4,8},{8,12},{12,0},{1,5},{5,9},{9,13},{13,1},{2,6},{6,10},{... | collective-permute-start | bytes 589832 | tf_op jit(solution)/shard_map/ppermute | solution.py:26
  328.6 65.3 %all-to-all-start.3 = ((bf16[4,192,1536]{2,1,0:T(8,128)(2,1)}), bf16[4,192,1536]{2,1,0:T(8,128)(2,1)}, u32[]{:S(2)}, u32[]{:S(2)}) async-start(bf16[4,192,1536]{2,1,0:T(8,128)(2,1)} %bitcast.290), calls=%async_computation.3 | async-start | bytes 4718592 | tf_op jit(solution)/shard_map/all_to_all | solution.py:104
  335.3 52.1 %collective-permute-start.45 = (bf16[64,1536]{1,0:T(8,128)(2,1)}, bf16[64,1536]{1,0:T(8,128)(2,1)}, u32[]{:S(2)}, u32[]{:S(2)}) collective-permute-start(bf16[64,1536]{1,0:T(8,128)(2,1)} %get-tuple-element.612), channel_id=1, source_target_pairs={{0,12},{4,0},{8,4},{12,8},{1,13},{5,1},{9,5},{13,9},{2,14},{6,2},{... | collective-permute-start | bytes 589832 | tf_op jit(solution)/shard_map/ppermute | solution.py:26
  338.1 50.9 %collective-permute-start.44 = (bf16[64,1536]{1,0:T(8,128)(2,1)}, bf16[64,1536]{1,0:T(8,128)(2,1)}, u32[]{:S(2)}, u32[]{:S(2)}) collective-permute-start(bf16[64,1536]{1,0:T(8,128)(2,1)} %get-tuple-element.613), channel_id=1, source_target_pairs={{0,8},{4,12},{8,0},{12,4},{1,9},{5,13},{9,1},{13,5},{2,10},{6,14},... | collective-permute-start | bytes 589832 | tf_op jit(solution)/shard_map/ppermute | solution.py:26
  341.2 47.8 %collective-permute-start.43 = (bf16[64,1536]{1,0:T(8,128)(2,1)}, bf16[64,1536]{1,0:T(8,128)(2,1)}, u32[]{:S(2)}, u32[]{:S(2)}) collective-permute-start(bf16[64,1536]{1,0:T(8,128)(2,1)} %get-tuple-element.614), channel_id=1, source_target_pairs={{0,4},{4,8},{8,12},{12,0},{1,5},{5,9},{9,13},{13,1},{2,6},{6,10},{... | collective-permute-start | bytes 589832 | tf_op jit(solution)/shard_map/ppermute | solution.py:26
  478.6 78.7 %collective-permute-start.48 = (bf16[64,1536]{1,0:T(8,128)(2,1)}, bf16[64,1536]{1,0:T(8,128)(2,1)}, u32[]{:S(2)}, u32[]{:S(2)}) collective-permute-start(bf16[64,1536]{1,0:T(8,128)(2,1)} %get-tuple-element.608), channel_id=1, source_target_pairs={{0,4},{4,8},{8,12},{12,0},{1,5},{5,9},{9,13},{13,1},{2,6},{6,10},{... | collective-permute-start | bytes 589832 | tf_op jit(solution)/shard_map/ppermute | solution.py:26
  585.0 378.7 %reduce-scatter.8.cloned.1.call-start = ((), (), s32[]{:S(2)}) async-start(), calls=%async_computation.20 | async-start | bytes 1966080 | tf_op jit(solution)/shard_map/reduce_scatter | solution.py:1025
  624.7 343.9 %reduce-scatter.12.cloned.1.call-start = ((), (), s32[]{:S(2)}) async-start(), calls=%async_computation.22 | async-start | bytes 491520 | tf_op jit(solution)/shard_map/reduce_scatter | solution.py:991
  641.9 326.7 %reduce-scatter.10.cloned.1.call-start = ((), (), s32[]{:S(2)}) async-start(), calls=%async_computation.21 | async-start | bytes 983040 | tf_op jit(solution)/shard_map/reduce_scatter | solution.py:991
  656.3 47.9 %collective-permute-start.58 = (bf16[128,1664]{1,0:T(8,128)(2,1)}, bf16[128,1664]{1,0:T(8,128)(2,1)S(1)}, u32[]{:S(2)}, u32[]{:S(2)}) collective-permute-start(bf16[128,1664]{1,0:T(8,128)(2,1)} %pad_maximum_fusion.17), channel_id=1, source_target_pairs={{0,2},{1,3},{2,0},{3,1},{4,6},{5,7},{6,4},{7,5},{8,10},{9,11},{10,... | collective-permute-start | bytes 1277960 | tf_op jit(solution)/shard_map/ppermute | solution.py:26
  656.3 47.9 %collective-permute-start.57 = (bf16[128,1664]{1,0:T(8,128)(2,1)}, bf16[128,1664]{1,0:T(8,128)(2,1)S(1)}, u32[]{:S(2)}, u32[]{:S(2)}) collective-permute-start(bf16[128,1664]{1,0:T(8,128)(2,1)} %pad_maximum_fusion.17), channel_id=1, source_target_pairs={{0,1},{1,2},{2,3},{3,0},{4,5},{5,6},{6,7},{7,4},{8,9},{9,10},{10,1... | collective-permute-start | bytes 1277960 | tf_op jit(solution)/shard_map/ppermute | solution.py:26
  823.5 145.2 %reduce-scatter.14.cloned.1.call-start = ((), (), s32[]{:S(2)}) async-start(), calls=%async_computation.23 | async-start | bytes 1474560 | tf_op jit(solution)/shard_map/reduce_scatter | solution.py:991
  832.0 91.3 %collective-permute-start.71 = (bf16[64,1536]{1,0:T(8,128)(2,1)}, bf16[64,1536]{1,0:T(8,128)(2,1)}, u32[]{:S(2)}, u32[]{:S(2)}) collective-permute-start(bf16[64,1536]{1,0:T(8,128)(2,1)} %get-tuple-element.589), channel_id=1, source_target_pairs={{0,4},{4,8},{8,12},{12,0},{1,5},{5,9},{9,13},{13,1},{2,6},{6,10},{... | collective-permute-start | bytes 589832 | tf_op jit(solution)/shard_map/ppermute | solution.py:26
  861.4 136.9 %reduce-scatter.16.cloned.1.call-start = ((), (), s32[]{:S(2)}) async-start(), calls=%async_computation.24 | async-start | bytes 2949120 | tf_op jit(solution)/shard_map/reduce_scatter | solution.py:991
  885.7 259.1 %reduce-scatter.20.cloned.1.call-start = ((), (), s32[]{:S(2)}) async-start(), calls=%async_computation.26 | async-start | bytes 491520 | tf_op jit(solution)/shard_map/reduce_scatter | solution.py:991
  960.4 37.9 %collective-permute-start.80 = (bf16[128,1664]{1,0:T(8,128)(2,1)}, bf16[128,1664]{1,0:T(8,128)(2,1)}, u32[]{:S(2)}, u32[]{:S(2)}) collective-permute-start(bf16[128,1664]{1,0:T(8,128)(2,1)} %pad_maximum_fusion.18), channel_id=1, source_target_pairs={{0,2},{1,3},{2,0},{3,1},{4,6},{5,7},{6,4},{7,5},{8,10},{9,11},{10,... | collective-permute-start | bytes 1277960 | tf_op jit(solution)/shard_map/ppermute | solution.py:26
  960.9 37.4 %collective-permute-start.79 = (bf16[128,1664]{1,0:T(8,128)(2,1)}, bf16[128,1664]{1,0:T(8,128)(2,1)}, u32[]{:S(2)}, u32[]{:S(2)}) collective-permute-start(bf16[128,1664]{1,0:T(8,128)(2,1)} %pad_maximum_fusion.18), channel_id=1, source_target_pairs={{0,1},{1,2},{2,3},{3,0},{4,5},{5,6},{6,7},{7,4},{8,9},{9,10},{10,1... | collective-permute-start | bytes 1277960 | tf_op jit(solution)/shard_map/ppermute | solution.py:26
  963.5 181.4 %reduce-scatter.18.cloned.1.call-start = ((), (), s32[]{:S(2)}) async-start(), calls=%async_computation.25 | async-start | bytes 983040 | tf_op jit(solution)/shard_map/reduce_scatter | solution.py:991
  1088.6 35.1 %collective-permute-start.101 = (bf16[128,1536]{1,0:T(8,128)(2,1)S(1)}, bf16[128,1536]{1,0:T(8,128)(2,1)S(1)}, u32[]{:S(2)}, u32[]{:S(2)}) collective-permute-start(bf16[128,1536]{1,0:T(8,128)(2,1)S(1)} %get-tuple-element.551), channel_id=1, source_target_pairs={{0,3},{1,0},{2,1},{3,2},{4,7},{5,4},{6,5},{7,6},{8,11},{9,8},{10,9... | collective-permute-start | bytes 1179656 | tf_op jit(solution)/shard_map/ppermute | solution.py:26
  (398 other events, 4667.8 us)
Sparse Core Ops, SparseCore 0:
  14.0 48.1 all-gather.5
  64.6 28.9 all-gather.7
  95.5 38.9 all-gather.9
  136.8 65.0 all-gather.11
  237.4 53.0 all-gather.13
  624.8 54.5 reduce-scatter.7
  682.2 35.3 reduce-scatter.11
  720.4 26.1 reduce-scatter.9
  861.5 28.0 reduce-scatter.13
  892.5 57.5 reduce-scatter.15
  963.6 24.3 reduce-scatter.19
  990.8 26.0 reduce-scatter.17

commit v11 on v10

--- a/solution.py
+++ b/solution.py
@@ -999,16 +999,14 @@
     if groups() > 1:
         own_rows, others = sent_back(answers[0])
         answers_back = [jnp.concatenate([own_rows, *others], axis=0), *answers_back]
-    shared_made_1 = [half_to_keep(*made) for made in shared_grads_1]
     grad_pre, to_proj, to_out, tail, rest_1 = mixer_back(
         1,
         grad_middle,
         along,
         rr_1,
         (wide_in_1, pre_1, y_1, scaled_1),
-        shared_made_1,
-    )
-    shared_sent_1 = [row_sums(each) for each in shared_made_1]
+        answers_back,
+    )
     whole = line_product(grad_pre, proj[1])
     grad_in = gathered_sum(whole)
     grad_1, grad_norm_in_1 = resid_back(out_0, norm_ins[1], grad_in, grad_middle)
@@ -1017,7 +1015,7 @@
         home = home_part(after(kept.shared_1[2], tokens_all), shared[1])
         home = [
             (outer(scaling[1][index], answer) + chunk_of(home, index)).astype(HALF)
-            for index, answer in enumerate(answers_back)
+            for index, answer in enumerate(after(answers_back, tokens_all))
         ]
         home = joined(home)
         if groups() > 1:
@@ -1025,9 +1023,9 @@
         kept.home = lax.psum_scatter(home, "col", scatter_dimension=0, tiled=True)
         own_proj, own_out, own_tail = after((to_proj, to_out, tail), home)
         given, given_out = half_to_give(*own_proj), half_to_give(*own_out)
-        made = ((*own_out, swapped(given_out)), (*own_proj, swapped(given)))
+        made = (*shared_grads_1, (*own_out, swapped(given_out)), (*own_proj, swapped(given)))
         made = [half_to_keep(*each) for each in after(made, (given, given_out))]
-        kept.sent_1 = [*shared_sent_1, *[row_sums(each) for each in made]]
+        kept.sent_1 = [row_sums(each) for each in made]
         kept.tail_1 = outer(own_proj[0], own_tail).astype(HALF)
         return made, kept.tail_1
 
@@ -1095,22 +1093,24 @@
     tail_received = row_received(tail_pieces)
     proj_half = half_to_keep(*after((*to_proj, swapped(given)), whole))
     given_out = half_to_give(*after(to_out, proj_half))
-    tail_received, lines = after((tail_received, lines), (proj_half, given_out))
+    line_received = sent_home(after(whole, proj_half))
+    proj_pieces = row_pieces(proj_half)
+    proj_received = row_received(proj_pieces)
+    out_half = half_to_keep(*to_out, swapped(given_out))
+    out_pieces = row_pieces(out_half)
+    out_received = row_received(out_pieces)
+    tail_received, lines, line_received, proj_received, out_received = after(
+        (tail_received, lines, line_received, proj_received, out_received)
+    )
     tail = total_of(tail_pieces[0], tail_received).astype(HALF)
     vector = jnp.sum(in_order(lines, "row"), axis=0)
     common = 2 * width + conv_state.shape[1] * state
     state_grad = tail[:, :state]
-    line_received = sent_home(after(whole, proj_half))
-    proj_pieces = row_pieces(after(proj_half, tail))
-    proj_received = row_received(proj_pieces)
-    out_half = half_to_keep(*after((*to_out, swapped(given_out)), tail))
-    out_pieces = row_pieces(out_half)
-    out_received = row_received(out_pieces)
     if groups() > 1:
         state_pieces = row_pieces(state_grad, "col")
         state_received = row_received(state_pieces, "col")
         lines = [shifted(vector[None, :common], "col", back) for back in range(n_col)]
-        state_received, lines = after((state_received, lines), out_half)
+        state_received, lines = after((state_received, lines))
         shared_sum = jnp.sum(in_order(lines, "col"), axis=0)
         state_grad = total_of(state_pieces[0], state_received).astype(HALF)
         state_lines = [shifted(state_grad, "col", back) for back in range(n_col)]
@@ -1118,11 +1118,8 @@
         state_grad = lax.psum(state_grad, "col")
         state_lines = [state_grad]
         shared_sum = lax.psum(vector[:common], "col")
-    expert_out = [keep + other.astype(FLOAT) for keep, other in after(expert_out, out_half)]
-    state_lines, line_received, proj_received, out_received = after(
-        (state_lines, line_received, proj_received, out_received), expert_out
-    )
-    state_grad = in_order(state_lines, "col")
+    expert_out = [keep + other.astype(FLOAT) for keep, other in after(expert_out, tail)]
+    state_grad = in_order(after(state_lines, expert_out), "col")
     grad_in = added_up(whole, line_received)
     sums_0.append(total_of(out_pieces[0], out_received).astype(HALF))
     sums_0.append(total_of(proj_pieces[0], proj_received).astype(HALF))

time: 1180 us -> 1210 us (1.025)
  waiting for transfers between devices: 455 us -> 472 us
    ppermute x93, waiting for transfers between devices: 364 us -> 385 us  [shifted(): lax.ppermute(block, axis, [(i, (i + distance) % count) for i in range(cou...]
    all_to_all x8, waiting for transfers between devices: 81.9 us -> 66.5 us  [exchanged(): return lax.all_to_all(rows, axis, split_axis=0, concat_axis=0, tiled=True)]
    unnamed x622 -> x600, local copies, waits for them, and re-layouts: 39.5 us -> 44.8 us
  transfers between devices with their start and end apart: 139 -> 139, of which waited for: 52 -> 53; matrix products, arithmetic and copies ran while one was open for 31% -> 28% of each run, Pallas kernels for 5% -> 3%
where the time goes in v11:
time: 1210 us; the launch traced here: 1200 us
  waiting for transfers between devices  472 us (39%)
  starting transfers between devices  241 us (20%)
  matrix products  236 us (20%)
  other arithmetic  89.9 us (7%)
  local copies, waits for them, and re-layouts  86 us (7%)
  Pallas kernels  59.2 us (5%)
  between operations  18.4 us (2%)
    ppermute x93, waiting for transfers between devices, shifted(): lax.ppermute(block, axis, [(i, (i + distance) % count) for i in range(cou...  385 us
    ppermute x93, starting transfers between devices, shifted(): lax.ppermute(block, axis, [(i, (i + distance) % count) for i in range(cou...  197 us
    dot_general x32, matrix products, outer(): lax.dot_general(left, right, (((0,), (0,)), ((), ())), preferred_element_...  94 us
    dot_general x36, matrix products, project(): return jnp.dot(left, right, preferred_element_type=FLOAT)  77.1 us
    all_to_all x8, waiting for transfers between devices, exchanged(): return lax.all_to_all(rows, axis, split_axis=0, concat_axis=0, tiled=True)  66.5 us
    dot_general x26, matrix products, project_back(): lax.dot_general(left, right, (((1,), (1,)), ((), ())), preferred_element_...  64.9 us
    unnamed x600, local copies, waits for them, and re-layouts  44.8 us
    all_to_all x8, starting transfers between devices, exchanged(): return lax.all_to_all(rows, axis, split_axis=0, concat_axis=0, tiled=True)  36.8 us
  transfers between devices with their start and end apart: 139, of which 53 were waited for; matrix products, arithmetic and copies ran while one was open for 28% of the time, Pallas kernels for 3%

profile of v11, /device:TPU:0, one launch (start us, length us, event | category | flops | bytes accessed | tf_op | source)
XLA Modules:
  0.0 1202.6 jit_solution(13172181038703353896)
XLA Ops:
  40.3 17.4 %collective-permute-done.1 = bf16[128,1536]{1,0:T(8,128)(2,1)S(1)} collective-permute-done((bf16[128,1536]{1,0:T(8,128)(2,1)S(1)}, bf16[128,1536]{1,0:T(8,128)(2,1)S(1)}, u32[]{:S(2)}, u32[]{:S(2)}) %collective-permute-start.1) | collective-permute-done | bytes 393248 | tf_op jit(solution)/shard_map/ppermute | solution.py:26
  69.7 12.6 %mixer_forward.2 = (f32[512,768]{1,0:T(8,128)S(1)}, bf16[512,768]{1,0:T(8,128)(2,1)S(1)}, f32[512,1]{1,0:T(8,128)S(1)}) custom-call(f32[512,1024]{1,0:T(8,128)S(1)} %fusion.33.pre_in_ref, f32[512,1024]{1,0:T(8,128)} %fusion.30.pre_other_in_ref, f32[4,768]{1,0:T(4,128)S(1)} %reshape.470.conv_input_ref, f32[4,256]{1,0:T(4,128)S(1)} %slice.595.conv_state_ref, ...), custom_call_target="tpu_custom_call" | custom-call | tf_op jit(solution)/shard_map/mixer_forward/pallas_call | solution.py:541
  105.6 7.9 collective-permute-done.11
  121.3 18.8 %collective-permute-done.10 = bf16[128,1664]{1,0:T(8,128)(2,1)S(1)} collective-permute-done((bf16[128,1664]{1,0:T(8,128)(2,1)S(1)}, bf16[128,1664]{1,0:T(8,128)(2,1)S(1)}, u32[]{:S(2)}, u32[]{:S(2)}) %collective-permute-start.10) | collective-permute-done | bytes 426016 | tf_op jit(solution)/shard_map/ppermute | solution.py:26
  168.7 10.4 collective-permute-done.20
  186.8 23.6 %collective-permute-done.26 = bf16[128,1536]{1,0:T(8,128)(2,1)} collective-permute-done((bf16[128,1536]{1,0:T(8,128)(2,1)S(1)}, bf16[128,1536]{1,0:T(8,128)(2,1)}, u32[]{:S(2)}, u32[]{:S(2)}) %collective-permute-start.26) | collective-permute-done | bytes 393248 | tf_op jit(solution)/shard_map/ppermute | solution.py:26
  246.6 19.0 %all-to-all-done.1 = bf16[4,192,1536]{2,1,0:T(8,128)(2,1)} async-done(((bf16[4,192,1536]{2,1,0:T(8,128)(2,1)}), bf16[4,192,1536]{2,1,0:T(8,128)(2,1)}, u32[]{:S(2)}, u32[]{:S(2)}) %all-to-all-start.1) | async-done | bytes 2359328 | tf_op jit(solution)/shard_map/all_to_all | solution.py:104
  269.3 12.9 %collective-permute-start.30 = (bf16[128,1536]{1,0:T(8,128)(2,1)S(1)}, bf16[128,1536]{1,0:T(8,128)(2,1)S(1)}, u32[]{:S(2)}, u32[]{:S(2)}) collective-permute-start(bf16[128,1536]{1,0:T(8,128)(2,1)S(1)} %get-tuple-element.581), channel_id=1, source_target_pairs={{0,1},{1,2},{2,3},{3,0},{4,5},{5,6},{6,7},{7,4},{8,9},{9,10},{10,1... | collective-permute-start | bytes 1179656 | tf_op jit(solution)/shard_map/ppermute | solution.py:26
  308.0 14.5 %collective-permute-start.33 = (bf16[128,1536]{1,0:T(8,128)(2,1)S(1)}, bf16[128,1536]{1,0:T(8,128)(2,1)}, u32[]{:S(2)}, u32[]{:S(2)}) collective-permute-start(bf16[128,1536]{1,0:T(8,128)(2,1)S(1)} %multiply_convert_fusion.9), channel_id=1, source_target_pairs={{0,3},{1,0},{2,1},{3,2},{4,7},{5,4},{6,5},{7,6},{8,11},{9,8},{10,9... | collective-permute-start | bytes 1179656 | tf_op jit(solution)/shard_map/ppermute | solution.py:26
  338.4 13.2 %collective-permute-done.32 = bf16[128,1536]{1,0:T(8,128)(2,1)} collective-permute-done((bf16[128,1536]{1,0:T(8,128)(2,1)S(1)}, bf16[128,1536]{1,0:T(8,128)(2,1)}, u32[]{:S(2)}, u32[]{:S(2)}) %collective-permute-start.32) | collective-permute-done | bytes 393248 | tf_op jit(solution)/shard_map/ppermute | solution.py:26
  361.1 11.6 mixer_forward.3
  400.4 16.0 %collective-permute-done.35 = bf16[128,1664]{1,0:T(8,128)(2,1)} collective-permute-done((bf16[128,1664]{1,0:T(8,128)(2,1)}, bf16[128,1664]{1,0:T(8,128)(2,1)}, u32[]{:S(2)}, u32[]{:S(2)}) %collective-permute-start.35) | collective-permute-done | bytes 426016 | tf_op jit(solution)/shard_map/ppermute | solution.py:26
  439.0 20.9 %collective-permute-done.41 = bf16[128,1536]{1,0:T(8,128)(2,1)S(1)} collective-permute-done((bf16[128,1536]{1,0:T(8,128)(2,1)S(1)}, bf16[128,1536]{1,0:T(8,128)(2,1)S(1)}, u32[]{:S(2)}, u32[]{:S(2)}) %collective-permute-start.41) | collective-permute-done | bytes 393248 | tf_op jit(solution)/shard_map/ppermute | solution.py:26
  476.8 17.7 %all-to-all-done.2 = bf16[4,192,1536]{2,1,0:T(8,128)(2,1)} async-done(((bf16[4,192,1536]{2,1,0:T(8,128)(2,1)}), bf16[4,192,1536]{2,1,0:T(8,128)(2,1)}, u32[]{:S(2)}, u32[]{:S(2)}) %all-to-all-start.2) | async-done | bytes 2359328 | tf_op jit(solution)/shard_map/all_to_all | solution.py:104
  558.7 12.8 %collective-permute-done.52 = bf16[128,1536]{1,0:T(8,128)(2,1)S(1)} collective-permute-done((bf16[128,1536]{1,0:T(8,128)(2,1)S(1)}, bf16[128,1536]{1,0:T(8,128)(2,1)S(1)}, u32[]{:S(2)}, u32[]{:S(2)}) %collective-permute-start.52) | collective-permute-done | bytes 393248 | tf_op jit(solution)/shard_map/ppermute | solution.py:26
  587.7 12.4 %collective-permute-start.59 = (bf16[128,1664]{1,0:T(8,128)(2,1)S(1)}, bf16[128,1664]{1,0:T(8,128)(2,1)S(1)}, u32[]{:S(2)}, u32[]{:S(2)}) collective-permute-start(bf16[128,1664]{1,0:T(8,128)(2,1)S(1)} %pad_maximum_fusion.18), channel_id=1, source_target_pairs={{0,3},{1,0},{2,1},{3,2},{4,7},{5,4},{6,5},{7,6},{8,11},{9,8},{10,9... | collective-permute-start | bytes 1277960 | tf_op jit(solution)/shard_map/ppermute | solution.py:26
  600.1 13.9 %collective-permute-done.56 = bf16[64,1536]{1,0:T(8,128)(2,1)S(1)} collective-permute-done((bf16[64,1536]{1,0:T(8,128)(2,1)S(1)}, bf16[64,1536]{1,0:T(8,128)(2,1)S(1)}, u32[]{:S(2)}, u32[]{:S(2)}) %collective-permute-start.56) | collective-permute-done | bytes 196640 | tf_op jit(solution)/shard_map/ppermute | solution.py:26
  614.0 9.7 collective-permute-start.57
  625.6 9.2 collective-permute-done.57
  641.6 17.5 %mixer_backward.2 = (bf16[512,1024]{1,0:T(8,128)(2,1)S(1)}, bf16[512,1024]{1,0:T(8,128)(2,1)S(1)}, f32[2,768]{1,0:T(2,128)S(1)}, f32[4,768]{1,0:T(4,128)S(1)}, f...) custom-call(f32[512,1024]{1,0:T(8,128)} %copy-done.3, f32[512,1024]{1,0:T(8,128)} %fusion.22.pre_other_in_ref, ...), custom_call_target="tpu_custom_call" | custom-call | tf_op jit(solution)/shard_map/mixer_backward/pallas_call | solution.py:566
  679.8 15.6 %collective-permute-done.61 = bf16[128,1536]{1,0:T(8,128)(2,1)} collective-permute-done((bf16[128,1536]{1,0:T(8,128)(2,1)}, bf16[128,1536]{1,0:T(8,128)(2,1)}, u32[]{:S(2)}, u32[]{:S(2)}) %collective-permute-start.61) | collective-permute-done | bytes 393248 | tf_op jit(solution)/shard_map/ppermute | solution.py:26
  701.8 9.8 collective-permute-start.65
  722.7 23.5 %collective-permute-done.64 = bf16[128,1536]{1,0:T(8,128)(2,1)S(1)} collective-permute-done((bf16[128,1536]{1,0:T(8,128)(2,1)S(1)}, bf16[128,1536]{1,0:T(8,128)(2,1)S(1)}, u32[]{:S(2)}, u32[]{:S(2)}) %collective-permute-start.64) | collective-permute-done | bytes 393248 | tf_op jit(solution)/shard_map/ppermute | solution.py:26
  800.0 13.0 %all-to-all-done.6 = bf16[4,192,1536]{2,1,0:T(8,128)(2,1)} async-done(((bf16[4,192,1536]{2,1,0:T(8,128)(2,1)}), bf16[4,192,1536]{2,1,0:T(8,128)(2,1)}, u32[]{:S(2)}, u32[]{:S(2)}) %all-to-all-start.6) | async-done | bytes 2359328 | tf_op jit(solution)/shard_map/all_to_all | solution.py:104
  864.0 14.9 %all-to-all-done.7 = bf16[4,192,1536]{2,1,0:T(8,128)(2,1)} async-done(((bf16[4,192,1536]{2,1,0:T(8,128)(2,1)}), bf16[4,192,1536]{2,1,0:T(8,128)(2,1)}, u32[]{:S(2)}, u32[]{:S(2)}) %all-to-all-start.7) | async-done | bytes 2359328 | tf_op jit(solution)/shard_map/all_to_all | solution.py:104
  896.7 14.9 %collective-permute-done.77 = bf16[128,1536]{1,0:T(8,128)(2,1)} collective-permute-done((bf16[128,1536]{1,0:T(8,128)(2,1)S(1)}, bf16[128,1536]{1,0:T(8,128)(2,1)}, u32[]{:S(2)}, u32[]{:S(2)}) %collective-permute-start.77) | collective-permute-done | bytes 393248 | tf_op jit(solution)/shard_map/ppermute | solution.py:26
  933.9 53.1 %collective-permute-done.80 = bf16[128,1664]{1,0:T(8,128)(2,1)S(1)} collective-permute-done((bf16[128,1664]{1,0:T(8,128)(2,1)}, bf16[128,1664]{1,0:T(8,128)(2,1)S(1)}, u32[]{:S(2)}, u32[]{:S(2)}) %collective-permute-start.80) | collective-permute-done | bytes 426016 | tf_op jit(solution)/shard_map/ppermute | solution.py:26
  992.4 17.5 %mixer_backward.3 = (bf16[512,1024]{1,0:T(8,128)(2,1)S(1)}, bf16[512,1024]{1,0:T(8,128)(2,1)S(1)}, f32[2,768]{1,0:T(2,128)S(1)}, f32[4,768]{1,0:T(4,128)S(1)}, f...) custom-call(f32[512,1024]{1,0:T(8,128)} %copy-done.2, f32[512,1024]{1,0:T(8,128)} %fusion.30.pre_other_in_ref, ...), custom_call_target="tpu_custom_call" | custom-call | tf_op jit(solution)/shard_map/mixer_backward/pallas_call | solution.py:566
  1046.0 9.1 collective-permute-done.84
  1061.4 13.8 %collective-permute-done.92 = bf16[128,1536]{1,0:T(8,128)(2,1)} collective-permute-done((bf16[128,1536]{1,0:T(8,128)(2,1)}, bf16[128,1536]{1,0:T(8,128)(2,1)}, u32[]{:S(2)}, u32[]{:S(2)}) %collective-permute-start.92) | collective-permute-done | bytes 393248 | tf_op jit(solution)/shard_map/ppermute | solution.py:26
  1082.6 13.0 %collective-permute-done.94 = bf16[384,768]{1,0:T(8,128)(2,1)} collective-permute-done((bf16[384,768]{1,0:T(8,128)(2,1)}, bf16[384,768]{1,0:T(8,128)(2,1)}, u32[]{:S(2)}, u32[]{:S(2)}) %collective-permute-start.94) | collective-permute-done | bytes 589856 | tf_op jit(solution)/shard_map/ppermute | solution.py:26
  1129.4 8.3 reduce-scatter.18.cloned.1.call-done
  (1179 shorter events, 685.5 us)
Async XLA Ops:
  7.2 54.9 %all-gather.6.cloned.1.call-start = ((), (), s32[]{:S(2)}) async-start(), calls=%async_computation.15 | async-start | bytes 7077888 | tf_op jit(solution)/shard_map/all_gather | solution.py:819
  13.8 79.8 %all-gather.8.cloned.1.call-start = ((), (), s32[]{:S(2)}) async-start(), calls=%async_computation.16 | async-start | bytes 2654208 | tf_op jit(solution)/shard_map/all_gather | solution.py:819
  16.6 221.5 %all-gather.10.cloned.1.call-start = ((), (), s32[]{:S(2)}) async-start(), calls=%async_computation.17 | async-start | bytes 5308416 | tf_op jit(solution)/shard_map/all_gather | solution.py:823
  17.6 334.1 %all-gather.12.cloned.1.call-start = ((), (), s32[]{:S(2)}) async-start(), calls=%async_computation.18 | async-start | bytes 7077888 | tf_op jit(solution)/shard_map/all_gather | solution.py:819
  33.2 50.3 %collective-permute-start.12 = (f32[128,12]{0,1:T(8,128)S(1)}, f32[128,12]{0,1:T(8,128)S(1)}, u32[]{:S(2)}, u32[]{:S(2)}) collective-permute-start(f32[128,12]{0,1:T(8,128)S(1)} %fusion.269), channel_id=1, source_target_pairs={{0,16},{16,0},{1,17},{17,1},{2,18},{18,2},{3,19},{19,3},{4,20},{20... | collective-permute-start | bytes 18440 | tf_op jit(solution)/shard_map/ppermute | solution.py:30
  164.9 45.5 %collective-permute-start.26 = (bf16[128,1536]{1,0:T(8,128)(2,1)S(1)}, bf16[128,1536]{1,0:T(8,128)(2,1)}, u32[]{:S(2)}, u32[]{:S(2)}) collective-permute-start(bf16[128,1536]{1,0:T(8,128)(2,1)S(1)} %copy-done.98), channel_id=1, source_target_pairs={{0,2},{1,3},{2,0},{3,1},{4,6},{5,7},{6,4},{7,5},{8,10},{9,11},{10,... | collective-permute-start | bytes 1179656 | tf_op jit(solution)/shard_map/ppermute | solution.py:26
  167.3 43.1 %collective-permute-start.25 = (bf16[128,1536]{1,0:T(8,128)(2,1)S(1)}, bf16[128,1536]{1,0:T(8,128)(2,1)}, u32[]{:S(2)}, u32[]{:S(2)}) collective-permute-start(bf16[128,1536]{1,0:T(8,128)(2,1)S(1)} %copy-done.98), channel_id=1, source_target_pairs={{0,1},{1,2},{2,3},{3,0},{4,5},{5,6},{6,7},{7,4},{8,9},{9,10},{10,1... | collective-permute-start | bytes 1179656 | tf_op jit(solution)/shard_map/ppermute | solution.py:26
  233.4 140.7 %all-gather.14.cloned.1.call-start = ((), (), s32[]{:S(2)}) async-start(), calls=%async_computation.19 | async-start | bytes 2654208 | tf_op jit(solution)/shard_map/all_gather | solution.py:819
  234.8 54.2 %collective-permute-start.24 = (bf16[64,1536]{1,0:T(8,128)(2,1)}, bf16[64,1536]{1,0:T(8,128)(2,1)}, u32[]{:S(2)}, u32[]{:S(2)}) collective-permute-start(bf16[64,1536]{1,0:T(8,128)(2,1)} %get-tuple-element.635), channel_id=1, source_target_pairs={{0,4},{4,8},{8,12},{12,0},{1,5},{5,9},{9,13},{13,1},{2,6},{6,10},{... | collective-permute-start | bytes 589832 | tf_op jit(solution)/shard_map/ppermute | solution.py:26
  325.9 63.6 %all-to-all-start.3 = ((bf16[4,192,1536]{2,1,0:T(8,128)(2,1)}), bf16[4,192,1536]{2,1,0:T(8,128)(2,1)}, u32[]{:S(2)}, u32[]{:S(2)}) async-start(bf16[4,192,1536]{2,1,0:T(8,128)(2,1)} %bitcast.293), calls=%async_computation.3 | async-start | bytes 4718592 | tf_op jit(solution)/shard_map/all_to_all | solution.py:104
  331.8 51.2 %collective-permute-start.45 = (bf16[64,1536]{1,0:T(8,128)(2,1)}, bf16[64,1536]{1,0:T(8,128)(2,1)}, u32[]{:S(2)}, u32[]{:S(2)}) collective-permute-start(bf16[64,1536]{1,0:T(8,128)(2,1)} %get-tuple-element.626), channel_id=1, source_target_pairs={{0,12},{4,0},{8,4},{12,8},{1,13},{5,1},{9,5},{13,9},{2,14},{6,2},{... | collective-permute-start | bytes 589832 | tf_op jit(solution)/shard_map/ppermute | solution.py:26
  334.6 50.0 %collective-permute-start.44 = (bf16[64,1536]{1,0:T(8,128)(2,1)}, bf16[64,1536]{1,0:T(8,128)(2,1)}, u32[]{:S(2)}, u32[]{:S(2)}) collective-permute-start(bf16[64,1536]{1,0:T(8,128)(2,1)} %get-tuple-element.627), channel_id=1, source_target_pairs={{0,8},{4,12},{8,0},{12,4},{1,9},{5,13},{9,1},{13,5},{2,10},{6,14},... | collective-permute-start | bytes 589832 | tf_op jit(solution)/shard_map/ppermute | solution.py:26
  337.7 47.0 %collective-permute-start.43 = (bf16[64,1536]{1,0:T(8,128)(2,1)}, bf16[64,1536]{1,0:T(8,128)(2,1)}, u32[]{:S(2)}, u32[]{:S(2)}) collective-permute-start(bf16[64,1536]{1,0:T(8,128)(2,1)} %get-tuple-element.628), channel_id=1, source_target_pairs={{0,4},{4,8},{8,12},{12,0},{1,5},{5,9},{9,13},{13,1},{2,6},{6,10},{... | collective-permute-start | bytes 589832 | tf_op jit(solution)/shard_map/ppermute | solution.py:26
  473.6 79.0 %collective-permute-start.48 = (bf16[64,1536]{1,0:T(8,128)(2,1)}, bf16[64,1536]{1,0:T(8,128)(2,1)}, u32[]{:S(2)}, u32[]{:S(2)}) collective-permute-start(bf16[64,1536]{1,0:T(8,128)(2,1)} %get-tuple-element.622), channel_id=1, source_target_pairs={{0,4},{4,8},{8,12},{12,0},{1,5},{5,9},{9,13},{13,1},{2,6},{6,10},{... | collective-permute-start | bytes 589832 | tf_op jit(solution)/shard_map/ppermute | solution.py:26
  575.2 59.6 %all-to-all-start.5 = ((bf16[4,192,1536]{2,1,0:T(8,128)(2,1)}), bf16[4,192,1536]{2,1,0:T(8,128)(2,1)}, u32[]{:S(2)}, u32[]{:S(2)}) async-start(bf16[4,192,1536]{2,1,0:T(8,128)(2,1)} %bitcast.292), calls=%async_computation.5 | async-start | bytes 4718592 | tf_op jit(solution)/shard_map/all_to_all | solution.py:104
  579.9 352.4 %reduce-scatter.12.cloned.1.call-start = ((), (), s32[]{:S(2)}) async-start(), calls=%async_computation.22 | async-start | bytes 491520 | tf_op jit(solution)/shard_map/reduce_scatter | solution.py:991
  782.0 150.3 %reduce-scatter.10.cloned.1.call-start = ((), (), s32[]{:S(2)}) async-start(), calls=%async_computation.21 | async-start | bytes 983040 | tf_op jit(solution)/shard_map/reduce_scatter | solution.py:991
  785.4 146.9 %reduce-scatter.14.cloned.1.call-start = ((), (), s32[]{:S(2)}) async-start(), calls=%async_computation.23 | async-start | bytes 1474560 | tf_op jit(solution)/shard_map/reduce_scatter | solution.py:991
  790.9 98.9 %collective-permute-start.71 = (bf16[64,1536]{1,0:T(8,128)(2,1)}, bf16[64,1536]{1,0:T(8,128)(2,1)}, u32[]{:S(2)}, u32[]{:S(2)}) collective-permute-start(bf16[64,1536]{1,0:T(8,128)(2,1)} %get-tuple-element.603), channel_id=1, source_target_pairs={{0,4},{4,8},{8,12},{12,0},{1,5},{5,9},{9,13},{13,1},{2,6},{6,10},{... | collective-permute-start | bytes 589832 | tf_op jit(solution)/shard_map/ppermute | solution.py:26
  796.2 190.8 %reduce-scatter.16.cloned.1.call-start = ((), (), s32[]{:S(2)}) async-start(), calls=%async_computation.24 | async-start | bytes 2949120 | tf_op jit(solution)/shard_map/reduce_scatter | solution.py:991
  845.3 258.0 %reduce-scatter.8.cloned.1.call-start = ((), (), s32[]{:S(2)}) async-start(), calls=%async_computation.20 | async-start | bytes 1966080 | tf_op jit(solution)/shard_map/reduce_scatter | solution.py:1023
  892.5 236.9 %reduce-scatter.20.cloned.1.call-start = ((), (), s32[]{:S(2)}) async-start(), calls=%async_computation.26 | async-start | bytes 491520 | tf_op jit(solution)/shard_map/reduce_scatter | solution.py:991
  923.0 64.1 %collective-permute-start.80 = (bf16[128,1664]{1,0:T(8,128)(2,1)}, bf16[128,1664]{1,0:T(8,128)(2,1)S(1)}, u32[]{:S(2)}, u32[]{:S(2)}) collective-permute-start(bf16[128,1664]{1,0:T(8,128)(2,1)} %pad_maximum_fusion.19), channel_id=1, source_target_pairs={{0,2},{1,3},{2,0},{3,1},{4,6},{5,7},{6,4},{7,5},{8,10},{9,11},{10,... | collective-permute-start | bytes 1277960 | tf_op jit(solution)/shard_map/ppermute | solution.py:26
  926.0 61.0 %collective-permute-start.79 = (bf16[128,1664]{1,0:T(8,128)(2,1)}, bf16[128,1664]{1,0:T(8,128)(2,1)S(1)}, u32[]{:S(2)}, u32[]{:S(2)}) collective-permute-start(bf16[128,1664]{1,0:T(8,128)(2,1)} %pad_maximum_fusion.19), channel_id=1, source_target_pairs={{0,1},{1,2},{2,3},{3,0},{4,5},{5,6},{6,7},{7,4},{8,9},{9,10},{10,1... | collective-permute-start | bytes 1277960 | tf_op jit(solution)/shard_map/ppermute | solution.py:26
  1036.0 40.1 %collective-permute-start.97 = (bf16[1536,384]{1,0:T(8,128)(2,1)}, bf16[1536,384]{1,0:T(8,128)(2,1)}, u32[]{:S(2)}, u32[]{:S(2)}) collective-permute-start(bf16[1536,384]{1,0:T(8,128)(2,1)} %convolution_convert_fusion.13), channel_id=1, source_target_pairs={{0,16},{16,0},{1,17},{17,1},{2,18},{18,2},{3,19},{19,3},{4,20},{20... | collective-permute-start | bytes 3538952 | tf_op jit(solution)/shard_map/ppermute | solution.py:30
  1061.4 76.3 %reduce-scatter.18.cloned.1.call-start = ((), (), s32[]{:S(2)}) async-start(), calls=%async_computation.25 | async-start | bytes 983040 | tf_op jit(solution)/shard_map/reduce_scatter | solution.py:991
  1075.2 49.1 %collective-permute-start.114 = (bf16[1536,512]{1,0:T(8,128)(2,1)}, bf16[1536,512]{1,0:T(8,128)(2,1)}, u32[]{:S(2)}, u32[]{:S(2)}) collective-permute-start(bf16[1536,512]{1,0:T(8,128)(2,1)} %get-tuple-element.531), channel_id=1, source_target_pairs={{0,16},{16,0},{1,17},{17,1},{2,18},{18,2},{3,19},{19,3},{4,20},{20... | collective-permute-start | bytes 4718600 | tf_op jit(solution)/shard_map/ppermute | solution.py:30
  1075.6 49.1 %collective-permute-start.113 = (bf16[1536,512]{1,0:T(8,128)(2,1)}, bf16[1536,512]{1,0:T(8,128)(2,1)}, u32[]{:S(2)}, u32[]{:S(2)}) collective-permute-start(bf16[1536,512]{1,0:T(8,128)(2,1)} %get-tuple-element.533), channel_id=1, source_target_pairs={{0,16},{16,0},{1,17},{17,1},{2,18},{18,2},{3,19},{19,3},{4,20},{20... | collective-permute-start | bytes 4718600 | tf_op jit(solution)/shard_map/ppermute | solution.py:30
  1075.8 49.0 %collective-permute-start.115 = (bf16[512,1536]{1,0:T(8,128)(2,1)}, bf16[512,1536]{1,0:T(8,128)(2,1)}, u32[]{:S(2)}, u32[]{:S(2)}) collective-permute-start(bf16[512,1536]{1,0:T(8,128)(2,1)} %get-tuple-element.529), channel_id=1, source_target_pairs={{0,16},{16,0},{1,17},{17,1},{2,18},{18,2},{3,19},{19,3},{4,20},{20... | collective-permute-start | bytes 4718600 | tf_op jit(solution)/shard_map/ppermute | solution.py:30
  1113.4 45.6 %collective-permute-start.108 = (f32[1,4096]{1,0:T(1,128)}, f32[1,4096]{1,0:T(1,128)}, u32[]{:S(2)}, u32[]{:S(2)}) collective-permute-start(f32[1,4096]{1,0:T(1,128)} %bitcast.69), channel_id=1, source_target_pairs={{0,3},{1,0},{2,1},{3,2},{4,7},{5,4},{6,5},{7,6},{8,11},{9,8},{10,9... | collective-permute-start | bytes 49160 | tf_op jit(solution)/shard_map/ppermute | solution.py:26
  1120.0 46.2 %collective-permute-start.107 = (f32[1,4096]{1,0:T(1,128)}, f32[1,4096]{1,0:T(1,128)}, u32[]{:S(2)}, u32[]{:S(2)}) collective-permute-start(f32[1,4096]{1,0:T(1,128)} %bitcast.69), channel_id=1, source_target_pairs={{0,2},{1,3},{2,0},{3,1},{4,6},{5,7},{6,4},{7,5},{8,10},{9,11},{10,... | collective-permute-start | bytes 49160 | tf_op jit(solution)/shard_map/ppermute | solution.py:26
  1124.3 41.9 %collective-permute-start.106 = (f32[1,4096]{1,0:T(1,128)}, f32[1,4096]{1,0:T(1,128)}, u32[]{:S(2)}, u32[]{:S(2)}) collective-permute-start(f32[1,4096]{1,0:T(1,128)} %bitcast.69), channel_id=1, source_target_pairs={{0,1},{1,2},{2,3},{3,0},{4,5},{5,6},{6,7},{7,4},{8,9},{9,10},{10,1... | collective-permute-start | bytes 49160 | tf_op jit(solution)/shard_map/ppermute | solution.py:26
  (388 other events, 4842.0 us)
Sparse Core Ops, SparseCore 0:
  14.0 48.1 all-gather.5
  64.6 29.0 all-gather.7
  95.5 38.9 all-gather.9
  136.8 68.2 all-gather.11
  235.8 54.1 all-gather.13
  775.8 32.8 reduce-scatter.11
  811.6 27.5 reduce-scatter.9
  842.7 45.9 reduce-scatter.13
  891.7 42.9 reduce-scatter.15
  936.9 49.8 reduce-scatter.7
  1061.5 48.1 reduce-scatter.19
  1112.4 25.2 reduce-scatter.17
